TPU v7x, 256 devices: a whole 4x4x8 slice. The times are simulated.
256 devices in a mesh: dp: 8 (over y, core), head: 32 (over x, z).
Axes of the slice: x: 4, y: 4, z: 8, core: 2. Of those that a mesh axis runs over, the one named last changes fastest.
Arguments:
- queries: bfloat16 [256, 32, 8192], P(('dp', 'head')), may hold values from -0.59765625 to 0.59765625
- keys: bfloat16 [256, 32, 8192], P(('dp', 'head')), may hold values from -6 to 6
- values: bfloat16 [256, 32, 8192], P(('dp', 'head')), may hold values from -6 to 6
- gate: bfloat16 [256, 32, 8192], P(('dp', 'head')), may hold values from -6 to 6
- states: bfloat16 [256, 64, 128, 128], P('dp', 'head'), may hold values from -6 to 6
- decay: float32 [64], P('head'), may hold values from 0.002 to 0.2
- ancestors: int32 [256, 32, 32], P('dp'), may hold values from 0 to 1, as said below
- tree_sizes: int32 [256], P('dp'), may hold values from 1 to 32, as said below
- gain: float32 [8192], replicated, may hold values from 0.5 to 1.5
- out_weight: bfloat16 [8192, 6144], P(None, 'head'), may hold values from -0.0625 to 0.0625
Outputs:
- projected: bfloat16 [256, 32, 6144], P('dp', None, 'head')
Inputs may be any that keep to these rules, and one draw needn't show every extreme that they name: ancestors[r, i, j] is 1 exactly when node j is node i or an ancestor of it; every node but node 0 has a parent of lower index, node 0 is the root. Nodes 0 to tree_sizes[r] - 1 are live; some request has all 32.
All inputs are finite; a program needn't handle non-finite values.
Results may differ from a plain program's by a relative error of at most 0.0062.
Values may be sent and summed in bfloat16 or wider, within the bound.
No kernel may reach another device: no remote copies, remote signals or barrier semaphores. Data moves between devices by JAX's collectives and lax.ppermute only.
A program may use at most 128 MiB of HBM per device.

v0:
```python
import jax
import jax.numpy as jnp
from jax import lax
from jax.sharding import PartitionSpec as P


def attend(queries, keys, values, states, decay, ancestors, tree_sizes):
    count, nodes, width = queries.shape
    local_heads = states.shape[1]
    head_size = states.shape[2]
    qs = queries.reshape(count, nodes, local_heads, head_size)
    ks = keys.reshape(count, nodes, local_heads, head_size)
    vs = values.reshape(count, nodes, local_heads, head_size)
    anc = ancestors.astype(jnp.float32)
    depth = jnp.sum(anc, axis=-1)
    live = (jnp.arange(nodes, dtype=jnp.int32)[None, :] < tree_sizes[:, None]).astype(jnp.float32)
    spread = depth[:, :, None] - depth[:, None, :]
    factor = anc[:, None, :, :] * jnp.exp(-decay[None, :, None, None] * spread[:, None, :, :])
    scores = jnp.einsum("rihd,rjhd->rhij", qs, ks, preferred_element_type=jnp.float32)
    mixed = (scores * factor).astype(jnp.bfloat16)
    intra = jnp.einsum("rhij,rjhe->rihe", mixed, vs, preferred_element_type=jnp.float32)
    inter = jnp.einsum("rihd,rhde->rihe", qs, states, preferred_element_type=jnp.float32)
    inter = inter * jnp.exp(-decay[None, None, :, None] * depth[:, :, None, None])
    total = (inter + intra) * live[:, :, None, None]
    return total.reshape(count, nodes, width).astype(jnp.bfloat16)


def per_device(queries, keys, values, gate, states, decay, ancestors, tree_sizes, gain, out_weight):
    qs, ks, vs = (
        lax.all_to_all(queries, "head", split_axis=2, concat_axis=0, tiled=True),
        lax.all_to_all(keys, "head", split_axis=2, concat_axis=0, tiled=True),
        lax.all_to_all(values, "head", split_axis=2, concat_axis=0, tiled=True),
    )
    attn = attend(qs, ks, vs, states, decay, ancestors, tree_sizes)
    rows = lax.all_to_all(attn, "head", split_axis=0, concat_axis=2, tiled=True)
    wide = rows.astype(jnp.float32)
    meansq = jnp.mean(wide * wide, axis=-1, keepdims=True)
    normed = (
        wide * lax.rsqrt(meansq + 1e-06) * gain * jax.nn.sigmoid(gate.astype(jnp.float32))
    ).astype(jnp.bfloat16)
    result = jnp.einsum(
        "rnf,fo->rno",
        lax.all_gather(normed, "head", axis=0, tiled=True),
        out_weight,
        preferred_element_type=jnp.float32,
    )
    return result.astype(jnp.bfloat16)


def solution(mesh):
    return jax.shard_map(
        per_device,
        mesh=mesh,
        in_specs=(
            P(("dp", "head"), None, None),
            P(("dp", "head"), None, None),
            P(("dp", "head"), None, None),
            P(("dp", "head"), None, None),
            P("dp", "head", None, None),
            P("head"),
            P("dp", None, None),
            P("dp"),
            P(),
            P(None, "head"),
        ),
        out_specs=P("dp", None, "head"),
        check_vma=False,
    )
```

profile of v0, /device:TPU:16, one launch (start us, length us, event | category | flops | bytes accessed | tf_op | source)
XLA Modules:
  0.0 477.8 jit_solution(15844555200535435348)
XLA Ops:
  6.5 8.7 %copy.26 = bf16[1,32,8192]{1,0,2:T(2,128)(2,1)} copy(bf16[1,32,8192]{2,1,0:T(8,128)(2,1)} %param.10) | data formatting | bytes 1048576 | tf_op args[0]
  15.3 0.6 broadcast.98
  15.9 46.6 %reduce.4 = bf16[8192,32]{1,0:T(8,128)(2,1)} reduce(bf16[8192,1,32]{2,1,0:T(2,128)(2,1)} %bitcast.74, bf16[]{:T(256)} %broadcast.98), dimensions={1}, to_apply=%bitcast.62.reduce_sub_computation | reduce | bytes 1048578
  62.5 4.4 reshape.146
  66.9 11.6 %all-to-all-start = ((bf16[32,2,4096]{2,1,0:T(2,128)(2,1)}), bf16[32,2,4096]{2,1,0:T(2,128)(2,1)}, u32[]{:S(2)}, u32[]{:S(2)}) async-start(bf16[32,2,4096]{2,1,0:T(2,128)(2,1)} %reshape.146), calls=%async_computation | async-start | bytes 1048576 | tf_op jit(solution)/shard_map/all_to_all | solution.py:30
  78.5 8.6 %copy.30 = bf16[1,32,8192]{1,0,2:T(2,128)(2,1)} copy(bf16[1,32,8192]{2,1,0:T(8,128)(2,1)} %param.11) | data formatting | bytes 1048576 | tf_op args[1]
  87.1 46.6 %reduce.6 = bf16[8192,32]{1,0:T(8,128)(2,1)} reduce(bf16[8192,1,32]{2,1,0:T(2,128)(2,1)} %bitcast.79, bf16[]{:T(256)} %broadcast.98), dimensions={1}, to_apply=%bitcast.66.reduce_sub_computation | reduce | bytes 1048578
  133.7 4.4 reshape.150
  138.1 0.0 all-to-all-done
  138.1 9.9 %all-to-all-start.1 = ((bf16[32,2,4096]{2,1,0:T(2,128)(2,1)}), bf16[32,2,4096]{2,1,0:T(2,128)(2,1)}, u32[]{:S(2)}, u32[]{:S(2)}) async-start(bf16[32,2,4096]{2,1,0:T(2,128)(2,1)} %reshape.150), calls=%async_computation.1 | async-start | bytes 1048576 | tf_op jit(solution)/shard_map/all_to_all | solution.py:31
  148.0 8.6 %copy.35 = bf16[1,32,8192]{1,0,2:T(2,128)(2,1)} copy(bf16[1,32,8192]{2,1,0:T(8,128)(2,1)} %param.12) | data formatting | bytes 1048576 | tf_op args[2]
  156.6 46.6 %reduce.5 = bf16[8192,32]{1,0:T(8,128)(2,1)} reduce(bf16[8192,1,32]{2,1,0:T(2,128)(2,1)} %bitcast.75, bf16[]{:T(256)} %broadcast.98), dimensions={1}, to_apply=%bitcast.64.reduce_sub_computation | reduce | bytes 1048578
  203.2 4.4 reshape.148
  207.6 0.1 fusion.24
  207.7 0.0 all-to-all-done.1
  207.7 9.6 %all-to-all-start.2 = ((bf16[32,2,4096]{2,1,0:T(2,128)(2,1)}), bf16[32,2,4096]{2,1,0:T(2,128)(2,1)}, u32[]{:S(2)}, u32[]{:S(2)}) async-start(bf16[32,2,4096]{2,1,0:T(2,128)(2,1)} %reshape.148), calls=%async_computation.2 | async-start | bytes 1048576 | tf_op jit(solution)/shard_map/all_to_all | solution.py:32
  217.3 0.3 all-gather.2.cloned.1.call-start
  217.6 1.3 convert_reduce_fusion
  218.9 1.9 convert_element_type.54
  220.8 0.1 multiply_exponential_fusion
  220.9 1.0 broadcast_subtract_fusion
  221.9 9.7 %reshape.147 = bf16[8192,1,32]{2,1,0:T(2,128)(2,1)} reshape(bf16[32,2,4096]{2,1,0:T(2,128)(2,1)} %all-to-all-done) | data formatting | bytes 1048576
  231.7 8.7 %copy.27 = bf16[1,32,8192]{2,1,0:T(8,128)(2,1)} copy(bf16[1,32,8192]{1,0,2:T(2,128)(2,1)} %bitcast.76) | data formatting | bytes 1048576 | tf_op jit(solution)/shard_map/all_to_all | solution.py:30
  240.4 1.2 copy.50
  241.5 0.8 bitcast_bitcast_fusion.2
  242.3 2.0 reshape.143
  244.3 9.7 %reshape.151 = bf16[8192,1,32]{2,1,0:T(2,128)(2,1)} reshape(bf16[32,2,4096]{2,1,0:T(2,128)(2,1)} %all-to-all-done.1) | data formatting | bytes 1048576
  254.1 8.7 %copy.31 = bf16[1,32,8192]{2,1,0:T(8,128)(2,1)} copy(bf16[1,32,8192]{1,0,2:T(2,128)(2,1)} %bitcast.77) | data formatting | bytes 1048576 | tf_op jit(solution)/shard_map/all_to_all | solution.py:31
  262.8 1.2 copy.51
  263.9 0.8 bitcast_bitcast_fusion.1
  264.8 2.0 reshape.144
  266.7 0.0 all-to-all-done.2
  266.7 9.7 %reshape.149 = bf16[8192,1,32]{2,1,0:T(2,128)(2,1)} reshape(bf16[32,2,4096]{2,1,0:T(2,128)(2,1)} %all-to-all-done.2) | data formatting | bytes 1048576
  276.5 8.7 %copy.36 = bf16[1,32,8192]{2,1,0:T(8,128)(2,1)} copy(bf16[1,32,8192]{1,0,2:T(2,128)(2,1)} %bitcast.78) | data formatting | bytes 1048576 | tf_op jit(solution)/shard_map/all_to_all | solution.py:32
  285.2 1.2 copy.52
  286.4 0.8 bitcast_bitcast_fusion
  287.2 2.0 reshape.145
  289.2 3.4 fusion.4
  292.6 4.1 fusion.10
  296.7 1.2 copy.64
  297.9 24.5 %all_to_all.54 = bf16[32,32,256]{2,1,0:T(8,128)(2,1)S(1)} all-to-all(bf16[32,32,256]{2,1,0:T(8,128)(2,1)S(1)} %bitcast.87), channel_id=1, replica_groups=mesh['dp'=8,'head'=32] {'head'}, dimensions={0} | all-to-all | bytes 1048576 | tf_op jit(solution)/shard_map/all_to_all | solution.py:35
  322.4 0.2 fusion.11
  322.7 0.1 convert_bitcast_fusion
  322.8 0.1 copy.49
  322.9 1.1 multiply_convert_fusion
  324.0 0.0 all-gather.2.cloned.1.call-update
  324.1 137.9 %all-gather.2.cloned.1.call-done = bf16[32,32,8192]{2,1,0:T(8,128)(2,1)} async-done(((bf16[1,32,8192]{2,1,0:T(8,128)(2,1)}), bf16[32,32,8192]{2,1,0:T(8,128)(2,1)}) %all-gather.2.cloned.1.call-update) | async-done | bytes 16777232 | tf_op jit(solution)/shard_map/all_gather | solution.py:43
  462.0 8.9 %fusion.7 = bf16[32,32,192]{2,1,0:T(8,128)(2,1)} fusion(bf16[32,32,8192]{2,1,0:T(8,128)(2,1)} %all-gather.2.cloned.1.call-done, bf16[8192,192]{0,1:T(8,128)(2,1)S(1)} %copy-done), kind=kOutput, calls=%fused_computation.12 | convolution fusion | flops 3221422080 | bytes 20316160 | tf_op jit(solution)/shard_map/rnf,fo->rno/dot_general | solution.py:41
  (12 shorter events, 0.0 us)
Async XLA Ops:
  6.5 455.5 %copy-start = (bf16[8192,192]{0,1:T(8,128)(2,1)S(1)}, bf16[8192,192]{0,1:T(8,128)(2,1)}, u32[]{:S(2)}) copy-start(bf16[8192,192]{0,1:T(8,128)(2,1)} %param.19) | copy-start | bytes 9437188
  66.9 71.2 %all-to-all-start = ((bf16[32,2,4096]{2,1,0:T(2,128)(2,1)}), bf16[32,2,4096]{2,1,0:T(2,128)(2,1)}, u32[]{:S(2)}, u32[]{:S(2)}) async-start(bf16[32,2,4096]{2,1,0:T(2,128)(2,1)} %reshape.146), calls=%async_computation | async-start | bytes 1048576 | tf_op jit(solution)/shard_map/all_to_all | solution.py:30
  138.1 69.6 %all-to-all-start.1 = ((bf16[32,2,4096]{2,1,0:T(2,128)(2,1)}), bf16[32,2,4096]{2,1,0:T(2,128)(2,1)}, u32[]{:S(2)}, u32[]{:S(2)}) async-start(bf16[32,2,4096]{2,1,0:T(2,128)(2,1)} %reshape.150), calls=%async_computation.1 | async-start | bytes 1048576 | tf_op jit(solution)/shard_map/all_to_all | solution.py:31
  156.6 51.0 %copy-start.3 = (s32[32]{0:T(128)S(1)}, s32[32]{0:T(128)}, u32[]{:S(2)}) copy-start(s32[32]{0:T(128)} %param.17) | copy-start | bytes 388
  203.2 17.6 %copy-start.4 = (f32[2]{0:T(128)S(1)}, f32[2]{0:T(128)}, u32[]{:S(2)}) copy-start(f32[2]{0:T(128)} %param.15) | copy-start | bytes 28
  207.7 59.0 %all-to-all-start.2 = ((bf16[32,2,4096]{2,1,0:T(2,128)(2,1)}), bf16[32,2,4096]{2,1,0:T(2,128)(2,1)}, u32[]{:S(2)}, u32[]{:S(2)}) async-start(bf16[32,2,4096]{2,1,0:T(2,128)(2,1)} %reshape.148), calls=%async_computation.2 | async-start | bytes 1048576 | tf_op jit(solution)/shard_map/all_to_all | solution.py:32
  217.3 244.7 %all-gather.2.cloned.1.call-start = ((), (), s32[]{:S(2)}) async-start(), calls=%async_computation.4 | async-start | bytes 17301504 | tf_op jit(solution)/shard_map/all_gather | solution.py:43
  296.7 26.2 %copy-start.1 = (bf16[1,32,8192]{2,1,0:T(8,128)(2,1)S(1)}, bf16[1,32,8192]{2,1,0:T(8,128)(2,1)}, u32[]{:S(2)}) copy-start(bf16[1,32,8192]{2,1,0:T(8,128)(2,1)} %param.13) | copy-start | bytes 1572868
  296.7 26.2 %copy-start.2 = (f32[8192]{0:T(1024)S(1)}, f32[8192]{0:T(1024)}, u32[]{:S(2)}) copy-start(f32[8192]{0:T(1024)} %param.18) | copy-start | bytes 98308
Sparse Core Ops, SparseCore 0:
  324.2 137.7 all-gather.1
where the time goes:
time: 485 us; the launch traced here: 478 us
  other arithmetic  146 us (30%)
  waiting for transfers between devices  138 us (28%)
  local copies, waits for them, and re-layouts  108 us (22%)
  starting transfers between devices  31.5 us (6%)
  blocking collectives  24.5 us (5%)
  matrix products  16.5 us (3%)
  between operations  13.5 us (3%)
    unnamed x4, other arithmetic  140 us
    all_gather x1, waiting for transfers between devices, per_device(): lax.all_gather(normed, 'head', axis=0, tiled=True)  138 us
    unnamed x23, local copies, waits for them, and re-layouts  72.5 us
    all_to_all x1, blocking collectives, per_device(): rows = lax.all_to_all(attn, 'head', split_axis=0, concat_axis=2, tiled=True)  24.5 us
    all_to_all x1, starting transfers between devices, per_device(): lax.all_to_all(queries, 'head', split_axis=2, concat_axis=0, tiled=True)  11.6 us
    all_to_all x1, starting transfers between devices, per_device(): lax.all_to_all(keys, 'head', split_axis=2, concat_axis=0, tiled=True)  9.89 us
  transfers between devices with their start and end apart: 4, of which 1 were waited for; matrix products, arithmetic and copies ran while one was open for 35% of the time, Pallas kernels for 0%

commit v1 on v0

v1 whole, which is shorter than its diff:
```python
import functools
import jax
import jax.numpy as jnp
from jax import lax
from jax.experimental import pallas as pl
from jax.experimental.pallas import tpu as pltpu
from jax.sharding import PartitionSpec as P

NX = 4
NZ = 8
NODES = 32
HD = 128
PAIR = 2 * HD
QUART = 2048
COLS = 192
ROWS = NX * NODES
WIDE = QUART + 128
ZSHIFTS = (1, 7, 2, 6, 3, 5, 4)
NT = (((1,), (1,)), ((), ()))
BF = jnp.bfloat16
F32 = jnp.float32


def zsend(array, shift):
    pairs = [(x * NZ + z, x * NZ + (z + shift) % NZ) for x in range(NX) for z in range(NZ)]
    return lax.ppermute(array, "head", pairs)


def xsend(array, shift):
    pairs = [(x * NZ + z, ((x + shift) % NX) * NZ + z) for x in range(NX) for z in range(NZ)]
    return lax.ppermute(array, "head", pairs)


def split3(value):
    hi = lax.reduce_precision(value, 8, 7)
    mid = lax.reduce_precision(value - hi, 8, 7)
    return hi, mid, value - hi - mid


def attend_kernel(pos, sizes, x0, x1, x2, x3, anc_ref, msg_ref, gain_ref, u_ref, ss_ref):
    x, z = pos[0], pos[1]
    extra = msg_ref[NX * PAIR : NX * PAIR + 16, :].astype(F32)
    rates = [extra[3 * j : 3 * j + 1] + extra[3 * j + 1 : 3 * j + 2] + extra[3 * j + 2 : 3 * j + 3] for j in range(2)]
    node = lax.broadcasted_iota(jnp.int32, (NODES, HD), 0)
    for slot, part in enumerate((x0, x1, x2, x3)):
        xa = lax.rem(x - slot + NX, NX)
        row = pl.multiple_of(xa * NODES, NODES)
        anc = anc_ref[xa, 0].astype(F32)
        depth = jnp.sum(anc, axis=1, keepdims=True)
        depth_t = lax.dot_general(jnp.ones((8, NODES), BF), anc.astype(BF), NT, preferred_element_type=F32)[0:1]
        live = (node < sizes[xa * NZ + z]).astype(F32)
        total = jnp.zeros((NODES, 1), F32)
        for j in range(2):
            cols = slice(j * HD, (j + 1) * HD)
            q = part[0, :, cols]
            k = part[1, :, cols]
            v = part[2, :, cols]
            state = msg_ref[pl.ds(pl.multiple_of((xa * 2 + j) * HD, HD), HD), :]
            rate = rates[j]
            scores = lax.dot_general(q, k, NT, preferred_element_type=F32)
            factor = anc * jnp.exp(-rate[:, :NODES] * (depth - depth_t))
            mix = (scores * factor).astype(BF)
            intra = jnp.dot(mix, v, preferred_element_type=F32)
            inter = jnp.dot(q, state, preferred_element_type=F32)
            attn = (live * (inter * jnp.exp(-rate * depth) + intra)).astype(BF).astype(F32)
            total = total + jnp.sum(attn * attn, axis=1, keepdims=True)
            scale = gain_ref[:, cols] / (1.0 + jnp.exp(-part[3, :, cols].astype(F32)))
            u_ref[pl.ds(row, NODES), cols] = (attn * scale).astype(BF)
        ss_ref[pl.ds(row, NODES), :] = jnp.broadcast_to(total, (NODES, 128))


def attend(pos, sizes, parts, anc, msg, gain):
    part_spec = pl.BlockSpec((4, NODES, PAIR), lambda i, pos, sizes: (0, 0, pos[2]))
    return pl.pallas_call(
        attend_kernel,
        grid_spec=pltpu.PrefetchScalarGridSpec(
            num_scalar_prefetch=2,
            grid=(1,),
            in_specs=[part_spec] * 4
            + [
                pl.BlockSpec((NX, 1, NODES, NODES), lambda i, pos, sizes: (0, pos[1], 0, 0)),
                pl.BlockSpec((NX * PAIR + 16, HD), lambda i, pos, sizes: (0, 0)),
                pl.BlockSpec((1, PAIR), lambda i, pos, sizes: (0, pos[0] * NZ + pos[2])),
            ],
            out_specs=[
                pl.BlockSpec((ROWS, PAIR), lambda i, pos, sizes: (0, 0)),
                pl.BlockSpec((ROWS, 128), lambda i, pos, sizes: (0, 0)),
            ],
        ),
        out_shape=[
            jax.ShapeDtypeStruct((ROWS, PAIR), BF),
            jax.ShapeDtypeStruct((ROWS, 128), F32),
        ],
        cost_estimate=pl.CostEstimate(flops=100_000_000, bytes_accessed=1_000_000, transcendentals=100_000),
    )(pos, sizes, *parts, anc, msg, gain)


def gather_kernel(pos, *refs):
    us, sums, out = refs[:NZ], refs[NZ : 2 * NZ], refs[2 * NZ]
    z = pos[1]
    total = sums[0][...]
    for ref in sums[1:]:
        total = total + ref[...]
    for shift, ref in zip((0,) + ZSHIFTS, us):
        col = lax.rem(z - shift + NZ, NZ) * PAIR
        out[:, pl.ds(pl.multiple_of(col, PAIR), PAIR)] = ref[...]
    hi = total.astype(BF).astype(F32)
    mid = (total - hi).astype(BF).astype(F32)
    low = total - hi - mid
    lane = lax.broadcasted_iota(jnp.int32, (ROWS, 128), 1)
    tail = jnp.where(lane == 64, hi, jnp.where(lane == 65, mid, jnp.where(lane == 66, low, 0.0)))
    out[:, QUART:WIDE] = tail.astype(BF)


def assemble(pos, us, sums):
    return pl.pallas_call(
        gather_kernel,
        in_specs=[pl.BlockSpec(memory_space=pltpu.SMEM)] + [pl.BlockSpec(memory_space=pltpu.VMEM)] * (2 * NZ),
        out_specs=pl.BlockSpec(memory_space=pltpu.VMEM),
        out_shape=jax.ShapeDtypeStruct((ROWS, WIDE), BF),
        cost_estimate=pl.CostEstimate(flops=1_000_000, bytes_accessed=2_000_000, transcendentals=0),
    )(pos, *us, *sums)


def project_kernel(count, *refs):
    pieces, weights, outs = refs[:count], refs[count : count + NX], refs[count + NX :]
    row = 0
    for piece in pieces:
        size = piece.shape[0]
        rows = slice(row, row + size)
        u = piece[:, :QUART]
        tail = piece[:, QUART + 64 : WIDE]
        for weight, out in zip(weights, outs):
            acc = lax.dot_general(u, weight[...], NT, preferred_element_type=F32)
            out[rows, :COLS] = acc.astype(out.dtype)
            out[rows, COLS:] = tail.astype(out.dtype)
        row += size


def project(pieces, weights):
    rows = sum(p.shape[0] for p in pieces)
    flops = 2 * rows * QUART * COLS * NX
    return pl.pallas_call(
        functools.partial(project_kernel, len(pieces)),
        in_specs=[pl.BlockSpec(memory_space=pltpu.VMEM)] * (len(pieces) + NX),
        out_specs=[pl.BlockSpec(memory_space=pltpu.VMEM)] * NX,
        out_shape=[jax.ShapeDtypeStruct((rows, 256), F32)] + [jax.ShapeDtypeStruct((rows, 256), BF)] * (NX - 1),
        cost_estimate=pl.CostEstimate(flops=flops, bytes_accessed=4_000_000, transcendentals=0),
        compiler_params=pltpu.CompilerParams(vmem_limit_bytes=32 * 1024 * 1024),
    )(*pieces, *weights)


def finish_kernel(layout, pos, *refs):
    out = refs[-1]
    z = pos[1]
    for g, places in enumerate(layout):
        own, a, b, c = refs[4 * g : 4 * g + 4]
        row = 0
        for shift, first, last in places:
            size = (last - first) * NODES
            rows = slice(row, row + size)
            total = own[rows, :] + a[rows, :].astype(F32) + b[rows, :].astype(F32) + c[rows, :].astype(F32)
            squares = total[:, COLS : COLS + 1] + total[:, COLS + 1 : COLS + 2] + total[:, COLS + 2 : COLS + 3]
            scaled = total[:, :COLS] * lax.rsqrt(squares * (1.0 / 8192.0) + 1e-06)
            source = lax.rem(z - shift + 2 * NZ, NZ)
            for x in range(first, last):
                part = scaled[(x - first) * NODES : (x - first + 1) * NODES]
                out[x, source] = part.astype(BF)
            row += size


def finish(pos, groups, layout):
    flat = [a for group in groups for a in group]
    return pl.pallas_call(
        functools.partial(finish_kernel, layout),
        in_specs=[pl.BlockSpec(memory_space=pltpu.SMEM)] + [pl.BlockSpec(memory_space=pltpu.VMEM)] * len(flat),
        out_specs=pl.BlockSpec(memory_space=pltpu.VMEM),
        out_shape=jax.ShapeDtypeStruct((NX, NZ, NODES, COLS), BF),
        cost_estimate=pl.CostEstimate(flops=2_000_000, bytes_accessed=4_000_000, transcendentals=0),
        compiler_params=pltpu.CompilerParams(vmem_limit_bytes=32 * 1024 * 1024),
    )(pos, *flat)


def per_device(queries, keys, values, gate, states, decay, ancestors, tree_sizes, gain, out_weight):
    me = lax.axis_index("head")
    x, z = me // NZ, me % NZ

    four = jnp.stack([queries[0], keys[0], values[0], gate[0]])

    def quarter(shift):
        return lax.dynamic_slice_in_dim(four, ((x + shift) % NX) * QUART, QUART, axis=2)

    parts = [quarter(0)] + [xsend(quarter(d), d) for d in range(1, NX)]

    hi, mid, low = split3(decay)
    rows = jnp.stack([hi[0], mid[0], low[0], hi[1], mid[1], low[1]])
    rows = jnp.concatenate([rows, jnp.zeros((10,), F32)]).astype(BF)
    extra = jnp.broadcast_to(rows[:, None], (16, HD))
    by_z = states.reshape(NX, NZ, 2, HD, HD)

    def message(shift):
        block = lax.dynamic_index_in_dim(by_z, (z + shift) % NZ, axis=1, keepdims=False)
        return jnp.concatenate([block.reshape(NX * PAIR, HD), extra])

    messages = [message(0)] + [zsend(message(d), d) for d in ZSHIFTS]

    weight = out_weight.T
    def weight_quarter(shift):
        return lax.dynamic_slice_in_dim(weight, ((x + shift) % NX) * QUART, QUART, axis=1)

    weights = [weight_quarter(0)] + [xsend(weight_quarter(d), d) for d in range(1, NX)]

    anc = ancestors.reshape(NX, NZ, NODES, NODES)
    gain = gain.reshape(1, -1)
    us, sums = [], []
    for shift, msg in zip((0,) + ZSHIFTS, messages):
        pos = jnp.stack([x, z, (z - shift) % NZ]).astype(jnp.int32)
        u, ss = attend(pos, tree_sizes, parts, anc, msg, gain)
        us.append(u)
        sums.append(ss)
    here = jnp.stack([x, z]).astype(jnp.int32)
    own = assemble(here, us, sums)

    up = dn = own
    batches = [[own]]
    layout = [[(0, 0, NX)]]
    for step in range(1, 4):
        up, dn = zsend(up, 1), zsend(dn, -1)
        batches.append([up, dn])
        layout.append([(step, 0, NX), (-step, 0, NX)])
    half = ROWS // 2
    batches.append([zsend(up[:half], 1), zsend(dn[half:], -1)])
    layout.append([(4, 0, NX // 2), (-4, NX // 2, NX)])
    batches[1] = batches[0] + batches[1]
    layout[1] = layout[0] + layout[1]

    groups = []
    for pieces in batches[1:]:
        own_part, *others = project(pieces, weights)
        groups.append([own_part] + [xsend(p, -d) for d, p in enumerate(others, 1)])
    out = finish(here, groups, layout[1:])
    return out.reshape(NX * NZ, NODES, COLS)


def solution(mesh):
    return jax.shard_map(
        per_device,
        mesh=mesh,
        in_specs=(
            P(("dp", "head"), None, None),
            P(("dp", "head"), None, None),
            P(("dp", "head"), None, None),
            P(("dp", "head"), None, None),
            P("dp", "head", None, None),
            P("head"),
            P("dp", None, None),
            P("dp"),
            P(),
            P(None, "head"),
        ),
        out_specs=P("dp", None, "head"),
        check_vma=False,
    )
```

time: 485 us -> 182 us (0.38); the launches traced: 478 us -> 181 us
  other arithmetic: 146 us -> 3.58 us
  local copies, waits for them, and re-layouts: 108 us -> 12.2 us
  waiting for transfers between devices: 138 us -> 63.8 us
  Pallas kernels: 0 us -> 41 us
  starting transfers between devices: 31.5 us -> 60.2 us
  blocking collectives: 24.5 us -> 0 us
  matrix products: 16.5 us -> 0 us
  between operations: 13.5 us -> 0.22 us
    unnamed x4 -> x0, other arithmetic: 140 us -> none
    all_gather x1 -> x0, waiting for transfers between devices: 138 us -> none  [per_device(): lax.all_gather(normed, 'head', axis=0, tiled=True)]
    unnamed x23 -> x25, local copies, waits for them, and re-layouts: 72.5 us -> 3.74 us
    ppermute x0 -> x33, waiting for transfers between devices: none -> 63.8 us  [the longest x18 32.8 us: xsend(): return lax.ppermute(array, 'head', pairs)]
    ppermute x0 -> x33, starting transfers between devices: none -> 60.2 us  [the longest x15 36.1 us: zsend(): return lax.ppermute(array, 'head', pairs)]
    pallas_call x0 -> x14, Pallas kernels: none -> 41 us  [the longest x8 27.1 us: attend(): pl.pallas_call(attend_kernel, grid_spec=pltpu.PrefetchScalarGridSpec(num_...]
    all_to_all x3 -> x0, starting transfers between devices: 31.2 us -> none  [the longest x1 11.6 us: per_device(): lax.all_to_all(queries, 'head', split_axis=2, concat_axis=0, tiled=True)]
    all_to_all x6 -> x0, local copies, waits for them, and re-layouts: 28.6 us -> none  [the longest x2 9.53 us: per_device(): lax.all_to_all(queries, 'head', split_axis=2, concat_axis=0, tiled=True)]
  transfers between devices with their start and end apart: 4 -> 33, of which waited for: 1 -> 12; matrix products, arithmetic and copies ran while one was open for 35% -> 6% of each run, Pallas kernels for 0% -> 18%
where the time goes in v1:
time: 182 us; the launch traced here: 181 us
  waiting for transfers between devices  63.8 us (35%)
  starting transfers between devices  60.2 us (33%)
  Pallas kernels  41 us (23%)
  local copies, waits for them, and re-layouts  12.2 us (7%)
  other arithmetic  3.58 us (2%)
    ppermute x15, starting transfers between devices, zsend(): return lax.ppermute(array, 'head', pairs)  36.1 us
    ppermute x18, waiting for transfers between devices, xsend(): return lax.ppermute(array, 'head', pairs)  32.8 us
    ppermute x15, waiting for transfers between devices, zsend(): return lax.ppermute(array, 'head', pairs)  31.1 us
    pallas_call x8, Pallas kernels, attend(): pl.pallas_call(attend_kernel, grid_spec=pltpu.PrefetchScalarGridSpec(num_...  27.1 us
    ppermute x18, starting transfers between devices, xsend(): return lax.ppermute(array, 'head', pairs)  24.2 us
    pallas_call x4, Pallas kernels, project(): pl.pallas_call(functools.partial(project_kernel, len(pieces)), in_specs=[...  9.48 us
    concatenate x2, local copies, waits for them, and re-layouts, per_device(): rows = jnp.concatenate([rows, jnp.zeros((10,), F32)]).astype(BF)  3.86 us
    unnamed x25, local copies, waits for them, and re-layouts  3.74 us
  transfers between devices with their start and end apart: 33, of which 12 were waited for; matrix products, arithmetic and copies ran while one was open for 6% of the time, Pallas kernels for 18%

profile of v1, /device:TPU:16, one launch (start us, length us, event | category | flops | bytes accessed | tf_op | source)
XLA Modules:
  0.0 181.1 jit_solution(16867880425190918521)
XLA Ops:
  0.0 1.2 constant_dynamic-update-slice_fusion.3
  1.2 1.1 constant_dynamic-update-slice_fusion.2
  2.4 1.2 constant_dynamic-slice_fusion.8
  3.6 1.5 collective-permute-start
  5.1 2.7 %collective-permute-start.1 = (bf16[4,32,2048]{2,1,0:T(8,128)(2,1)S(1)}, bf16[4,32,2048]{2,1,0:T(8,128)(2,1)S(1)}, u32[]{:S(2)}, u32[]{:S(2)}) collective-permute-start(bf16[4,32,2048]{2,1,0:T(8,128)(2,1)S(1)} %get-tuple-element.84), channel_id=1, source_target_pairs={{0,16},{1,17},{2,18},{3,19},{4,20},{5,21},{6,22},{7,23},{8,24},{9,... | collective-permute-start | bytes 1572872 | tf_op jit(solution)/shard_map/ppermute | solution.py:31
  7.8 1.4 collective-permute-start.2
  10.6 3.9 %concatenate.35 = bf16[16]{0:T(256)(128)(2,1)S(1)} concatenate(bf16[1]{0:T(256)(128)(2,1)} %get-tuple-element.107, bf16[1]{0:T(256)(128)(2,1)} %get-tuple-element.111, bf16[1]{0:T(256)(128)(2,1)} %get-tuple-element.103, bf16[1]{0:T(256)(128)(2,1)} %get-tuple-element.106, bf16[1]{0:T(256)(128)(2,1)} %get-tuple-element.112, bf16[1]{0:T(256)(128)(2,1)} %get-tuple-element.102, ...), dimensions={0} | concatenate | bytes 64 | tf_op jit(solution)/shard_map/concatenate | solution.py:197
  14.4 1.7 constant_dynamic-slice_fusion
  16.1 1.7 pad_maximum_fusion.7
  17.7 1.9 %collective-permute-start.3 = (bf16[1040,128]{1,0:T(8,128)(2,1)}, bf16[1040,128]{1,0:T(8,128)(2,1)}, u32[]{:S(2)}, u32[]{:S(2)}) collective-permute-start(bf16[1040,128]{1,0:T(8,128)(2,1)} %get-tuple-element.88), channel_id=1, source_target_pairs={{0,1},{1,2},{2,3},{3,4},{4,5},{5,6},{6,7},{7,0},{8,9},{9,10},{10,1... | collective-permute-start | bytes 798728 | tf_op jit(solution)/shard_map/ppermute | solution.py:26
  19.7 3.9 %collective-permute-start.4 = (bf16[1040,128]{1,0:T(8,128)(2,1)}, bf16[1040,128]{1,0:T(8,128)(2,1)}, u32[]{:S(2)}, u32[]{:S(2)}) collective-permute-start(bf16[1040,128]{1,0:T(8,128)(2,1)} %get-tuple-element.89), channel_id=1, source_target_pairs={{0,7},{1,0},{2,1},{3,2},{4,3},{5,4},{6,5},{7,6},{8,15},{9,8},{10,9... | collective-permute-start | bytes 798728 | tf_op jit(solution)/shard_map/ppermute | solution.py:26
  24.2 5.3 %collective-permute-done.3.msg_ref = bf16[1040,128]{1,0:T(8,128)(2,1)} collective-permute-done((bf16[1040,128]{1,0:T(8,128)(2,1)}, bf16[1040,128]{1,0:T(8,128)(2,1)}, u32[]{:S(2)}, u32[]{:S(2)}) %collective-permute-start.3) | collective-permute-done | bytes 266272 | tf_op jit(solution)/shard_map/ppermute | solution.py:26
  30.1 4.1 %collective-permute-start.6 = (bf16[1040,128]{1,0:T(8,128)(2,1)}, bf16[1040,128]{1,0:T(8,128)(2,1)}, u32[]{:S(2)}, u32[]{:S(2)}) collective-permute-start(bf16[1040,128]{1,0:T(8,128)(2,1)} %get-tuple-element.91), channel_id=1, source_target_pairs={{0,6},{1,7},{2,0},{3,1},{4,2},{5,3},{6,4},{7,5},{8,14},{9,15},{10,... | collective-permute-start | bytes 798728 | tf_op jit(solution)/shard_map/ppermute | solution.py:26
  34.3 5.0 %collective-permute-start.8 = (bf16[1040,128]{1,0:T(8,128)(2,1)S(1)}, bf16[1040,128]{1,0:T(8,128)(2,1)S(1)}, u32[]{:S(2)}, u32[]{:S(2)}) collective-permute-start(bf16[1040,128]{1,0:T(8,128)(2,1)S(1)} %get-tuple-element.93), channel_id=1, source_target_pairs={{0,5},{1,6},{2,7},{3,0},{4,1},{5,2},{6,3},{7,4},{8,13},{9,14},{10,... | collective-permute-start | bytes 798728 | tf_op jit(solution)/shard_map/ppermute | solution.py:26
  39.3 4.3 %collective-permute-start.9 = (bf16[1040,128]{1,0:T(8,128)(2,1)S(1)}, bf16[1040,128]{1,0:T(8,128)(2,1)S(1)}, u32[]{:S(2)}, u32[]{:S(2)}) collective-permute-start(bf16[1040,128]{1,0:T(8,128)(2,1)S(1)} %get-tuple-element.87), channel_id=1, source_target_pairs={{0,4},{1,5},{2,6},{3,7},{4,0},{5,1},{6,2},{7,3},{8,12},{9,13},{10,... | collective-permute-start | bytes 798728 | tf_op jit(solution)/shard_map/ppermute | solution.py:26
  44.3 3.4 %shard_map.100 = (bf16[128,256]{1,0:T(8,128)(2,1)}, f32[128,128]{1,0:T(8,128)}) custom-call(s32[3]{0:T(128)} %get-tuple-element.101.pos, s32[32]{0:T(128)} %sizes.15, bf16[4,32,2048]{2,1,0:T(8,128)(2,1)} %get-tuple-element.86.x0, bf16[4,32,2048]{2,1,0:T(8,128)(2,1)} %copy-done.2, bf16[4,32,2048]{2,1,0:T(8,128)(2,1)} %copy-done.3, ...), custom_call_target="tpu_custom_call" | custom-call | flops 100000000 | bytes 1000000 | tf_op jit(solution)/shard_map/pallas_call | solution.py:74
  47.7 3.4 %shard_map.101 = (bf16[128,256]{1,0:T(8,128)(2,1)}, f32[128,128]{1,0:T(8,128)}) custom-call(s32[3]{0:T(128)} %get-tuple-element.100.pos, s32[32]{0:T(128)} %sizes.15, bf16[4,32,2048]{2,1,0:T(8,128)(2,1)} %get-tuple-element.86.x0, bf16[4,32,2048]{2,1,0:T(8,128)(2,1)} %copy-done.2, bf16[4,32,2048]{2,1,0:T(8,128)(2,1)} %copy-done.3, ...), custom_call_target="tpu_custom_call" | custom-call | flops 100000000 | bytes 1000000 | tf_op jit(solution)/shard_map/pallas_call | solution.py:74
  51.0 3.4 %shard_map.102 = (bf16[128,256]{1,0:T(8,128)(2,1)}, f32[128,128]{1,0:T(8,128)}) custom-call(s32[3]{0:T(128)} %get-tuple-element.99.pos, s32[32]{0:T(128)} %sizes.15, bf16[4,32,2048]{2,1,0:T(8,128)(2,1)} %get-tuple-element.86.x0, bf16[4,32,2048]{2,1,0:T(8,128)(2,1)} %copy-done.2, bf16[4,32,2048]{2,1,0:T(8,128)(2,1)} %copy-done.3, ...), custom_call_target="tpu_custom_call" | custom-call | flops 100000000 | bytes 1000000 | tf_op jit(solution)/shard_map/pallas_call | solution.py:74
  54.4 3.4 %shard_map.103 = (bf16[128,256]{1,0:T(8,128)(2,1)}, f32[128,128]{1,0:T(8,128)}) custom-call(s32[3]{0:T(128)} %get-tuple-element.98.pos, s32[32]{0:T(128)} %sizes.15, bf16[4,32,2048]{2,1,0:T(8,128)(2,1)} %get-tuple-element.86.x0, bf16[4,32,2048]{2,1,0:T(8,128)(2,1)} %copy-done.2, bf16[4,32,2048]{2,1,0:T(8,128)(2,1)} %copy-done.3, ...), custom_call_target="tpu_custom_call" | custom-call | flops 100000000 | bytes 1000000 | tf_op jit(solution)/shard_map/pallas_call | solution.py:74
  57.7 3.4 %shard_map.104 = (bf16[128,256]{1,0:T(8,128)(2,1)}, f32[128,128]{1,0:T(8,128)}) custom-call(s32[3]{0:T(128)} %get-tuple-element.97.pos, s32[32]{0:T(128)} %sizes.15, bf16[4,32,2048]{2,1,0:T(8,128)(2,1)} %get-tuple-element.86.x0, bf16[4,32,2048]{2,1,0:T(8,128)(2,1)} %copy-done.2, bf16[4,32,2048]{2,1,0:T(8,128)(2,1)} %copy-done.3, ...), custom_call_target="tpu_custom_call" | custom-call | flops 100000000 | bytes 1000000 | tf_op jit(solution)/shard_map/pallas_call | solution.py:74
  61.1 6.3 %collective-permute-done.7.msg_ref = bf16[1040,128]{1,0:T(8,128)(2,1)} collective-permute-done((bf16[1040,128]{1,0:T(8,128)(2,1)}, bf16[1040,128]{1,0:T(8,128)(2,1)}, u32[]{:S(2)}, u32[]{:S(2)}) %collective-permute-start.7) | collective-permute-done | bytes 266272 | tf_op jit(solution)/shard_map/ppermute | solution.py:26
  67.4 3.4 %shard_map.105 = (bf16[128,256]{1,0:T(8,128)(2,1)}, f32[128,128]{1,0:T(8,128)}) custom-call(s32[3]{0:T(128)} %get-tuple-element.96.pos, s32[32]{0:T(128)} %sizes.15, bf16[4,32,2048]{2,1,0:T(8,128)(2,1)} %get-tuple-element.86.x0, bf16[4,32,2048]{2,1,0:T(8,128)(2,1)} %copy-done.2, bf16[4,32,2048]{2,1,0:T(8,128)(2,1)} %copy-done.3, ...), custom_call_target="tpu_custom_call" | custom-call | flops 100000000 | bytes 1000000 | tf_op jit(solution)/shard_map/pallas_call | solution.py:74
  71.4 3.4 %shard_map.106 = (bf16[128,256]{1,0:T(8,128)(2,1)}, f32[128,128]{1,0:T(8,128)}) custom-call(s32[3]{0:T(128)} %get-tuple-element.95.pos, s32[32]{0:T(128)} %sizes.15, bf16[4,32,2048]{2,1,0:T(8,128)(2,1)} %get-tuple-element.86.x0, bf16[4,32,2048]{2,1,0:T(8,128)(2,1)} %copy-done.2, bf16[4,32,2048]{2,1,0:T(8,128)(2,1)} %copy-done.3, ...), custom_call_target="tpu_custom_call" | custom-call | flops 100000000 | bytes 1000000 | tf_op jit(solution)/shard_map/pallas_call | solution.py:74
  75.5 3.6 %shard_map.107 = (bf16[128,256]{1,0:T(8,128)(2,1)}, f32[128,128]{1,0:T(8,128)}) custom-call(s32[3]{0:T(128)} %get-tuple-element.69.pos, s32[32]{0:T(128)} %sizes.15, bf16[4,32,2048]{2,1,0:T(8,128)(2,1)} %get-tuple-element.86.x0, bf16[4,32,2048]{2,1,0:T(8,128)(2,1)} %copy-done.2, bf16[4,32,2048]{2,1,0:T(8,128)(2,1)} %copy-done.3, ...), custom_call_target="tpu_custom_call" | custom-call | flops 100000000 | bytes 1000000 | tf_op jit(solution)/shard_map/pallas_call | solution.py:74
  79.1 2.2 %shard_map.108.refs_0_ = bf16[128,2176]{1,0:T(8,128)(2,1)} custom-call(s32[2]{0:T(128)} %pad_add_fusion.pos, bf16[128,256]{1,0:T(8,128)(2,1)} %get-tuple-element.37.refs_0_, bf16[128,256]{1,0:T(8,128)(2,1)} %get-tuple-element.38.refs_1_, bf16[128,256]{1,0:T(8,128)(2,1)} %get-tuple-element.39.refs_2_, bf16[128,256]{1,0:T(8,128)(2,1)} %get-tuple-element.40.refs_3_, ...), custom_call_target="tpu_custom_call" | custom-call | flops 1000000 | bytes 2000000 | tf_op jit(solution)/shard_map/pallas_call | solution.py:116
  81.3 6.1 %collective-permute-start.10 = (bf16[128,2176]{1,0:T(8,128)(2,1)}, bf16[128,2176]{1,0:T(8,128)(2,1)S(1)}, u32[]{:S(2)}, u32[]{:S(2)}) collective-permute-start(bf16[128,2176]{1,0:T(8,128)(2,1)} %shard_map.108.refs_0_), channel_id=1, source_target_pairs={{0,1},{1,2},{2,3},{3,4},{4,5},{5,6},{6,7},{7,0},{8,9},{9,10},{10,1... | collective-permute-start | bytes 1671176 | tf_op jit(solution)/shard_map/ppermute | solution.py:26
  87.4 12.1 %collective-permute-done.10.refs_1_ = bf16[128,2176]{1,0:T(8,128)(2,1)S(1)} collective-permute-done((bf16[128,2176]{1,0:T(8,128)(2,1)}, bf16[128,2176]{1,0:T(8,128)(2,1)S(1)}, u32[]{:S(2)}, u32[]{:S(2)}) %collective-permute-start.10) | collective-permute-done | bytes 557088 | tf_op jit(solution)/shard_map/ppermute | solution.py:26
  99.6 2.4 %collective-permute-start.18 = (bf16[128,2176]{1,0:T(8,128)(2,1)S(1)}, bf16[128,2176]{1,0:T(8,128)(2,1)S(1)}, u32[]{:S(2)}, u32[]{:S(2)}) collective-permute-start(bf16[128,2176]{1,0:T(8,128)(2,1)S(1)} %collective-permute-done.10.refs_1_), channel_id=1, source_target_pairs={{0,1},{1,2},{2,3},{3,4},{4,5},{5,6},{6,7},{7,0},{8,9},{9,10},{10,1... | collective-permute-start | bytes 1671176 | tf_op jit(solution)/shard_map/ppermute | solution.py:26
  102.0 1.2 collective-permute-start.19
  103.6 2.2 %collective-permute-start.13 = (bf16[192,2048]{1,0:T(8,128)(2,1)S(1)}, bf16[192,2048]{1,0:T(8,128)(2,1)S(1)}, u32[]{:S(2)}, u32[]{:S(2)}) collective-permute-start(bf16[192,2048]{1,0:T(8,128)(2,1)S(1)} %get-tuple-element.74), channel_id=1, source_target_pairs={{0,16},{1,17},{2,18},{3,19},{4,20},{5,21},{6,22},{7,23},{8,24},{9,... | collective-permute-start | bytes 2359304 | tf_op jit(solution)/shard_map/ppermute | solution.py:31
  106.9 7.4 %collective-permute-done.18.refs_0_ = bf16[128,2176]{1,0:T(8,128)(2,1)S(1)} collective-permute-done((bf16[128,2176]{1,0:T(8,128)(2,1)S(1)}, bf16[128,2176]{1,0:T(8,128)(2,1)S(1)}, u32[]{:S(2)}, u32[]{:S(2)}) %collective-permute-start.18) | collective-permute-done | bytes 557088 | tf_op jit(solution)/shard_map/ppermute | solution.py:26
  114.2 1.2 collective-permute-start.23
  115.4 2.5 %collective-permute-start.24 = (bf16[128,2176]{1,0:T(8,128)(2,1)S(1)}, bf16[128,2176]{1,0:T(8,128)(2,1)S(1)}, u32[]{:S(2)}, u32[]{:S(2)}) collective-permute-start(bf16[128,2176]{1,0:T(8,128)(2,1)S(1)} %collective-permute-done.19.refs_1_), channel_id=1, source_target_pairs={{0,7},{1,0},{2,1},{3,2},{4,3},{5,4},{6,5},{7,6},{8,15},{9,8},{10,9... | collective-permute-start | bytes 1671176 | tf_op jit(solution)/shard_map/ppermute | solution.py:26
  117.8 21.9 %collective-permute-done.12.refs_4_.refs_3_ = bf16[192,2048]{1,0:T(8,128)(2,1)S(1)} collective-permute-done((bf16[192,2048]{1,0:T(8,128)(2,1)S(1)}, bf16[192,2048]{1,0:T(8,128)(2,1)S(1)}, u32[]{:S(2)}, u32[]{:S(2)}) %collective-permute-start.12) | collective-permute-done | bytes 786464 | tf_op jit(solution)/shard_map/ppermute | solution.py:31
  140.4 3.1 %shard_map.109 = (f32[384,256]{1,0:T(8,128)S(1)}, bf16[384,256]{1,0:T(8,128)(2,1)S(1)}, bf16[384,256]{1,0:T(8,128)(2,1)S(1)}, bf16[384,256]{1,0:T(8,128)(2,1)S(1)}) custom-call(bf16[128,2176]{1,0:T(8,128)(2,1)S(1)} %copy-done, bf16[128,2176]{1,0:T(8,128)(2,1)S(1)} %collective-permute-done.10.refs_1_, bf16[128,2176]{1,0:T(8,128)(2,1)S(1)} %collective-permute-done.11.refs_2_, ...), custom_call_target="tpu_custom_call" | custom-call | flops 1207959552 | bytes 4000000 | tf_op jit(solution)/shard_map/pallas_call | solution.py:143
  143.5 2.4 %collective-permute-start.15 = (bf16[384,256]{1,0:T(8,128)(2,1)S(1)}, bf16[384,256]{1,0:T(8,128)(2,1)S(1)}, u32[]{:S(2)}, u32[]{:S(2)}) collective-permute-start(bf16[384,256]{1,0:T(8,128)(2,1)S(1)} %get-tuple-element.54), channel_id=1, source_target_pairs={{0,24},{1,25},{2,26},{3,27},{4,28},{5,29},{6,30},{7,31},{8,0},{9,1... | collective-permute-start | bytes 589832 | tf_op jit(solution)/shard_map/ppermute | solution.py:31
  146.6 2.8 %collective-permute-start.29 = (bf16[64,2176]{1,0:T(8,128)(2,1)S(1)}, bf16[64,2176]{1,0:T(8,128)(2,1)S(1)}, u32[]{:S(2)}, u32[]{:S(2)}) collective-permute-start(bf16[64,2176]{1,0:T(8,128)(2,1)S(1)} %slice.39), channel_id=1, source_target_pairs={{0,7},{1,0},{2,1},{3,2},{4,3},{5,4},{6,5},{7,6},{8,15},{9,8},{10,9... | collective-permute-start | bytes 835592 | tf_op jit(solution)/shard_map/ppermute | solution.py:26
  150.3 2.1 %shard_map.110 = (f32[256,256]{1,0:T(8,128)S(1)}, bf16[256,256]{1,0:T(8,128)(2,1)S(1)}, bf16[256,256]{1,0:T(8,128)(2,1)S(1)}, bf16[256,256]{1,0:T(8,128)(2,1)S(1)}) custom-call(bf16[128,2176]{1,0:T(8,128)(2,1)S(1)} %collective-permute-done.18.refs_0_, bf16[128,2176]{1,0:T(8,128)(2,1)S(1)} %collective-permute-done.19.refs_1_, ...), custom_call_target="tpu_custom_call" | custom-call | flops 805306368 | bytes 4000000 | tf_op jit(solution)/shard_map/pallas_call | solution.py:143
  152.4 2.3 %collective-permute-done.15.refs_1_ = bf16[384,256]{1,0:T(8,128)(2,1)S(1)} collective-permute-done((bf16[384,256]{1,0:T(8,128)(2,1)S(1)}, bf16[384,256]{1,0:T(8,128)(2,1)S(1)}, u32[]{:S(2)}, u32[]{:S(2)}) %collective-permute-start.15) | collective-permute-done | bytes 196640 | tf_op jit(solution)/shard_map/ppermute | solution.py:31
  154.7 3.7 %collective-permute-start.20 = (bf16[256,256]{1,0:T(8,128)(2,1)S(1)}, bf16[256,256]{1,0:T(8,128)(2,1)S(1)}, u32[]{:S(2)}, u32[]{:S(2)}) collective-permute-start(bf16[256,256]{1,0:T(8,128)(2,1)S(1)} %get-tuple-element.58), channel_id=1, source_target_pairs={{0,24},{1,25},{2,26},{3,27},{4,28},{5,29},{6,30},{7,31},{8,0},{9,1... | collective-permute-start | bytes 393224 | tf_op jit(solution)/shard_map/ppermute | solution.py:31
  158.3 2.1 %shard_map.111 = (f32[256,256]{1,0:T(8,128)S(1)}, bf16[256,256]{1,0:T(8,128)(2,1)S(1)}, bf16[256,256]{1,0:T(8,128)(2,1)S(1)}, bf16[256,256]{1,0:T(8,128)(2,1)S(1)}) custom-call(bf16[128,2176]{1,0:T(8,128)(2,1)S(1)} %collective-permute-done.23.refs_0_, bf16[128,2176]{1,0:T(8,128)(2,1)S(1)} %collective-permute-done.24.refs_1_, ...), custom_call_target="tpu_custom_call" | custom-call | flops 805306368 | bytes 4000000 | tf_op jit(solution)/shard_map/pallas_call | solution.py:143
  161.5 3.1 %collective-permute-start.25 = (bf16[256,256]{1,0:T(8,128)(2,1)S(1)}, bf16[256,256]{1,0:T(8,128)(2,1)S(1)}, u32[]{:S(2)}, u32[]{:S(2)}) collective-permute-start(bf16[256,256]{1,0:T(8,128)(2,1)S(1)} %get-tuple-element.62), channel_id=1, source_target_pairs={{0,24},{1,25},{2,26},{3,27},{4,28},{5,29},{6,30},{7,31},{8,0},{9,1... | collective-permute-start | bytes 393224 | tf_op jit(solution)/shard_map/ppermute | solution.py:31
  164.6 1.6 collective-permute-start.26
  166.2 2.1 %shard_map.112 = (f32[128,256]{1,0:T(8,128)S(1)}, bf16[128,256]{1,0:T(8,128)(2,1)S(1)}, bf16[128,256]{1,0:T(8,128)(2,1)S(1)}, bf16[128,256]{1,0:T(8,128)(2,1)S(1)}) custom-call(bf16[64,2176]{1,0:T(8,128)(2,1)S(1)} %collective-permute-done.28.refs_0_, bf16[64,2176]{1,0:T(8,128)(2,1)S(1)} %collective-permute-done.29.refs_1_, ...), custom_call_target="tpu_custom_call" | custom-call | flops 402653184 | bytes 4000000 | tf_op jit(solution)/shard_map/pallas_call | solution.py:143
  168.3 3.3 %collective-permute-start.30 = (bf16[128,256]{1,0:T(8,128)(2,1)S(1)}, bf16[128,256]{1,0:T(8,128)(2,1)S(1)}, u32[]{:S(2)}, u32[]{:S(2)}) collective-permute-start(bf16[128,256]{1,0:T(8,128)(2,1)S(1)} %get-tuple-element.66), channel_id=1, source_target_pairs={{0,24},{1,25},{2,26},{3,27},{4,28},{5,29},{6,30},{7,31},{8,0},{9,1... | collective-permute-start | bytes 196616 | tf_op jit(solution)/shard_map/ppermute | solution.py:31
  172.7 3.0 %collective-permute-done.27.refs_11_ = bf16[256,256]{1,0:T(8,128)(2,1)S(1)} collective-permute-done((bf16[256,256]{1,0:T(8,128)(2,1)S(1)}, bf16[256,256]{1,0:T(8,128)(2,1)S(1)}, u32[]{:S(2)}, u32[]{:S(2)}) %collective-permute-start.27) | collective-permute-done | bytes 131104 | tf_op jit(solution)/shard_map/ppermute | solution.py:31
  175.7 2.8 %collective-permute-done.31.refs_14_ = bf16[128,256]{1,0:T(8,128)(2,1)S(1)} collective-permute-done((bf16[128,256]{1,0:T(8,128)(2,1)S(1)}, bf16[128,256]{1,0:T(8,128)(2,1)S(1)}, u32[]{:S(2)}, u32[]{:S(2)}) %collective-permute-start.31) | collective-permute-done | bytes 65568 | tf_op jit(solution)/shard_map/ppermute | solution.py:31
  178.8 2.3 %shard_map.113 = bf16[4,8,32,192]{3,2,1,0:T(8,128)(2,1)} custom-call(s32[2]{0:T(128)S(1)} %copy-done.1, f32[384,256]{1,0:T(8,128)S(1)} %get-tuple-element.53.refs_0_, bf16[384,256]{1,0:T(8,128)(2,1)S(1)} %collective-permute-done.15.refs_1_, bf16[384,256]{1,0:T(8,128)(2,1)S(1)} %collective-permute-done.16.refs_2_, ...), custom_call_target="tpu_custom_call" | custom-call | flops 2000000 | bytes 4000000 | tf_op jit(solution)/shard_map/pallas_call | solution.py:174
  (73 shorter events, 10.7 us)
Async XLA Ops:
  0.0 2.3 %copy-start.6 = (bf16[1,32,8192]{2,1,0:T(8,128)(2,1)S(1)}, bf16[1,32,8192]{2,1,0:T(8,128)(2,1)}, u32[]{:S(2)}) copy-start(bf16[1,32,8192]{2,1,0:T(8,128)(2,1)} %param.12) | copy-start | bytes 1572868
  0.0 2.3 %copy-start.7 = (bf16[1,32,8192]{2,1,0:T(8,128)(2,1)S(1)}, bf16[1,32,8192]{2,1,0:T(8,128)(2,1)}, u32[]{:S(2)}) copy-start(bf16[1,32,8192]{2,1,0:T(8,128)(2,1)} %param.13) | copy-start | bytes 1572868
  2.4 6.9 %copy-start.10 = (f32[2]{0:T(128)S(1)}, f32[2]{0:T(128)}, u32[]{:S(2)}) copy-start(f32[2]{0:T(128)} %param.15) | copy-start | bytes 28
  3.6 30.7 %collective-permute-start = (bf16[4,32,2048]{2,1,0:T(8,128)(2,1)}, bf16[4,32,2048]{2,1,0:T(8,128)(2,1)S(1)}, u32[]{:S(2)}, u32[]{:S(2)}) collective-permute-start(bf16[4,32,2048]{2,1,0:T(8,128)(2,1)} %get-tuple-element.85), channel_id=1, source_target_pairs={{0,8},{1,9},{2,10},{3,11},{4,12},{5,13},{6,14},{7,15},{8,16},{9,17... | collective-permute-start | bytes 1572872 | tf_op jit(solution)/shard_map/ppermute | solution.py:31
  5.1 29.2 %collective-permute-start.1 = (bf16[4,32,2048]{2,1,0:T(8,128)(2,1)S(1)}, bf16[4,32,2048]{2,1,0:T(8,128)(2,1)S(1)}, u32[]{:S(2)}, u32[]{:S(2)}) collective-permute-start(bf16[4,32,2048]{2,1,0:T(8,128)(2,1)S(1)} %get-tuple-element.84), channel_id=1, source_target_pairs={{0,16},{1,17},{2,18},{3,19},{4,20},{5,21},{6,22},{7,23},{8,24},{9,... | collective-permute-start | bytes 1572872 | tf_op jit(solution)/shard_map/ppermute | solution.py:31
  7.8 31.5 %collective-permute-start.2 = (bf16[4,32,2048]{2,1,0:T(8,128)(2,1)S(1)}, bf16[4,32,2048]{2,1,0:T(8,128)(2,1)S(1)}, u32[]{:S(2)}, u32[]{:S(2)}) collective-permute-start(bf16[4,32,2048]{2,1,0:T(8,128)(2,1)S(1)} %get-tuple-element.83), channel_id=1, source_target_pairs={{0,24},{1,25},{2,26},{3,27},{4,28},{5,29},{6,30},{7,31},{8,0},{9,1... | collective-permute-start | bytes 1572872 | tf_op jit(solution)/shard_map/ppermute | solution.py:31
  17.7 11.7 %collective-permute-start.3 = (bf16[1040,128]{1,0:T(8,128)(2,1)}, bf16[1040,128]{1,0:T(8,128)(2,1)}, u32[]{:S(2)}, u32[]{:S(2)}) collective-permute-start(bf16[1040,128]{1,0:T(8,128)(2,1)} %get-tuple-element.88), channel_id=1, source_target_pairs={{0,1},{1,2},{2,3},{3,4},{4,5},{5,6},{6,7},{7,0},{8,9},{9,10},{10,1... | collective-permute-start | bytes 798728 | tf_op jit(solution)/shard_map/ppermute | solution.py:26
  19.7 10.5 %collective-permute-start.4 = (bf16[1040,128]{1,0:T(8,128)(2,1)}, bf16[1040,128]{1,0:T(8,128)(2,1)}, u32[]{:S(2)}, u32[]{:S(2)}) collective-permute-start(bf16[1040,128]{1,0:T(8,128)(2,1)} %get-tuple-element.89), channel_id=1, source_target_pairs={{0,7},{1,0},{2,1},{3,2},{4,3},{5,4},{6,5},{7,6},{8,15},{9,8},{10,9... | collective-permute-start | bytes 798728 | tf_op jit(solution)/shard_map/ppermute | solution.py:26
  29.5 24.9 %collective-permute-start.5 = (bf16[1040,128]{1,0:T(8,128)(2,1)}, bf16[1040,128]{1,0:T(8,128)(2,1)}, u32[]{:S(2)}, u32[]{:S(2)}) collective-permute-start(bf16[1040,128]{1,0:T(8,128)(2,1)} %get-tuple-element.90), channel_id=1, source_target_pairs={{0,2},{1,3},{2,4},{3,5},{4,6},{5,7},{6,0},{7,1},{8,10},{9,11},{10,... | collective-permute-start | bytes 798728 | tf_op jit(solution)/shard_map/ppermute | solution.py:26
  30.1 27.6 %collective-permute-start.6 = (bf16[1040,128]{1,0:T(8,128)(2,1)}, bf16[1040,128]{1,0:T(8,128)(2,1)}, u32[]{:S(2)}, u32[]{:S(2)}) collective-permute-start(bf16[1040,128]{1,0:T(8,128)(2,1)} %get-tuple-element.91), channel_id=1, source_target_pairs={{0,6},{1,7},{2,0},{3,1},{4,2},{5,3},{6,4},{7,5},{8,14},{9,15},{10,... | collective-permute-start | bytes 798728 | tf_op jit(solution)/shard_map/ppermute | solution.py:26
  34.3 10.0 %copy-start.2 = (bf16[4,32,2048]{2,1,0:T(8,128)(2,1)}, bf16[4,32,2048]{2,1,0:T(8,128)(2,1)S(1)}, u32[]{:S(2)}) copy-start(bf16[4,32,2048]{2,1,0:T(8,128)(2,1)S(1)} %collective-permute-done.x1) | copy-start | bytes 1572868
  34.3 33.1 %collective-permute-start.7 = (bf16[1040,128]{1,0:T(8,128)(2,1)}, bf16[1040,128]{1,0:T(8,128)(2,1)}, u32[]{:S(2)}, u32[]{:S(2)}) collective-permute-start(bf16[1040,128]{1,0:T(8,128)(2,1)} %get-tuple-element.92), channel_id=1, source_target_pairs={{0,3},{1,4},{2,5},{3,6},{4,7},{5,0},{6,1},{7,2},{8,11},{9,12},{10,... | collective-permute-start | bytes 798728 | tf_op jit(solution)/shard_map/ppermute | solution.py:26
  34.3 10.0 %copy-start.3 = (bf16[4,32,2048]{2,1,0:T(8,128)(2,1)}, bf16[4,32,2048]{2,1,0:T(8,128)(2,1)S(1)}, u32[]{:S(2)}) copy-start(bf16[4,32,2048]{2,1,0:T(8,128)(2,1)S(1)} %collective-permute-done.1.x2) | copy-start | bytes 1572868
  34.3 36.4 %collective-permute-start.8 = (bf16[1040,128]{1,0:T(8,128)(2,1)S(1)}, bf16[1040,128]{1,0:T(8,128)(2,1)S(1)}, u32[]{:S(2)}, u32[]{:S(2)}) collective-permute-start(bf16[1040,128]{1,0:T(8,128)(2,1)S(1)} %get-tuple-element.93), channel_id=1, source_target_pairs={{0,5},{1,6},{2,7},{3,0},{4,1},{5,2},{6,3},{7,4},{8,13},{9,14},{10,... | collective-permute-start | bytes 798728 | tf_op jit(solution)/shard_map/ppermute | solution.py:26
  39.3 5.0 %copy-start.4 = (bf16[4,32,2048]{2,1,0:T(8,128)(2,1)}, bf16[4,32,2048]{2,1,0:T(8,128)(2,1)S(1)}, u32[]{:S(2)}) copy-start(bf16[4,32,2048]{2,1,0:T(8,128)(2,1)S(1)} %collective-permute-done.2.x3) | copy-start | bytes 1572868
  39.3 35.5 %collective-permute-start.9 = (bf16[1040,128]{1,0:T(8,128)(2,1)S(1)}, bf16[1040,128]{1,0:T(8,128)(2,1)S(1)}, u32[]{:S(2)}, u32[]{:S(2)}) collective-permute-start(bf16[1040,128]{1,0:T(8,128)(2,1)S(1)} %get-tuple-element.87), channel_id=1, source_target_pairs={{0,4},{1,5},{2,6},{3,7},{4,0},{5,1},{6,2},{7,3},{8,12},{9,13},{10,... | collective-permute-start | bytes 798728 | tf_op jit(solution)/shard_map/ppermute | solution.py:26
  70.7 0.7 copy-start.9
  74.8 0.7 copy-start.8
  75.5 27.7 %copy-start.5 = (bf16[8192,192]{0,1:T(8,128)(2,1)S(1)}, bf16[8192,192]{0,1:T(8,128)(2,1)}, u32[]{:S(2)}) copy-start(bf16[8192,192]{0,1:T(8,128)(2,1)} %param.19) | copy-start | bytes 9437188
  81.3 59.1 %copy-start = (bf16[128,2176]{1,0:T(8,128)(2,1)S(1)}, bf16[128,2176]{1,0:T(8,128)(2,1)}, u32[]{:S(2)}) copy-start(bf16[128,2176]{1,0:T(8,128)(2,1)} %shard_map.108.refs_0_) | copy-start | bytes 1671172
  81.3 18.3 %collective-permute-start.10 = (bf16[128,2176]{1,0:T(8,128)(2,1)}, bf16[128,2176]{1,0:T(8,128)(2,1)S(1)}, u32[]{:S(2)}, u32[]{:S(2)}) collective-permute-start(bf16[128,2176]{1,0:T(8,128)(2,1)} %shard_map.108.refs_0_), channel_id=1, source_target_pairs={{0,1},{1,2},{2,3},{3,4},{4,5},{5,6},{6,7},{7,0},{8,9},{9,10},{10,1... | collective-permute-start | bytes 1671176 | tf_op jit(solution)/shard_map/ppermute | solution.py:26
  87.4 14.5 %collective-permute-start.11 = (bf16[128,2176]{1,0:T(8,128)(2,1)}, bf16[128,2176]{1,0:T(8,128)(2,1)S(1)}, u32[]{:S(2)}, u32[]{:S(2)}) collective-permute-start(bf16[128,2176]{1,0:T(8,128)(2,1)} %shard_map.108.refs_0_), channel_id=1, source_target_pairs={{0,7},{1,0},{2,1},{3,2},{4,3},{5,4},{6,5},{7,6},{8,15},{9,8},{10,9... | collective-permute-start | bytes 1671176 | tf_op jit(solution)/shard_map/ppermute | solution.py:26
  99.6 14.7 %collective-permute-start.18 = (bf16[128,2176]{1,0:T(8,128)(2,1)S(1)}, bf16[128,2176]{1,0:T(8,128)(2,1)S(1)}, u32[]{:S(2)}, u32[]{:S(2)}) collective-permute-start(bf16[128,2176]{1,0:T(8,128)(2,1)S(1)} %collective-permute-done.10.refs_1_), channel_id=1, source_target_pairs={{0,1},{1,2},{2,3},{3,4},{4,5},{5,6},{6,7},{7,0},{8,9},{9,10},{10,1... | collective-permute-start | bytes 1671176 | tf_op jit(solution)/shard_map/ppermute | solution.py:26
  102.0 13.4 %collective-permute-start.19 = (bf16[128,2176]{1,0:T(8,128)(2,1)S(1)}, bf16[128,2176]{1,0:T(8,128)(2,1)S(1)}, u32[]{:S(2)}, u32[]{:S(2)}) collective-permute-start(bf16[128,2176]{1,0:T(8,128)(2,1)S(1)} %collective-permute-done.11.refs_2_), channel_id=1, source_target_pairs={{0,7},{1,0},{2,1},{3,2},{4,3},{5,4},{6,5},{7,6},{8,15},{9,8},{10,9... | collective-permute-start | bytes 1671176 | tf_op jit(solution)/shard_map/ppermute | solution.py:26
  103.6 36.2 %collective-permute-start.12 = (bf16[192,2048]{1,0:T(8,128)(2,1)S(1)}, bf16[192,2048]{1,0:T(8,128)(2,1)S(1)}, u32[]{:S(2)}, u32[]{:S(2)}) collective-permute-start(bf16[192,2048]{1,0:T(8,128)(2,1)S(1)} %get-tuple-element.72), channel_id=1, source_target_pairs={{0,8},{1,9},{2,10},{3,11},{4,12},{5,13},{6,14},{7,15},{8,16},{9,17... | collective-permute-start | bytes 2359304 | tf_op jit(solution)/shard_map/ppermute | solution.py:31
  103.6 36.1 %collective-permute-start.13 = (bf16[192,2048]{1,0:T(8,128)(2,1)S(1)}, bf16[192,2048]{1,0:T(8,128)(2,1)S(1)}, u32[]{:S(2)}, u32[]{:S(2)}) collective-permute-start(bf16[192,2048]{1,0:T(8,128)(2,1)S(1)} %get-tuple-element.74), channel_id=1, source_target_pairs={{0,16},{1,17},{2,18},{3,19},{4,20},{5,21},{6,22},{7,23},{8,24},{9,... | collective-permute-start | bytes 2359304 | tf_op jit(solution)/shard_map/ppermute | solution.py:31
  105.9 34.5 %collective-permute-start.14 = (bf16[192,2048]{1,0:T(8,128)(2,1)S(1)}, bf16[192,2048]{1,0:T(8,128)(2,1)S(1)}, u32[]{:S(2)}, u32[]{:S(2)}) collective-permute-start(bf16[192,2048]{1,0:T(8,128)(2,1)S(1)} %get-tuple-element.71), channel_id=1, source_target_pairs={{0,24},{1,25},{2,26},{3,27},{4,28},{5,29},{6,30},{7,31},{8,0},{9,1... | collective-permute-start | bytes 2359304 | tf_op jit(solution)/shard_map/ppermute | solution.py:31
  114.2 31.7 %collective-permute-start.23 = (bf16[128,2176]{1,0:T(8,128)(2,1)S(1)}, bf16[128,2176]{1,0:T(8,128)(2,1)S(1)}, u32[]{:S(2)}, u32[]{:S(2)}) collective-permute-start(bf16[128,2176]{1,0:T(8,128)(2,1)S(1)} %collective-permute-done.18.refs_0_), channel_id=1, source_target_pairs={{0,1},{1,2},{2,3},{3,4},{4,5},{5,6},{6,7},{7,0},{8,9},{9,10},{10,1... | collective-permute-start | bytes 1671176 | tf_op jit(solution)/shard_map/ppermute | solution.py:26
  115.4 31.1 %collective-permute-start.24 = (bf16[128,2176]{1,0:T(8,128)(2,1)S(1)}, bf16[128,2176]{1,0:T(8,128)(2,1)S(1)}, u32[]{:S(2)}, u32[]{:S(2)}) collective-permute-start(bf16[128,2176]{1,0:T(8,128)(2,1)S(1)} %collective-permute-done.19.refs_1_), channel_id=1, source_target_pairs={{0,7},{1,0},{2,1},{3,2},{4,3},{5,4},{6,5},{7,6},{8,15},{9,8},{10,9... | collective-permute-start | bytes 1671176 | tf_op jit(solution)/shard_map/ppermute | solution.py:26
  143.5 11.1 %collective-permute-start.15 = (bf16[384,256]{1,0:T(8,128)(2,1)S(1)}, bf16[384,256]{1,0:T(8,128)(2,1)S(1)}, u32[]{:S(2)}, u32[]{:S(2)}) collective-permute-start(bf16[384,256]{1,0:T(8,128)(2,1)S(1)} %get-tuple-element.54), channel_id=1, source_target_pairs={{0,24},{1,25},{2,26},{3,27},{4,28},{5,29},{6,30},{7,31},{8,0},{9,1... | collective-permute-start | bytes 589832 | tf_op jit(solution)/shard_map/ppermute | solution.py:31
  146.0 18.6 %collective-permute-start.28 = (bf16[64,2176]{1,0:T(8,128)(2,1)S(1)}, bf16[64,2176]{1,0:T(8,128)(2,1)S(1)}, u32[]{:S(2)}, u32[]{:S(2)}) collective-permute-start(bf16[64,2176]{1,0:T(8,128)(2,1)S(1)} %slice.38), channel_id=1, source_target_pairs={{0,1},{1,2},{2,3},{3,4},{4,5},{5,6},{6,7},{7,0},{8,9},{9,10},{10,1... | collective-permute-start | bytes 835592 | tf_op jit(solution)/shard_map/ppermute | solution.py:26
  146.6 19.6 %collective-permute-start.29 = (bf16[64,2176]{1,0:T(8,128)(2,1)S(1)}, bf16[64,2176]{1,0:T(8,128)(2,1)S(1)}, u32[]{:S(2)}, u32[]{:S(2)}) collective-permute-start(bf16[64,2176]{1,0:T(8,128)(2,1)S(1)} %slice.39), channel_id=1, source_target_pairs={{0,7},{1,0},{2,1},{3,2},{4,3},{5,4},{6,5},{7,6},{8,15},{9,8},{10,9... | collective-permute-start | bytes 835592 | tf_op jit(solution)/shard_map/ppermute | solution.py:26
  149.4 11.1 %collective-permute-start.16 = (bf16[384,256]{1,0:T(8,128)(2,1)S(1)}, bf16[384,256]{1,0:T(8,128)(2,1)S(1)}, u32[]{:S(2)}, u32[]{:S(2)}) collective-permute-start(bf16[384,256]{1,0:T(8,128)(2,1)S(1)} %get-tuple-element.55), channel_id=1, source_target_pairs={{0,16},{1,17},{2,18},{3,19},{4,20},{5,21},{6,22},{7,23},{8,24},{9,... | collective-permute-start | bytes 589832 | tf_op jit(solution)/shard_map/ppermute | solution.py:31
  149.4 12.0 %collective-permute-start.17 = (bf16[384,256]{1,0:T(8,128)(2,1)S(1)}, bf16[384,256]{1,0:T(8,128)(2,1)S(1)}, u32[]{:S(2)}, u32[]{:S(2)}) collective-permute-start(bf16[384,256]{1,0:T(8,128)(2,1)S(1)} %get-tuple-element.56), channel_id=1, source_target_pairs={{0,8},{1,9},{2,10},{3,11},{4,12},{5,13},{6,14},{7,15},{8,16},{9,17... | collective-permute-start | bytes 589832 | tf_op jit(solution)/shard_map/ppermute | solution.py:31
  154.7 6.8 %collective-permute-start.20 = (bf16[256,256]{1,0:T(8,128)(2,1)S(1)}, bf16[256,256]{1,0:T(8,128)(2,1)S(1)}, u32[]{:S(2)}, u32[]{:S(2)}) collective-permute-start(bf16[256,256]{1,0:T(8,128)(2,1)S(1)} %get-tuple-element.58), channel_id=1, source_target_pairs={{0,24},{1,25},{2,26},{3,27},{4,28},{5,29},{6,30},{7,31},{8,0},{9,1... | collective-permute-start | bytes 393224 | tf_op jit(solution)/shard_map/ppermute | solution.py:31
  160.5 18.3 %copy-start.1 = (s32[2]{0:T(128)S(1)}, s32[2]{0:T(128)}, u32[]{:S(2)}) copy-start(s32[2]{0:T(128)} %pad_add_fusion.pos) | copy-start | bytes 28
  160.5 7.8 %collective-permute-start.21 = (bf16[256,256]{1,0:T(8,128)(2,1)S(1)}, bf16[256,256]{1,0:T(8,128)(2,1)S(1)}, u32[]{:S(2)}, u32[]{:S(2)}) collective-permute-start(bf16[256,256]{1,0:T(8,128)(2,1)S(1)} %get-tuple-element.59), channel_id=1, source_target_pairs={{0,16},{1,17},{2,18},{3,19},{4,20},{5,21},{6,22},{7,23},{8,24},{9,... | collective-permute-start | bytes 393224 | tf_op jit(solution)/shard_map/ppermute | solution.py:31
  161.4 11.3 %collective-permute-start.22 = (bf16[256,256]{1,0:T(8,128)(2,1)S(1)}, bf16[256,256]{1,0:T(8,128)(2,1)S(1)}, u32[]{:S(2)}, u32[]{:S(2)}) collective-permute-start(bf16[256,256]{1,0:T(8,128)(2,1)S(1)} %get-tuple-element.60), channel_id=1, source_target_pairs={{0,8},{1,9},{2,10},{3,11},{4,12},{5,13},{6,14},{7,15},{8,16},{9,17... | collective-permute-start | bytes 393224 | tf_op jit(solution)/shard_map/ppermute | solution.py:31
  161.5 11.2 %collective-permute-start.25 = (bf16[256,256]{1,0:T(8,128)(2,1)S(1)}, bf16[256,256]{1,0:T(8,128)(2,1)S(1)}, u32[]{:S(2)}, u32[]{:S(2)}) collective-permute-start(bf16[256,256]{1,0:T(8,128)(2,1)S(1)} %get-tuple-element.62), channel_id=1, source_target_pairs={{0,24},{1,25},{2,26},{3,27},{4,28},{5,29},{6,30},{7,31},{8,0},{9,1... | collective-permute-start | bytes 393224 | tf_op jit(solution)/shard_map/ppermute | solution.py:31
  164.6 8.1 %collective-permute-start.26 = (bf16[256,256]{1,0:T(8,128)(2,1)S(1)}, bf16[256,256]{1,0:T(8,128)(2,1)S(1)}, u32[]{:S(2)}, u32[]{:S(2)}) collective-permute-start(bf16[256,256]{1,0:T(8,128)(2,1)S(1)} %get-tuple-element.63), channel_id=1, source_target_pairs={{0,16},{1,17},{2,18},{3,19},{4,20},{5,21},{6,22},{7,23},{8,24},{9,... | collective-permute-start | bytes 393224 | tf_op jit(solution)/shard_map/ppermute | solution.py:31
  166.2 9.5 %collective-permute-start.27 = (bf16[256,256]{1,0:T(8,128)(2,1)S(1)}, bf16[256,256]{1,0:T(8,128)(2,1)S(1)}, u32[]{:S(2)}, u32[]{:S(2)}) collective-permute-start(bf16[256,256]{1,0:T(8,128)(2,1)S(1)} %get-tuple-element.64), channel_id=1, source_target_pairs={{0,8},{1,9},{2,10},{3,11},{4,12},{5,13},{6,14},{7,15},{8,16},{9,17... | collective-permute-start | bytes 393224 | tf_op jit(solution)/shard_map/ppermute | solution.py:31
  168.3 7.4 %collective-permute-start.30 = (bf16[128,256]{1,0:T(8,128)(2,1)S(1)}, bf16[128,256]{1,0:T(8,128)(2,1)S(1)}, u32[]{:S(2)}, u32[]{:S(2)}) collective-permute-start(bf16[128,256]{1,0:T(8,128)(2,1)S(1)} %get-tuple-element.66), channel_id=1, source_target_pairs={{0,24},{1,25},{2,26},{3,27},{4,28},{5,29},{6,30},{7,31},{8,0},{9,1... | collective-permute-start | bytes 196616 | tf_op jit(solution)/shard_map/ppermute | solution.py:31
  172.6 5.9 %collective-permute-start.31 = (bf16[128,256]{1,0:T(8,128)(2,1)S(1)}, bf16[128,256]{1,0:T(8,128)(2,1)S(1)}, u32[]{:S(2)}, u32[]{:S(2)}) collective-permute-start(bf16[128,256]{1,0:T(8,128)(2,1)S(1)} %get-tuple-element.67), channel_id=1, source_target_pairs={{0,16},{1,17},{2,18},{3,19},{4,20},{5,21},{6,22},{7,23},{8,24},{9,... | collective-permute-start | bytes 196616 | tf_op jit(solution)/shard_map/ppermute | solution.py:31
  172.6 6.2 %collective-permute-start.32 = (bf16[128,256]{1,0:T(8,128)(2,1)S(1)}, bf16[128,256]{1,0:T(8,128)(2,1)S(1)}, u32[]{:S(2)}, u32[]{:S(2)}) collective-permute-start(bf16[128,256]{1,0:T(8,128)(2,1)S(1)} %get-tuple-element.68), channel_id=1, source_target_pairs={{0,8},{1,9},{2,10},{3,11},{4,12},{5,13},{6,14},{7,15},{8,16},{9,17... | collective-permute-start | bytes 196616 | tf_op jit(solution)/shard_map/ppermute | solution.py:31

commit v2 on v0

v2 whole, which is shorter than its diff:
```python
import functools
import jax
import jax.numpy as jnp
from jax import lax
from jax.experimental import pallas as pl
from jax.experimental.pallas import tpu as pltpu
from jax.sharding import PartitionSpec as P

NX = 4
NZ = 8
NODES = 32
HEADS = 64
HD = 128
PAIR = 2 * HD
QUART = 2048
HALF = QUART // 2
COLS = 192
ROWS = NX * NODES
QROWS = 2 * NODES + 16
NT = (((1,), (1,)), ((), ()))
BF = jnp.bfloat16
F32 = jnp.float32
ANY = pl.BlockSpec(memory_space=pl.ANY)
HBM = pl.BlockSpec(memory_space=pltpu.HBM)
VMEM = pl.BlockSpec(memory_space=pltpu.VMEM)
SMEM = pl.BlockSpec(memory_space=pltpu.SMEM)
PARAMS = pltpu.CompilerParams(vmem_limit_bytes=16 * 1024 * 1024)


def zsend(array, shift):
    pairs = [(x * NZ + z, x * NZ + (z + shift) % NZ) for x in range(NX) for z in range(NZ)]
    return lax.ppermute(array, "head", pairs)


def xsend(array, shift):
    pairs = [(x * NZ + z, ((x + shift) % NX) * NZ + z) for x in range(NX) for z in range(NZ)]
    return lax.ppermute(array, "head", pairs)


def swap_core(array):
    return lax.ppermute(array, "dp", [(i, i ^ 1) for i in range(8)])


def place():
    me = lax.axis_index("head")
    return lax.div(me, NZ), lax.rem(me, NZ)


def core():
    return lax.rem(lax.axis_index("dp"), 2)


def cost(flops, size, trans=0):
    return pl.CostEstimate(flops=flops, bytes_accessed=size, transcendentals=trans)


def run_copies(pairs, sems):
    copies = [pltpu.make_async_copy(a, b, sems.at[n]) for n, (a, b) in enumerate(pairs)]
    for copy in copies:
        copy.start()
    return copies


def split3(value):
    hi = value.astype(BF).astype(F32)
    mid = (value - hi).astype(BF).astype(F32)
    return hi, mid, value - hi - mid


def pack_queries_kernel(decay, q_hbm, out, q, sems):
    cuts = [slice(n * QUART, (n + 1) * QUART) for n in range(NX)]
    copies = run_copies([(q_hbm.at[0, :, cut], q.at[:, cut]) for cut in cuts], sems)
    row = lax.broadcasted_iota(jnp.int32, (16, HD), 0)
    rows = jnp.zeros((16, HD), F32)
    for j in range(2):
        for n, piece in enumerate(split3(jnp.full((16, HD), decay[j], F32))):
            rows = jnp.where(row == 3 * j + n, piece, rows)
    tail = rows.astype(BF)
    for n in range(NX * NZ):
        out[n, 2 * NODES :, :] = tail
    for n in range(NX * NZ):
        if n % NZ == 0:
            copies[n // NZ].wait()
        for j in range(2):
            out[n, j * NODES : (j + 1) * NODES, :] = q[:, (2 * n + j) * HD : (2 * n + j + 1) * HD]


def pack_queries(decay, q):
    return pl.pallas_call(
        pack_queries_kernel,
        in_specs=[SMEM, HBM],
        out_specs=VMEM,
        out_shape=jax.ShapeDtypeStruct((NX * NZ, QROWS, HD), BF),
        scratch_shapes=[pltpu.VMEM((NODES, HEADS * HD), BF), pltpu.SemaphoreType.DMA((NX,))],
        cost_estimate=cost(0, 1_000_000),
        compiler_params=pltpu.CompilerParams(vmem_limit_bytes=60 * 1024 * 1024),
    )(decay, q)


def pack_weights_kernel(w, *refs):
    o0, o1, o2, o3, sems = refs[-5:]
    x, _ = place()
    pairs = [(w.at[:, pl.ds(pl.multiple_of(x * QUART, QUART), QUART)], o0)]
    for n, out in enumerate((o1, o2, o3), 1):
        col = pl.multiple_of(lax.rem(x + n, NX) * QUART + core() * HALF, HALF)
        pairs.append((w.at[:, pl.ds(col, HALF)], out))
    for copy in run_copies(pairs, sems):
        copy.wait()


def pack_weights(w, after):
    return pl.pallas_call(
        pack_weights_kernel,
        in_specs=[HBM] + [ANY] * len(after),
        out_specs=[VMEM] * NX,
        out_shape=[jax.ShapeDtypeStruct((COLS, QUART), BF)] + [jax.ShapeDtypeStruct((COLS, HALF), BF)] * 3,
        scratch_shapes=[pltpu.SemaphoreType.DMA((4,))],
        cost_estimate=cost(0, 4_000_000),
        compiler_params=PARAMS,
    )(w, *after)


def inter_kernel(decay, queries, states, anc_ref, *refs):
    out = refs[-1]
    for r in range(NX * NZ):
        depth = jnp.sum(anc_ref[r].astype(F32), axis=1, keepdims=True)
        for j in range(2):
            rows = slice(j * NODES, (j + 1) * NODES)
            inter = jnp.dot(queries[r, rows, :], states[r, j], preferred_element_type=F32)
            value = inter * jnp.exp(jnp.broadcast_to(-decay[j] * depth, (NODES, HD)))
            out[r, :, j * HD : (j + 1) * HD] = value.astype(BF)


def inter_part(decay, queries, states, anc, marks):
    return pl.pallas_call(
        inter_kernel,
        in_specs=[SMEM] + [VMEM] * 3 + [ANY] * len(marks),
        out_specs=VMEM,
        out_shape=jax.ShapeDtypeStruct((NX * NZ, NODES, PAIR), BF),
        cost_estimate=cost(70_000_000, 4_000_000, 100_000),
        compiler_params=PARAMS,
    )(decay, queries, states, anc, *marks)


def intra_kernel(q_ref, k_ref, v_ref, gate_ref, spread_ref, anc_ref, gain_ref, intra_ref, scale_ref):
    anc = anc_ref[lax.axis_index("head")].astype(F32)
    depth = jnp.sum(anc, axis=1, keepdims=True)
    depth_t = lax.dot_general(jnp.ones((8, NODES), BF), anc.astype(BF), NT, preferred_element_type=F32)[0:1]
    gaps = depth - depth_t
    for n in range(NX * NZ):
        extra = spread_ref[n, 2 * NODES :, :].astype(F32)
        for j in range(2):
            cols = slice((2 * n + j) * HD, (2 * n + j + 1) * HD)
            rate = extra[3 * j : 3 * j + 1] + extra[3 * j + 1 : 3 * j + 2] + extra[3 * j + 2 : 3 * j + 3]
            scores = lax.dot_general(q_ref[0, :, cols], k_ref[0, :, cols], NT, preferred_element_type=F32)
            mix = (scores * (anc * jnp.exp(-rate[:, :NODES] * gaps))).astype(BF)
            intra_ref[:, cols] = jnp.dot(mix, v_ref[0, :, cols], preferred_element_type=F32)
            scale_ref[:, cols] = gain_ref[:, cols] / (1.0 + jnp.exp(-gate_ref[0, :, cols].astype(F32)))


def intra_part(q, k, v, gate, spread, anc, gain):
    return pl.pallas_call(
        intra_kernel,
        in_specs=[VMEM] * 7,
        out_specs=[VMEM] * 2,
        out_shape=[jax.ShapeDtypeStruct((NODES, HEADS * HD), F32)] * 2,
        cost_estimate=cost(100_000_000, 4_000_000, 200_000),
        compiler_params=PARAMS,
    )(q, k, v, gate, spread, anc, gain)


def merge_kernel(sizes, inter_ref, intra_ref, scale_ref, o0, o1, o2, o3, attn_ref):
    x, _ = place()
    node = lax.broadcasted_iota(jnp.int32, (NODES, HD), 0)
    live = (node < sizes[lax.axis_index("head")]).astype(F32)
    squares = jnp.zeros((NODES, HD), F32)
    for h in range(HEADS):
        cols = slice(h * HD, (h + 1) * HD)
        inter = inter_ref[h // 2, :, (h % 2) * HD : (h % 2 + 1) * HD].astype(F32)
        attn = (live * (inter + intra_ref[:, cols])).astype(BF)
        attn_ref[:, cols] = attn
        attn = attn.astype(F32)
        squares = squares + attn * attn
    mean = jnp.sum(squares, axis=1, keepdims=True) * (1.0 / (HEADS * HD))
    norm = jnp.broadcast_to(lax.rsqrt(mean + 1e-06), (NODES, HD))
    for shift, out in enumerate((o0, o1, o2, o3)):
        base = lax.rem(x + shift, NX) * QUART
        for h in range(HEADS // NX):
            cols = pl.ds(pl.multiple_of(base + h * HD, HD), HD)
            normed = attn_ref[:, cols].astype(F32) * norm * scale_ref[:, cols]
            out[:, h * HD : (h + 1) * HD] = normed.astype(BF)


def merge(sizes, inter, intra, scale):
    return pl.pallas_call(
        merge_kernel,
        in_specs=[SMEM] + [VMEM] * 3,
        out_specs=[VMEM] * NX,
        out_shape=[jax.ShapeDtypeStruct((NODES, QUART), BF)] * NX,
        scratch_shapes=[pltpu.VMEM((NODES, HEADS * HD), BF)],
        cost_estimate=cost(10_000_000, 4_000_000),
        compiler_params=PARAMS,
    )(sizes, inter, intra, scale)


def stack_kernel(p0, p1, p2, p3, out):
    x, _ = place()
    for slot, part in enumerate((p0, p1, p2, p3)):
        row = pl.multiple_of(lax.rem(x - slot + NX, NX) * NODES, NODES)
        out[pl.ds(row, NODES), :] = part[...]


def stack_rows(parts):
    return pl.pallas_call(
        stack_kernel,
        in_specs=[VMEM] * NX,
        out_specs=VMEM,
        out_shape=jax.ShapeDtypeStruct((ROWS, QUART), BF),
        cost_estimate=cost(0, 1_000_000),
        compiler_params=PARAMS,
    )(*parts)


def project_kernel(count, *refs):
    pieces, (w0, w1, w2, w3, swapped) = refs[:count], refs[count : count + 5]
    outs, lhs = refs[count + 5 : count + 5 + NX], refs[-1]
    mine = pl.multiple_of(core() * HALF, HALF)
    other = pl.multiple_of(HALF - core() * HALF, HALF)
    if count == 1:
        lhs = pieces[0]
    else:
        row = 0
        for piece in pieces:
            lhs[row : row + piece.shape[0], :] = piece[...]
            row += piece.shape[0]
    for n, (weight, out) in enumerate(zip((w0, w1, w2, w3), outs)):
        if n == 0:
            acc = lax.dot_general(lhs[...], weight[...], NT, preferred_element_type=F32)
        else:
            acc = lax.dot_general(lhs[:, pl.ds(mine, HALF)], weight[...], NT, preferred_element_type=F32)
            acc = acc + lax.dot_general(lhs[:, pl.ds(other, HALF)], swapped[n - 1], NT, preferred_element_type=F32)
        out[...] = acc.astype(out.dtype)


def project(pieces, weights):
    rows = sum(p.shape[0] for p in pieces)
    return pl.pallas_call(
        functools.partial(project_kernel, len(pieces)),
        in_specs=[VMEM] * (len(pieces) + 5),
        out_specs=[VMEM] * NX,
        out_shape=[jax.ShapeDtypeStruct((rows, COLS), F32)] + [jax.ShapeDtypeStruct((rows, COLS), BF)] * (NX - 1),
        scratch_shapes=[pltpu.VMEM((rows, QUART), BF)],
        cost_estimate=cost(2 * rows * QUART * COLS * NX, 4_000_000),
        compiler_params=PARAMS,
    )(*pieces, *weights)


def finish_kernel(layout, *refs):
    out = refs[-1]
    _, z = place()
    for g, places in enumerate(layout):
        own, a, b, c = refs[4 * g : 4 * g + 4]
        row = 0
        for shift, first, last in places:
            size = (last - first) * NODES
            rows = slice(row, row + size)
            total = own[rows, :] + a[rows, :].astype(F32) + b[rows, :].astype(F32) + c[rows, :].astype(F32)
            source = lax.rem(z - shift + 2 * NZ, NZ)
            for x in range(first, last):
                part = total[(x - first) * NODES : (x - first + 1) * NODES]
                out[x, source] = part.astype(BF)
            row += size


def finish(groups, layout):
    flat = [a for group in groups for a in group]
    return pl.pallas_call(
        functools.partial(finish_kernel, layout),
        in_specs=[VMEM] * len(flat),
        out_specs=VMEM,
        out_shape=jax.ShapeDtypeStruct((NX, NZ, NODES, COLS), BF),
        cost_estimate=cost(2_000_000, 4_000_000),
        compiler_params=PARAMS,
    )(*flat)


def tie(arrays, *marks):
    return lax.optimization_barrier((*arrays, *marks))[: len(arrays)]


def per_device(queries, keys, values, gate, states, decay, ancestors, tree_sizes, gain, out_weight):
    packed = pack_queries(decay, queries)
    w0, w1, w2, w3 = pack_weights(out_weight.T, [packed])
    w1, w3 = xsend(w1, 1), xsend(w3, 3)
    spread = lax.all_to_all(packed, "head", 0, 0, tiled=True)
    inter = inter_part(decay, spread, states, ancestors, [w1, w3])
    w2 = xsend(tie((w2,), inter)[0], 2)
    inter = lax.all_to_all(inter, "head", 0, 0, tiled=True)
    intra, scale = intra_part(queries, keys, values, gate, spread, ancestors, gain.reshape(1, -1))
    swapped = swap_core(jnp.stack(tie((w1, w2, w3), scale)))
    weights = [w0, w1, w2, w3, swapped]
    n0, n1, n2, n3 = merge(tree_sizes, inter, intra, scale)
    own = stack_rows([n0, xsend(n1, 1), xsend(n2, 2), xsend(n3, 3)])

    groups, layout = [], []
    half = ROWS // 2

    def send_sums(pieces, places):
        own_part, *others = project(pieces, weights)
        groups.append([own_part] + [xsend(p, -d) for d, p in enumerate(others, 1)])
        layout.append(places)
        return own_part

    up, dn = zsend(own, 1), zsend(own, -1)
    mark = send_sums([own], [(0, 0, NX)])
    for step in range(1, 4):
        up, dn = tie((up, dn), *groups[-1])
        pieces = up, dn
        if step < 3:
            up, dn = zsend(up, 1), zsend(dn, -1)
        else:
            up, dn = zsend(up[:half], 1), zsend(dn[half:], -1)
        mark = send_sums(pieces, [(step, 0, NX), (-step, 0, NX)])
    last = tie((up, dn), mark)
    send_sums(last, [(4, 0, NX // 2), (-4, NX // 2, NX)])
    out = finish(groups, layout)
    return out.reshape(NX * NZ, NODES, COLS)


def solution(mesh):
    return jax.shard_map(
        per_device,
        mesh=mesh,
        in_specs=(
            P(("dp", "head"), None, None),
            P(("dp", "head"), None, None),
            P(("dp", "head"), None, None),
            P(("dp", "head"), None, None),
            P("dp", "head", None, None),
            P("head"),
            P("dp", None, None),
            P("dp"),
            P(),
            P(None, "head"),
        ),
        out_specs=P("dp", None, "head"),
        check_vma=False,
    )
```

time: 485 us -> 144 us (0.30); the launches traced: 478 us -> 143 us
  other arithmetic: 146 us -> 1.29 us
  local copies, waits for them, and re-layouts: 108 us -> 13.1 us
  waiting for transfers between devices: 138 us -> 46.3 us
  starting transfers between devices: 31.5 us -> 60.5 us
  blocking collectives: 24.5 us -> 0 us
  Pallas kernels: 0 us -> 21.8 us
  matrix products: 16.5 us -> 0 us
  between operations: 13.5 us -> 0.19 us
    unnamed x4 -> x0, other arithmetic: 140 us -> none
    all_gather x1 -> x0, waiting for transfers between devices: 138 us -> none  [per_device(): lax.all_gather(normed, 'head', axis=0, tiled=True)]
    unnamed x23 -> x34, local copies, waits for them, and re-layouts: 72.5 us -> 13 us
    ppermute x0 -> x30, waiting for transfers between devices: none -> 44.6 us  [the longest x21 42.6 us: xsend(): return lax.ppermute(array, 'head', pairs)]
    ppermute x0 -> x30, starting transfers between devices: none -> 41.1 us  [the longest x21 27.7 us: xsend(): return lax.ppermute(array, 'head', pairs)]
    all_to_all x6 -> x0, local copies, waits for them, and re-layouts: 28.6 us -> none  [the longest x2 9.53 us: per_device(): lax.all_to_all(queries, 'head', split_axis=2, concat_axis=0, tiled=True)]
    all_to_all x1 -> x0, blocking collectives: 24.5 us -> none  [per_device(): rows = lax.all_to_all(attn, 'head', split_axis=0, concat_axis=2, tiled=True)]
    pallas_call x0 -> x12, Pallas kernels: none -> 21.8 us  [the longest x1 8.06 us: intra_part(): pl.pallas_call(intra_kernel, in_specs=[VMEM] * 7, out_specs=[VMEM] * 2, o...]
  transfers between devices with their start and end apart: 4 -> 32, of which waited for: 1 -> 21; matrix products, arithmetic and copies ran while one was open for 35% -> 1% of each run, Pallas kernels for 0% -> 12%
where the time goes in v2:
time: 144 us; the launch traced here: 143 us
  starting transfers between devices  60.5 us (42%)
  waiting for transfers between devices  46.3 us (32%)
  Pallas kernels  21.8 us (15%)
  local copies, waits for them, and re-layouts  13.1 us (9%)
    ppermute x21, waiting for transfers between devices, xsend(): return lax.ppermute(array, 'head', pairs)  42.6 us
    ppermute x21, starting transfers between devices, xsend(): return lax.ppermute(array, 'head', pairs)  27.7 us
    ppermute x8, starting transfers between devices, zsend(): return lax.ppermute(array, 'head', pairs)  13.4 us
    unnamed x34, local copies, waits for them, and re-layouts  13 us
    all_to_all x1, starting transfers between devices, per_device(): spread = lax.all_to_all(packed, 'head', 0, 0, tiled=True)  11.5 us
    pallas_call x1, Pallas kernels, intra_part(): pl.pallas_call(intra_kernel, in_specs=[VMEM] * 7, out_specs=[VMEM] * 2, o...  8.06 us
    all_to_all x1, starting transfers between devices, per_device(): inter = lax.all_to_all(inter, 'head', 0, 0, tiled=True)  7.91 us
    pallas_call x5, Pallas kernels, project(): pl.pallas_call(functools.partial(project_kernel, len(pieces)), in_specs=[...  6.26 us
  transfers between devices with their start and end apart: 32, of which 21 were waited for; matrix products, arithmetic and copies ran while one was open for 1% of the time, Pallas kernels for 12%

profile of v2, /device:TPU:16, one launch (start us, length us, event | category | flops | bytes accessed | tf_op | source)
XLA Modules:
  0.0 143.2 jit_solution(8792344720630916846)
XLA Ops:
  0.0 2.7 %shard_map.100.refs_0_ = bf16[32,80,128]{2,1,0:T(8,128)(2,1)} custom-call(f32[2]{0:T(128)} %decay.3, bf16[1,32,8192]{2,1,0:T(8,128)(2,1)} %q_ref.1), custom_call_target="tpu_custom_call" | custom-call | bytes 1000000 | tf_op jit(solution)/shard_map/pallas_call | solution.py:89
  2.7 11.5 %all-to-all-start = ((bf16[32,80,128]{2,1,0:T(8,128)(2,1)}), bf16[32,80,128]{2,1,0:T(8,128)(2,1)S(1)}, u32[]{:S(2)}, u32[]{:S(2)}) async-start(bf16[32,80,128]{2,1,0:T(8,128)(2,1)} %shard_map.100.refs_0_), calls=%async_computation | async-start | bytes 1310720 | tf_op jit(solution)/shard_map/all_to_all | solution.py:295
  14.2 1.9 %copy-done.1 = bf16[8192,192]{0,1:T(8,128)(2,1)S(1)} copy-done((bf16[8192,192]{0,1:T(8,128)(2,1)S(1)}, bf16[8192,192]{0,1:T(8,128)(2,1)}, u32[]{:S(2)}) %copy-start.1) | copy-done | bytes 3145752
  17.1 1.9 %collective-permute-start = (bf16[192,1024]{1,0:T(8,128)(2,1)S(1)}, bf16[192,1024]{1,0:T(8,128)(2,1)S(1)}, u32[]{:S(2)}, u32[]{:S(2)}) collective-permute-start(bf16[192,1024]{1,0:T(8,128)(2,1)S(1)} %get-tuple-element.47), channel_id=1, source_target_pairs={{0,8},{1,9},{2,10},{3,11},{4,12},{5,13},{6,14},{7,15},{8,16},{9,17... | collective-permute-start | bytes 1179656 | tf_op jit(solution)/shard_map/ppermute | solution.py:37
  18.9 1.4 %collective-permute-start.1 = (bf16[192,1024]{1,0:T(8,128)(2,1)S(1)}, bf16[192,1024]{1,0:T(8,128)(2,1)S(1)}, u32[]{:S(2)}, u32[]{:S(2)}) collective-permute-start(bf16[192,1024]{1,0:T(8,128)(2,1)S(1)} %get-tuple-element.48), channel_id=1, source_target_pairs={{0,24},{1,25},{2,26},{3,27},{4,28},{5,29},{6,30},{7,31},{8,0},{9,1... | collective-permute-start | bytes 1179656 | tf_op jit(solution)/shard_map/ppermute | solution.py:37
  20.4 14.0 %collective-permute-done.refs_0_.refs_2_.refs_3_ = bf16[192,1024]{1,0:T(8,128)(2,1)S(1)} collective-permute-done((bf16[192,1024]{1,0:T(8,128)(2,1)S(1)}, bf16[192,1024]{1,0:T(8,128)(2,1)S(1)}, u32[]{:S(2)}, u32[]{:S(2)}) %collective-permute-start) | collective-permute-done | bytes 393248 | tf_op jit(solution)/shard_map/ppermute | solution.py:37
  35.6 1.6 %copy-done.4 = bf16[32,2,128,128]{3,2,1,0:T(8,128)(2,1)S(1)} copy-done((bf16[32,2,128,128]{3,2,1,0:T(8,128)(2,1)S(1)}, bf16[32,2,128,128]{3,2,1,0:T(8,128)(2,1)}, u32[]{:S(2)}) %copy-start.4) | copy-done | bytes 2097176
  37.2 1.2 shard_map.102
  39.2 2.2 %collective-permute-start.5 = (bf16[192,1024]{1,0:T(8,128)(2,1)}, bf16[192,1024]{1,0:T(8,128)(2,1)S(1)}, u32[]{:S(2)}, u32[]{:S(2)}) collective-permute-start(bf16[192,1024]{1,0:T(8,128)(2,1)} %get-tuple-element.57), channel_id=1, source_target_pairs={{0,16},{1,17},{2,18},{3,19},{4,20},{5,21},{6,22},{7,23},{8,24},{9,... | collective-permute-start | bytes 1179656 | tf_op jit(solution)/shard_map/ppermute | solution.py:37
  41.4 7.9 %all-to-all-start.1 = ((bf16[32,32,256]{2,1,0:T(8,128)(2,1)}), bf16[32,32,256]{2,1,0:T(8,128)(2,1)}, u32[]{:S(2)}, u32[]{:S(2)}) async-start(bf16[32,32,256]{2,1,0:T(8,128)(2,1)} %copy-done.6), calls=%async_computation.1 | async-start | bytes 1048576 | tf_op jit(solution)/shard_map/all_to_all | solution.py:298
  53.6 8.1 %shard_map.103 = (f32[32,8192]{1,0:T(8,128)S(1)}, f32[32,8192]{1,0:T(8,128)S(1)}) custom-call(bf16[1,32,8192]{2,1,0:T(8,128)(2,1)S(1)} %copy-done.5, bf16[1,32,8192]{2,1,0:T(8,128)(2,1)S(1)} %copy-done.11, bf16[1,32,8192]{2,1,0:T(8,128)(2,1)S(1)} %copy-done.12, bf16[1,32,8192]{2,1,0:T(8,128)(2,1)S(1)} %copy-done.13, ...), custom_call_target="tpu_custom_call" | custom-call | flops 100000000 | bytes 4000000 | tf_op jit(solution)/shard_map/pallas_call | solution.py:162
  62.6 1.3 pad_maximum_fusion
  64.0 1.5 %all-to-all-done.1.inter_ref = bf16[32,32,256]{2,1,0:T(8,128)(2,1)} async-done(((bf16[32,32,256]{2,1,0:T(8,128)(2,1)}), bf16[32,32,256]{2,1,0:T(8,128)(2,1)}, u32[]{:S(2)}, u32[]{:S(2)}) %all-to-all-start.1) | async-done | bytes 524320 | tf_op jit(solution)/shard_map/all_to_all | solution.py:298
  65.5 1.2 copy-done.8
  66.7 1.2 copy-done.10
  68.0 1.6 %shard_map.104 = (bf16[32,2048]{1,0:T(8,128)(2,1)S(1)}, bf16[32,2048]{1,0:T(8,128)(2,1)S(1)}, bf16[32,2048]{1,0:T(8,128)(2,1)S(1)}, bf16[32,2048]{1,0:T(8,128)(2,1)S(1)}) custom-call(s32[32]{0:T(128)S(1)} %copy-done.16, bf16[32,32,256]{2,1,0:T(8,128)(2,1)} %all-to-all-done.1.inter_ref, f32[32,8192]{1,0:T(8,128)S(1)} %copy-done.8, f32[32,8192]{1,0:T(8,128)S(1)} %copy-done.10), custom_call_target="tpu_custom_call" | custom-call | flops 10000000 | bytes 4000000 | tf_op jit(solution)/shard_map/pallas_call | solution.py:195
  69.9 2.7 %collective-permute-start.3 = (bf16[32,2048]{1,0:T(8,128)(2,1)S(1)}, bf16[32,2048]{1,0:T(8,128)(2,1)S(1)}, u32[]{:S(2)}, u32[]{:S(2)}) collective-permute-start(bf16[32,2048]{1,0:T(8,128)(2,1)S(1)} %get-tuple-element.53), channel_id=1, source_target_pairs={{0,16},{1,17},{2,18},{3,19},{4,20},{5,21},{6,22},{7,23},{8,24},{9,... | collective-permute-start | bytes 393224 | tf_op jit(solution)/shard_map/ppermute | solution.py:37
  72.6 1.4 collective-permute-start.4
  74.0 1.8 %collective-permute-done.2.p1 = bf16[32,2048]{1,0:T(8,128)(2,1)S(1)} collective-permute-done((bf16[32,2048]{1,0:T(8,128)(2,1)S(1)}, bf16[32,2048]{1,0:T(8,128)(2,1)S(1)}, u32[]{:S(2)}, u32[]{:S(2)}) %collective-permute-start.2) | collective-permute-done | bytes 131104 | tf_op jit(solution)/shard_map/ppermute | solution.py:37
  75.8 3.5 %collective-permute-done.3.p2 = bf16[32,2048]{1,0:T(8,128)(2,1)S(1)} collective-permute-done((bf16[32,2048]{1,0:T(8,128)(2,1)S(1)}, bf16[32,2048]{1,0:T(8,128)(2,1)S(1)}, u32[]{:S(2)}, u32[]{:S(2)}) %collective-permute-start.3) | collective-permute-done | bytes 131104 | tf_op jit(solution)/shard_map/ppermute | solution.py:37
  79.4 1.6 %collective-permute-start.10 = (bf16[128,2048]{1,0:T(8,128)(2,1)S(1)}, bf16[128,2048]{1,0:T(8,128)(2,1)S(1)}, u32[]{:S(2)}, u32[]{:S(2)}) collective-permute-start(bf16[128,2048]{1,0:T(8,128)(2,1)S(1)} %shard_map.105.refs_0_), channel_id=1, source_target_pairs={{0,1},{1,2},{2,3},{3,4},{4,5},{5,6},{6,7},{7,0},{8,9},{9,10},{10,1... | collective-permute-start | bytes 1572872 | tf_op jit(solution)/shard_map/ppermute | solution.py:32
  81.0 1.7 %collective-permute-start.11 = (bf16[128,2048]{1,0:T(8,128)(2,1)S(1)}, bf16[128,2048]{1,0:T(8,128)(2,1)S(1)}, u32[]{:S(2)}, u32[]{:S(2)}) collective-permute-start(bf16[128,2048]{1,0:T(8,128)(2,1)S(1)} %shard_map.105.refs_0_), channel_id=1, source_target_pairs={{0,7},{1,0},{2,1},{3,2},{4,3},{5,4},{6,5},{7,6},{8,15},{9,8},{10,9... | collective-permute-start | bytes 1572872 | tf_op jit(solution)/shard_map/ppermute | solution.py:32
  82.7 1.2 shard_map.106
  83.9 2.7 %collective-permute-start.7 = (bf16[128,192]{1,0:T(8,128)(2,1)S(1)}, bf16[128,192]{1,0:T(8,128)(2,1)S(1)}, u32[]{:S(2)}, u32[]{:S(2)}) collective-permute-start(bf16[128,192]{1,0:T(8,128)(2,1)S(1)} %get-tuple-element.62), channel_id=1, source_target_pairs={{0,24},{1,25},{2,26},{3,27},{4,28},{5,29},{6,30},{7,31},{8,0},{9,1... | collective-permute-start | bytes 147464 | tf_op jit(solution)/shard_map/ppermute | solution.py:37
  88.6 3.7 %collective-permute-done.8.refs_2_ = bf16[128,192]{1,0:T(8,128)(2,1)S(1)} collective-permute-done((bf16[128,192]{1,0:T(8,128)(2,1)S(1)}, bf16[128,192]{1,0:T(8,128)(2,1)S(1)}, u32[]{:S(2)}, u32[]{:S(2)}) %collective-permute-start.8) | collective-permute-done | bytes 49184 | tf_op jit(solution)/shard_map/ppermute | solution.py:37
  93.0 1.1 collective-permute-done.10.refs_0_
  94.2 1.4 %collective-permute-start.15 = (bf16[128,2048]{1,0:T(8,128)(2,1)S(1)}, bf16[128,2048]{1,0:T(8,128)(2,1)S(1)}, u32[]{:S(2)}, u32[]{:S(2)}) collective-permute-start(bf16[128,2048]{1,0:T(8,128)(2,1)S(1)} %collective-permute-done.10.refs_0_), channel_id=1, source_target_pairs={{0,1},{1,2},{2,3},{3,4},{4,5},{5,6},{6,7},{7,0},{8,9},{9,10},{10,1... | collective-permute-start | bytes 1572872 | tf_op jit(solution)/shard_map/ppermute | solution.py:32
  95.6 1.8 %collective-permute-start.16 = (bf16[128,2048]{1,0:T(8,128)(2,1)S(1)}, bf16[128,2048]{1,0:T(8,128)(2,1)S(1)}, u32[]{:S(2)}, u32[]{:S(2)}) collective-permute-start(bf16[128,2048]{1,0:T(8,128)(2,1)S(1)} %collective-permute-done.11.refs_1_), channel_id=1, source_target_pairs={{0,7},{1,0},{2,1},{3,2},{4,3},{5,4},{6,5},{7,6},{8,15},{9,8},{10,9... | collective-permute-start | bytes 1572872 | tf_op jit(solution)/shard_map/ppermute | solution.py:32
  97.4 1.3 shard_map.107
  98.7 2.6 %collective-permute-start.12 = (bf16[256,192]{1,0:T(8,128)(2,1)S(1)}, bf16[256,192]{1,0:T(8,128)(2,1)S(1)}, u32[]{:S(2)}, u32[]{:S(2)}) collective-permute-start(bf16[256,192]{1,0:T(8,128)(2,1)S(1)} %get-tuple-element.68), channel_id=1, source_target_pairs={{0,24},{1,25},{2,26},{3,27},{4,28},{5,29},{6,30},{7,31},{8,0},{9,1... | collective-permute-start | bytes 294920 | tf_op jit(solution)/shard_map/ppermute | solution.py:37
  102.6 2.7 %collective-permute-done.12.refs_5_ = bf16[256,192]{1,0:T(8,128)(2,1)S(1)} collective-permute-done((bf16[256,192]{1,0:T(8,128)(2,1)S(1)}, bf16[256,192]{1,0:T(8,128)(2,1)S(1)}, u32[]{:S(2)}, u32[]{:S(2)}) %collective-permute-start.12) | collective-permute-done | bytes 98336 | tf_op jit(solution)/shard_map/ppermute | solution.py:37
  105.2 2.7 %collective-permute-done.13.refs_6_ = bf16[256,192]{1,0:T(8,128)(2,1)S(1)} collective-permute-done((bf16[256,192]{1,0:T(8,128)(2,1)S(1)}, bf16[256,192]{1,0:T(8,128)(2,1)S(1)}, u32[]{:S(2)}, u32[]{:S(2)}) %collective-permute-start.13) | collective-permute-done | bytes 98336 | tf_op jit(solution)/shard_map/ppermute | solution.py:37
  107.9 1.3 collective-permute-done.14.refs_7_
  109.2 2.1 %collective-permute-start.20 = (bf16[128,2048]{1,0:T(8,128)(2,1)S(1)}, bf16[128,2048]{1,0:T(8,128)(2,1)S(1)}, u32[]{:S(2)}, u32[]{:S(2)}) collective-permute-start(bf16[128,2048]{1,0:T(8,128)(2,1)S(1)} %collective-permute-done.15.refs_0_), channel_id=1, source_target_pairs={{0,1},{1,2},{2,3},{3,4},{4,5},{5,6},{6,7},{7,0},{8,9},{9,10},{10,1... | collective-permute-start | bytes 1572872 | tf_op jit(solution)/shard_map/ppermute | solution.py:32
  112.4 1.3 shard_map.108
  113.7 1.9 %collective-permute-start.17 = (bf16[256,192]{1,0:T(8,128)(2,1)S(1)}, bf16[256,192]{1,0:T(8,128)(2,1)S(1)}, u32[]{:S(2)}, u32[]{:S(2)}) collective-permute-start(bf16[256,192]{1,0:T(8,128)(2,1)S(1)} %get-tuple-element.74), channel_id=1, source_target_pairs={{0,24},{1,25},{2,26},{3,27},{4,28},{5,29},{6,30},{7,31},{8,0},{9,1... | collective-permute-start | bytes 294920 | tf_op jit(solution)/shard_map/ppermute | solution.py:37
  116.7 2.9 %collective-permute-done.17.refs_9_ = bf16[256,192]{1,0:T(8,128)(2,1)S(1)} collective-permute-done((bf16[256,192]{1,0:T(8,128)(2,1)S(1)}, bf16[256,192]{1,0:T(8,128)(2,1)S(1)}, u32[]{:S(2)}, u32[]{:S(2)}) %collective-permute-start.17) | collective-permute-done | bytes 98336 | tf_op jit(solution)/shard_map/ppermute | solution.py:37
  119.6 2.7 %collective-permute-done.18.refs_10_ = bf16[256,192]{1,0:T(8,128)(2,1)S(1)} collective-permute-done((bf16[256,192]{1,0:T(8,128)(2,1)S(1)}, bf16[256,192]{1,0:T(8,128)(2,1)S(1)}, u32[]{:S(2)}, u32[]{:S(2)}) %collective-permute-start.18) | collective-permute-done | bytes 98336 | tf_op jit(solution)/shard_map/ppermute | solution.py:37
  122.2 1.3 collective-permute-done.19.refs_11_
  123.5 1.5 %collective-permute-start.25 = (bf16[64,2048]{1,0:T(8,128)(2,1)S(1)}, bf16[64,2048]{1,0:T(8,128)(2,1)S(1)}, u32[]{:S(2)}, u32[]{:S(2)}) collective-permute-start(bf16[64,2048]{1,0:T(8,128)(2,1)S(1)} %slice.6), channel_id=1, source_target_pairs={{0,1},{1,2},{2,3},{3,4},{4,5},{5,6},{6,7},{7,0},{8,9},{9,10},{10,1... | collective-permute-start | bytes 786440 | tf_op jit(solution)/shard_map/ppermute | solution.py:32
  125.1 2.1 %collective-permute-start.26 = (bf16[64,2048]{1,0:T(8,128)(2,1)S(1)}, bf16[64,2048]{1,0:T(8,128)(2,1)S(1)}, u32[]{:S(2)}, u32[]{:S(2)}) collective-permute-start(bf16[64,2048]{1,0:T(8,128)(2,1)S(1)} %slice.7), channel_id=1, source_target_pairs={{0,7},{1,0},{2,1},{3,2},{4,3},{5,4},{6,5},{7,6},{8,15},{9,8},{10,9... | collective-permute-start | bytes 786440 | tf_op jit(solution)/shard_map/ppermute | solution.py:32
  127.2 1.3 shard_map.109
  128.5 1.4 collective-permute-start.22
  131.7 1.2 shard_map.110
  132.9 1.8 %collective-permute-start.27 = (bf16[128,192]{1,0:T(8,128)(2,1)S(1)}, bf16[128,192]{1,0:T(8,128)(2,1)S(1)}, u32[]{:S(2)}, u32[]{:S(2)}) collective-permute-start(bf16[128,192]{1,0:T(8,128)(2,1)S(1)} %get-tuple-element.86), channel_id=1, source_target_pairs={{0,24},{1,25},{2,26},{3,27},{4,28},{5,29},{6,30},{7,31},{8,0},{9,1... | collective-permute-start | bytes 147464 | tf_op jit(solution)/shard_map/ppermute | solution.py:37
  134.7 2.0 %collective-permute-start.28 = (bf16[128,192]{1,0:T(8,128)(2,1)S(1)}, bf16[128,192]{1,0:T(8,128)(2,1)S(1)}, u32[]{:S(2)}, u32[]{:S(2)}) collective-permute-start(bf16[128,192]{1,0:T(8,128)(2,1)S(1)} %get-tuple-element.87), channel_id=1, source_target_pairs={{0,16},{1,17},{2,18},{3,19},{4,20},{5,21},{6,22},{7,23},{8,24},{9,... | collective-permute-start | bytes 147464 | tf_op jit(solution)/shard_map/ppermute | solution.py:37
  138.3 2.1 %collective-permute-done.28.refs_18_ = bf16[128,192]{1,0:T(8,128)(2,1)S(1)} collective-permute-done((bf16[128,192]{1,0:T(8,128)(2,1)S(1)}, bf16[128,192]{1,0:T(8,128)(2,1)S(1)}, u32[]{:S(2)}, u32[]{:S(2)}) %collective-permute-start.28) | collective-permute-done | bytes 49184 | tf_op jit(solution)/shard_map/ppermute | solution.py:37
  140.5 1.7 %collective-permute-done.29.refs_19_ = bf16[128,192]{1,0:T(8,128)(2,1)S(1)} collective-permute-done((bf16[128,192]{1,0:T(8,128)(2,1)S(1)}, bf16[128,192]{1,0:T(8,128)(2,1)S(1)}, u32[]{:S(2)}, u32[]{:S(2)}) %collective-permute-start.29) | collective-permute-done | bytes 49184 | tf_op jit(solution)/shard_map/ppermute | solution.py:37
  (65 shorter events, 19.5 us)
Async XLA Ops:
  2.7 11.5 %copy-start = (bf16[32,80,128]{2,1,0:T(8,128)(2,1)S(1)}, bf16[32,80,128]{2,1,0:T(8,128)(2,1)}, u32[]{:S(2)}) copy-start(bf16[32,80,128]{2,1,0:T(8,128)(2,1)} %shard_map.100.refs_0_) | copy-start | bytes 1966084
  2.7 31.9 %all-to-all-start = ((bf16[32,80,128]{2,1,0:T(8,128)(2,1)}), bf16[32,80,128]{2,1,0:T(8,128)(2,1)S(1)}, u32[]{:S(2)}, u32[]{:S(2)}) async-start(bf16[32,80,128]{2,1,0:T(8,128)(2,1)} %shard_map.100.refs_0_), calls=%async_computation | async-start | bytes 1310720 | tf_op jit(solution)/shard_map/all_to_all | solution.py:295
  14.2 1.9 %copy-start.1 = (bf16[8192,192]{0,1:T(8,128)(2,1)S(1)}, bf16[8192,192]{0,1:T(8,128)(2,1)}, u32[]{:S(2)}) copy-start(bf16[8192,192]{0,1:T(8,128)(2,1)} %param.19) | copy-start | bytes 9437188
  16.1 18.5 %copy-start.15 = (f32[2]{0:T(128)S(1)}, f32[2]{0:T(128)}, u32[]{:S(2)}) copy-start(f32[2]{0:T(128)} %decay.3) | copy-start | bytes 28
  17.1 17.3 %collective-permute-start = (bf16[192,1024]{1,0:T(8,128)(2,1)S(1)}, bf16[192,1024]{1,0:T(8,128)(2,1)S(1)}, u32[]{:S(2)}, u32[]{:S(2)}) collective-permute-start(bf16[192,1024]{1,0:T(8,128)(2,1)S(1)} %get-tuple-element.47), channel_id=1, source_target_pairs={{0,8},{1,9},{2,10},{3,11},{4,12},{5,13},{6,14},{7,15},{8,16},{9,17... | collective-permute-start | bytes 1179656 | tf_op jit(solution)/shard_map/ppermute | solution.py:37
  18.9 15.4 %collective-permute-start.1 = (bf16[192,1024]{1,0:T(8,128)(2,1)S(1)}, bf16[192,1024]{1,0:T(8,128)(2,1)S(1)}, u32[]{:S(2)}, u32[]{:S(2)}) collective-permute-start(bf16[192,1024]{1,0:T(8,128)(2,1)S(1)} %get-tuple-element.48), channel_id=1, source_target_pairs={{0,24},{1,25},{2,26},{3,27},{4,28},{5,29},{6,30},{7,31},{8,0},{9,1... | collective-permute-start | bytes 1179656 | tf_op jit(solution)/shard_map/ppermute | solution.py:37
  34.6 1.0 copy-start.2
  35.6 1.6 %copy-start.4 = (bf16[32,2,128,128]{3,2,1,0:T(8,128)(2,1)S(1)}, bf16[32,2,128,128]{3,2,1,0:T(8,128)(2,1)}, u32[]{:S(2)}) copy-start(bf16[32,2,128,128]{3,2,1,0:T(8,128)(2,1)} %states.1) | copy-start | bytes 6291460
  37.2 12.1 %copy-start.14 = (f32[8192]{0:T(1024)S(1)}, f32[8192]{0:T(1024)}, u32[]{:S(2)}) copy-start(f32[8192]{0:T(1024)} %param.18) | copy-start | bytes 98308
  39.2 10.1 %copy-start.5 = (bf16[1,32,8192]{2,1,0:T(8,128)(2,1)S(1)}, bf16[1,32,8192]{2,1,0:T(8,128)(2,1)}, u32[]{:S(2)}) copy-start(bf16[1,32,8192]{2,1,0:T(8,128)(2,1)} %q_ref.1) | copy-start | bytes 1572868
  39.2 23.4 %collective-permute-start.5 = (bf16[192,1024]{1,0:T(8,128)(2,1)}, bf16[192,1024]{1,0:T(8,128)(2,1)S(1)}, u32[]{:S(2)}, u32[]{:S(2)}) collective-permute-start(bf16[192,1024]{1,0:T(8,128)(2,1)} %get-tuple-element.57), channel_id=1, source_target_pairs={{0,16},{1,17},{2,18},{3,19},{4,20},{5,21},{6,22},{7,23},{8,24},{9,... | collective-permute-start | bytes 1179656 | tf_op jit(solution)/shard_map/ppermute | solution.py:37
  41.4 24.1 %all-to-all-start.1 = ((bf16[32,32,256]{2,1,0:T(8,128)(2,1)}), bf16[32,32,256]{2,1,0:T(8,128)(2,1)}, u32[]{:S(2)}, u32[]{:S(2)}) async-start(bf16[32,32,256]{2,1,0:T(8,128)(2,1)} %copy-done.6), calls=%async_computation.1 | async-start | bytes 1048576 | tf_op jit(solution)/shard_map/all_to_all | solution.py:298
  49.4 1.0 copy-start.3
  50.4 1.0 copy-start.11
  51.5 1.0 copy-start.12
  52.5 1.0 copy-start.13
  61.6 1.0 copy-start.7
  62.6 1.4 copy-start.9
  62.6 2.9 %copy-start.16 = (s32[32]{0:T(128)S(1)}, s32[32]{0:T(128)}, u32[]{:S(2)}) copy-start(s32[32]{0:T(128)} %sizes.1) | copy-start | bytes 388
  64.0 18.7 %collective-permute-start.6 = (bf16[3,192,1024]{2,1,0:T(8,128)(2,1)}, bf16[3,192,1024]{2,1,0:T(8,128)(2,1)S(1)}, u32[]{:S(2)}, u32[]{:S(2)}) collective-permute-start(bf16[3,192,1024]{2,1,0:T(8,128)(2,1)} %pad_maximum_fusion), channel_id=1, source_target_pairs={{0,32},{32,0},{64,96},{96,64},{128,160},{160,128},{192,224},{224,1... | collective-permute-start | bytes 3538952 | tf_op jit(solution)/shard_map/ppermute | solution.py:41
  65.5 1.2 copy-start.8
  66.7 1.2 copy-start.10
  69.5 6.3 %collective-permute-start.2 = (bf16[32,2048]{1,0:T(8,128)(2,1)S(1)}, bf16[32,2048]{1,0:T(8,128)(2,1)S(1)}, u32[]{:S(2)}, u32[]{:S(2)}) collective-permute-start(bf16[32,2048]{1,0:T(8,128)(2,1)S(1)} %get-tuple-element.52), channel_id=1, source_target_pairs={{0,8},{1,9},{2,10},{3,11},{4,12},{5,13},{6,14},{7,15},{8,16},{9,17... | collective-permute-start | bytes 393224 | tf_op jit(solution)/shard_map/ppermute | solution.py:37
  69.9 9.4 %collective-permute-start.3 = (bf16[32,2048]{1,0:T(8,128)(2,1)S(1)}, bf16[32,2048]{1,0:T(8,128)(2,1)S(1)}, u32[]{:S(2)}, u32[]{:S(2)}) collective-permute-start(bf16[32,2048]{1,0:T(8,128)(2,1)S(1)} %get-tuple-element.53), channel_id=1, source_target_pairs={{0,16},{1,17},{2,18},{3,19},{4,20},{5,21},{6,22},{7,23},{8,24},{9,... | collective-permute-start | bytes 393224 | tf_op jit(solution)/shard_map/ppermute | solution.py:37
  72.6 6.8 %collective-permute-start.4 = (bf16[32,2048]{1,0:T(8,128)(2,1)S(1)}, bf16[32,2048]{1,0:T(8,128)(2,1)S(1)}, u32[]{:S(2)}, u32[]{:S(2)}) collective-permute-start(bf16[32,2048]{1,0:T(8,128)(2,1)S(1)} %get-tuple-element.54), channel_id=1, source_target_pairs={{0,24},{1,25},{2,26},{3,27},{4,28},{5,29},{6,30},{7,31},{8,0},{9,1... | collective-permute-start | bytes 393224 | tf_op jit(solution)/shard_map/ppermute | solution.py:37
  79.4 14.8 %collective-permute-start.10 = (bf16[128,2048]{1,0:T(8,128)(2,1)S(1)}, bf16[128,2048]{1,0:T(8,128)(2,1)S(1)}, u32[]{:S(2)}, u32[]{:S(2)}) collective-permute-start(bf16[128,2048]{1,0:T(8,128)(2,1)S(1)} %shard_map.105.refs_0_), channel_id=1, source_target_pairs={{0,1},{1,2},{2,3},{3,4},{4,5},{5,6},{6,7},{7,0},{8,9},{9,10},{10,1... | collective-permute-start | bytes 1572872 | tf_op jit(solution)/shard_map/ppermute | solution.py:32
  81.0 13.2 %collective-permute-start.11 = (bf16[128,2048]{1,0:T(8,128)(2,1)S(1)}, bf16[128,2048]{1,0:T(8,128)(2,1)S(1)}, u32[]{:S(2)}, u32[]{:S(2)}) collective-permute-start(bf16[128,2048]{1,0:T(8,128)(2,1)S(1)} %shard_map.105.refs_0_), channel_id=1, source_target_pairs={{0,7},{1,0},{2,1},{3,2},{4,3},{5,4},{6,5},{7,6},{8,15},{9,8},{10,9... | collective-permute-start | bytes 1572872 | tf_op jit(solution)/shard_map/ppermute | solution.py:32
  83.9 4.8 %collective-permute-start.7 = (bf16[128,192]{1,0:T(8,128)(2,1)S(1)}, bf16[128,192]{1,0:T(8,128)(2,1)S(1)}, u32[]{:S(2)}, u32[]{:S(2)}) collective-permute-start(bf16[128,192]{1,0:T(8,128)(2,1)S(1)} %get-tuple-element.62), channel_id=1, source_target_pairs={{0,24},{1,25},{2,26},{3,27},{4,28},{5,29},{6,30},{7,31},{8,0},{9,1... | collective-permute-start | bytes 147464 | tf_op jit(solution)/shard_map/ppermute | solution.py:37
  86.6 5.8 %collective-permute-start.8 = (bf16[128,192]{1,0:T(8,128)(2,1)S(1)}, bf16[128,192]{1,0:T(8,128)(2,1)S(1)}, u32[]{:S(2)}, u32[]{:S(2)}) collective-permute-start(bf16[128,192]{1,0:T(8,128)(2,1)S(1)} %get-tuple-element.63), channel_id=1, source_target_pairs={{0,16},{1,17},{2,18},{3,19},{4,20},{5,21},{6,22},{7,23},{8,24},{9,... | collective-permute-start | bytes 147464 | tf_op jit(solution)/shard_map/ppermute | solution.py:37
  87.2 5.9 %collective-permute-start.9 = (bf16[128,192]{1,0:T(8,128)(2,1)S(1)}, bf16[128,192]{1,0:T(8,128)(2,1)S(1)}, u32[]{:S(2)}, u32[]{:S(2)}) collective-permute-start(bf16[128,192]{1,0:T(8,128)(2,1)S(1)} %get-tuple-element.64), channel_id=1, source_target_pairs={{0,8},{1,9},{2,10},{3,11},{4,12},{5,13},{6,14},{7,15},{8,16},{9,17... | collective-permute-start | bytes 147464 | tf_op jit(solution)/shard_map/ppermute | solution.py:37
  94.2 15.0 %collective-permute-start.15 = (bf16[128,2048]{1,0:T(8,128)(2,1)S(1)}, bf16[128,2048]{1,0:T(8,128)(2,1)S(1)}, u32[]{:S(2)}, u32[]{:S(2)}) collective-permute-start(bf16[128,2048]{1,0:T(8,128)(2,1)S(1)} %collective-permute-done.10.refs_0_), channel_id=1, source_target_pairs={{0,1},{1,2},{2,3},{3,4},{4,5},{5,6},{6,7},{7,0},{8,9},{9,10},{10,1... | collective-permute-start | bytes 1572872 | tf_op jit(solution)/shard_map/ppermute | solution.py:32
  95.6 13.6 %collective-permute-start.16 = (bf16[128,2048]{1,0:T(8,128)(2,1)S(1)}, bf16[128,2048]{1,0:T(8,128)(2,1)S(1)}, u32[]{:S(2)}, u32[]{:S(2)}) collective-permute-start(bf16[128,2048]{1,0:T(8,128)(2,1)S(1)} %collective-permute-done.11.refs_1_), channel_id=1, source_target_pairs={{0,7},{1,0},{2,1},{3,2},{4,3},{5,4},{6,5},{7,6},{8,15},{9,8},{10,9... | collective-permute-start | bytes 1572872 | tf_op jit(solution)/shard_map/ppermute | solution.py:32
  98.7 6.5 %collective-permute-start.12 = (bf16[256,192]{1,0:T(8,128)(2,1)S(1)}, bf16[256,192]{1,0:T(8,128)(2,1)S(1)}, u32[]{:S(2)}, u32[]{:S(2)}) collective-permute-start(bf16[256,192]{1,0:T(8,128)(2,1)S(1)} %get-tuple-element.68), channel_id=1, source_target_pairs={{0,24},{1,25},{2,26},{3,27},{4,28},{5,29},{6,30},{7,31},{8,0},{9,1... | collective-permute-start | bytes 294920 | tf_op jit(solution)/shard_map/ppermute | solution.py:37
  101.3 6.6 %collective-permute-start.13 = (bf16[256,192]{1,0:T(8,128)(2,1)S(1)}, bf16[256,192]{1,0:T(8,128)(2,1)S(1)}, u32[]{:S(2)}, u32[]{:S(2)}) collective-permute-start(bf16[256,192]{1,0:T(8,128)(2,1)S(1)} %get-tuple-element.69), channel_id=1, source_target_pairs={{0,16},{1,17},{2,18},{3,19},{4,20},{5,21},{6,22},{7,23},{8,24},{9,... | collective-permute-start | bytes 294920 | tf_op jit(solution)/shard_map/ppermute | solution.py:37
  101.6 7.6 %collective-permute-start.14 = (bf16[256,192]{1,0:T(8,128)(2,1)S(1)}, bf16[256,192]{1,0:T(8,128)(2,1)S(1)}, u32[]{:S(2)}, u32[]{:S(2)}) collective-permute-start(bf16[256,192]{1,0:T(8,128)(2,1)S(1)} %get-tuple-element.70), channel_id=1, source_target_pairs={{0,8},{1,9},{2,10},{3,11},{4,12},{5,13},{6,14},{7,15},{8,16},{9,17... | collective-permute-start | bytes 294920 | tf_op jit(solution)/shard_map/ppermute | solution.py:37
  109.2 14.3 %collective-permute-start.20 = (bf16[128,2048]{1,0:T(8,128)(2,1)S(1)}, bf16[128,2048]{1,0:T(8,128)(2,1)S(1)}, u32[]{:S(2)}, u32[]{:S(2)}) collective-permute-start(bf16[128,2048]{1,0:T(8,128)(2,1)S(1)} %collective-permute-done.15.refs_0_), channel_id=1, source_target_pairs={{0,1},{1,2},{2,3},{3,4},{4,5},{5,6},{6,7},{7,0},{8,9},{9,10},{10,1... | collective-permute-start | bytes 1572872 | tf_op jit(solution)/shard_map/ppermute | solution.py:32
  111.3 12.2 %collective-permute-start.21 = (bf16[128,2048]{1,0:T(8,128)(2,1)S(1)}, bf16[128,2048]{1,0:T(8,128)(2,1)S(1)}, u32[]{:S(2)}, u32[]{:S(2)}) collective-permute-start(bf16[128,2048]{1,0:T(8,128)(2,1)S(1)} %collective-permute-done.16.refs_1_), channel_id=1, source_target_pairs={{0,7},{1,0},{2,1},{3,2},{4,3},{5,4},{6,5},{7,6},{8,15},{9,8},{10,9... | collective-permute-start | bytes 1572872 | tf_op jit(solution)/shard_map/ppermute | solution.py:32
  113.7 5.8 %collective-permute-start.17 = (bf16[256,192]{1,0:T(8,128)(2,1)S(1)}, bf16[256,192]{1,0:T(8,128)(2,1)S(1)}, u32[]{:S(2)}, u32[]{:S(2)}) collective-permute-start(bf16[256,192]{1,0:T(8,128)(2,1)S(1)} %get-tuple-element.74), channel_id=1, source_target_pairs={{0,24},{1,25},{2,26},{3,27},{4,28},{5,29},{6,30},{7,31},{8,0},{9,1... | collective-permute-start | bytes 294920 | tf_op jit(solution)/shard_map/ppermute | solution.py:37
  115.6 6.6 %collective-permute-start.18 = (bf16[256,192]{1,0:T(8,128)(2,1)S(1)}, bf16[256,192]{1,0:T(8,128)(2,1)S(1)}, u32[]{:S(2)}, u32[]{:S(2)}) collective-permute-start(bf16[256,192]{1,0:T(8,128)(2,1)S(1)} %get-tuple-element.75), channel_id=1, source_target_pairs={{0,16},{1,17},{2,18},{3,19},{4,20},{5,21},{6,22},{7,23},{8,24},{9,... | collective-permute-start | bytes 294920 | tf_op jit(solution)/shard_map/ppermute | solution.py:37
  116.0 7.5 %collective-permute-start.19 = (bf16[256,192]{1,0:T(8,128)(2,1)S(1)}, bf16[256,192]{1,0:T(8,128)(2,1)S(1)}, u32[]{:S(2)}, u32[]{:S(2)}) collective-permute-start(bf16[256,192]{1,0:T(8,128)(2,1)S(1)} %get-tuple-element.76), channel_id=1, source_target_pairs={{0,8},{1,9},{2,10},{3,11},{4,12},{5,13},{6,14},{7,15},{8,16},{9,17... | collective-permute-start | bytes 294920 | tf_op jit(solution)/shard_map/ppermute | solution.py:37
  123.5 7.7 %collective-permute-start.25 = (bf16[64,2048]{1,0:T(8,128)(2,1)S(1)}, bf16[64,2048]{1,0:T(8,128)(2,1)S(1)}, u32[]{:S(2)}, u32[]{:S(2)}) collective-permute-start(bf16[64,2048]{1,0:T(8,128)(2,1)S(1)} %slice.6), channel_id=1, source_target_pairs={{0,1},{1,2},{2,3},{3,4},{4,5},{5,6},{6,7},{7,0},{8,9},{9,10},{10,1... | collective-permute-start | bytes 786440 | tf_op jit(solution)/shard_map/ppermute | solution.py:32
  125.1 6.7 %collective-permute-start.26 = (bf16[64,2048]{1,0:T(8,128)(2,1)S(1)}, bf16[64,2048]{1,0:T(8,128)(2,1)S(1)}, u32[]{:S(2)}, u32[]{:S(2)}) collective-permute-start(bf16[64,2048]{1,0:T(8,128)(2,1)S(1)} %slice.7), channel_id=1, source_target_pairs={{0,7},{1,0},{2,1},{3,2},{4,3},{5,4},{6,5},{7,6},{8,15},{9,8},{10,9... | collective-permute-start | bytes 786440 | tf_op jit(solution)/shard_map/ppermute | solution.py:32
  128.5 8.2 %collective-permute-start.22 = (bf16[256,192]{1,0:T(8,128)(2,1)S(1)}, bf16[256,192]{1,0:T(8,128)(2,1)S(1)}, u32[]{:S(2)}, u32[]{:S(2)}) collective-permute-start(bf16[256,192]{1,0:T(8,128)(2,1)S(1)} %get-tuple-element.80), channel_id=1, source_target_pairs={{0,24},{1,25},{2,26},{3,27},{4,28},{5,29},{6,30},{7,31},{8,0},{9,1... | collective-permute-start | bytes 294920 | tf_op jit(solution)/shard_map/ppermute | solution.py:37
  129.9 7.6 %collective-permute-start.23 = (bf16[256,192]{1,0:T(8,128)(2,1)S(1)}, bf16[256,192]{1,0:T(8,128)(2,1)S(1)}, u32[]{:S(2)}, u32[]{:S(2)}) collective-permute-start(bf16[256,192]{1,0:T(8,128)(2,1)S(1)} %get-tuple-element.81), channel_id=1, source_target_pairs={{0,16},{1,17},{2,18},{3,19},{4,20},{5,21},{6,22},{7,23},{8,24},{9,... | collective-permute-start | bytes 294920 | tf_op jit(solution)/shard_map/ppermute | solution.py:37
  129.9 8.4 %collective-permute-start.24 = (bf16[256,192]{1,0:T(8,128)(2,1)S(1)}, bf16[256,192]{1,0:T(8,128)(2,1)S(1)}, u32[]{:S(2)}, u32[]{:S(2)}) collective-permute-start(bf16[256,192]{1,0:T(8,128)(2,1)S(1)} %get-tuple-element.82), channel_id=1, source_target_pairs={{0,8},{1,9},{2,10},{3,11},{4,12},{5,13},{6,14},{7,15},{8,16},{9,17... | collective-permute-start | bytes 294920 | tf_op jit(solution)/shard_map/ppermute | solution.py:37
  132.9 5.4 %collective-permute-start.27 = (bf16[128,192]{1,0:T(8,128)(2,1)S(1)}, bf16[128,192]{1,0:T(8,128)(2,1)S(1)}, u32[]{:S(2)}, u32[]{:S(2)}) collective-permute-start(bf16[128,192]{1,0:T(8,128)(2,1)S(1)} %get-tuple-element.86), channel_id=1, source_target_pairs={{0,24},{1,25},{2,26},{3,27},{4,28},{5,29},{6,30},{7,31},{8,0},{9,1... | collective-permute-start | bytes 147464 | tf_op jit(solution)/shard_map/ppermute | solution.py:37
  134.7 5.8 %collective-permute-start.28 = (bf16[128,192]{1,0:T(8,128)(2,1)S(1)}, bf16[128,192]{1,0:T(8,128)(2,1)S(1)}, u32[]{:S(2)}, u32[]{:S(2)}) collective-permute-start(bf16[128,192]{1,0:T(8,128)(2,1)S(1)} %get-tuple-element.87), channel_id=1, source_target_pairs={{0,16},{1,17},{2,18},{3,19},{4,20},{5,21},{6,22},{7,23},{8,24},{9,... | collective-permute-start | bytes 147464 | tf_op jit(solution)/shard_map/ppermute | solution.py:37
  136.7 5.5 %collective-permute-start.29 = (bf16[128,192]{1,0:T(8,128)(2,1)S(1)}, bf16[128,192]{1,0:T(8,128)(2,1)S(1)}, u32[]{:S(2)}, u32[]{:S(2)}) collective-permute-start(bf16[128,192]{1,0:T(8,128)(2,1)S(1)} %get-tuple-element.88), channel_id=1, source_target_pairs={{0,8},{1,9},{2,10},{3,11},{4,12},{5,13},{6,14},{7,15},{8,16},{9,17... | collective-permute-start | bytes 147464 | tf_op jit(solution)/shard_map/ppermute | solution.py:37
  (1 other events, 0.8 us)

commit v3 on v2

v3 whole, which is shorter than its diff:
```python
import functools
import jax
import jax.numpy as jnp
from jax import lax
from jax.experimental import pallas as pl
from jax.experimental.pallas import tpu as pltpu
from jax.sharding import PartitionSpec as P

NX = 4
NZ = 8
NODES = 32
HEADS = 64
HD = 128
PAIR = 2 * HD
QUART = 2048
PART = QUART // 4

NY = 4
COLS = 192
MSG = NODES * 8 + 2 * COLS
HROWS = 64
PIECE = 16 * HROWS + 16
ROWS = NX * NODES
QROWS = 2 * NODES + 16
NT = (((1,), (1,)), ((), ()))
BF = jnp.bfloat16
F32 = jnp.float32
ANY = pl.BlockSpec(memory_space=pl.ANY)
HBM = pl.BlockSpec(memory_space=pltpu.HBM)
VMEM = pl.BlockSpec(memory_space=pltpu.VMEM)
SMEM = pl.BlockSpec(memory_space=pltpu.SMEM)
WIDEST = pltpu.CompilerParams(vmem_limit_bytes=60 * 1024 * 1024)
PARAMS = pltpu.CompilerParams(vmem_limit_bytes=16 * 1024 * 1024)


def zsend(array, shift):
    pairs = [(x * NZ + z, x * NZ + (z + shift) % NZ) for x in range(NX) for z in range(NZ)]
    return lax.ppermute(array, "head", pairs)


def xsend(array, shift):
    pairs = [(x * NZ + z, ((x + shift) % NX) * NZ + z) for x in range(NX) for z in range(NZ)]
    return lax.ppermute(array, "head", pairs)


def swap_y(array):
    return lax.ppermute(array, "dp", [(i, i ^ 2) for i in range(2 * NY)])


def swap_core(array):
    return lax.ppermute(array, "dp", [(i, i ^ 1) for i in range(2 * NY)])


def place():
    me = lax.axis_index("head")
    return lax.div(me, NZ), lax.rem(me, NZ)


def cost(flops, size, trans=0):
    return pl.CostEstimate(flops=flops, bytes_accessed=size, transcendentals=trans)


def run_copies(pairs, sems):
    copies = [pltpu.make_async_copy(a, b, sems.at[n]) for n, (a, b) in enumerate(pairs)]
    for copy in copies:
        copy.start()
    return copies


def split3(value):
    hi = value.astype(BF).astype(F32)
    mid = (value - hi).astype(BF).astype(F32)
    return hi, mid, value - hi - mid


def pack_queries_kernel(decay, q_hbm, out, q, sems):
    cuts = [slice(n * QUART, (n + 1) * QUART) for n in range(NX)]
    copies = run_copies([(q_hbm.at[0, :, cut], q.at[:, cut]) for cut in cuts], sems)
    row = lax.broadcasted_iota(jnp.int32, (16, HD), 0)
    rows = jnp.zeros((16, HD), F32)
    for j in range(2):
        for n, piece in enumerate(split3(jnp.full((16, HD), decay[j], F32))):
            rows = jnp.where(row == 3 * j + n, piece, rows)
    tail = rows.astype(BF)
    for n in range(NX * NZ):
        out[n, 2 * NODES :, :] = tail
    for n in range(NX * NZ):
        if n % NZ == 0:
            copies[n // NZ].wait()
        for j in range(2):
            out[n, j * NODES : (j + 1) * NODES, :] = q[:, (2 * n + j) * HD : (2 * n + j + 1) * HD]


def pack_queries(decay, q):
    return pl.pallas_call(
        pack_queries_kernel,
        in_specs=[SMEM, HBM],
        out_specs=VMEM,
        out_shape=jax.ShapeDtypeStruct((NX * NZ, QROWS, HD), BF),
        scratch_shapes=[pltpu.VMEM((NODES, HEADS * HD), BF), pltpu.SemaphoreType.DMA((NX,))],
        cost_estimate=cost(0, 1_000_000),
        compiler_params=WIDEST,
    )(decay, q)


def pack_messages_kernel(gate_hbm, w, after, w0_hbm, *refs):
    outs_hbm, (gate, w0, outs, sems) = refs[:NX], refs[NX:]
    x, _ = place()
    cuts = [slice(n * QUART, (n + 1) * QUART) for n in range(NX)]
    pairs = [(gate_hbm.at[0, :, cut], gate.at[:, cut]) for cut in cuts]
    bases = [lax.rem(x + n, NX) * QUART for n in range(NX)]
    for n in (2, 1, 3):
        for b in range(2):
            col = pl.multiple_of(bases[n] + lax.rem(lax.axis_index("dp"), 4) * PART + b * PAIR, PAIR)
            pairs.append((w.at[:, pl.ds(col, PAIR)], outs.at[n, pl.ds(NZ * NODES + b * COLS, COLS)]))
    pairs.append((w.at[:, pl.ds(pl.multiple_of(x * QUART, QUART), QUART)], w0))
    copies = run_copies(pairs, sems)
    for copy in copies[:NX]:
        copy.wait()
    sends = []
    for i, n in enumerate((2, 1, 3, 0)):
        for b in range(NZ):
            cols = pl.ds(pl.multiple_of(bases[n] + b * PAIR, PAIR), PAIR)
            outs[n, b * NODES : (b + 1) * NODES, :] = gate[:, cols]
        rows = pl.ds(0, NZ * NODES)
        if n:
            copies[NX + 2 * i].wait()
            copies[NX + 2 * i + 1].wait()
            rows = pl.ds(0, MSG)
        sends.append(pltpu.make_async_copy(outs.at[n, rows], outs_hbm[n].at[rows], sems.at[len(pairs) + n]))
        sends[-1].start()
    copies[-1].wait()
    sends.append(pltpu.make_async_copy(w0, w0_hbm, sems.at[len(pairs) + NX]))
    sends[-1].start()
    for send in sends:
        send.wait()


def pack_messages(gate, w, after):
    return pl.pallas_call(
        pack_messages_kernel,
        in_specs=[HBM] * 2 + [ANY],
        out_specs=[HBM] * (1 + NX),
        out_shape=[jax.ShapeDtypeStruct((COLS, QUART), BF)] + [jax.ShapeDtypeStruct((NZ * NODES, PAIR), BF)]
        + [jax.ShapeDtypeStruct((MSG, PAIR), BF)] * (NX - 1),
        scratch_shapes=[
            pltpu.VMEM((NODES, HEADS * HD), BF),
            pltpu.VMEM((COLS, QUART), BF),
            pltpu.VMEM((NX, MSG, PAIR), BF),
            pltpu.SemaphoreType.DMA((NX + 7 + NX + 1,)),
        ],
        cost_estimate=cost(0, 4_000_000),
        compiler_params=WIDEST,
    )(gate, w, after)


def join_weights_kernel(w0, m0, m1, theirs, out):
    part = lax.rem(lax.axis_index("dp"), 4)
    flip = 1 - 2 * lax.rem(part, 2)
    far = lax.rem(part + 2, 4)
    out[0] = w0[...]
    for s, (ref, mine) in enumerate(((m0, part), (m1, far))):
        for d in range(NX - 1):
            for b in range(2):
                near = pl.ds(pl.multiple_of(mine * PART + b * PAIR, PAIR), PAIR)
                other = pl.ds(pl.multiple_of((mine + flip) * PART + b * PAIR, PAIR), PAIR)
                out[d + 1, :, near] = ref[d, b * COLS : (b + 1) * COLS]
                out[d + 1, :, other] = theirs[s, d, b * COLS : (b + 1) * COLS]


def join_weights(w0, m0, m1, theirs):
    return pl.pallas_call(
        join_weights_kernel,
        in_specs=[VMEM] * 4,
        out_specs=VMEM,
        out_shape=jax.ShapeDtypeStruct((NX, COLS, QUART), BF),
        cost_estimate=cost(0, 6_000_000),
        compiler_params=PARAMS,
    )(w0, m0, m1, theirs)


def inter_kernel(queries, states, *refs):
    out, extras = refs[-2:]
    for r in range(NX * NZ):
        x, z = divmod(r, NZ)
        for j in range(2):
            rows = slice(j * NODES, (j + 1) * NODES)
            inter = jnp.dot(queries[r, rows, :], states[r, j], preferred_element_type=F32)
            out[z, x * NODES : (x + 1) * NODES, j * HD : (j + 1) * HD] = inter.astype(BF)
        extras[r] = queries[r, 2 * NODES :, :]


def inter_part(queries, states, marks):
    return pl.pallas_call(
        inter_kernel,
        in_specs=[VMEM] * 2 + [ANY] * len(marks),
        out_specs=[VMEM] * 2,
        out_shape=[
            jax.ShapeDtypeStruct((NZ, ROWS, PAIR), BF),
            jax.ShapeDtypeStruct((NX * NZ, 16, HD), BF),
        ],
        cost_estimate=cost(70_000_000, 4_000_000, 100_000),
        compiler_params=PARAMS,
    )(queries, states, *marks)


CHUNKS = 4
STEP = HEADS * HD // CHUNKS


def decay_rows(extra):
    extra = extra.astype(F32)
    return [extra[3 * j : 3 * j + 1] + extra[3 * j + 1 : 3 * j + 2] + extra[3 * j + 2 : 3 * j + 3] for j in range(2)]


def intra_kernel(sizes, q_hbm, k_hbm, v_hbm, extras_hbm, anc_hbm, m1, m2, m3, *refs):
    outs_hbm, weights_hbm, (parts, extras, tree, out, weights, sems) = refs[:NX], refs[NX], refs[NX + 1 :]
    me = lax.axis_index("head")
    x, _ = place()
    cuts = [pl.ds(c * STEP, STEP) for c in range(CHUNKS)]
    pairs = [(anc_hbm.at[me], tree), (extras_hbm, extras)]
    for cut in cuts:
        pairs += [(ref.at[0, :, cut], parts.at[n, :, cut]) for n, ref in enumerate((q_hbm, k_hbm, v_hbm))]
    pairs += [(m.at[pl.ds(NZ * NODES, 2 * COLS)], weights.at[n]) for n, m in enumerate((m1, m2, m3))]
    copies = run_copies(pairs, sems)
    node = lax.broadcasted_iota(jnp.int32, (NODES, HD), 0)
    lane = lax.broadcasted_iota(jnp.int32, (NODES, HD), 1)
    live = (node < sizes[me]).astype(F32)
    copies[0].wait()
    copies[1].wait()
    anc = tree[...].astype(F32)
    depth = jnp.sum(anc, axis=1, keepdims=True)
    depth_t = lax.dot_general(jnp.ones((8, NODES), BF), anc.astype(BF), NT, preferred_element_type=F32)[0:1]
    blocks = HD // NODES
    wide_anc = jnp.concatenate([anc] * blocks, axis=1)
    wide_gaps = jnp.concatenate([depth - depth_t] * blocks, axis=1)
    own = [lane // NODES == n for n in range(blocks)]
    mask = jnp.concatenate([jnp.where(m, wide_anc, 0.0) for m in own])
    gaps = jnp.concatenate([jnp.where(m, wide_gaps, 0.0) for m in own])
    quarter = HEADS // NX
    for c in range(CHUNKS):
        for n in range(3):
            copies[2 + 3 * c + n].wait()
        shift = lax.rem(c - x + NX, NX)
        for first in range(c * quarter, (c + 1) * quarter, blocks):
            heads = range(first, first + blocks)
            q, k, v = (jnp.concatenate([parts[n, :, h * HD : (h + 1) * HD] for h in heads]) for n in range(3))
            rates = [jnp.broadcast_to(decay_rows(extras[h // 2])[h % 2], (NODES, HD)) for h in heads]
            scores = lax.dot_general(q, k, NT, preferred_element_type=F32)
            mix = (scores * (mask * jnp.exp(-jnp.concatenate(rates) * gaps))).astype(BF)
            intra = jnp.dot(mix, v, preferred_element_type=F32)
            for n, h in enumerate(heads):
                near = h % quarter
                value = live * intra[n * NODES : (n + 1) * NODES]
                out[shift, :, near * HD : (near + 1) * HD] = value.astype(BF)
    for copy in copies[2 + 3 * CHUNKS :]:
        copy.wait()
    sends = [pltpu.make_async_copy(out.at[n], outs_hbm[n], sems.at[len(pairs) + n]) for n in range(NX)]
    sends.append(pltpu.make_async_copy(weights, weights_hbm, sems.at[len(pairs) + NX]))
    for send in sends:
        send.start()
    for send in sends:
        send.wait()


def intra_part(sizes, q, k, v, extras, anc, messages):
    return pl.pallas_call(
        intra_kernel,
        in_specs=[SMEM] + [HBM] * 8,
        out_specs=[HBM] * (NX + 1),
        out_shape=[jax.ShapeDtypeStruct((NODES, QUART), BF)] * NX
        + [jax.ShapeDtypeStruct((NX - 1, 2 * COLS, PAIR), BF)],
        scratch_shapes=[
            pltpu.VMEM((3, NODES, HEADS * HD), BF),
            pltpu.VMEM((NX * NZ, 16, HD), BF),
            pltpu.VMEM((NODES, NODES), jnp.int32),
            pltpu.VMEM((NX, NODES, QUART), BF),
            pltpu.VMEM((NX - 1, 2 * COLS, PAIR), BF),
            pltpu.SemaphoreType.DMA((2 + 3 * CHUNKS + 3 + NX + 1,)),
        ],
        cost_estimate=cost(100_000_000, 4_000_000, 200_000),
        compiler_params=WIDEST,
    )(sizes, q, k, v, extras, anc, *messages)


def merge_kernel(sizes, inter_hbm, gain_hbm, extras_hbm, anc_hbm, *refs):
    intras, gates, refs = refs[:NX], refs[NX : 2 * NX], refs[2 * NX :]
    out, inter_ref, gate_ref, gain, extras, tree, square_ref, sems = refs
    x, z = place()
    spots = [lax.rem(x - slot + NX, NX) for slot in range(NX)]
    pairs = [(inter_hbm, inter_ref), (extras_hbm.at[pl.ds(x * NZ, NZ)], extras)]
    pairs.append((gain_hbm.at[pl.ds(pl.multiple_of(x * 2 * NZ, 2 * NZ), 2 * NZ)], gain))
    for slot, xa in enumerate(spots):
        pairs.append((anc_hbm.at[xa * NZ + z], tree.at[slot]))
        pairs.append((gates[slot].at[pl.ds(0, NZ * NODES)], gate_ref.at[slot]))
    copies = run_copies(pairs, sems)
    node = lax.broadcasted_iota(jnp.int32, (NODES, HD), 0)
    lane = lax.broadcasted_iota(jnp.int32, (1, HD), 1)
    copies[1].wait()
    rates = jnp.zeros((1, HD), F32)
    for h in range(2 * NZ):
        rates = jnp.where(lane == h, decay_rows(extras[h // 2])[h % 2], rates)
    copies[0].wait()
    copies[2].wait()
    for slot, xa in enumerate(spots):
        rows = pl.ds(pl.multiple_of(xa * NODES, NODES), NODES)
        half = lax.div(xa, 2)
        near = lax.rem(xa, 2) * NODES
        for copy in copies[3 + 2 * slot : 5 + 2 * slot]:
            copy.wait()
        depth = jnp.sum(tree[slot].astype(F32), axis=1, keepdims=True)
        live = (node < sizes[xa * NZ + z]).astype(F32)
        fade = live * jnp.exp(-rates * depth)
        squares = jnp.zeros((NODES, HD), F32)
        for h in range(2 * NZ):
            lanes = slice((h % 2) * HD, (h % 2 + 1) * HD)
            inter = inter_ref[h // 2, rows, lanes].astype(F32)
            intra = intras[slot][:, h * HD : (h + 1) * HD].astype(F32)
            attn = (fade[:, h : h + 1] * inter + intra).astype(BF).astype(F32)
            squares = squares + attn * attn
            gate = gate_ref[slot, (h // 2) * NODES : (h // 2 + 1) * NODES, lanes].astype(F32)
            place_rows = pl.ds(pl.multiple_of(h * HROWS + near, NODES), NODES)
            out[half, place_rows, :] = (attn * gain[h : h + 1, :] / (1.0 + jnp.exp(-gate))).astype(BF)
        square_ref[rows, :] = squares
    ones = jnp.ones((16, HD), BF)
    total = jnp.zeros((16, ROWS), F32)
    for piece in split3(square_ref[...]):
        total = total + lax.dot_general(ones, piece.astype(BF), NT, preferred_element_type=F32)
    row = lax.broadcasted_iota(jnp.int32, (16, ROWS), 0)
    hi, mid, low = split3(total)
    tail = jnp.where(row == 0, hi, jnp.where(row == 1, mid, jnp.where(row == 2, low, 0.0))).astype(BF)
    for half in range(2):
        out[half, 16 * HROWS :, :] = tail


def merge(sizes, inter, gain, extras, anc, intras, gates):
    return pl.pallas_call(
        merge_kernel,
        in_specs=[SMEM] + [HBM] * 4 + [VMEM] * NX + [HBM] * NX,
        out_specs=VMEM,
        out_shape=jax.ShapeDtypeStruct((2, PIECE, HD), BF),
        scratch_shapes=[
            pltpu.VMEM((NZ, ROWS, PAIR), BF),
            pltpu.VMEM((NX, NZ * NODES, PAIR), BF),
            pltpu.VMEM((2 * NZ, HD), F32),
            pltpu.VMEM((NZ, 16, HD), BF),
            pltpu.VMEM((NX, NODES, NODES), jnp.int32),
            pltpu.VMEM((ROWS, HD), F32),
            pltpu.SemaphoreType.DMA((3 + 2 * NX,)),
        ],
        cost_estimate=cost(10_000_000, 4_000_000),
        compiler_params=PARAMS,
    )(sizes, inter, gain, extras, anc, *intras, *gates)


def project_kernel(halves, count, *refs):
    pieces, weights, outs, lhs = refs[:count], refs[count], refs[count + 1 : count + 1 + NX], refs[-1]
    pick = lax.broadcasted_iota(jnp.int32, (16, 64), 0) == lax.broadcasted_iota(jnp.int32, (16, 64), 1)
    pick = pick.astype(F32).astype(BF)
    for n, (ref, which, half) in enumerate(halves):
        piece = pieces[ref] if which is None else pieces[ref].at[which]
        rows = slice(n * HROWS, (n + 1) * HROWS)
        for h in range(2 * NZ):
            lhs[rows, h * HD : (h + 1) * HD] = piece[h * HROWS : (h + 1) * HROWS, :]
        sums = lax.dot_general(
            piece[16 * HROWS :, :], pick, (((0,), (0,)), ((), ())), preferred_element_type=F32
        )[half * HROWS : (half + 1) * HROWS]
        for out in outs:
            out[rows, COLS:] = sums.astype(out.dtype)
    for n, out in enumerate(outs):
        acc = lax.dot_general(lhs[...], weights[n], NT, preferred_element_type=F32)
        out[:, :COLS] = acc.astype(out.dtype)


def project(pieces, weights):
    halves = []
    for ref, piece in enumerate(pieces):
        if piece.ndim == 3:
            halves += [(ref, 0, 0), (ref, 1, 1)]
        else:
            halves.append((ref, None, ref))
    rows = len(halves) * HROWS
    return pl.pallas_call(
        functools.partial(project_kernel, halves, len(pieces)),
        in_specs=[VMEM] * (len(pieces) + 1),
        out_specs=[VMEM] * NX,
        out_shape=[jax.ShapeDtypeStruct((rows, 256), F32)] + [jax.ShapeDtypeStruct((rows, 256), BF)] * (NX - 1),
        scratch_shapes=[pltpu.VMEM((rows, QUART), BF)],
        cost_estimate=cost(2 * rows * QUART * COLS * NX, 4_000_000),
        compiler_params=PARAMS,
    )(*pieces, weights)


def finish_kernel(layout, *refs):
    out = refs[-1]
    _, z = place()
    for g, places in enumerate(layout):
        own, a, b, c = refs[4 * g : 4 * g + 4]
        row = 0
        for shift, first, last in places:
            size = (last - first) * NODES
            rows = slice(row, row + size)
            total = own[rows, :] + a[rows, :].astype(F32) + b[rows, :].astype(F32) + c[rows, :].astype(F32)
            squares = total[:, COLS : COLS + 1] + total[:, COLS + 1 : COLS + 2] + total[:, COLS + 2 : COLS + 3]
            scaled = total[:, :COLS] * lax.rsqrt(squares * (1.0 / (HEADS * HD)) + 1e-06)
            source = lax.rem(z - shift + 2 * NZ, NZ)
            for x in range(first, last):
                part = scaled[(x - first) * NODES : (x - first + 1) * NODES]
                out[x, source] = part.astype(BF)
            row += size


def finish(groups, layout):
    flat = [a for group in groups for a in group]
    return pl.pallas_call(
        functools.partial(finish_kernel, layout),
        in_specs=[VMEM] * len(flat),
        out_specs=VMEM,
        out_shape=jax.ShapeDtypeStruct((NX, NZ, NODES, COLS), BF),
        cost_estimate=cost(2_000_000, 4_000_000),
        compiler_params=PARAMS,
    )(*flat)


ZLINES = [[x * NZ + z for z in range(NZ)] for x in range(NX)]


def tie(arrays, *marks):
    return lax.optimization_barrier((*arrays, *marks))[: len(arrays)]


def per_device(queries, keys, values, gate, states, decay, ancestors, tree_sizes, gain, out_weight):
    packed = pack_queries(decay, queries)
    w0, m0, m1, m2, m3 = pack_messages(gate, out_weight.T, packed)
    m2, m1, m3 = xsend(m2, 2), xsend(m1, 1), xsend(m3, 3)
    spread = lax.all_to_all(packed, "head", 0, 0, tiled=True)
    inter, extras = inter_part(spread, states, [])
    (inter,) = tie((inter,), m1, m2, m3)
    inter = lax.all_to_all(inter, "head", 0, 0, axis_index_groups=ZLINES, tiled=True)
    t0, t1, t2, t3, mine = intra_part(tree_sizes, queries, keys, values, extras, ancestors, (m1, m2, m3))
    t2, t1, t3 = xsend(t2, 2), xsend(t1, 1), xsend(t3, 3)
    yours = swap_y(mine)
    gain = gain.reshape(HEADS, HD)
    own = merge(tree_sizes, inter, gain, extras, ancestors, (t0, t1, t2, t3), (m0, m1, m2, m3))
    theirs = swap_core(jnp.stack(tie((mine, yours), own)))
    weights = join_weights(w0, mine, yours, theirs)

    groups, layout = [], []

    def send_sums(pieces, places):
        own_part, *others = project(pieces, weights)
        groups.append([own_part] + [xsend(p, -d) for d, p in enumerate(others, 1)])
        layout.append(places)
        return own_part

    up, dn = zsend(own, 1), zsend(own, -1)
    mark = send_sums([own], [(0, 0, NX)])
    for step in range(1, 4):
        up, dn = tie((up, dn), *groups[-1])
        pieces = up, dn
        if step < 3:
            up, dn = zsend(up, 1), zsend(dn, -1)
        else:
            up, dn = zsend(up[0], 1), zsend(dn[1], -1)
        mark = send_sums(pieces, [(step, 0, NX), (-step, 0, NX)])
    last = tie((up, dn), mark)
    send_sums(last, [(4, 0, NX // 2), (-4, NX // 2, NX)])
    out = finish(groups, layout)
    return out.reshape(NX * NZ, NODES, COLS)


def solution(mesh):
    return jax.shard_map(
        per_device,
        mesh=mesh,
        in_specs=(
            P(("dp", "head"), None, None),
            P(("dp", "head"), None, None),
            P(("dp", "head"), None, None),
            P(("dp", "head"), None, None),
            P("dp", "head", None, None),
            P("head"),
            P("dp", None, None),
            P("dp"),
            P(),
            P(None, "head"),
        ),
        out_specs=P("dp", None, "head"),
        check_vma=False,
    )
```

time: 144 us -> 138 us (0.958)
  local copies, waits for them, and re-layouts: 13.1 us -> 3.6 us
  starting transfers between devices: 60.5 us -> 62.8 us
  waiting for transfers between devices: 46.3 us -> 47.8 us
    ppermute x21, waiting for transfers between devices: 42.6 us -> 29.3 us  [xsend(): return lax.ppermute(array, 'head', pairs)]
    all_to_all x1, waiting for transfers between devices: 0.23 us -> 11.6 us  [per_device(): spread = lax.all_to_all(packed, 'head', 0, 0, tiled=True)]
    unnamed x34 -> x30, local copies, waits for them, and re-layouts: 13 us -> 3.56 us
    ppermute x8, waiting for transfers between devices: 2.05 us -> 6.81 us  [zsend(): return lax.ppermute(array, 'head', pairs)]
    ppermute x21, starting transfers between devices: 27.7 us -> 30.8 us  [xsend(): return lax.ppermute(array, 'head', pairs)]
    all_to_all x1, starting transfers between devices: 7.91 us -> 5.73 us  [per_device(): lax.all_to_all(inter, 'head', 0, 0, axis_index_groups=ZLINES, tiled=True)]
    all_to_all x1, waiting for transfers between devices: 1.48 us -> 0.01 us  [per_device(): lax.all_to_all(inter, 'head', 0, 0, axis_index_groups=ZLINES, tiled=True)]
    ppermute x1 -> x2, starting transfers between devices: 0.01 us -> 1.46 us  [the longest x1 1.37 us: swap_y(): return lax.ppermute(array, 'dp', [(i, i ^ 2) for i in range(2 * NY)])]
  transfers between devices with their start and end apart: 32 -> 33, of which waited for: 21 -> 17; matrix products, arithmetic and copies ran while one was open for 1% -> 0% of each run, Pallas kernels for 12% -> 14%
where the time goes in v3:
time: 138 us
  starting transfers between devices  62.8 us (46%)
  waiting for transfers between devices  47.8 us (35%)
  Pallas kernels  23.2 us (17%)
  local copies, waits for them, and re-layouts  3.6 us (3%)
    ppermute x21, starting transfers between devices, xsend(): return lax.ppermute(array, 'head', pairs)  30.8 us
    ppermute x21, waiting for transfers between devices, xsend(): return lax.ppermute(array, 'head', pairs)  29.3 us
    ppermute x8, starting transfers between devices, zsend(): return lax.ppermute(array, 'head', pairs)  13.5 us
    all_to_all x1, waiting for transfers between devices, per_device(): spread = lax.all_to_all(packed, 'head', 0, 0, tiled=True)  11.6 us
    all_to_all x1, starting transfers between devices, per_device(): spread = lax.all_to_all(packed, 'head', 0, 0, tiled=True)  11.3 us
    ppermute x8, waiting for transfers between devices, zsend(): return lax.ppermute(array, 'head', pairs)  6.81 us
    pallas_call x5, Pallas kernels, project(): pl.pallas_call(functools.partial(project_kernel, halves, len(pieces)), in...  6.28 us
    pallas_call x1, Pallas kernels, intra_part(): pl.pallas_call(intra_kernel, in_specs=[SMEM] + [HBM] * 8, out_specs=[HBM]...  6.12 us
  transfers between devices with their start and end apart: 33, of which 17 were waited for; matrix products, arithmetic and copies ran while one was open for 0% of the time, Pallas kernels for 14%

profile of v3, /device:TPU:16, one launch (start us, length us, event | category | flops | bytes accessed | tf_op | source)
XLA Modules:
  0.0 137.8 jit_solution(2973731461640410447)
XLA Ops:
  0.0 2.6 %shard_map.100.after = bf16[32,80,128]{2,1,0:T(8,128)(2,1)} custom-call(f32[2]{0:T(128)} %decay.1, bf16[1,32,8192]{2,1,0:T(8,128)(2,1)} %q_hbm.3), custom_call_target="tpu_custom_call" | custom-call | bytes 1000000 | tf_op jit(solution)/shard_map/pallas_call | solution.py:95
  2.7 11.3 %all-to-all-start = ((bf16[32,80,128]{2,1,0:T(8,128)(2,1)}), bf16[32,80,128]{2,1,0:T(8,128)(2,1)S(1)}, u32[]{:S(2)}, u32[]{:S(2)}) async-start(bf16[32,80,128]{2,1,0:T(8,128)(2,1)} %shard_map.100.after), calls=%async_computation | async-start | bytes 1310720 | tf_op jit(solution)/shard_map/all_to_all | solution.py:436
  14.0 2.8 %shard_map.102 = (bf16[192,2048]{1,0:T(8,128)(2,1)}, bf16[256,256]{1,0:T(8,128)(2,1)}, bf16[640,256]{1,0:T(8,128)(2,1)}, bf16[640,256]{1,0:T(8,128)(2,1)}, bf16[640,256]{1,0:T(8,128)(2,1)}) custom-call(bf16[1,32,8192]{2,1,0:T(8,128)(2,1)} %gate_hbm.1, bf16[192,8192]{1,0:T(8,128)(2,1)} %bitcast.12, bf16[32,80,128]{2,1,0:T(8,128)(2,1)} %shard_map.100.after), custom_call_target="tpu_custom_call" | custom-call | bytes 4000000 | tf_op jit(solution)/shard_map/pallas_call | solution.py:140
  16.8 1.9 %collective-permute-start = (bf16[640,256]{1,0:T(8,128)(2,1)}, bf16[640,256]{1,0:T(8,128)(2,1)S(1)}, u32[]{:S(2)}, u32[]{:S(2)}) collective-permute-start(bf16[640,256]{1,0:T(8,128)(2,1)} %get-tuple-element.49), channel_id=1, source_target_pairs={{0,8},{1,9},{2,10},{3,11},{4,12},{5,13},{6,14},{7,15},{8,16},{9,17... | collective-permute-start | bytes 983048 | tf_op jit(solution)/shard_map/ppermute | solution.py:43
  18.7 2.7 %collective-permute-start.1 = (bf16[640,256]{1,0:T(8,128)(2,1)}, bf16[640,256]{1,0:T(8,128)(2,1)S(1)}, u32[]{:S(2)}, u32[]{:S(2)}) collective-permute-start(bf16[640,256]{1,0:T(8,128)(2,1)} %get-tuple-element.50), channel_id=1, source_target_pairs={{0,16},{1,17},{2,18},{3,19},{4,20},{5,21},{6,22},{7,23},{8,24},{9,... | collective-permute-start | bytes 983048 | tf_op jit(solution)/shard_map/ppermute | solution.py:43
  21.4 1.4 %collective-permute-start.2 = (bf16[640,256]{1,0:T(8,128)(2,1)}, bf16[640,256]{1,0:T(8,128)(2,1)}, u32[]{:S(2)}, u32[]{:S(2)}) collective-permute-start(bf16[640,256]{1,0:T(8,128)(2,1)} %get-tuple-element.51), channel_id=1, source_target_pairs={{0,24},{1,25},{2,26},{3,27},{4,28},{5,29},{6,30},{7,31},{8,0},{9,1... | collective-permute-start | bytes 983048 | tf_op jit(solution)/shard_map/ppermute | solution.py:43
  22.8 11.6 %all-to-all-done.queries = bf16[32,80,128]{2,1,0:T(8,128)(2,1)S(1)} async-done(((bf16[32,80,128]{2,1,0:T(8,128)(2,1)}), bf16[32,80,128]{2,1,0:T(8,128)(2,1)S(1)}, u32[]{:S(2)}, u32[]{:S(2)}) %all-to-all-start) | async-done | bytes 655392 | tf_op jit(solution)/shard_map/all_to_all | solution.py:436
  35.8 5.0 %collective-permute-done.1.m2.refs_6_ = bf16[640,256]{1,0:T(8,128)(2,1)S(1)} collective-permute-done((bf16[640,256]{1,0:T(8,128)(2,1)}, bf16[640,256]{1,0:T(8,128)(2,1)S(1)}, u32[]{:S(2)}, u32[]{:S(2)}) %collective-permute-start.1) | collective-permute-done | bytes 327712 | tf_op jit(solution)/shard_map/ppermute | solution.py:43
  40.8 5.7 %all-to-all-start.1 = ((bf16[8,128,256]{2,1,0:T(8,128)(2,1)}), bf16[8,128,256]{2,1,0:T(8,128)(2,1)S(1)}, u32[]{:S(2)}, u32[]{:S(2)}) async-start(bf16[8,128,256]{2,1,0:T(8,128)(2,1)} %copy-done.8), calls=%async_computation.1 | async-start | bytes 1048576 | tf_op jit(solution)/shard_map/all_to_all | solution.py:439
  46.6 6.1 %shard_map.103 = (bf16[32,2048]{1,0:T(8,128)(2,1)}, bf16[32,2048]{1,0:T(8,128)(2,1)}, bf16[32,2048]{1,0:T(8,128)(2,1)}, bf16[32,2048]{1,0:T(8,128)(2,1)}, bf16[3,384,256]{2,1,0:T(8,128)(2,1)}) custom-call(s32[32]{0:T(128)} %sizes.3, bf16[1,32,8192]{2,1,0:T(8,128)(2,1)} %q_hbm.3, bf16[1,32,8192]{2,1,0:T(8,128)(2,1)} %k_hbm.1, bf16[1,32,8192]{2,1,0:T(8,128)(2,1)} %v_hbm.1, ...), custom_call_target="tpu_custom_call" | custom-call | flops 100000000 | bytes 4000000 | tf_op jit(solution)/shard_map/pallas_call | solution.py:267
  52.7 1.4 collective-permute-start.6
  54.1 1.6 %collective-permute-start.3 = (bf16[32,2048]{1,0:T(8,128)(2,1)}, bf16[32,2048]{1,0:T(8,128)(2,1)S(1)}, u32[]{:S(2)}, u32[]{:S(2)}) collective-permute-start(bf16[32,2048]{1,0:T(8,128)(2,1)} %get-tuple-element.55), channel_id=1, source_target_pairs={{0,8},{1,9},{2,10},{3,11},{4,12},{5,13},{6,14},{7,15},{8,16},{9,17... | collective-permute-start | bytes 393224 | tf_op jit(solution)/shard_map/ppermute | solution.py:43
  55.7 2.4 %collective-permute-start.4 = (bf16[32,2048]{1,0:T(8,128)(2,1)}, bf16[32,2048]{1,0:T(8,128)(2,1)S(1)}, u32[]{:S(2)}, u32[]{:S(2)}) collective-permute-start(bf16[32,2048]{1,0:T(8,128)(2,1)} %get-tuple-element.56), channel_id=1, source_target_pairs={{0,16},{1,17},{2,18},{3,19},{4,20},{5,21},{6,22},{7,23},{8,24},{9,... | collective-permute-start | bytes 393224 | tf_op jit(solution)/shard_map/ppermute | solution.py:43
  58.1 1.4 %collective-permute-start.5 = (bf16[32,2048]{1,0:T(8,128)(2,1)}, bf16[32,2048]{1,0:T(8,128)(2,1)S(1)}, u32[]{:S(2)}, u32[]{:S(2)}) collective-permute-start(bf16[32,2048]{1,0:T(8,128)(2,1)} %get-tuple-element.57), channel_id=1, source_target_pairs={{0,24},{1,25},{2,26},{3,27},{4,28},{5,29},{6,30},{7,31},{8,0},{9,1... | collective-permute-start | bytes 393224 | tf_op jit(solution)/shard_map/ppermute | solution.py:43
  59.5 1.9 %collective-permute-done.3.refs_1_ = bf16[32,2048]{1,0:T(8,128)(2,1)S(1)} collective-permute-done((bf16[32,2048]{1,0:T(8,128)(2,1)}, bf16[32,2048]{1,0:T(8,128)(2,1)S(1)}, u32[]{:S(2)}, u32[]{:S(2)}) %collective-permute-start.3) | collective-permute-done | bytes 131104 | tf_op jit(solution)/shard_map/ppermute | solution.py:43
  61.4 2.5 %collective-permute-done.4.refs_2_ = bf16[32,2048]{1,0:T(8,128)(2,1)S(1)} collective-permute-done((bf16[32,2048]{1,0:T(8,128)(2,1)}, bf16[32,2048]{1,0:T(8,128)(2,1)S(1)}, u32[]{:S(2)}, u32[]{:S(2)}) %collective-permute-start.4) | collective-permute-done | bytes 131104 | tf_op jit(solution)/shard_map/ppermute | solution.py:43
  65.0 1.0 copy-done.6
  66.9 2.7 %shard_map.104.refs_0_ = bf16[2,1040,128]{2,1,0:T(8,128)(2,1)S(1)} custom-call(s32[32]{0:T(128)S(1)} %copy-done.14, bf16[8,128,256]{2,1,0:T(8,128)(2,1)S(1)} %all-to-all-done.1.inter_hbm, f32[64,128]{1,0:T(8,128)S(1)} %bitcast.11, bf16[32,16,128]{2,1,0:T(8,128)(2,1)S(1)} %copy-done.10, s32[32,32,32]{2,1,0:T(8,128)S(1)} %copy-done.2, ...), custom_call_target="tpu_custom_call" | custom-call | flops 10000000 | bytes 4000000 | tf_op jit(solution)/shard_map/pallas_call | solution.py:337
  69.8 1.8 %collective-permute-start.11 = (bf16[2,1040,128]{2,1,0:T(8,128)(2,1)S(1)}, bf16[2,1040,128]{2,1,0:T(8,128)(2,1)S(1)}, u32[]{:S(2)}, u32[]{:S(2)}) collective-permute-start(bf16[2,1040,128]{2,1,0:T(8,128)(2,1)S(1)} %shard_map.104.refs_0_), channel_id=1, source_target_pairs={{0,1},{1,2},{2,3},{3,4},{4,5},{5,6},{6,7},{7,0},{8,9},{9,10},{10,1... | collective-permute-start | bytes 1597448 | tf_op jit(solution)/shard_map/ppermute | solution.py:38
  71.7 1.5 %collective-permute-start.12 = (bf16[2,1040,128]{2,1,0:T(8,128)(2,1)S(1)}, bf16[2,1040,128]{2,1,0:T(8,128)(2,1)S(1)}, u32[]{:S(2)}, u32[]{:S(2)}) collective-permute-start(bf16[2,1040,128]{2,1,0:T(8,128)(2,1)S(1)} %shard_map.104.refs_0_), channel_id=1, source_target_pairs={{0,7},{1,0},{2,1},{3,2},{4,3},{5,4},{6,5},{7,6},{8,15},{9,8},{10,9... | collective-permute-start | bytes 1597448 | tf_op jit(solution)/shard_map/ppermute | solution.py:38
  73.5 1.1 shard_map.106
  74.6 1.6 %collective-permute-start.10 = (bf16[128,256]{1,0:T(8,128)(2,1)S(1)}, bf16[128,256]{1,0:T(8,128)(2,1)S(1)}, u32[]{:S(2)}, u32[]{:S(2)}) collective-permute-start(bf16[128,256]{1,0:T(8,128)(2,1)S(1)} %get-tuple-element.66), channel_id=1, source_target_pairs={{0,8},{1,9},{2,10},{3,11},{4,12},{5,13},{6,14},{7,15},{8,16},{9,17... | collective-permute-start | bytes 196616 | tf_op jit(solution)/shard_map/ppermute | solution.py:43
  76.2 1.9 %collective-permute-start.8 = (bf16[128,256]{1,0:T(8,128)(2,1)S(1)}, bf16[128,256]{1,0:T(8,128)(2,1)S(1)}, u32[]{:S(2)}, u32[]{:S(2)}) collective-permute-start(bf16[128,256]{1,0:T(8,128)(2,1)S(1)} %get-tuple-element.64), channel_id=1, source_target_pairs={{0,24},{1,25},{2,26},{3,27},{4,28},{5,29},{6,30},{7,31},{8,0},{9,1... | collective-permute-start | bytes 196616 | tf_op jit(solution)/shard_map/ppermute | solution.py:43
  79.1 6.5 %collective-permute-done.11.refs_0_ = bf16[2,1040,128]{2,1,0:T(8,128)(2,1)S(1)} collective-permute-done((bf16[2,1040,128]{2,1,0:T(8,128)(2,1)S(1)}, bf16[2,1040,128]{2,1,0:T(8,128)(2,1)S(1)}, u32[]{:S(2)}, u32[]{:S(2)}) %collective-permute-start.11) | collective-permute-done | bytes 532512 | tf_op jit(solution)/shard_map/ppermute | solution.py:38
  85.8 1.5 %collective-permute-start.16 = (bf16[2,1040,128]{2,1,0:T(8,128)(2,1)S(1)}, bf16[2,1040,128]{2,1,0:T(8,128)(2,1)S(1)}, u32[]{:S(2)}, u32[]{:S(2)}) collective-permute-start(bf16[2,1040,128]{2,1,0:T(8,128)(2,1)S(1)} %collective-permute-done.11.refs_0_), channel_id=1, source_target_pairs={{0,1},{1,2},{2,3},{3,4},{4,5},{5,6},{6,7},{7,0},{8,9},{9,10},{10,1... | collective-permute-start | bytes 1597448 | tf_op jit(solution)/shard_map/ppermute | solution.py:38
  87.4 1.8 %collective-permute-start.17 = (bf16[2,1040,128]{2,1,0:T(8,128)(2,1)S(1)}, bf16[2,1040,128]{2,1,0:T(8,128)(2,1)S(1)}, u32[]{:S(2)}, u32[]{:S(2)}) collective-permute-start(bf16[2,1040,128]{2,1,0:T(8,128)(2,1)S(1)} %collective-permute-done.12.refs_1_), channel_id=1, source_target_pairs={{0,7},{1,0},{2,1},{3,2},{4,3},{5,4},{6,5},{7,6},{8,15},{9,8},{10,9... | collective-permute-start | bytes 1597448 | tf_op jit(solution)/shard_map/ppermute | solution.py:38
  89.1 1.4 shard_map.107
  90.5 2.7 %collective-permute-start.13 = (bf16[256,256]{1,0:T(8,128)(2,1)S(1)}, bf16[256,256]{1,0:T(8,128)(2,1)S(1)}, u32[]{:S(2)}, u32[]{:S(2)}) collective-permute-start(bf16[256,256]{1,0:T(8,128)(2,1)S(1)} %get-tuple-element.70), channel_id=1, source_target_pairs={{0,24},{1,25},{2,26},{3,27},{4,28},{5,29},{6,30},{7,31},{8,0},{9,1... | collective-permute-start | bytes 393224 | tf_op jit(solution)/shard_map/ppermute | solution.py:43
  94.1 3.8 %collective-permute-done.13.refs_5_ = bf16[256,256]{1,0:T(8,128)(2,1)S(1)} collective-permute-done((bf16[256,256]{1,0:T(8,128)(2,1)S(1)}, bf16[256,256]{1,0:T(8,128)(2,1)S(1)}, u32[]{:S(2)}, u32[]{:S(2)}) %collective-permute-start.13) | collective-permute-done | bytes 131104 | tf_op jit(solution)/shard_map/ppermute | solution.py:43
  97.9 2.3 %collective-permute-done.14.refs_6_ = bf16[256,256]{1,0:T(8,128)(2,1)S(1)} collective-permute-done((bf16[256,256]{1,0:T(8,128)(2,1)S(1)}, bf16[256,256]{1,0:T(8,128)(2,1)S(1)}, u32[]{:S(2)}, u32[]{:S(2)}) %collective-permute-start.14) | collective-permute-done | bytes 131104 | tf_op jit(solution)/shard_map/ppermute | solution.py:43
  100.2 1.3 collective-permute-done.15.refs_7_
  101.6 2.4 %collective-permute-start.21 = (bf16[2,1040,128]{2,1,0:T(8,128)(2,1)S(1)}, bf16[2,1040,128]{2,1,0:T(8,128)(2,1)S(1)}, u32[]{:S(2)}, u32[]{:S(2)}) collective-permute-start(bf16[2,1040,128]{2,1,0:T(8,128)(2,1)S(1)} %collective-permute-done.16.refs_0_), channel_id=1, source_target_pairs={{0,1},{1,2},{2,3},{3,4},{4,5},{5,6},{6,7},{7,0},{8,9},{9,10},{10,1... | collective-permute-start | bytes 1597448 | tf_op jit(solution)/shard_map/ppermute | solution.py:38
  104.8 1.4 shard_map.108
  106.2 2.5 %collective-permute-start.18 = (bf16[256,256]{1,0:T(8,128)(2,1)S(1)}, bf16[256,256]{1,0:T(8,128)(2,1)S(1)}, u32[]{:S(2)}, u32[]{:S(2)}) collective-permute-start(bf16[256,256]{1,0:T(8,128)(2,1)S(1)} %get-tuple-element.76), channel_id=1, source_target_pairs={{0,24},{1,25},{2,26},{3,27},{4,28},{5,29},{6,30},{7,31},{8,0},{9,1... | collective-permute-start | bytes 393224 | tf_op jit(solution)/shard_map/ppermute | solution.py:43
  109.6 3.0 %collective-permute-done.18.refs_9_ = bf16[256,256]{1,0:T(8,128)(2,1)S(1)} collective-permute-done((bf16[256,256]{1,0:T(8,128)(2,1)S(1)}, bf16[256,256]{1,0:T(8,128)(2,1)S(1)}, u32[]{:S(2)}, u32[]{:S(2)}) %collective-permute-start.18) | collective-permute-done | bytes 131104 | tf_op jit(solution)/shard_map/ppermute | solution.py:43
  112.6 2.6 %collective-permute-done.19.refs_10_ = bf16[256,256]{1,0:T(8,128)(2,1)S(1)} collective-permute-done((bf16[256,256]{1,0:T(8,128)(2,1)S(1)}, bf16[256,256]{1,0:T(8,128)(2,1)S(1)}, u32[]{:S(2)}, u32[]{:S(2)}) %collective-permute-start.19) | collective-permute-done | bytes 131104 | tf_op jit(solution)/shard_map/ppermute | solution.py:43
  115.3 1.3 collective-permute-done.20.refs_11_
  116.6 1.5 %collective-permute-start.26 = (bf16[1040,128]{1,0:T(8,128)(2,1)S(1)}, bf16[1040,128]{1,0:T(8,128)(2,1)S(1)}, u32[]{:S(2)}, u32[]{:S(2)}) collective-permute-start(bf16[1040,128]{1,0:T(8,128)(2,1)S(1)} %slice_bitcast_fusion.1), channel_id=1, source_target_pairs={{0,1},{1,2},{2,3},{3,4},{4,5},{5,6},{6,7},{7,0},{8,9},{9,10},{10,1... | collective-permute-start | bytes 798728 | tf_op jit(solution)/shard_map/ppermute | solution.py:38
  118.1 2.1 %collective-permute-start.27 = (bf16[1040,128]{1,0:T(8,128)(2,1)S(1)}, bf16[1040,128]{1,0:T(8,128)(2,1)S(1)}, u32[]{:S(2)}, u32[]{:S(2)}) collective-permute-start(bf16[1040,128]{1,0:T(8,128)(2,1)S(1)} %slice_bitcast_fusion), channel_id=1, source_target_pairs={{0,7},{1,0},{2,1},{3,2},{4,3},{5,4},{6,5},{7,6},{8,15},{9,8},{10,9... | collective-permute-start | bytes 798728 | tf_op jit(solution)/shard_map/ppermute | solution.py:38
  120.2 1.4 shard_map.109
  121.6 2.3 %collective-permute-start.23 = (bf16[256,256]{1,0:T(8,128)(2,1)S(1)}, bf16[256,256]{1,0:T(8,128)(2,1)S(1)}, u32[]{:S(2)}, u32[]{:S(2)}) collective-permute-start(bf16[256,256]{1,0:T(8,128)(2,1)S(1)} %get-tuple-element.82), channel_id=1, source_target_pairs={{0,24},{1,25},{2,26},{3,27},{4,28},{5,29},{6,30},{7,31},{8,0},{9,1... | collective-permute-start | bytes 393224 | tf_op jit(solution)/shard_map/ppermute | solution.py:43
  124.8 1.1 shard_map.110
  125.9 2.9 %collective-permute-start.28 = (bf16[128,256]{1,0:T(8,128)(2,1)S(1)}, bf16[128,256]{1,0:T(8,128)(2,1)S(1)}, u32[]{:S(2)}, u32[]{:S(2)}) collective-permute-start(bf16[128,256]{1,0:T(8,128)(2,1)S(1)} %get-tuple-element.88), channel_id=1, source_target_pairs={{0,24},{1,25},{2,26},{3,27},{4,28},{5,29},{6,30},{7,31},{8,0},{9,1... | collective-permute-start | bytes 196616 | tf_op jit(solution)/shard_map/ppermute | solution.py:43
  128.8 1.8 %collective-permute-start.29 = (bf16[128,256]{1,0:T(8,128)(2,1)S(1)}, bf16[128,256]{1,0:T(8,128)(2,1)S(1)}, u32[]{:S(2)}, u32[]{:S(2)}) collective-permute-start(bf16[128,256]{1,0:T(8,128)(2,1)S(1)} %get-tuple-element.89), channel_id=1, source_target_pairs={{0,16},{1,17},{2,18},{3,19},{4,20},{5,21},{6,22},{7,23},{8,24},{9,... | collective-permute-start | bytes 196616 | tf_op jit(solution)/shard_map/ppermute | solution.py:43
  131.3 1.4 collective-permute-done.25.refs_15_
  132.6 1.9 %collective-permute-done.29.refs_18_ = bf16[128,256]{1,0:T(8,128)(2,1)S(1)} collective-permute-done((bf16[128,256]{1,0:T(8,128)(2,1)S(1)}, bf16[128,256]{1,0:T(8,128)(2,1)S(1)}, u32[]{:S(2)}, u32[]{:S(2)}) %collective-permute-start.29) | collective-permute-done | bytes 65568 | tf_op jit(solution)/shard_map/ppermute | solution.py:43
  134.6 1.5 %collective-permute-done.30.refs_19_ = bf16[128,256]{1,0:T(8,128)(2,1)S(1)} collective-permute-done((bf16[128,256]{1,0:T(8,128)(2,1)S(1)}, bf16[128,256]{1,0:T(8,128)(2,1)S(1)}, u32[]{:S(2)}, u32[]{:S(2)}) %collective-permute-start.30) | collective-permute-done | bytes 65568 | tf_op jit(solution)/shard_map/ppermute | solution.py:43
  136.1 1.7 %shard_map.111 = bf16[4,8,32,192]{3,2,1,0:T(8,128)(2,1)} custom-call(f32[128,256]{1,0:T(8,128)S(1)} %get-tuple-element.63.refs_0_, bf16[128,256]{1,0:T(8,128)(2,1)S(1)} %collective-permute-done.8.refs_1_, bf16[128,256]{1,0:T(8,128)(2,1)S(1)} %collective-permute-done.9.refs_2_, bf16[128,256]{1,0:T(8,128)(2,1)S(1)} %collective-permute-done.10.refs_3_, ...), custom_call_target="tpu_custom_call" | custom-call | flops 2000000 | bytes 4000000 | tf_op jit(solution)/shard_map/pallas_call | solution.py:415
  (63 shorter events, 9.5 us)
Async XLA Ops:
  2.7 31.8 %all-to-all-start = ((bf16[32,80,128]{2,1,0:T(8,128)(2,1)}), bf16[32,80,128]{2,1,0:T(8,128)(2,1)S(1)}, u32[]{:S(2)}, u32[]{:S(2)}) async-start(bf16[32,80,128]{2,1,0:T(8,128)(2,1)} %shard_map.100.after), calls=%async_computation | async-start | bytes 1310720 | tf_op jit(solution)/shard_map/all_to_all | solution.py:436
  14.0 20.4 %copy-start.1 = (bf16[32,2,128,128]{3,2,1,0:T(8,128)(2,1)S(1)}, bf16[32,2,128,128]{3,2,1,0:T(8,128)(2,1)}, u32[]{:S(2)}) copy-start(bf16[32,2,128,128]{3,2,1,0:T(8,128)(2,1)} %states.1) | copy-start | bytes 6291460
  16.8 19.0 %collective-permute-start = (bf16[640,256]{1,0:T(8,128)(2,1)}, bf16[640,256]{1,0:T(8,128)(2,1)S(1)}, u32[]{:S(2)}, u32[]{:S(2)}) collective-permute-start(bf16[640,256]{1,0:T(8,128)(2,1)} %get-tuple-element.49), channel_id=1, source_target_pairs={{0,8},{1,9},{2,10},{3,11},{4,12},{5,13},{6,14},{7,15},{8,16},{9,17... | collective-permute-start | bytes 983048 | tf_op jit(solution)/shard_map/ppermute | solution.py:43
  18.7 22.1 %collective-permute-start.1 = (bf16[640,256]{1,0:T(8,128)(2,1)}, bf16[640,256]{1,0:T(8,128)(2,1)S(1)}, u32[]{:S(2)}, u32[]{:S(2)}) collective-permute-start(bf16[640,256]{1,0:T(8,128)(2,1)} %get-tuple-element.50), channel_id=1, source_target_pairs={{0,16},{1,17},{2,18},{3,19},{4,20},{5,21},{6,22},{7,23},{8,24},{9,... | collective-permute-start | bytes 983048 | tf_op jit(solution)/shard_map/ppermute | solution.py:43
  21.4 19.4 %collective-permute-start.2 = (bf16[640,256]{1,0:T(8,128)(2,1)}, bf16[640,256]{1,0:T(8,128)(2,1)}, u32[]{:S(2)}, u32[]{:S(2)}) collective-permute-start(bf16[640,256]{1,0:T(8,128)(2,1)} %get-tuple-element.51), channel_id=1, source_target_pairs={{0,24},{1,25},{2,26},{3,27},{4,28},{5,29},{6,30},{7,31},{8,0},{9,1... | collective-permute-start | bytes 983048 | tf_op jit(solution)/shard_map/ppermute | solution.py:43
  35.1 0.7 copy-start.9
  35.8 5.0 %copy-start.8 = (bf16[8,128,256]{2,1,0:T(8,128)(2,1)}, bf16[8,128,256]{2,1,0:T(8,128)(2,1)S(1)}, u32[]{:S(2)}) copy-start(bf16[8,128,256]{2,1,0:T(8,128)(2,1)S(1)} %get-tuple-element.52) | copy-start | bytes 1572868
  35.8 10.7 %copy-start.3 = (bf16[640,256]{1,0:T(8,128)(2,1)}, bf16[640,256]{1,0:T(8,128)(2,1)S(1)}, u32[]{:S(2)}) copy-start(bf16[640,256]{1,0:T(8,128)(2,1)S(1)} %collective-permute-done.m1.refs_5_) | copy-start | bytes 983044
  40.7 5.8 %copy-start.5 = (bf16[640,256]{1,0:T(8,128)(2,1)}, bf16[640,256]{1,0:T(8,128)(2,1)S(1)}, u32[]{:S(2)}) copy-start(bf16[640,256]{1,0:T(8,128)(2,1)S(1)} %collective-permute-done.1.m2.refs_6_) | copy-start | bytes 983044
  40.8 23.2 %all-to-all-start.1 = ((bf16[8,128,256]{2,1,0:T(8,128)(2,1)}), bf16[8,128,256]{2,1,0:T(8,128)(2,1)S(1)}, u32[]{:S(2)}, u32[]{:S(2)}) async-start(bf16[8,128,256]{2,1,0:T(8,128)(2,1)} %copy-done.8), calls=%async_computation.1 | async-start | bytes 1048576 | tf_op jit(solution)/shard_map/all_to_all | solution.py:439
  46.5 17.5 %copy-start.2 = (s32[32,32,32]{2,1,0:T(8,128)S(1)}, s32[32,32,32]{2,1,0:T(8,128)}, u32[]{:S(2)}) copy-start(s32[32,32,32]{2,1,0:T(8,128)} %anc_hbm.3) | copy-start | bytes 393220
  46.5 17.5 %copy-start.10 = (bf16[32,16,128]{2,1,0:T(8,128)(2,1)S(1)}, bf16[32,16,128]{2,1,0:T(8,128)(2,1)}, u32[]{:S(2)}) copy-start(bf16[32,16,128]{2,1,0:T(8,128)(2,1)} %copy-done.9) | copy-start | bytes 393220
  46.5 17.5 %copy-start.11 = (bf16[256,256]{1,0:T(8,128)(2,1)S(1)}, bf16[256,256]{1,0:T(8,128)(2,1)}, u32[]{:S(2)}) copy-start(bf16[256,256]{1,0:T(8,128)(2,1)} %get-tuple-element.58.refs_4_) | copy-start | bytes 393220
  46.5 17.5 %copy-start.13 = (f32[8192]{0:T(1024)S(1)}, f32[8192]{0:T(1024)}, u32[]{:S(2)}) copy-start(f32[8192]{0:T(1024)} %param.18) | copy-start | bytes 98308
  46.6 17.5 %copy-start.14 = (s32[32]{0:T(128)S(1)}, s32[32]{0:T(128)}, u32[]{:S(2)}) copy-start(s32[32]{0:T(128)} %sizes.3) | copy-start | bytes 388
  52.7 16.9 %collective-permute-start.6 = (bf16[3,384,256]{2,1,0:T(8,128)(2,1)}, bf16[3,384,256]{2,1,0:T(8,128)(2,1)S(1)}, u32[]{:S(2)}, u32[]{:S(2)}) collective-permute-start(bf16[3,384,256]{2,1,0:T(8,128)(2,1)} %get-tuple-element.61.m0), channel_id=1, source_target_pairs={{0,64},{32,96},{64,0},{96,32},{128,192},{160,224},{192,128},{224,1... | collective-permute-start | bytes 1769480 | tf_op jit(solution)/shard_map/ppermute | solution.py:47
  54.1 7.3 %collective-permute-start.3 = (bf16[32,2048]{1,0:T(8,128)(2,1)}, bf16[32,2048]{1,0:T(8,128)(2,1)S(1)}, u32[]{:S(2)}, u32[]{:S(2)}) collective-permute-start(bf16[32,2048]{1,0:T(8,128)(2,1)} %get-tuple-element.55), channel_id=1, source_target_pairs={{0,8},{1,9},{2,10},{3,11},{4,12},{5,13},{6,14},{7,15},{8,16},{9,17... | collective-permute-start | bytes 393224 | tf_op jit(solution)/shard_map/ppermute | solution.py:43
  55.7 8.2 %collective-permute-start.4 = (bf16[32,2048]{1,0:T(8,128)(2,1)}, bf16[32,2048]{1,0:T(8,128)(2,1)S(1)}, u32[]{:S(2)}, u32[]{:S(2)}) collective-permute-start(bf16[32,2048]{1,0:T(8,128)(2,1)} %get-tuple-element.56), channel_id=1, source_target_pairs={{0,16},{1,17},{2,18},{3,19},{4,20},{5,21},{6,22},{7,23},{8,24},{9,... | collective-permute-start | bytes 393224 | tf_op jit(solution)/shard_map/ppermute | solution.py:43
  58.1 5.9 %collective-permute-start.5 = (bf16[32,2048]{1,0:T(8,128)(2,1)}, bf16[32,2048]{1,0:T(8,128)(2,1)S(1)}, u32[]{:S(2)}, u32[]{:S(2)}) collective-permute-start(bf16[32,2048]{1,0:T(8,128)(2,1)} %get-tuple-element.57), channel_id=1, source_target_pairs={{0,24},{1,25},{2,26},{3,27},{4,28},{5,29},{6,30},{7,31},{8,0},{9,1... | collective-permute-start | bytes 393224 | tf_op jit(solution)/shard_map/ppermute | solution.py:43
  64.0 1.0 copy-start.4
  65.0 1.0 copy-start.6
  66.0 0.9 copy-start.12
  66.9 2.7 %copy-start = (bf16[3,384,256]{2,1,0:T(8,128)(2,1)S(1)}, bf16[3,384,256]{2,1,0:T(8,128)(2,1)}, u32[]{:S(2)}) copy-start(bf16[3,384,256]{2,1,0:T(8,128)(2,1)} %get-tuple-element.61.m0) | copy-start | bytes 1769476
  69.6 3.5 %copy-start.7 = (bf16[192,2048]{1,0:T(8,128)(2,1)S(1)}, bf16[192,2048]{1,0:T(8,128)(2,1)}, u32[]{:S(2)}) copy-start(bf16[192,2048]{1,0:T(8,128)(2,1)} %get-tuple-element.59.w0) | copy-start | bytes 2359300
  69.7 3.4 %collective-permute-start.7 = (bf16[2,3,384,256]{3,2,1,0:T(8,128)(2,1)S(1)}, bf16[2,3,384,256]{3,2,1,0:T(8,128)(2,1)S(1)}, u32[]{:S(2)}, u32[]{:S(2)}) collective-permute-start(bf16[2,3,384,256]{3,2,1,0:T(8,128)(2,1)S(1)} %pad_maximum_fusion), channel_id=1, source_target_pairs={{0,32},{32,0},{64,96},{96,64},{128,160},{160,128},{192,224},{224,1... | collective-permute-start | bytes 3538952 | tf_op jit(solution)/shard_map/ppermute | solution.py:51
  69.8 15.7 %collective-permute-start.11 = (bf16[2,1040,128]{2,1,0:T(8,128)(2,1)S(1)}, bf16[2,1040,128]{2,1,0:T(8,128)(2,1)S(1)}, u32[]{:S(2)}, u32[]{:S(2)}) collective-permute-start(bf16[2,1040,128]{2,1,0:T(8,128)(2,1)S(1)} %shard_map.104.refs_0_), channel_id=1, source_target_pairs={{0,1},{1,2},{2,3},{3,4},{4,5},{5,6},{6,7},{7,0},{8,9},{9,10},{10,1... | collective-permute-start | bytes 1597448 | tf_op jit(solution)/shard_map/ppermute | solution.py:38
  71.7 14.2 %collective-permute-start.12 = (bf16[2,1040,128]{2,1,0:T(8,128)(2,1)S(1)}, bf16[2,1040,128]{2,1,0:T(8,128)(2,1)S(1)}, u32[]{:S(2)}, u32[]{:S(2)}) collective-permute-start(bf16[2,1040,128]{2,1,0:T(8,128)(2,1)S(1)} %shard_map.104.refs_0_), channel_id=1, source_target_pairs={{0,7},{1,0},{2,1},{3,2},{4,3},{5,4},{6,5},{7,6},{8,15},{9,8},{10,9... | collective-permute-start | bytes 1597448 | tf_op jit(solution)/shard_map/ppermute | solution.py:38
  74.6 11.2 %collective-permute-start.10 = (bf16[128,256]{1,0:T(8,128)(2,1)S(1)}, bf16[128,256]{1,0:T(8,128)(2,1)S(1)}, u32[]{:S(2)}, u32[]{:S(2)}) collective-permute-start(bf16[128,256]{1,0:T(8,128)(2,1)S(1)} %get-tuple-element.66), channel_id=1, source_target_pairs={{0,8},{1,9},{2,10},{3,11},{4,12},{5,13},{6,14},{7,15},{8,16},{9,17... | collective-permute-start | bytes 196616 | tf_op jit(solution)/shard_map/ppermute | solution.py:43
  76.2 9.7 %collective-permute-start.8 = (bf16[128,256]{1,0:T(8,128)(2,1)S(1)}, bf16[128,256]{1,0:T(8,128)(2,1)S(1)}, u32[]{:S(2)}, u32[]{:S(2)}) collective-permute-start(bf16[128,256]{1,0:T(8,128)(2,1)S(1)} %get-tuple-element.64), channel_id=1, source_target_pairs={{0,24},{1,25},{2,26},{3,27},{4,28},{5,29},{6,30},{7,31},{8,0},{9,1... | collective-permute-start | bytes 196616 | tf_op jit(solution)/shard_map/ppermute | solution.py:43
  78.1 7.7 %collective-permute-start.9 = (bf16[128,256]{1,0:T(8,128)(2,1)S(1)}, bf16[128,256]{1,0:T(8,128)(2,1)S(1)}, u32[]{:S(2)}, u32[]{:S(2)}) collective-permute-start(bf16[128,256]{1,0:T(8,128)(2,1)S(1)} %get-tuple-element.65), channel_id=1, source_target_pairs={{0,16},{1,17},{2,18},{3,19},{4,20},{5,21},{6,22},{7,23},{8,24},{9,... | collective-permute-start | bytes 196616 | tf_op jit(solution)/shard_map/ppermute | solution.py:43
  85.8 15.8 %collective-permute-start.16 = (bf16[2,1040,128]{2,1,0:T(8,128)(2,1)S(1)}, bf16[2,1040,128]{2,1,0:T(8,128)(2,1)S(1)}, u32[]{:S(2)}, u32[]{:S(2)}) collective-permute-start(bf16[2,1040,128]{2,1,0:T(8,128)(2,1)S(1)} %collective-permute-done.11.refs_0_), channel_id=1, source_target_pairs={{0,1},{1,2},{2,3},{3,4},{4,5},{5,6},{6,7},{7,0},{8,9},{9,10},{10,1... | collective-permute-start | bytes 1597448 | tf_op jit(solution)/shard_map/ppermute | solution.py:38
  87.4 14.2 %collective-permute-start.17 = (bf16[2,1040,128]{2,1,0:T(8,128)(2,1)S(1)}, bf16[2,1040,128]{2,1,0:T(8,128)(2,1)S(1)}, u32[]{:S(2)}, u32[]{:S(2)}) collective-permute-start(bf16[2,1040,128]{2,1,0:T(8,128)(2,1)S(1)} %collective-permute-done.12.refs_1_), channel_id=1, source_target_pairs={{0,7},{1,0},{2,1},{3,2},{4,3},{5,4},{6,5},{7,6},{8,15},{9,8},{10,9... | collective-permute-start | bytes 1597448 | tf_op jit(solution)/shard_map/ppermute | solution.py:38
  90.5 7.4 %collective-permute-start.13 = (bf16[256,256]{1,0:T(8,128)(2,1)S(1)}, bf16[256,256]{1,0:T(8,128)(2,1)S(1)}, u32[]{:S(2)}, u32[]{:S(2)}) collective-permute-start(bf16[256,256]{1,0:T(8,128)(2,1)S(1)} %get-tuple-element.70), channel_id=1, source_target_pairs={{0,24},{1,25},{2,26},{3,27},{4,28},{5,29},{6,30},{7,31},{8,0},{9,1... | collective-permute-start | bytes 393224 | tf_op jit(solution)/shard_map/ppermute | solution.py:43
  93.2 7.1 %collective-permute-start.14 = (bf16[256,256]{1,0:T(8,128)(2,1)S(1)}, bf16[256,256]{1,0:T(8,128)(2,1)S(1)}, u32[]{:S(2)}, u32[]{:S(2)}) collective-permute-start(bf16[256,256]{1,0:T(8,128)(2,1)S(1)} %get-tuple-element.71), channel_id=1, source_target_pairs={{0,16},{1,17},{2,18},{3,19},{4,20},{5,21},{6,22},{7,23},{8,24},{9,... | collective-permute-start | bytes 393224 | tf_op jit(solution)/shard_map/ppermute | solution.py:43
  93.7 7.9 %collective-permute-start.15 = (bf16[256,256]{1,0:T(8,128)(2,1)S(1)}, bf16[256,256]{1,0:T(8,128)(2,1)S(1)}, u32[]{:S(2)}, u32[]{:S(2)}) collective-permute-start(bf16[256,256]{1,0:T(8,128)(2,1)S(1)} %get-tuple-element.72), channel_id=1, source_target_pairs={{0,8},{1,9},{2,10},{3,11},{4,12},{5,13},{6,14},{7,15},{8,16},{9,17... | collective-permute-start | bytes 393224 | tf_op jit(solution)/shard_map/ppermute | solution.py:43
  101.6 15.0 %collective-permute-start.21 = (bf16[2,1040,128]{2,1,0:T(8,128)(2,1)S(1)}, bf16[2,1040,128]{2,1,0:T(8,128)(2,1)S(1)}, u32[]{:S(2)}, u32[]{:S(2)}) collective-permute-start(bf16[2,1040,128]{2,1,0:T(8,128)(2,1)S(1)} %collective-permute-done.16.refs_0_), channel_id=1, source_target_pairs={{0,1},{1,2},{2,3},{3,4},{4,5},{5,6},{6,7},{7,0},{8,9},{9,10},{10,1... | collective-permute-start | bytes 1597448 | tf_op jit(solution)/shard_map/ppermute | solution.py:38
  104.0 12.5 %collective-permute-start.22 = (bf16[2,1040,128]{2,1,0:T(8,128)(2,1)S(1)}, bf16[2,1040,128]{2,1,0:T(8,128)(2,1)S(1)}, u32[]{:S(2)}, u32[]{:S(2)}) collective-permute-start(bf16[2,1040,128]{2,1,0:T(8,128)(2,1)S(1)} %collective-permute-done.17.refs_1_), channel_id=1, source_target_pairs={{0,7},{1,0},{2,1},{3,2},{4,3},{5,4},{6,5},{7,6},{8,15},{9,8},{10,9... | collective-permute-start | bytes 1597448 | tf_op jit(solution)/shard_map/ppermute | solution.py:38
  106.2 6.4 %collective-permute-start.18 = (bf16[256,256]{1,0:T(8,128)(2,1)S(1)}, bf16[256,256]{1,0:T(8,128)(2,1)S(1)}, u32[]{:S(2)}, u32[]{:S(2)}) collective-permute-start(bf16[256,256]{1,0:T(8,128)(2,1)S(1)} %get-tuple-element.76), channel_id=1, source_target_pairs={{0,24},{1,25},{2,26},{3,27},{4,28},{5,29},{6,30},{7,31},{8,0},{9,1... | collective-permute-start | bytes 393224 | tf_op jit(solution)/shard_map/ppermute | solution.py:43
  108.7 6.6 %collective-permute-start.19 = (bf16[256,256]{1,0:T(8,128)(2,1)S(1)}, bf16[256,256]{1,0:T(8,128)(2,1)S(1)}, u32[]{:S(2)}, u32[]{:S(2)}) collective-permute-start(bf16[256,256]{1,0:T(8,128)(2,1)S(1)} %get-tuple-element.77), channel_id=1, source_target_pairs={{0,16},{1,17},{2,18},{3,19},{4,20},{5,21},{6,22},{7,23},{8,24},{9,... | collective-permute-start | bytes 393224 | tf_op jit(solution)/shard_map/ppermute | solution.py:43
  109.2 7.4 %collective-permute-start.20 = (bf16[256,256]{1,0:T(8,128)(2,1)S(1)}, bf16[256,256]{1,0:T(8,128)(2,1)S(1)}, u32[]{:S(2)}, u32[]{:S(2)}) collective-permute-start(bf16[256,256]{1,0:T(8,128)(2,1)S(1)} %get-tuple-element.78), channel_id=1, source_target_pairs={{0,8},{1,9},{2,10},{3,11},{4,12},{5,13},{6,14},{7,15},{8,16},{9,17... | collective-permute-start | bytes 393224 | tf_op jit(solution)/shard_map/ppermute | solution.py:43
  116.6 8.2 %collective-permute-start.26 = (bf16[1040,128]{1,0:T(8,128)(2,1)S(1)}, bf16[1040,128]{1,0:T(8,128)(2,1)S(1)}, u32[]{:S(2)}, u32[]{:S(2)}) collective-permute-start(bf16[1040,128]{1,0:T(8,128)(2,1)S(1)} %slice_bitcast_fusion.1), channel_id=1, source_target_pairs={{0,1},{1,2},{2,3},{3,4},{4,5},{5,6},{6,7},{7,0},{8,9},{9,10},{10,1... | collective-permute-start | bytes 798728 | tf_op jit(solution)/shard_map/ppermute | solution.py:38
  118.1 6.7 %collective-permute-start.27 = (bf16[1040,128]{1,0:T(8,128)(2,1)S(1)}, bf16[1040,128]{1,0:T(8,128)(2,1)S(1)}, u32[]{:S(2)}, u32[]{:S(2)}) collective-permute-start(bf16[1040,128]{1,0:T(8,128)(2,1)S(1)} %slice_bitcast_fusion), channel_id=1, source_target_pairs={{0,7},{1,0},{2,1},{3,2},{4,3},{5,4},{6,5},{7,6},{8,15},{9,8},{10,9... | collective-permute-start | bytes 798728 | tf_op jit(solution)/shard_map/ppermute | solution.py:38
  121.6 9.0 %collective-permute-start.23 = (bf16[256,256]{1,0:T(8,128)(2,1)S(1)}, bf16[256,256]{1,0:T(8,128)(2,1)S(1)}, u32[]{:S(2)}, u32[]{:S(2)}) collective-permute-start(bf16[256,256]{1,0:T(8,128)(2,1)S(1)} %get-tuple-element.82), channel_id=1, source_target_pairs={{0,24},{1,25},{2,26},{3,27},{4,28},{5,29},{6,30},{7,31},{8,0},{9,1... | collective-permute-start | bytes 393224 | tf_op jit(solution)/shard_map/ppermute | solution.py:43
  123.9 7.4 %collective-permute-start.24 = (bf16[256,256]{1,0:T(8,128)(2,1)S(1)}, bf16[256,256]{1,0:T(8,128)(2,1)S(1)}, u32[]{:S(2)}, u32[]{:S(2)}) collective-permute-start(bf16[256,256]{1,0:T(8,128)(2,1)S(1)} %get-tuple-element.83), channel_id=1, source_target_pairs={{0,16},{1,17},{2,18},{3,19},{4,20},{5,21},{6,22},{7,23},{8,24},{9,... | collective-permute-start | bytes 393224 | tf_op jit(solution)/shard_map/ppermute | solution.py:43
  124.4 8.2 %collective-permute-start.25 = (bf16[256,256]{1,0:T(8,128)(2,1)S(1)}, bf16[256,256]{1,0:T(8,128)(2,1)S(1)}, u32[]{:S(2)}, u32[]{:S(2)}) collective-permute-start(bf16[256,256]{1,0:T(8,128)(2,1)S(1)} %get-tuple-element.84), channel_id=1, source_target_pairs={{0,8},{1,9},{2,10},{3,11},{4,12},{5,13},{6,14},{7,15},{8,16},{9,17... | collective-permute-start | bytes 393224 | tf_op jit(solution)/shard_map/ppermute | solution.py:43
  125.9 6.7 %collective-permute-start.28 = (bf16[128,256]{1,0:T(8,128)(2,1)S(1)}, bf16[128,256]{1,0:T(8,128)(2,1)S(1)}, u32[]{:S(2)}, u32[]{:S(2)}) collective-permute-start(bf16[128,256]{1,0:T(8,128)(2,1)S(1)} %get-tuple-element.88), channel_id=1, source_target_pairs={{0,24},{1,25},{2,26},{3,27},{4,28},{5,29},{6,30},{7,31},{8,0},{9,1... | collective-permute-start | bytes 196616 | tf_op jit(solution)/shard_map/ppermute | solution.py:43
  128.8 5.8 %collective-permute-start.29 = (bf16[128,256]{1,0:T(8,128)(2,1)S(1)}, bf16[128,256]{1,0:T(8,128)(2,1)S(1)}, u32[]{:S(2)}, u32[]{:S(2)}) collective-permute-start(bf16[128,256]{1,0:T(8,128)(2,1)S(1)} %get-tuple-element.89), channel_id=1, source_target_pairs={{0,16},{1,17},{2,18},{3,19},{4,20},{5,21},{6,22},{7,23},{8,24},{9,... | collective-permute-start | bytes 196616 | tf_op jit(solution)/shard_map/ppermute | solution.py:43
  130.6 5.5 %collective-permute-start.30 = (bf16[128,256]{1,0:T(8,128)(2,1)S(1)}, bf16[128,256]{1,0:T(8,128)(2,1)S(1)}, u32[]{:S(2)}, u32[]{:S(2)}) collective-permute-start(bf16[128,256]{1,0:T(8,128)(2,1)S(1)} %get-tuple-element.90), channel_id=1, source_target_pairs={{0,8},{1,9},{2,10},{3,11},{4,12},{5,13},{6,14},{7,15},{8,16},{9,17... | collective-permute-start | bytes 196616 | tf_op jit(solution)/shard_map/ppermute | solution.py:43

commit v4 on v3

--- a/solution.py
+++ b/solution.py
@@ -21,7 +21,8 @@
 HROWS = 64
 PIECE = 16 * HROWS + 16
 ROWS = NX * NODES
-QROWS = 2 * NODES + 16
+EXTRA = 8
+QROWS = 2 * NODES + EXTRA
 NT = (((1,), (1,)), ((), ()))
 BF = jnp.bfloat16
 F32 = jnp.float32
@@ -76,10 +77,10 @@
 def pack_queries_kernel(decay, q_hbm, out, q, sems):
     cuts = [slice(n * QUART, (n + 1) * QUART) for n in range(NX)]
     copies = run_copies([(q_hbm.at[0, :, cut], q.at[:, cut]) for cut in cuts], sems)
-    row = lax.broadcasted_iota(jnp.int32, (16, HD), 0)
-    rows = jnp.zeros((16, HD), F32)
+    row = lax.broadcasted_iota(jnp.int32, (EXTRA, HD), 0)
+    rows = jnp.zeros((EXTRA, HD), F32)
     for j in range(2):
-        for n, piece in enumerate(split3(jnp.full((16, HD), decay[j], F32))):
+        for n, piece in enumerate(split3(jnp.full((EXTRA, HD), decay[j], F32))):
             rows = jnp.where(row == 3 * j + n, piece, rows)
     tail = rows.astype(BF)
     for n in range(NX * NZ):
@@ -158,14 +159,14 @@
     part = lax.rem(lax.axis_index("dp"), 4)
     flip = 1 - 2 * lax.rem(part, 2)
     far = lax.rem(part + 2, 4)
-    out[0] = w0[...]
+    out[:COLS, :] = w0[...]
     for s, (ref, mine) in enumerate(((m0, part), (m1, far))):
         for d in range(NX - 1):
             for b in range(2):
                 near = pl.ds(pl.multiple_of(mine * PART + b * PAIR, PAIR), PAIR)
                 other = pl.ds(pl.multiple_of((mine + flip) * PART + b * PAIR, PAIR), PAIR)
-                out[d + 1, :, near] = ref[d, b * COLS : (b + 1) * COLS]
-                out[d + 1, :, other] = theirs[s, d, b * COLS : (b + 1) * COLS]
+                out[(d + 1) * COLS : (d + 2) * COLS, near] = ref[d, b * COLS : (b + 1) * COLS]
+                out[(d + 1) * COLS : (d + 2) * COLS, other] = theirs[s, d, b * COLS : (b + 1) * COLS]
 
 
 def join_weights(w0, m0, m1, theirs):
@@ -173,7 +174,7 @@
         join_weights_kernel,
         in_specs=[VMEM] * 4,
         out_specs=VMEM,
-        out_shape=jax.ShapeDtypeStruct((NX, COLS, QUART), BF),
+        out_shape=jax.ShapeDtypeStruct((NX * COLS, QUART), BF),
         cost_estimate=cost(0, 6_000_000),
         compiler_params=PARAMS,
     )(w0, m0, m1, theirs)
@@ -197,7 +198,7 @@
         out_specs=[VMEM] * 2,
         out_shape=[
             jax.ShapeDtypeStruct((NZ, ROWS, PAIR), BF),
-            jax.ShapeDtypeStruct((NX * NZ, 16, HD), BF),
+            jax.ShapeDtypeStruct((NX * NZ, EXTRA, HD), BF),
         ],
         cost_estimate=cost(70_000_000, 4_000_000, 100_000),
         compiler_params=PARAMS,
@@ -213,8 +214,9 @@
     return [extra[3 * j : 3 * j + 1] + extra[3 * j + 1 : 3 * j + 2] + extra[3 * j + 2 : 3 * j + 3] for j in range(2)]
 
 
-def intra_kernel(sizes, q_hbm, k_hbm, v_hbm, extras_hbm, anc_hbm, m1, m2, m3, *refs):
-    outs_hbm, weights_hbm, (parts, extras, tree, out, weights, sems) = refs[:NX], refs[NX], refs[NX + 1 :]
+def intra_kernel(sizes, q_hbm, k_hbm, v_hbm, extras_hbm, anc_hbm, m0, m1, m2, m3, *refs):
+    outs_hbm, refs = refs[:NX], refs[NX:]
+    weights_hbm, gates_hbm, parts, extras, tree, out, weights, gates, sems = refs
     me = lax.axis_index("head")
     x, _ = place()
     cuts = [pl.ds(c * STEP, STEP) for c in range(CHUNKS)]
@@ -222,6 +224,7 @@
     for cut in cuts:
         pairs += [(ref.at[0, :, cut], parts.at[n, :, cut]) for n, ref in enumerate((q_hbm, k_hbm, v_hbm))]
     pairs += [(m.at[pl.ds(NZ * NODES, 2 * COLS)], weights.at[n]) for n, m in enumerate((m1, m2, m3))]
+    pairs += [(m.at[pl.ds(0, NZ * NODES)], gates.at[n]) for n, m in enumerate((m0, m1, m2, m3))]
     copies = run_copies(pairs, sems)
     node = lax.broadcasted_iota(jnp.int32, (NODES, HD), 0)
     lane = lax.broadcasted_iota(jnp.int32, (NODES, HD), 1)
@@ -257,6 +260,7 @@
         copy.wait()
     sends = [pltpu.make_async_copy(out.at[n], outs_hbm[n], sems.at[len(pairs) + n]) for n in range(NX)]
     sends.append(pltpu.make_async_copy(weights, weights_hbm, sems.at[len(pairs) + NX]))
+    sends.append(pltpu.make_async_copy(gates, gates_hbm, sems.at[len(pairs) + NX + 1]))
     for send in sends:
         send.start()
     for send in sends:
@@ -266,17 +270,18 @@
 def intra_part(sizes, q, k, v, extras, anc, messages):
     return pl.pallas_call(
         intra_kernel,
-        in_specs=[SMEM] + [HBM] * 8,
-        out_specs=[HBM] * (NX + 1),
+        in_specs=[SMEM] + [HBM] * 9,
+        out_specs=[HBM] * (NX + 2),
         out_shape=[jax.ShapeDtypeStruct((NODES, QUART), BF)] * NX
-        + [jax.ShapeDtypeStruct((NX - 1, 2 * COLS, PAIR), BF)],
+        + [jax.ShapeDtypeStruct((NX - 1, 2 * COLS, PAIR), BF), jax.ShapeDtypeStruct((NX, NZ * NODES, PAIR), BF)],
         scratch_shapes=[
             pltpu.VMEM((3, NODES, HEADS * HD), BF),
-            pltpu.VMEM((NX * NZ, 16, HD), BF),
+            pltpu.VMEM((NX * NZ, EXTRA, HD), BF),
             pltpu.VMEM((NODES, NODES), jnp.int32),
             pltpu.VMEM((NX, NODES, QUART), BF),
             pltpu.VMEM((NX - 1, 2 * COLS, PAIR), BF),
-            pltpu.SemaphoreType.DMA((2 + 3 * CHUNKS + 3 + NX + 1,)),
+            pltpu.VMEM((NX, NZ * NODES, PAIR), BF),
+            pltpu.SemaphoreType.DMA((2 + 3 * CHUNKS + 7 + NX + 2,)),
         ],
         cost_estimate=cost(100_000_000, 4_000_000, 200_000),
         compiler_params=WIDEST,
@@ -284,7 +289,7 @@
 
 
 def merge_kernel(sizes, inter_hbm, gain_hbm, extras_hbm, anc_hbm, *refs):
-    intras, gates, refs = refs[:NX], refs[NX : 2 * NX], refs[2 * NX :]
+    intras, gates, refs = refs[:NX], refs[NX], refs[NX + 1 :]
     out, inter_ref, gate_ref, gain, extras, tree, square_ref, sems = refs
     x, z = place()
     spots = [lax.rem(x - slot + NX, NX) for slot in range(NX)]
@@ -292,7 +297,7 @@
     pairs.append((gain_hbm.at[pl.ds(pl.multiple_of(x * 2 * NZ, 2 * NZ), 2 * NZ)], gain))
     for slot, xa in enumerate(spots):
         pairs.append((anc_hbm.at[xa * NZ + z], tree.at[slot]))
-        pairs.append((gates[slot].at[pl.ds(0, NZ * NODES)], gate_ref.at[slot]))
+        pairs.append((gates.at[slot], gate_ref.at[slot]))
     copies = run_copies(pairs, sems)
     node = lax.broadcasted_iota(jnp.int32, (NODES, HD), 0)
     lane = lax.broadcasted_iota(jnp.int32, (1, HD), 1)
@@ -336,55 +341,51 @@
 def merge(sizes, inter, gain, extras, anc, intras, gates):
     return pl.pallas_call(
         merge_kernel,
-        in_specs=[SMEM] + [HBM] * 4 + [VMEM] * NX + [HBM] * NX,
+        in_specs=[SMEM] + [HBM] * 4 + [VMEM] * NX + [HBM],
         out_specs=VMEM,
         out_shape=jax.ShapeDtypeStruct((2, PIECE, HD), BF),
         scratch_shapes=[
             pltpu.VMEM((NZ, ROWS, PAIR), BF),
             pltpu.VMEM((NX, NZ * NODES, PAIR), BF),
             pltpu.VMEM((2 * NZ, HD), F32),
-            pltpu.VMEM((NZ, 16, HD), BF),
+            pltpu.VMEM((NZ, EXTRA, HD), BF),
             pltpu.VMEM((NX, NODES, NODES), jnp.int32),
             pltpu.VMEM((ROWS, HD), F32),
             pltpu.SemaphoreType.DMA((3 + 2 * NX,)),
         ],
         cost_estimate=cost(10_000_000, 4_000_000),
         compiler_params=PARAMS,
-    )(sizes, inter, gain, extras, anc, *intras, *gates)
-
-
-def project_kernel(halves, count, *refs):
-    pieces, weights, outs, lhs = refs[:count], refs[count], refs[count + 1 : count + 1 + NX], refs[-1]
-    pick = lax.broadcasted_iota(jnp.int32, (16, 64), 0) == lax.broadcasted_iota(jnp.int32, (16, 64), 1)
-    pick = pick.astype(F32).astype(BF)
-    for n, (ref, which, half) in enumerate(halves):
-        piece = pieces[ref] if which is None else pieces[ref].at[which]
-        rows = slice(n * HROWS, (n + 1) * HROWS)
+    )(sizes, inter, gain, extras, anc, *intras, gates)
+
+
+def project_kernel(count, *refs):
+    pieces, weights, outs, u = refs[:count], refs[count], refs[count + 1 : count + 1 + NX], refs[-1]
+    if len(pieces[0].shape) == 3:
+        halves = [piece.at[half] for piece in pieces for half in range(2)]
+        tails = [piece[0, 16 * HROWS :, :] for piece in pieces]
+    else:
+        halves = pieces
+        lane = lax.broadcasted_iota(jnp.int32, (16, ROWS), 1)
+        first, second = (piece[16 * HROWS :, :].astype(F32) for piece in pieces)
+        tails = [jnp.where(lane < HROWS, first, second).astype(BF)]
+    for n, half in enumerate(halves):
         for h in range(2 * NZ):
-            lhs[rows, h * HD : (h + 1) * HD] = piece[h * HROWS : (h + 1) * HROWS, :]
-        sums = lax.dot_general(
-            piece[16 * HROWS :, :], pick, (((0,), (0,)), ((), ())), preferred_element_type=F32
-        )[half * HROWS : (half + 1) * HROWS]
-        for out in outs:
-            out[rows, COLS:] = sums.astype(out.dtype)
+            u[n * HROWS : (n + 1) * HROWS, h * HD : (h + 1) * HD] = half[h * HROWS : (h + 1) * HROWS, :]
+    acc = lax.dot_general(weights[...], u[...], NT, preferred_element_type=F32)
     for n, out in enumerate(outs):
-        acc = lax.dot_general(lhs[...], weights[n], NT, preferred_element_type=F32)
-        out[:, :COLS] = acc.astype(out.dtype)
+        out[:COLS, :] = acc[n * COLS : (n + 1) * COLS].astype(out.dtype)
+        for p, tail in enumerate(tails):
+            out[COLS:, p * ROWS : (p + 1) * ROWS] = tail.astype(out.dtype)
 
 
 def project(pieces, weights):
-    halves = []
-    for ref, piece in enumerate(pieces):
-        if piece.ndim == 3:
-            halves += [(ref, 0, 0), (ref, 1, 1)]
-        else:
-            halves.append((ref, None, ref))
-    rows = len(halves) * HROWS
-    return pl.pallas_call(
-        functools.partial(project_kernel, halves, len(pieces)),
+    rows = ROWS * len(pieces) if pieces[0].ndim == 3 else ROWS
+    shape = (COLS + 16, rows)
+    return pl.pallas_call(
+        functools.partial(project_kernel, len(pieces)),
         in_specs=[VMEM] * (len(pieces) + 1),
         out_specs=[VMEM] * NX,
-        out_shape=[jax.ShapeDtypeStruct((rows, 256), F32)] + [jax.ShapeDtypeStruct((rows, 256), BF)] * (NX - 1),
+        out_shape=[jax.ShapeDtypeStruct(shape, F32)] + [jax.ShapeDtypeStruct(shape, BF)] * (NX - 1),
         scratch_shapes=[pltpu.VMEM((rows, QUART), BF)],
         cost_estimate=cost(2 * rows * QUART * COLS * NX, 4_000_000),
         compiler_params=PARAMS,
@@ -392,34 +393,44 @@
 
 
 def finish_kernel(layout, *refs):
-    out = refs[-1]
+    out_hbm, out, sems = refs[-3:]
     _, z = place()
-    for g, places in enumerate(layout):
-        own, a, b, c = refs[4 * g : 4 * g + 4]
-        row = 0
-        for shift, first, last in places:
-            size = (last - first) * NODES
-            rows = slice(row, row + size)
-            total = own[rows, :] + a[rows, :].astype(F32) + b[rows, :].astype(F32) + c[rows, :].astype(F32)
-            squares = total[:, COLS : COLS + 1] + total[:, COLS + 1 : COLS + 2] + total[:, COLS + 2 : COLS + 3]
-            scaled = total[:, :COLS] * lax.rsqrt(squares * (1.0 / (HEADS * HD)) + 1e-06)
+    sends = []
+    for g, shifts in enumerate(layout):
+        parts = refs[4 * g : 4 * g + 4]
+        for p, shift in enumerate(shifts):
+            cols = slice(p * ROWS, (p + 1) * ROWS)
+            total = sum(part[:, cols].astype(F32) for part in parts)
+            squares = total[COLS : COLS + 1] + total[COLS + 1 : COLS + 2] + total[COLS + 2 : COLS + 3]
+            scaled = total[:COLS] * lax.rsqrt(squares * (1.0 / (HEADS * HD)) + 1e-06)
+            rest = jnp.concatenate([scaled[HD:], jnp.zeros((2 * HD - COLS, ROWS), F32)])
+            left, right = scaled[:HD].T, rest.T
             source = lax.rem(z - shift + 2 * NZ, NZ)
-            for x in range(first, last):
-                part = scaled[(x - first) * NODES : (x - first + 1) * NODES]
-                out[x, source] = part.astype(BF)
-            row += size
-
-
-def finish(groups, layout):
+            for x in range(NX):
+                n = len(sends)
+                rows = slice(x * NODES, (x + 1) * NODES)
+                out[n, :, :HD] = left[rows].astype(BF)
+                out[n, :, HD:] = right[rows, : COLS - HD].astype(BF)
+                sends.append(pltpu.make_async_copy(out.at[n], out_hbm.at[x, source], sems.at[n]))
+                sends[-1].start()
+    for send in sends:
+        send.wait()
+
+
+def finish(groups, layout, before=None):
     flat = [a for group in groups for a in group]
+    blocks = NX * sum(len(shifts) for shifts in layout)
+    extra = [] if before is None else [before]
     return pl.pallas_call(
         functools.partial(finish_kernel, layout),
-        in_specs=[VMEM] * len(flat),
-        out_specs=VMEM,
+        in_specs=[VMEM] * len(flat) + [HBM] * len(extra),
+        out_specs=HBM,
         out_shape=jax.ShapeDtypeStruct((NX, NZ, NODES, COLS), BF),
+        scratch_shapes=[pltpu.VMEM((blocks, NODES, COLS), BF), pltpu.SemaphoreType.DMA((blocks,))],
+        input_output_aliases={len(flat): 0} if extra else {},
         cost_estimate=cost(2_000_000, 4_000_000),
         compiler_params=PARAMS,
-    )(*flat)
+    )(*flat, *extra)
 
 
 ZLINES = [[x * NZ + z for z in range(NZ)] for x in range(NX)]
@@ -435,13 +446,14 @@
     m2, m1, m3 = xsend(m2, 2), xsend(m1, 1), xsend(m3, 3)
     spread = lax.all_to_all(packed, "head", 0, 0, tiled=True)
     inter, extras = inter_part(spread, states, [])
-    (inter,) = tie((inter,), m1, m2, m3)
+    (inter,) = tie((inter,), m2, m1, m3)
     inter = lax.all_to_all(inter, "head", 0, 0, axis_index_groups=ZLINES, tiled=True)
-    t0, t1, t2, t3, mine = intra_part(tree_sizes, queries, keys, values, extras, ancestors, (m1, m2, m3))
+    messages = (m0, m1, m2, m3)
+    t0, t1, t2, t3, mine, gates = intra_part(tree_sizes, queries, keys, values, extras, ancestors, messages)
     t2, t1, t3 = xsend(t2, 2), xsend(t1, 1), xsend(t3, 3)
     yours = swap_y(mine)
     gain = gain.reshape(HEADS, HD)
-    own = merge(tree_sizes, inter, gain, extras, ancestors, (t0, t1, t2, t3), (m0, m1, m2, m3))
+    own = merge(tree_sizes, inter, gain, extras, ancestors, (t0, t1, t2, t3), gates)
     theirs = swap_core(jnp.stack(tie((mine, yours), own)))
     weights = join_weights(w0, mine, yours, theirs)
 
@@ -454,7 +466,7 @@
         return own_part
 
     up, dn = zsend(own, 1), zsend(own, -1)
-    mark = send_sums([own], [(0, 0, NX)])
+    mark = send_sums([own], [0])
     for step in range(1, 4):
         up, dn = tie((up, dn), *groups[-1])
         pieces = up, dn
@@ -462,10 +474,11 @@
             up, dn = zsend(up, 1), zsend(dn, -1)
         else:
             up, dn = zsend(up[0], 1), zsend(dn[1], -1)
-        mark = send_sums(pieces, [(step, 0, NX), (-step, 0, NX)])
+        mark = send_sums(pieces, [step, -step])
     last = tie((up, dn), mark)
-    send_sums(last, [(4, 0, NX // 2), (-4, NX // 2, NX)])
-    out = finish(groups, layout)
+    send_sums(last, [4])
+    out = finish(groups[:3], layout[:3])
+    out = finish(groups[3:], layout[3:], out)
     return out.reshape(NX * NZ, NODES, COLS)
 
 

time: 138 us -> 135 us (0.978)
  waiting for transfers between devices: 47.8 us -> 46.3 us
    ppermute x8, waiting for transfers between devices: 6.81 us -> 10 us  [zsend(): return lax.ppermute(array, 'head', pairs)]
    all_to_all x1, waiting for transfers between devices: 11.6 us -> 9.06 us  [per_device(): spread = lax.all_to_all(packed, 'head', 0, 0, tiled=True)]
    ppermute x21, waiting for transfers between devices: 29.3 us -> 27.2 us  [xsend(): return lax.ppermute(array, 'head', pairs)]
    unnamed x30 -> x24, local copies, waits for them, and re-layouts: 3.56 us -> 2.6 us
  transfers between devices with their start and end apart: 33 -> 33, of which waited for: 17 -> 20; matrix products, arithmetic and copies ran while one was open for 0% -> 0% of each run, Pallas kernels for 14% -> 15%
where the time goes in v4:
time: 135 us
  starting transfers between devices  61.8 us (46%)
  waiting for transfers between devices  46.3 us (34%)
  Pallas kernels  23.7 us (18%)
  local copies, waits for them, and re-layouts  2.64 us (2%)
    ppermute x21, starting transfers between devices, xsend(): return lax.ppermute(array, 'head', pairs)  29.4 us
    ppermute x21, waiting for transfers between devices, xsend(): return lax.ppermute(array, 'head', pairs)  27.2 us
    ppermute x8, starting transfers between devices, zsend(): return lax.ppermute(array, 'head', pairs)  13.5 us
    all_to_all x1, starting transfers between devices, per_device(): spread = lax.all_to_all(packed, 'head', 0, 0, tiled=True)  11.3 us
    ppermute x8, waiting for transfers between devices, zsend(): return lax.ppermute(array, 'head', pairs)  10 us
    all_to_all x1, waiting for transfers between devices, per_device(): spread = lax.all_to_all(packed, 'head', 0, 0, tiled=True)  9.06 us
    pallas_call x1, Pallas kernels, intra_part(): pl.pallas_call(intra_kernel, in_specs=[SMEM] + [HBM] * 9, out_specs=[HBM]...  6.33 us
    all_to_all x1, starting transfers between devices, per_device(): lax.all_to_all(inter, 'head', 0, 0, axis_index_groups=ZLINES, tiled=True)  6.09 us
  transfers between devices with their start and end apart: 33, of which 20 were waited for; matrix products, arithmetic and copies ran while one was open for 0% of the time, Pallas kernels for 15%

profile of v4, /device:TPU:16, one launch (start us, length us, event | category | flops | bytes accessed | tf_op | source)
XLA Modules:
  0.0 135.0 jit_solution(3611149291363242183)
XLA Ops:
  0.0 2.6 %shard_map.100.after = bf16[32,72,128]{2,1,0:T(8,128)(2,1)} custom-call(f32[2]{0:T(128)} %decay.1, bf16[1,32,8192]{2,1,0:T(8,128)(2,1)} %q_hbm.3), custom_call_target="tpu_custom_call" | custom-call | bytes 1000000 | tf_op jit(solution)/shard_map/pallas_call | solution.py:96
  2.6 11.3 %all-to-all-start = ((bf16[32,72,128]{2,1,0:T(8,128)(2,1)}), bf16[32,72,128]{2,1,0:T(8,128)(2,1)S(1)}, u32[]{:S(2)}, u32[]{:S(2)}) async-start(bf16[32,72,128]{2,1,0:T(8,128)(2,1)} %shard_map.100.after), calls=%async_computation | async-start | bytes 1179648 | tf_op jit(solution)/shard_map/all_to_all | solution.py:447
  14.0 2.8 %shard_map.102 = (bf16[192,2048]{1,0:T(8,128)(2,1)}, bf16[256,256]{1,0:T(8,128)(2,1)}, bf16[640,256]{1,0:T(8,128)(2,1)}, bf16[640,256]{1,0:T(8,128)(2,1)}, bf16[640,256]{1,0:T(8,128)(2,1)}) custom-call(bf16[1,32,8192]{2,1,0:T(8,128)(2,1)} %gate_hbm.1, bf16[192,8192]{1,0:T(8,128)(2,1)} %bitcast.12, bf16[32,72,128]{2,1,0:T(8,128)(2,1)} %shard_map.100.after), custom_call_target="tpu_custom_call" | custom-call | bytes 4000000 | tf_op jit(solution)/shard_map/pallas_call | solution.py:141
  16.8 3.4 %collective-permute-start = (bf16[640,256]{1,0:T(8,128)(2,1)}, bf16[640,256]{1,0:T(8,128)(2,1)S(1)}, u32[]{:S(2)}, u32[]{:S(2)}) collective-permute-start(bf16[640,256]{1,0:T(8,128)(2,1)} %get-tuple-element.50), channel_id=1, source_target_pairs={{0,16},{1,17},{2,18},{3,19},{4,20},{5,21},{6,22},{7,23},{8,24},{9,... | collective-permute-start | bytes 983048 | tf_op jit(solution)/shard_map/ppermute | solution.py:44
  20.7 2.6 %collective-permute-start.2 = (bf16[640,256]{1,0:T(8,128)(2,1)}, bf16[640,256]{1,0:T(8,128)(2,1)}, u32[]{:S(2)}, u32[]{:S(2)}) collective-permute-start(bf16[640,256]{1,0:T(8,128)(2,1)} %get-tuple-element.52), channel_id=1, source_target_pairs={{0,24},{1,25},{2,26},{3,27},{4,28},{5,29},{6,30},{7,31},{8,0},{9,1... | collective-permute-start | bytes 983048 | tf_op jit(solution)/shard_map/ppermute | solution.py:44
  23.4 9.1 %all-to-all-done.queries = bf16[32,72,128]{2,1,0:T(8,128)(2,1)S(1)} async-done(((bf16[32,72,128]{2,1,0:T(8,128)(2,1)}), bf16[32,72,128]{2,1,0:T(8,128)(2,1)S(1)}, u32[]{:S(2)}, u32[]{:S(2)}) %all-to-all-start) | async-done | bytes 589856 | tf_op jit(solution)/shard_map/all_to_all | solution.py:447
  32.4 1.5 %shard_map.101 = (bf16[8,128,256]{2,1,0:T(8,128)(2,1)}, bf16[32,8,128]{2,1,0:T(8,128)(2,1)S(1)}) custom-call(bf16[32,72,128]{2,1,0:T(8,128)(2,1)S(1)} %all-to-all-done.queries, bf16[32,2,128,128]{3,2,1,0:T(8,128)(2,1)S(1)} %copy-done.1), custom_call_target="tpu_custom_call" | custom-call | flops 70000000 | bytes 4000000 | tf_op jit(solution)/shard_map/pallas_call | solution.py:195
  34.5 5.0 %collective-permute-done.1.m1 = bf16[640,256]{1,0:T(8,128)(2,1)S(1)} collective-permute-done((bf16[640,256]{1,0:T(8,128)(2,1)}, bf16[640,256]{1,0:T(8,128)(2,1)S(1)}, u32[]{:S(2)}, u32[]{:S(2)}) %collective-permute-start.1) | collective-permute-done | bytes 327712 | tf_op jit(solution)/shard_map/ppermute | solution.py:44
  39.5 6.1 %all-to-all-start.1 = ((bf16[8,128,256]{2,1,0:T(8,128)(2,1)}), bf16[8,128,256]{2,1,0:T(8,128)(2,1)S(1)}, u32[]{:S(2)}, u32[]{:S(2)}) async-start(bf16[8,128,256]{2,1,0:T(8,128)(2,1)} %get-tuple-element.53), calls=%async_computation.1 | async-start | bytes 1048576 | tf_op jit(solution)/shard_map/all_to_all | solution.py:450
  45.6 6.3 %shard_map.103 = (bf16[32,2048]{1,0:T(8,128)(2,1)}, bf16[32,2048]{1,0:T(8,128)(2,1)}, bf16[32,2048]{1,0:T(8,128)(2,1)}, bf16[32,2048]{1,0:T(8,128)(2,1)}, bf16[3...) custom-call(s32[32]{0:T(128)} %sizes.3, bf16[1,32,8192]{2,1,0:T(8,128)(2,1)} %q_hbm.3, bf16[1,32,8192]{2,1,0:T(8,128)(2,1)} %k_hbm.1, ...), custom_call_target="tpu_custom_call" | custom-call | flops 100000000 | bytes 4000000 | tf_op jit(solution)/shard_map/pallas_call | solution.py:271
  52.0 1.4 %collective-permute-start.8 = (bf16[3,384,256]{2,1,0:T(8,128)(2,1)}, bf16[3,384,256]{2,1,0:T(8,128)(2,1)S(1)}, u32[]{:S(2)}, u32[]{:S(2)}) collective-permute-start(bf16[3,384,256]{2,1,0:T(8,128)(2,1)} %get-tuple-element.63.m0), channel_id=1, source_target_pairs={{0,64},{32,96},{64,0},{96,32},{128,192},{160,224},{192,128},{224,1... | collective-permute-start | bytes 1769480 | tf_op jit(solution)/shard_map/ppermute | solution.py:48
  53.4 1.5 %collective-permute-start.3 = (bf16[32,2048]{1,0:T(8,128)(2,1)}, bf16[32,2048]{1,0:T(8,128)(2,1)S(1)}, u32[]{:S(2)}, u32[]{:S(2)}) collective-permute-start(bf16[32,2048]{1,0:T(8,128)(2,1)} %get-tuple-element.57), channel_id=1, source_target_pairs={{0,8},{1,9},{2,10},{3,11},{4,12},{5,13},{6,14},{7,15},{8,16},{9,17... | collective-permute-start | bytes 393224 | tf_op jit(solution)/shard_map/ppermute | solution.py:44
  54.8 2.5 %collective-permute-start.4 = (bf16[32,2048]{1,0:T(8,128)(2,1)}, bf16[32,2048]{1,0:T(8,128)(2,1)S(1)}, u32[]{:S(2)}, u32[]{:S(2)}) collective-permute-start(bf16[32,2048]{1,0:T(8,128)(2,1)} %get-tuple-element.58), channel_id=1, source_target_pairs={{0,16},{1,17},{2,18},{3,19},{4,20},{5,21},{6,22},{7,23},{8,24},{9,... | collective-permute-start | bytes 393224 | tf_op jit(solution)/shard_map/ppermute | solution.py:44
  57.4 0.9 collective-permute-start.5
  58.3 2.2 %collective-permute-done.3.refs_1_ = bf16[32,2048]{1,0:T(8,128)(2,1)S(1)} collective-permute-done((bf16[32,2048]{1,0:T(8,128)(2,1)}, bf16[32,2048]{1,0:T(8,128)(2,1)S(1)}, u32[]{:S(2)}, u32[]{:S(2)}) %collective-permute-start.3) | collective-permute-done | bytes 131104 | tf_op jit(solution)/shard_map/ppermute | solution.py:44
  60.5 2.7 %collective-permute-done.4.refs_2_ = bf16[32,2048]{1,0:T(8,128)(2,1)S(1)} collective-permute-done((bf16[32,2048]{1,0:T(8,128)(2,1)}, bf16[32,2048]{1,0:T(8,128)(2,1)S(1)}, u32[]{:S(2)}, u32[]{:S(2)}) %collective-permute-start.4) | collective-permute-done | bytes 131104 | tf_op jit(solution)/shard_map/ppermute | solution.py:44
  63.4 1.0 copy-done.4
  64.4 0.9 copy-done.7
  65.3 2.9 %shard_map.104.refs_0_ = bf16[2,1040,128]{2,1,0:T(8,128)(2,1)S(1)} custom-call(s32[32]{0:T(128)S(1)} %copy-done.9, bf16[8,128,256]{2,1,0:T(8,128)(2,1)S(1)} %all-to-all-done.1.inter_hbm, f32[64,128]{1,0:T(8,128)S(1)} %bitcast.11, bf16[32,8,128]{2,1,0:T(8,128)(2,1)S(1)} %copy-done.6, s32[32,32,32]{2,1,0:T(8,128)S(1)} %copy-done.2, ...), custom_call_target="tpu_custom_call" | custom-call | flops 10000000 | bytes 4000000 | tf_op jit(solution)/shard_map/pallas_call | solution.py:342
  68.4 1.8 %collective-permute-start.6 = (bf16[2,1040,128]{2,1,0:T(8,128)(2,1)S(1)}, bf16[2,1040,128]{2,1,0:T(8,128)(2,1)S(1)}, u32[]{:S(2)}, u32[]{:S(2)}) collective-permute-start(bf16[2,1040,128]{2,1,0:T(8,128)(2,1)S(1)} %shard_map.104.refs_0_), channel_id=1, source_target_pairs={{0,1},{1,2},{2,3},{3,4},{4,5},{5,6},{6,7},{7,0},{8,9},{9,10},{10,1... | collective-permute-start | bytes 1597448 | tf_op jit(solution)/shard_map/ppermute | solution.py:39
  70.2 1.5 %collective-permute-start.7 = (bf16[2,1040,128]{2,1,0:T(8,128)(2,1)S(1)}, bf16[2,1040,128]{2,1,0:T(8,128)(2,1)S(1)}, u32[]{:S(2)}, u32[]{:S(2)}) collective-permute-start(bf16[2,1040,128]{2,1,0:T(8,128)(2,1)S(1)} %shard_map.104.refs_0_), channel_id=1, source_target_pairs={{0,7},{1,0},{2,1},{3,2},{4,3},{5,4},{6,5},{7,6},{8,15},{9,8},{10,9... | collective-permute-start | bytes 1597448 | tf_op jit(solution)/shard_map/ppermute | solution.py:39
  72.1 1.0 shard_map.106
  73.1 2.8 %collective-permute-start.10 = (bf16[208,128]{1,0:T(8,128)(2,1)S(1)}, bf16[208,128]{1,0:T(8,128)(2,1)S(1)}, u32[]{:S(2)}, u32[]{:S(2)}) collective-permute-start(bf16[208,128]{1,0:T(8,128)(2,1)S(1)} %get-tuple-element.66), channel_id=1, source_target_pairs={{0,24},{1,25},{2,26},{3,27},{4,28},{5,29},{6,30},{7,31},{8,0},{9,1... | collective-permute-start | bytes 159752 | tf_op jit(solution)/shard_map/ppermute | solution.py:44
  76.9 7.3 %collective-permute-done.6.refs_0_ = bf16[2,1040,128]{2,1,0:T(8,128)(2,1)S(1)} collective-permute-done((bf16[2,1040,128]{2,1,0:T(8,128)(2,1)S(1)}, bf16[2,1040,128]{2,1,0:T(8,128)(2,1)S(1)}, u32[]{:S(2)}, u32[]{:S(2)}) %collective-permute-start.6) | collective-permute-done | bytes 532512 | tf_op jit(solution)/shard_map/ppermute | solution.py:39
  84.4 1.5 %collective-permute-start.13 = (bf16[2,1040,128]{2,1,0:T(8,128)(2,1)S(1)}, bf16[2,1040,128]{2,1,0:T(8,128)(2,1)S(1)}, u32[]{:S(2)}, u32[]{:S(2)}) collective-permute-start(bf16[2,1040,128]{2,1,0:T(8,128)(2,1)S(1)} %collective-permute-done.6.refs_0_), channel_id=1, source_target_pairs={{0,1},{1,2},{2,3},{3,4},{4,5},{5,6},{6,7},{7,0},{8,9},{9,10},{10,1... | collective-permute-start | bytes 1597448 | tf_op jit(solution)/shard_map/ppermute | solution.py:39
  86.0 1.8 %collective-permute-start.14 = (bf16[2,1040,128]{2,1,0:T(8,128)(2,1)S(1)}, bf16[2,1040,128]{2,1,0:T(8,128)(2,1)S(1)}, u32[]{:S(2)}, u32[]{:S(2)}) collective-permute-start(bf16[2,1040,128]{2,1,0:T(8,128)(2,1)S(1)} %collective-permute-done.7.refs_1_), channel_id=1, source_target_pairs={{0,7},{1,0},{2,1},{3,2},{4,3},{5,4},{6,5},{7,6},{8,15},{9,8},{10,9... | collective-permute-start | bytes 1597448 | tf_op jit(solution)/shard_map/ppermute | solution.py:39
  87.7 1.1 shard_map.107
  88.9 2.4 %collective-permute-start.15 = (bf16[208,256]{1,0:T(8,128)(2,1)S(1)}, bf16[208,256]{1,0:T(8,128)(2,1)S(1)}, u32[]{:S(2)}, u32[]{:S(2)}) collective-permute-start(bf16[208,256]{1,0:T(8,128)(2,1)S(1)} %get-tuple-element.72), channel_id=1, source_target_pairs={{0,24},{1,25},{2,26},{3,27},{4,28},{5,29},{6,30},{7,31},{8,0},{9,1... | collective-permute-start | bytes 319496 | tf_op jit(solution)/shard_map/ppermute | solution.py:44
  92.2 2.8 %collective-permute-done.15.refs_5_ = bf16[208,256]{1,0:T(8,128)(2,1)S(1)} collective-permute-done((bf16[208,256]{1,0:T(8,128)(2,1)S(1)}, bf16[208,256]{1,0:T(8,128)(2,1)S(1)}, u32[]{:S(2)}, u32[]{:S(2)}) %collective-permute-start.15) | collective-permute-done | bytes 106528 | tf_op jit(solution)/shard_map/ppermute | solution.py:44
  95.0 2.6 %collective-permute-done.16.refs_6_ = bf16[208,256]{1,0:T(8,128)(2,1)S(1)} collective-permute-done((bf16[208,256]{1,0:T(8,128)(2,1)S(1)}, bf16[208,256]{1,0:T(8,128)(2,1)S(1)}, u32[]{:S(2)}, u32[]{:S(2)}) %collective-permute-start.16) | collective-permute-done | bytes 106528 | tf_op jit(solution)/shard_map/ppermute | solution.py:44
  97.6 1.1 collective-permute-done.17.refs_7_
  100.0 2.6 %collective-permute-start.18 = (bf16[2,1040,128]{2,1,0:T(8,128)(2,1)S(1)}, bf16[2,1040,128]{2,1,0:T(8,128)(2,1)S(1)}, u32[]{:S(2)}, u32[]{:S(2)}) collective-permute-start(bf16[2,1040,128]{2,1,0:T(8,128)(2,1)S(1)} %collective-permute-done.13.refs_0_), channel_id=1, source_target_pairs={{0,1},{1,2},{2,3},{3,4},{4,5},{5,6},{6,7},{7,0},{8,9},{9,10},{10,1... | collective-permute-start | bytes 1597448 | tf_op jit(solution)/shard_map/ppermute | solution.py:39
  103.2 1.1 shard_map.108
  104.4 2.4 %collective-permute-start.20 = (bf16[208,256]{1,0:T(8,128)(2,1)S(1)}, bf16[208,256]{1,0:T(8,128)(2,1)S(1)}, u32[]{:S(2)}, u32[]{:S(2)}) collective-permute-start(bf16[208,256]{1,0:T(8,128)(2,1)S(1)} %get-tuple-element.78), channel_id=1, source_target_pairs={{0,24},{1,25},{2,26},{3,27},{4,28},{5,29},{6,30},{7,31},{8,0},{9,1... | collective-permute-start | bytes 319496 | tf_op jit(solution)/shard_map/ppermute | solution.py:44
  107.7 2.4 %collective-permute-done.20.refs_9_ = bf16[208,256]{1,0:T(8,128)(2,1)S(1)} collective-permute-done((bf16[208,256]{1,0:T(8,128)(2,1)S(1)}, bf16[208,256]{1,0:T(8,128)(2,1)S(1)}, u32[]{:S(2)}, u32[]{:S(2)}) %collective-permute-start.20) | collective-permute-done | bytes 106528 | tf_op jit(solution)/shard_map/ppermute | solution.py:44
  110.1 2.9 %collective-permute-done.21.refs_10_ = bf16[208,256]{1,0:T(8,128)(2,1)S(1)} collective-permute-done((bf16[208,256]{1,0:T(8,128)(2,1)S(1)}, bf16[208,256]{1,0:T(8,128)(2,1)S(1)}, u32[]{:S(2)}, u32[]{:S(2)}) %collective-permute-start.21) | collective-permute-done | bytes 106528 | tf_op jit(solution)/shard_map/ppermute | solution.py:44
  113.0 1.0 collective-permute-done.22.refs_11_
  114.8 1.9 %collective-permute-start.26 = (bf16[1040,128]{1,0:T(8,128)(2,1)S(1)}, bf16[1040,128]{1,0:T(8,128)(2,1)S(1)}, u32[]{:S(2)}, u32[]{:S(2)}) collective-permute-start(bf16[1040,128]{1,0:T(8,128)(2,1)S(1)} %slice_bitcast_fusion.1), channel_id=1, source_target_pairs={{0,1},{1,2},{2,3},{3,4},{4,5},{5,6},{6,7},{7,0},{8,9},{9,10},{10,1... | collective-permute-start | bytes 798728 | tf_op jit(solution)/shard_map/ppermute | solution.py:39
  116.7 1.7 %collective-permute-start.27 = (bf16[1040,128]{1,0:T(8,128)(2,1)S(1)}, bf16[1040,128]{1,0:T(8,128)(2,1)S(1)}, u32[]{:S(2)}, u32[]{:S(2)}) collective-permute-start(bf16[1040,128]{1,0:T(8,128)(2,1)S(1)} %slice_bitcast_fusion), channel_id=1, source_target_pairs={{0,7},{1,0},{2,1},{3,2},{4,3},{5,4},{6,5},{7,6},{8,15},{9,8},{10,9... | collective-permute-start | bytes 798728 | tf_op jit(solution)/shard_map/ppermute | solution.py:39
  118.4 1.1 shard_map.109
  119.5 2.4 %collective-permute-start.23 = (bf16[208,256]{1,0:T(8,128)(2,1)S(1)}, bf16[208,256]{1,0:T(8,128)(2,1)S(1)}, u32[]{:S(2)}, u32[]{:S(2)}) collective-permute-start(bf16[208,256]{1,0:T(8,128)(2,1)S(1)} %get-tuple-element.84), channel_id=1, source_target_pairs={{0,24},{1,25},{2,26},{3,27},{4,28},{5,29},{6,30},{7,31},{8,0},{9,1... | collective-permute-start | bytes 319496 | tf_op jit(solution)/shard_map/ppermute | solution.py:44
  123.4 1.0 shard_map.110
  124.5 2.4 %collective-permute-start.28 = (bf16[208,128]{1,0:T(8,128)(2,1)S(1)}, bf16[208,128]{1,0:T(8,128)(2,1)S(1)}, u32[]{:S(2)}, u32[]{:S(2)}) collective-permute-start(bf16[208,128]{1,0:T(8,128)(2,1)S(1)} %get-tuple-element.90), channel_id=1, source_target_pairs={{0,24},{1,25},{2,26},{3,27},{4,28},{5,29},{6,30},{7,31},{8,0},{9,1... | collective-permute-start | bytes 159752 | tf_op jit(solution)/shard_map/ppermute | solution.py:44
  126.9 1.7 %collective-permute-start.29 = (bf16[208,128]{1,0:T(8,128)(2,1)S(1)}, bf16[208,128]{1,0:T(8,128)(2,1)S(1)}, u32[]{:S(2)}, u32[]{:S(2)}) collective-permute-start(bf16[208,128]{1,0:T(8,128)(2,1)S(1)} %get-tuple-element.91), channel_id=1, source_target_pairs={{0,16},{1,17},{2,18},{3,19},{4,20},{5,21},{6,22},{7,23},{8,24},{9,... | collective-permute-start | bytes 159752 | tf_op jit(solution)/shard_map/ppermute | solution.py:44
  128.6 1.0 shard_map.111.refs_8_
  130.0 2.5 %collective-permute-done.29.refs_6_ = bf16[208,128]{1,0:T(8,128)(2,1)S(1)} collective-permute-done((bf16[208,128]{1,0:T(8,128)(2,1)S(1)}, bf16[208,128]{1,0:T(8,128)(2,1)S(1)}, u32[]{:S(2)}, u32[]{:S(2)}) %collective-permute-start.29) | collective-permute-done | bytes 53280 | tf_op jit(solution)/shard_map/ppermute | solution.py:44
  132.5 1.5 %collective-permute-done.30.refs_7_ = bf16[208,128]{1,0:T(8,128)(2,1)S(1)} collective-permute-done((bf16[208,128]{1,0:T(8,128)(2,1)S(1)}, bf16[208,128]{1,0:T(8,128)(2,1)S(1)}, u32[]{:S(2)}, u32[]{:S(2)}) %collective-permute-start.30) | collective-permute-done | bytes 53280 | tf_op jit(solution)/shard_map/ppermute | solution.py:44
  133.9 0.9 shard_map.112
  (58 shorter events, 9.4 us)
Async XLA Ops:
  2.6 29.8 %all-to-all-start = ((bf16[32,72,128]{2,1,0:T(8,128)(2,1)}), bf16[32,72,128]{2,1,0:T(8,128)(2,1)S(1)}, u32[]{:S(2)}, u32[]{:S(2)}) async-start(bf16[32,72,128]{2,1,0:T(8,128)(2,1)} %shard_map.100.after), calls=%async_computation | async-start | bytes 1179648 | tf_op jit(solution)/shard_map/all_to_all | solution.py:447
  14.0 18.5 %copy-start.1 = (bf16[32,2,128,128]{3,2,1,0:T(8,128)(2,1)S(1)}, bf16[32,2,128,128]{3,2,1,0:T(8,128)(2,1)}, u32[]{:S(2)}) copy-start(bf16[32,2,128,128]{3,2,1,0:T(8,128)(2,1)} %states.1) | copy-start | bytes 6291460
  16.8 17.8 %collective-permute-start = (bf16[640,256]{1,0:T(8,128)(2,1)}, bf16[640,256]{1,0:T(8,128)(2,1)S(1)}, u32[]{:S(2)}, u32[]{:S(2)}) collective-permute-start(bf16[640,256]{1,0:T(8,128)(2,1)} %get-tuple-element.50), channel_id=1, source_target_pairs={{0,16},{1,17},{2,18},{3,19},{4,20},{5,21},{6,22},{7,23},{8,24},{9,... | collective-permute-start | bytes 983048 | tf_op jit(solution)/shard_map/ppermute | solution.py:44
  20.1 19.3 %collective-permute-start.1 = (bf16[640,256]{1,0:T(8,128)(2,1)}, bf16[640,256]{1,0:T(8,128)(2,1)S(1)}, u32[]{:S(2)}, u32[]{:S(2)}) collective-permute-start(bf16[640,256]{1,0:T(8,128)(2,1)} %get-tuple-element.51), channel_id=1, source_target_pairs={{0,8},{1,9},{2,10},{3,11},{4,12},{5,13},{6,14},{7,15},{8,16},{9,17... | collective-permute-start | bytes 983048 | tf_op jit(solution)/shard_map/ppermute | solution.py:44
  20.7 18.7 %collective-permute-start.2 = (bf16[640,256]{1,0:T(8,128)(2,1)}, bf16[640,256]{1,0:T(8,128)(2,1)}, u32[]{:S(2)}, u32[]{:S(2)}) collective-permute-start(bf16[640,256]{1,0:T(8,128)(2,1)} %get-tuple-element.52), channel_id=1, source_target_pairs={{0,24},{1,25},{2,26},{3,27},{4,28},{5,29},{6,30},{7,31},{8,0},{9,1... | collective-permute-start | bytes 983048 | tf_op jit(solution)/shard_map/ppermute | solution.py:44
  33.9 0.6 copy-start.5
  34.5 11.1 %copy-start.10 = (bf16[640,256]{1,0:T(8,128)(2,1)}, bf16[640,256]{1,0:T(8,128)(2,1)S(1)}, u32[]{:S(2)}) copy-start(bf16[640,256]{1,0:T(8,128)(2,1)S(1)} %collective-permute-done.m2) | copy-start | bytes 983044
  39.5 6.1 %copy-start.11 = (bf16[640,256]{1,0:T(8,128)(2,1)}, bf16[640,256]{1,0:T(8,128)(2,1)S(1)}, u32[]{:S(2)}) copy-start(bf16[640,256]{1,0:T(8,128)(2,1)S(1)} %collective-permute-done.1.m1) | copy-start | bytes 983044
  39.5 23.8 %all-to-all-start.1 = ((bf16[8,128,256]{2,1,0:T(8,128)(2,1)}), bf16[8,128,256]{2,1,0:T(8,128)(2,1)S(1)}, u32[]{:S(2)}, u32[]{:S(2)}) async-start(bf16[8,128,256]{2,1,0:T(8,128)(2,1)} %get-tuple-element.53), calls=%async_computation.1 | async-start | bytes 1048576 | tf_op jit(solution)/shard_map/all_to_all | solution.py:450
  45.6 17.7 %copy-start.2 = (s32[32,32,32]{2,1,0:T(8,128)S(1)}, s32[32,32,32]{2,1,0:T(8,128)}, u32[]{:S(2)}) copy-start(s32[32,32,32]{2,1,0:T(8,128)} %anc_hbm.3) | copy-start | bytes 393220
  45.6 17.7 %copy-start.6 = (bf16[32,8,128]{2,1,0:T(8,128)(2,1)S(1)}, bf16[32,8,128]{2,1,0:T(8,128)(2,1)}, u32[]{:S(2)}) copy-start(bf16[32,8,128]{2,1,0:T(8,128)(2,1)} %copy-done.5) | copy-start | bytes 196612
  45.6 17.7 %copy-start.8 = (f32[8192]{0:T(1024)S(1)}, f32[8192]{0:T(1024)}, u32[]{:S(2)}) copy-start(f32[8192]{0:T(1024)} %param.18) | copy-start | bytes 98308
  45.6 17.7 %copy-start.9 = (s32[32]{0:T(128)S(1)}, s32[32]{0:T(128)}, u32[]{:S(2)}) copy-start(s32[32]{0:T(128)} %sizes.3) | copy-start | bytes 388
  52.0 16.2 %collective-permute-start.8 = (bf16[3,384,256]{2,1,0:T(8,128)(2,1)}, bf16[3,384,256]{2,1,0:T(8,128)(2,1)S(1)}, u32[]{:S(2)}, u32[]{:S(2)}) collective-permute-start(bf16[3,384,256]{2,1,0:T(8,128)(2,1)} %get-tuple-element.63.m0), channel_id=1, source_target_pairs={{0,64},{32,96},{64,0},{96,32},{128,192},{160,224},{192,128},{224,1... | collective-permute-start | bytes 1769480 | tf_op jit(solution)/shard_map/ppermute | solution.py:48
  53.4 7.2 %collective-permute-start.3 = (bf16[32,2048]{1,0:T(8,128)(2,1)}, bf16[32,2048]{1,0:T(8,128)(2,1)S(1)}, u32[]{:S(2)}, u32[]{:S(2)}) collective-permute-start(bf16[32,2048]{1,0:T(8,128)(2,1)} %get-tuple-element.57), channel_id=1, source_target_pairs={{0,8},{1,9},{2,10},{3,11},{4,12},{5,13},{6,14},{7,15},{8,16},{9,17... | collective-permute-start | bytes 393224 | tf_op jit(solution)/shard_map/ppermute | solution.py:44
  54.8 8.4 %collective-permute-start.4 = (bf16[32,2048]{1,0:T(8,128)(2,1)}, bf16[32,2048]{1,0:T(8,128)(2,1)S(1)}, u32[]{:S(2)}, u32[]{:S(2)}) collective-permute-start(bf16[32,2048]{1,0:T(8,128)(2,1)} %get-tuple-element.58), channel_id=1, source_target_pairs={{0,16},{1,17},{2,18},{3,19},{4,20},{5,21},{6,22},{7,23},{8,24},{9,... | collective-permute-start | bytes 393224 | tf_op jit(solution)/shard_map/ppermute | solution.py:44
  57.4 6.0 %collective-permute-start.5 = (bf16[32,2048]{1,0:T(8,128)(2,1)}, bf16[32,2048]{1,0:T(8,128)(2,1)S(1)}, u32[]{:S(2)}, u32[]{:S(2)}) collective-permute-start(bf16[32,2048]{1,0:T(8,128)(2,1)} %get-tuple-element.59), channel_id=1, source_target_pairs={{0,24},{1,25},{2,26},{3,27},{4,28},{5,29},{6,30},{7,31},{8,0},{9,1... | collective-permute-start | bytes 393224 | tf_op jit(solution)/shard_map/ppermute | solution.py:44
  63.4 1.0 copy-start.4
  64.4 0.9 copy-start.7
  65.3 2.9 %copy-start = (bf16[3,384,256]{2,1,0:T(8,128)(2,1)S(1)}, bf16[3,384,256]{2,1,0:T(8,128)(2,1)}, u32[]{:S(2)}) copy-start(bf16[3,384,256]{2,1,0:T(8,128)(2,1)} %get-tuple-element.63.m0) | copy-start | bytes 1769476
  68.2 3.5 %copy-start.3 = (bf16[192,2048]{1,0:T(8,128)(2,1)S(1)}, bf16[192,2048]{1,0:T(8,128)(2,1)}, u32[]{:S(2)}) copy-start(bf16[192,2048]{1,0:T(8,128)(2,1)} %get-tuple-element.61.w0) | copy-start | bytes 2359300
  68.3 3.4 %collective-permute-start.9 = (bf16[2,3,384,256]{3,2,1,0:T(8,128)(2,1)S(1)}, bf16[2,3,384,256]{3,2,1,0:T(8,128)(2,1)S(1)}, u32[]{:S(2)}, u32[]{:S(2)}) collective-permute-start(bf16[2,3,384,256]{3,2,1,0:T(8,128)(2,1)S(1)} %pad_maximum_fusion), channel_id=1, source_target_pairs={{0,32},{32,0},{64,96},{96,64},{128,160},{160,128},{192,224},{224,1... | collective-permute-start | bytes 3538952 | tf_op jit(solution)/shard_map/ppermute | solution.py:52
  68.4 15.7 %collective-permute-start.6 = (bf16[2,1040,128]{2,1,0:T(8,128)(2,1)S(1)}, bf16[2,1040,128]{2,1,0:T(8,128)(2,1)S(1)}, u32[]{:S(2)}, u32[]{:S(2)}) collective-permute-start(bf16[2,1040,128]{2,1,0:T(8,128)(2,1)S(1)} %shard_map.104.refs_0_), channel_id=1, source_target_pairs={{0,1},{1,2},{2,3},{3,4},{4,5},{5,6},{6,7},{7,0},{8,9},{9,10},{10,1... | collective-permute-start | bytes 1597448 | tf_op jit(solution)/shard_map/ppermute | solution.py:39
  70.2 14.2 %collective-permute-start.7 = (bf16[2,1040,128]{2,1,0:T(8,128)(2,1)S(1)}, bf16[2,1040,128]{2,1,0:T(8,128)(2,1)S(1)}, u32[]{:S(2)}, u32[]{:S(2)}) collective-permute-start(bf16[2,1040,128]{2,1,0:T(8,128)(2,1)S(1)} %shard_map.104.refs_0_), channel_id=1, source_target_pairs={{0,7},{1,0},{2,1},{3,2},{4,3},{5,4},{6,5},{7,6},{8,15},{9,8},{10,9... | collective-permute-start | bytes 1597448 | tf_op jit(solution)/shard_map/ppermute | solution.py:39
  73.1 11.3 %collective-permute-start.10 = (bf16[208,128]{1,0:T(8,128)(2,1)S(1)}, bf16[208,128]{1,0:T(8,128)(2,1)S(1)}, u32[]{:S(2)}, u32[]{:S(2)}) collective-permute-start(bf16[208,128]{1,0:T(8,128)(2,1)S(1)} %get-tuple-element.66), channel_id=1, source_target_pairs={{0,24},{1,25},{2,26},{3,27},{4,28},{5,29},{6,30},{7,31},{8,0},{9,1... | collective-permute-start | bytes 159752 | tf_op jit(solution)/shard_map/ppermute | solution.py:44
  75.9 8.5 %collective-permute-start.11 = (bf16[208,128]{1,0:T(8,128)(2,1)S(1)}, bf16[208,128]{1,0:T(8,128)(2,1)S(1)}, u32[]{:S(2)}, u32[]{:S(2)}) collective-permute-start(bf16[208,128]{1,0:T(8,128)(2,1)S(1)} %get-tuple-element.67), channel_id=1, source_target_pairs={{0,16},{1,17},{2,18},{3,19},{4,20},{5,21},{6,22},{7,23},{8,24},{9,... | collective-permute-start | bytes 159752 | tf_op jit(solution)/shard_map/ppermute | solution.py:44
  76.7 7.7 %collective-permute-start.12 = (bf16[208,128]{1,0:T(8,128)(2,1)S(1)}, bf16[208,128]{1,0:T(8,128)(2,1)S(1)}, u32[]{:S(2)}, u32[]{:S(2)}) collective-permute-start(bf16[208,128]{1,0:T(8,128)(2,1)S(1)} %get-tuple-element.68), channel_id=1, source_target_pairs={{0,8},{1,9},{2,10},{3,11},{4,12},{5,13},{6,14},{7,15},{8,16},{9,17... | collective-permute-start | bytes 159752 | tf_op jit(solution)/shard_map/ppermute | solution.py:44
  84.4 14.7 %collective-permute-start.13 = (bf16[2,1040,128]{2,1,0:T(8,128)(2,1)S(1)}, bf16[2,1040,128]{2,1,0:T(8,128)(2,1)S(1)}, u32[]{:S(2)}, u32[]{:S(2)}) collective-permute-start(bf16[2,1040,128]{2,1,0:T(8,128)(2,1)S(1)} %collective-permute-done.6.refs_0_), channel_id=1, source_target_pairs={{0,1},{1,2},{2,3},{3,4},{4,5},{5,6},{6,7},{7,0},{8,9},{9,10},{10,1... | collective-permute-start | bytes 1597448 | tf_op jit(solution)/shard_map/ppermute | solution.py:39
  86.0 14.0 %collective-permute-start.14 = (bf16[2,1040,128]{2,1,0:T(8,128)(2,1)S(1)}, bf16[2,1040,128]{2,1,0:T(8,128)(2,1)S(1)}, u32[]{:S(2)}, u32[]{:S(2)}) collective-permute-start(bf16[2,1040,128]{2,1,0:T(8,128)(2,1)S(1)} %collective-permute-done.7.refs_1_), channel_id=1, source_target_pairs={{0,7},{1,0},{2,1},{3,2},{4,3},{5,4},{6,5},{7,6},{8,15},{9,8},{10,9... | collective-permute-start | bytes 1597448 | tf_op jit(solution)/shard_map/ppermute | solution.py:39
  88.9 6.2 %collective-permute-start.15 = (bf16[208,256]{1,0:T(8,128)(2,1)S(1)}, bf16[208,256]{1,0:T(8,128)(2,1)S(1)}, u32[]{:S(2)}, u32[]{:S(2)}) collective-permute-start(bf16[208,256]{1,0:T(8,128)(2,1)S(1)} %get-tuple-element.72), channel_id=1, source_target_pairs={{0,24},{1,25},{2,26},{3,27},{4,28},{5,29},{6,30},{7,31},{8,0},{9,1... | collective-permute-start | bytes 319496 | tf_op jit(solution)/shard_map/ppermute | solution.py:44
  91.2 6.4 %collective-permute-start.16 = (bf16[208,256]{1,0:T(8,128)(2,1)S(1)}, bf16[208,256]{1,0:T(8,128)(2,1)S(1)}, u32[]{:S(2)}, u32[]{:S(2)}) collective-permute-start(bf16[208,256]{1,0:T(8,128)(2,1)S(1)} %get-tuple-element.73), channel_id=1, source_target_pairs={{0,16},{1,17},{2,18},{3,19},{4,20},{5,21},{6,22},{7,23},{8,24},{9,... | collective-permute-start | bytes 319496 | tf_op jit(solution)/shard_map/ppermute | solution.py:44
  92.0 6.7 %collective-permute-start.17 = (bf16[208,256]{1,0:T(8,128)(2,1)S(1)}, bf16[208,256]{1,0:T(8,128)(2,1)S(1)}, u32[]{:S(2)}, u32[]{:S(2)}) collective-permute-start(bf16[208,256]{1,0:T(8,128)(2,1)S(1)} %get-tuple-element.74), channel_id=1, source_target_pairs={{0,8},{1,9},{2,10},{3,11},{4,12},{5,13},{6,14},{7,15},{8,16},{9,17... | collective-permute-start | bytes 319496 | tf_op jit(solution)/shard_map/ppermute | solution.py:44
  100.0 14.1 %collective-permute-start.18 = (bf16[2,1040,128]{2,1,0:T(8,128)(2,1)S(1)}, bf16[2,1040,128]{2,1,0:T(8,128)(2,1)S(1)}, u32[]{:S(2)}, u32[]{:S(2)}) collective-permute-start(bf16[2,1040,128]{2,1,0:T(8,128)(2,1)S(1)} %collective-permute-done.13.refs_0_), channel_id=1, source_target_pairs={{0,1},{1,2},{2,3},{3,4},{4,5},{5,6},{6,7},{7,0},{8,9},{9,10},{10,1... | collective-permute-start | bytes 1597448 | tf_op jit(solution)/shard_map/ppermute | solution.py:39
  102.6 12.1 %collective-permute-start.19 = (bf16[2,1040,128]{2,1,0:T(8,128)(2,1)S(1)}, bf16[2,1040,128]{2,1,0:T(8,128)(2,1)S(1)}, u32[]{:S(2)}, u32[]{:S(2)}) collective-permute-start(bf16[2,1040,128]{2,1,0:T(8,128)(2,1)S(1)} %collective-permute-done.14.refs_1_), channel_id=1, source_target_pairs={{0,7},{1,0},{2,1},{3,2},{4,3},{5,4},{6,5},{7,6},{8,15},{9,8},{10,9... | collective-permute-start | bytes 1597448 | tf_op jit(solution)/shard_map/ppermute | solution.py:39
  104.4 5.8 %collective-permute-start.20 = (bf16[208,256]{1,0:T(8,128)(2,1)S(1)}, bf16[208,256]{1,0:T(8,128)(2,1)S(1)}, u32[]{:S(2)}, u32[]{:S(2)}) collective-permute-start(bf16[208,256]{1,0:T(8,128)(2,1)S(1)} %get-tuple-element.78), channel_id=1, source_target_pairs={{0,24},{1,25},{2,26},{3,27},{4,28},{5,29},{6,30},{7,31},{8,0},{9,1... | collective-permute-start | bytes 319496 | tf_op jit(solution)/shard_map/ppermute | solution.py:44
  106.7 6.3 %collective-permute-start.21 = (bf16[208,256]{1,0:T(8,128)(2,1)S(1)}, bf16[208,256]{1,0:T(8,128)(2,1)S(1)}, u32[]{:S(2)}, u32[]{:S(2)}) collective-permute-start(bf16[208,256]{1,0:T(8,128)(2,1)S(1)} %get-tuple-element.79), channel_id=1, source_target_pairs={{0,16},{1,17},{2,18},{3,19},{4,20},{5,21},{6,22},{7,23},{8,24},{9,... | collective-permute-start | bytes 319496 | tf_op jit(solution)/shard_map/ppermute | solution.py:44
  107.2 6.9 %collective-permute-start.22 = (bf16[208,256]{1,0:T(8,128)(2,1)S(1)}, bf16[208,256]{1,0:T(8,128)(2,1)S(1)}, u32[]{:S(2)}, u32[]{:S(2)}) collective-permute-start(bf16[208,256]{1,0:T(8,128)(2,1)S(1)} %get-tuple-element.80), channel_id=1, source_target_pairs={{0,8},{1,9},{2,10},{3,11},{4,12},{5,13},{6,14},{7,15},{8,16},{9,17... | collective-permute-start | bytes 319496 | tf_op jit(solution)/shard_map/ppermute | solution.py:44
  114.8 8.1 %collective-permute-start.26 = (bf16[1040,128]{1,0:T(8,128)(2,1)S(1)}, bf16[1040,128]{1,0:T(8,128)(2,1)S(1)}, u32[]{:S(2)}, u32[]{:S(2)}) collective-permute-start(bf16[1040,128]{1,0:T(8,128)(2,1)S(1)} %slice_bitcast_fusion.1), channel_id=1, source_target_pairs={{0,1},{1,2},{2,3},{3,4},{4,5},{5,6},{6,7},{7,0},{8,9},{9,10},{10,1... | collective-permute-start | bytes 798728 | tf_op jit(solution)/shard_map/ppermute | solution.py:39
  116.7 6.7 %collective-permute-start.27 = (bf16[1040,128]{1,0:T(8,128)(2,1)S(1)}, bf16[1040,128]{1,0:T(8,128)(2,1)S(1)}, u32[]{:S(2)}, u32[]{:S(2)}) collective-permute-start(bf16[1040,128]{1,0:T(8,128)(2,1)S(1)} %slice_bitcast_fusion), channel_id=1, source_target_pairs={{0,7},{1,0},{2,1},{3,2},{4,3},{5,4},{6,5},{7,6},{8,15},{9,8},{10,9... | collective-permute-start | bytes 798728 | tf_op jit(solution)/shard_map/ppermute | solution.py:39
  119.5 9.1 %collective-permute-start.23 = (bf16[208,256]{1,0:T(8,128)(2,1)S(1)}, bf16[208,256]{1,0:T(8,128)(2,1)S(1)}, u32[]{:S(2)}, u32[]{:S(2)}) collective-permute-start(bf16[208,256]{1,0:T(8,128)(2,1)S(1)} %get-tuple-element.84), channel_id=1, source_target_pairs={{0,24},{1,25},{2,26},{3,27},{4,28},{5,29},{6,30},{7,31},{8,0},{9,1... | collective-permute-start | bytes 319496 | tf_op jit(solution)/shard_map/ppermute | solution.py:44
  121.9 7.7 %collective-permute-start.24 = (bf16[208,256]{1,0:T(8,128)(2,1)S(1)}, bf16[208,256]{1,0:T(8,128)(2,1)S(1)}, u32[]{:S(2)}, u32[]{:S(2)}) collective-permute-start(bf16[208,256]{1,0:T(8,128)(2,1)S(1)} %get-tuple-element.85), channel_id=1, source_target_pairs={{0,16},{1,17},{2,18},{3,19},{4,20},{5,21},{6,22},{7,23},{8,24},{9,... | collective-permute-start | bytes 319496 | tf_op jit(solution)/shard_map/ppermute | solution.py:44
  122.4 7.6 %collective-permute-start.25 = (bf16[208,256]{1,0:T(8,128)(2,1)S(1)}, bf16[208,256]{1,0:T(8,128)(2,1)S(1)}, u32[]{:S(2)}, u32[]{:S(2)}) collective-permute-start(bf16[208,256]{1,0:T(8,128)(2,1)S(1)} %get-tuple-element.86), channel_id=1, source_target_pairs={{0,8},{1,9},{2,10},{3,11},{4,12},{5,13},{6,14},{7,15},{8,16},{9,17... | collective-permute-start | bytes 319496 | tf_op jit(solution)/shard_map/ppermute | solution.py:44
  124.5 5.5 %collective-permute-start.28 = (bf16[208,128]{1,0:T(8,128)(2,1)S(1)}, bf16[208,128]{1,0:T(8,128)(2,1)S(1)}, u32[]{:S(2)}, u32[]{:S(2)}) collective-permute-start(bf16[208,128]{1,0:T(8,128)(2,1)S(1)} %get-tuple-element.90), channel_id=1, source_target_pairs={{0,24},{1,25},{2,26},{3,27},{4,28},{5,29},{6,30},{7,31},{8,0},{9,1... | collective-permute-start | bytes 159752 | tf_op jit(solution)/shard_map/ppermute | solution.py:44
  126.9 5.6 %collective-permute-start.29 = (bf16[208,128]{1,0:T(8,128)(2,1)S(1)}, bf16[208,128]{1,0:T(8,128)(2,1)S(1)}, u32[]{:S(2)}, u32[]{:S(2)}) collective-permute-start(bf16[208,128]{1,0:T(8,128)(2,1)S(1)} %get-tuple-element.91), channel_id=1, source_target_pairs={{0,16},{1,17},{2,18},{3,19},{4,20},{5,21},{6,22},{7,23},{8,24},{9,... | collective-permute-start | bytes 159752 | tf_op jit(solution)/shard_map/ppermute | solution.py:44
  128.6 5.3 %collective-permute-start.30 = (bf16[208,128]{1,0:T(8,128)(2,1)S(1)}, bf16[208,128]{1,0:T(8,128)(2,1)S(1)}, u32[]{:S(2)}, u32[]{:S(2)}) collective-permute-start(bf16[208,128]{1,0:T(8,128)(2,1)S(1)} %get-tuple-element.92), channel_id=1, source_target_pairs={{0,8},{1,9},{2,10},{3,11},{4,12},{5,13},{6,14},{7,15},{8,16},{9,17... | collective-permute-start | bytes 159752 | tf_op jit(solution)/shard_map/ppermute | solution.py:44

commit v5 on v4

--- a/solution.py
+++ b/solution.py
@@ -104,8 +104,8 @@
     )(decay, q)
 
 
-def pack_messages_kernel(gate_hbm, w, after, w0_hbm, *refs):
-    outs_hbm, (gate, w0, outs, sems) = refs[:NX], refs[NX:]
+def pack_messages_kernel(gate_hbm, w, after, *refs):
+    outs_hbm, (gate, outs, sems) = refs[:NX], refs[NX:]
     x, _ = place()
     cuts = [slice(n * QUART, (n + 1) * QUART) for n in range(NX)]
     pairs = [(gate_hbm.at[0, :, cut], gate.at[:, cut]) for cut in cuts]
@@ -114,7 +114,6 @@
         for b in range(2):
             col = pl.multiple_of(bases[n] + lax.rem(lax.axis_index("dp"), 4) * PART + b * PAIR, PAIR)
             pairs.append((w.at[:, pl.ds(col, PAIR)], outs.at[n, pl.ds(NZ * NODES + b * COLS, COLS)]))
-    pairs.append((w.at[:, pl.ds(pl.multiple_of(x * QUART, QUART), QUART)], w0))
     copies = run_copies(pairs, sems)
     for copy in copies[:NX]:
         copy.wait()
@@ -130,9 +129,6 @@
             rows = pl.ds(0, MSG)
         sends.append(pltpu.make_async_copy(outs.at[n, rows], outs_hbm[n].at[rows], sems.at[len(pairs) + n]))
         sends[-1].start()
-    copies[-1].wait()
-    sends.append(pltpu.make_async_copy(w0, w0_hbm, sems.at[len(pairs) + NX]))
-    sends[-1].start()
     for send in sends:
         send.wait()
 
@@ -141,14 +137,13 @@
     return pl.pallas_call(
         pack_messages_kernel,
         in_specs=[HBM] * 2 + [ANY],
-        out_specs=[HBM] * (1 + NX),
-        out_shape=[jax.ShapeDtypeStruct((COLS, QUART), BF)] + [jax.ShapeDtypeStruct((NZ * NODES, PAIR), BF)]
+        out_specs=[HBM] * NX,
+        out_shape=[jax.ShapeDtypeStruct((NZ * NODES, PAIR), BF)]
         + [jax.ShapeDtypeStruct((MSG, PAIR), BF)] * (NX - 1),
         scratch_shapes=[
             pltpu.VMEM((NODES, HEADS * HD), BF),
-            pltpu.VMEM((COLS, QUART), BF),
             pltpu.VMEM((NX, MSG, PAIR), BF),
-            pltpu.SemaphoreType.DMA((NX + 7 + NX + 1,)),
+            pltpu.SemaphoreType.DMA((NX + 6 + NX,)),
         ],
         cost_estimate=cost(0, 4_000_000),
         compiler_params=WIDEST,
@@ -205,26 +200,22 @@
     )(queries, states, *marks)
 
 
-CHUNKS = 4
-STEP = HEADS * HD // CHUNKS
-
-
 def decay_rows(extra):
     extra = extra.astype(F32)
     return [extra[3 * j : 3 * j + 1] + extra[3 * j + 1 : 3 * j + 2] + extra[3 * j + 2 : 3 * j + 3] for j in range(2)]
 
 
-def intra_kernel(sizes, q_hbm, k_hbm, v_hbm, extras_hbm, anc_hbm, m0, m1, m2, m3, *refs):
-    outs_hbm, refs = refs[:NX], refs[NX:]
-    weights_hbm, gates_hbm, parts, extras, tree, out, weights, gates, sems = refs
+def intra_kernel(sizes, q_hbm, k_hbm, v_hbm, extras_hbm, anc_hbm, m1, m2, m3, *refs):
+    outs_hbm, (weights_hbm, parts, extras, tree, out, weights, sems) = refs[:NX], refs[NX:]
     me = lax.axis_index("head")
     x, _ = place()
-    cuts = [pl.ds(c * STEP, STEP) for c in range(CHUNKS)]
+    order = (2, 1, 3, 0)
+    quarters = [lax.rem(x + n, NX) for n in order]
     pairs = [(anc_hbm.at[me], tree), (extras_hbm, extras)]
-    for cut in cuts:
-        pairs += [(ref.at[0, :, cut], parts.at[n, :, cut]) for n, ref in enumerate((q_hbm, k_hbm, v_hbm))]
+    for n, quarter in zip(order, quarters):
+        cut = pl.ds(pl.multiple_of(quarter * QUART, QUART), QUART)
+        pairs += [(ref.at[0, :, cut], parts.at[n, i]) for i, ref in enumerate((q_hbm, k_hbm, v_hbm))]
     pairs += [(m.at[pl.ds(NZ * NODES, 2 * COLS)], weights.at[n]) for n, m in enumerate((m1, m2, m3))]
-    pairs += [(m.at[pl.ds(0, NZ * NODES)], gates.at[n]) for n, m in enumerate((m0, m1, m2, m3))]
     copies = run_copies(pairs, sems)
     node = lax.broadcasted_iota(jnp.int32, (NODES, HD), 0)
     lane = lax.broadcasted_iota(jnp.int32, (NODES, HD), 1)
@@ -240,29 +231,29 @@
     own = [lane // NODES == n for n in range(blocks)]
     mask = jnp.concatenate([jnp.where(m, wide_anc, 0.0) for m in own])
     gaps = jnp.concatenate([jnp.where(m, wide_gaps, 0.0) for m in own])
-    quarter = HEADS // NX
-    for c in range(CHUNKS):
+    sends = []
+    for i, (shift, quarter) in enumerate(zip(order, quarters)):
         for n in range(3):
-            copies[2 + 3 * c + n].wait()
-        shift = lax.rem(c - x + NX, NX)
-        for first in range(c * quarter, (c + 1) * quarter, blocks):
+            copies[2 + 3 * i + n].wait()
+        for first in range(0, 2 * NZ, blocks):
             heads = range(first, first + blocks)
-            q, k, v = (jnp.concatenate([parts[n, :, h * HD : (h + 1) * HD] for h in heads]) for n in range(3))
-            rates = [jnp.broadcast_to(decay_rows(extras[h // 2])[h % 2], (NODES, HD)) for h in heads]
+            q, k, v = (jnp.concatenate([parts[shift, n, :, h * HD : (h + 1) * HD] for h in heads]) for n in range(3))
+            rates = []
+            for h in heads:
+                rate = decay_rows(extras[quarter * NZ + h // 2])[h % 2]
+                rates.append(jnp.broadcast_to(rate, (NODES, HD)))
             scores = lax.dot_general(q, k, NT, preferred_element_type=F32)
             mix = (scores * (mask * jnp.exp(-jnp.concatenate(rates) * gaps))).astype(BF)
             intra = jnp.dot(mix, v, preferred_element_type=F32)
             for n, h in enumerate(heads):
-                near = h % quarter
-                value = live * intra[n * NODES : (n + 1) * NODES]
-                out[shift, :, near * HD : (near + 1) * HD] = value.astype(BF)
-    for copy in copies[2 + 3 * CHUNKS :]:
-        copy.wait()
-    sends = [pltpu.make_async_copy(out.at[n], outs_hbm[n], sems.at[len(pairs) + n]) for n in range(NX)]
-    sends.append(pltpu.make_async_copy(weights, weights_hbm, sems.at[len(pairs) + NX]))
-    sends.append(pltpu.make_async_copy(gates, gates_hbm, sems.at[len(pairs) + NX + 1]))
-    for send in sends:
-        send.start()
+                out[shift, :, h * HD : (h + 1) * HD] = (live * intra[n * NODES : (n + 1) * NODES]).astype(BF)
+        sends.append(pltpu.make_async_copy(out.at[shift], outs_hbm[shift], sems.at[len(pairs) + shift]))
+        sends[-1].start()
+        if i == 1:
+            for copy in copies[2 + 3 * NX :]:
+                copy.wait()
+            sends.append(pltpu.make_async_copy(weights, weights_hbm, sems.at[len(pairs) + NX]))
+            sends[-1].start()
     for send in sends:
         send.wait()
 
@@ -270,22 +261,51 @@
 def intra_part(sizes, q, k, v, extras, anc, messages):
     return pl.pallas_call(
         intra_kernel,
-        in_specs=[SMEM] + [HBM] * 9,
-        out_specs=[HBM] * (NX + 2),
+        in_specs=[SMEM] + [HBM] * 8,
+        out_specs=[HBM] * (NX + 1),
         out_shape=[jax.ShapeDtypeStruct((NODES, QUART), BF)] * NX
-        + [jax.ShapeDtypeStruct((NX - 1, 2 * COLS, PAIR), BF), jax.ShapeDtypeStruct((NX, NZ * NODES, PAIR), BF)],
+        + [jax.ShapeDtypeStruct((NX - 1, 2 * COLS, PAIR), BF)],
         scratch_shapes=[
-            pltpu.VMEM((3, NODES, HEADS * HD), BF),
+            pltpu.VMEM((NX, 3, NODES, QUART), BF),
             pltpu.VMEM((NX * NZ, EXTRA, HD), BF),
             pltpu.VMEM((NODES, NODES), jnp.int32),
             pltpu.VMEM((NX, NODES, QUART), BF),
             pltpu.VMEM((NX - 1, 2 * COLS, PAIR), BF),
-            pltpu.VMEM((NX, NZ * NODES, PAIR), BF),
-            pltpu.SemaphoreType.DMA((2 + 3 * CHUNKS + 7 + NX + 2,)),
+            pltpu.SemaphoreType.DMA((2 + 3 * NX + 3 + NX + 1,)),
         ],
         cost_estimate=cost(100_000_000, 4_000_000, 200_000),
         compiler_params=WIDEST,
     )(sizes, q, k, v, extras, anc, *messages)
+
+
+def late_kernel(w_hbm, m0, m1, m2, m3, w0_hbm, gates_hbm, w0, gates, sems):
+    x, _ = place()
+    pairs = [(m.at[pl.ds(0, NZ * NODES)], gates.at[n]) for n, m in enumerate((m0, m1, m2, m3))]
+    pairs.append((w_hbm.at[:, pl.ds(pl.multiple_of(x * QUART, QUART), QUART)], w0))
+    copies = run_copies(pairs, sems)
+    sends = [pltpu.make_async_copy(gates.at[n], gates_hbm.at[n], sems.at[len(pairs) + n]) for n in range(NX)]
+    sends.append(pltpu.make_async_copy(w0, w0_hbm, sems.at[len(pairs) + NX]))
+    for copy, send in zip(copies, sends):
+        copy.wait()
+        send.start()
+    for send in sends:
+        send.wait()
+
+
+def late_part(w, messages):
+    return pl.pallas_call(
+        late_kernel,
+        in_specs=[HBM] * 5,
+        out_specs=[HBM] * 2,
+        out_shape=[jax.ShapeDtypeStruct((COLS, QUART), BF), jax.ShapeDtypeStruct((NX, NZ * NODES, PAIR), BF)],
+        scratch_shapes=[
+            pltpu.VMEM((COLS, QUART), BF),
+            pltpu.VMEM((NX, NZ * NODES, PAIR), BF),
+            pltpu.SemaphoreType.DMA((2 * NX + 2,)),
+        ],
+        cost_estimate=cost(0, 3_000_000),
+        compiler_params=WIDEST,
+    )(w, *messages)
 
 
 def merge_kernel(sizes, inter_hbm, gain_hbm, extras_hbm, anc_hbm, *refs):
@@ -442,15 +462,15 @@
 
 def per_device(queries, keys, values, gate, states, decay, ancestors, tree_sizes, gain, out_weight):
     packed = pack_queries(decay, queries)
-    w0, m0, m1, m2, m3 = pack_messages(gate, out_weight.T, packed)
+    m0, m1, m2, m3 = pack_messages(gate, out_weight.T, packed)
     m2, m1, m3 = xsend(m2, 2), xsend(m1, 1), xsend(m3, 3)
     spread = lax.all_to_all(packed, "head", 0, 0, tiled=True)
     inter, extras = inter_part(spread, states, [])
-    (inter,) = tie((inter,), m2, m1, m3)
+    (inter,) = tie((inter,), m1, m3)
     inter = lax.all_to_all(inter, "head", 0, 0, axis_index_groups=ZLINES, tiled=True)
-    messages = (m0, m1, m2, m3)
-    t0, t1, t2, t3, mine, gates = intra_part(tree_sizes, queries, keys, values, extras, ancestors, messages)
+    t0, t1, t2, t3, mine = intra_part(tree_sizes, queries, keys, values, extras, ancestors, (m1, m2, m3))
     t2, t1, t3 = xsend(t2, 2), xsend(t1, 1), xsend(t3, 3)
+    w0, gates = late_part(out_weight.T, tie((m0, m1, m2, m3), t1))
     yours = swap_y(mine)
     gain = gain.reshape(HEADS, HD)
     own = merge(tree_sizes, inter, gain, extras, ancestors, (t0, t1, t2, t3), gates)

time: 135 us -> 130 us (0.963)
  waiting for transfers between devices: 46.3 us -> 41.7 us
  Pallas kernels: 23.7 us -> 25.1 us
    ppermute x21, waiting for transfers between devices: 27.2 us -> 18.2 us  [xsend(): return lax.ppermute(array, 'head', pairs)]
    ppermute x21, starting transfers between devices: 29.4 us -> 26.5 us  [xsend(): return lax.ppermute(array, 'head', pairs)]
    ppermute x8, waiting for transfers between devices: 10 us -> 12.8 us  [zsend(): return lax.ppermute(array, 'head', pairs)]
    all_to_all x1, starting transfers between devices: 6.09 us -> 7.83 us  [per_device(): lax.all_to_all(inter, 'head', 0, 0, axis_index_groups=ZLINES, tiled=True)]
    pallas_call x1 -> x2, Pallas kernels: 6.33 us -> 8.03 us  [the longest x1 5.59 us: intra_part(): pl.pallas_call(intra_kernel, in_specs=[SMEM] + [HBM] * 8, out_specs=[HBM]...]
    all_to_all x1, waiting for transfers between devices: 9.06 us -> 10.6 us  [per_device(): spread = lax.all_to_all(packed, 'head', 0, 0, tiled=True)]
  transfers between devices with their start and end apart: 33 -> 33, of which waited for: 20 -> 19; matrix products, arithmetic and copies ran while one was open for 0% -> 0% of each run, Pallas kernels for 15% -> 17%
where the time goes in v5:
time: 130 us
  starting transfers between devices  60.7 us (47%)
  waiting for transfers between devices  41.7 us (32%)
  Pallas kernels  25.1 us (19%)
  local copies, waits for them, and re-layouts  1.73 us (1%)
    ppermute x21, starting transfers between devices, xsend(): return lax.ppermute(array, 'head', pairs)  26.5 us
    ppermute x21, waiting for transfers between devices, xsend(): return lax.ppermute(array, 'head', pairs)  18.2 us
    ppermute x8, starting transfers between devices, zsend(): return lax.ppermute(array, 'head', pairs)  13.6 us
    ppermute x8, waiting for transfers between devices, zsend(): return lax.ppermute(array, 'head', pairs)  12.8 us
    all_to_all x1, starting transfers between devices, per_device(): spread = lax.all_to_all(packed, 'head', 0, 0, tiled=True)  11.3 us
    all_to_all x1, waiting for transfers between devices, per_device(): spread = lax.all_to_all(packed, 'head', 0, 0, tiled=True)  10.6 us
    all_to_all x1, starting transfers between devices, per_device(): lax.all_to_all(inter, 'head', 0, 0, axis_index_groups=ZLINES, tiled=True)  7.83 us
    pallas_call x1, Pallas kernels, intra_part(): pl.pallas_call(intra_kernel, in_specs=[SMEM] + [HBM] * 8, out_specs=[HBM]...  5.59 us
  transfers between devices with their start and end apart: 33, of which 19 were waited for; matrix products, arithmetic and copies ran while one was open for 0% of the time, Pallas kernels for 17%

profile of v5, /device:TPU:16, one launch (start us, length us, event | category | flops | bytes accessed | tf_op | source)
XLA Modules:
  0.0 129.8 jit_solution(14040693922233227628)
XLA Ops:
  0.0 2.6 %shard_map.100.after = bf16[32,72,128]{2,1,0:T(8,128)(2,1)} custom-call(f32[2]{0:T(128)} %decay.1, bf16[1,32,8192]{2,1,0:T(8,128)(2,1)} %q_hbm.3), custom_call_target="tpu_custom_call" | custom-call | bytes 1000000 | tf_op jit(solution)/shard_map/pallas_call | solution.py:96
  2.7 11.3 %all-to-all-start = ((bf16[32,72,128]{2,1,0:T(8,128)(2,1)}), bf16[32,72,128]{2,1,0:T(8,128)(2,1)S(1)}, u32[]{:S(2)}, u32[]{:S(2)}) async-start(bf16[32,72,128]{2,1,0:T(8,128)(2,1)} %shard_map.100.after), calls=%async_computation | async-start | bytes 1179648 | tf_op jit(solution)/shard_map/all_to_all | solution.py:467
  14.0 2.4 %shard_map.102 = (bf16[256,256]{1,0:T(8,128)(2,1)}, bf16[640,256]{1,0:T(8,128)(2,1)}, bf16[640,256]{1,0:T(8,128)(2,1)}, bf16[640,256]{1,0:T(8,128)(2,1)}) custom-call(bf16[1,32,8192]{2,1,0:T(8,128)(2,1)} %gate_hbm.1, bf16[192,8192]{1,0:T(8,128)(2,1)} %bitcast.12, bf16[32,72,128]{2,1,0:T(8,128)(2,1)} %shard_map.100.after), custom_call_target="tpu_custom_call" | custom-call | bytes 4000000 | tf_op jit(solution)/shard_map/pallas_call | solution.py:137
  16.4 1.9 %collective-permute-start = (bf16[640,256]{1,0:T(8,128)(2,1)}, bf16[640,256]{1,0:T(8,128)(2,1)S(1)}, u32[]{:S(2)}, u32[]{:S(2)}) collective-permute-start(bf16[640,256]{1,0:T(8,128)(2,1)} %get-tuple-element.54), channel_id=1, source_target_pairs={{0,8},{1,9},{2,10},{3,11},{4,12},{5,13},{6,14},{7,15},{8,16},{9,17... | collective-permute-start | bytes 983048 | tf_op jit(solution)/shard_map/ppermute | solution.py:44
  18.3 1.4 %collective-permute-start.1 = (bf16[640,256]{1,0:T(8,128)(2,1)}, bf16[640,256]{1,0:T(8,128)(2,1)S(1)}, u32[]{:S(2)}, u32[]{:S(2)}) collective-permute-start(bf16[640,256]{1,0:T(8,128)(2,1)} %get-tuple-element.55), channel_id=1, source_target_pairs={{0,24},{1,25},{2,26},{3,27},{4,28},{5,29},{6,30},{7,31},{8,0},{9,1... | collective-permute-start | bytes 983048 | tf_op jit(solution)/shard_map/ppermute | solution.py:44
  19.8 2.1 %collective-permute-start.2 = (bf16[640,256]{1,0:T(8,128)(2,1)}, bf16[640,256]{1,0:T(8,128)(2,1)}, u32[]{:S(2)}, u32[]{:S(2)}) collective-permute-start(bf16[640,256]{1,0:T(8,128)(2,1)} %get-tuple-element.58), channel_id=1, source_target_pairs={{0,16},{1,17},{2,18},{3,19},{4,20},{5,21},{6,22},{7,23},{8,24},{9,... | collective-permute-start | bytes 983048 | tf_op jit(solution)/shard_map/ppermute | solution.py:44
  21.8 10.6 %all-to-all-done.queries = bf16[32,72,128]{2,1,0:T(8,128)(2,1)S(1)} async-done(((bf16[32,72,128]{2,1,0:T(8,128)(2,1)}), bf16[32,72,128]{2,1,0:T(8,128)(2,1)S(1)}, u32[]{:S(2)}, u32[]{:S(2)}) %all-to-all-start) | async-done | bytes 589856 | tf_op jit(solution)/shard_map/all_to_all | solution.py:467
  32.5 1.5 %shard_map.101 = (bf16[8,128,256]{2,1,0:T(8,128)(2,1)}, bf16[32,8,128]{2,1,0:T(8,128)(2,1)S(1)}) custom-call(bf16[32,72,128]{2,1,0:T(8,128)(2,1)S(1)} %all-to-all-done.queries, bf16[32,2,128,128]{3,2,1,0:T(8,128)(2,1)S(1)} %copy-done.1), custom_call_target="tpu_custom_call" | custom-call | flops 70000000 | bytes 4000000 | tf_op jit(solution)/shard_map/pallas_call | solution.py:190
  34.6 7.8 %all-to-all-start.1 = ((bf16[8,128,256]{2,1,0:T(8,128)(2,1)}), bf16[8,128,256]{2,1,0:T(8,128)(2,1)S(1)}, u32[]{:S(2)}, u32[]{:S(2)}) async-start(bf16[8,128,256]{2,1,0:T(8,128)(2,1)} %get-tuple-element.56), calls=%async_computation.1 | async-start | bytes 1048576 | tf_op jit(solution)/shard_map/all_to_all | solution.py:470
  42.4 5.6 %shard_map.103 = (bf16[32,2048]{1,0:T(8,128)(2,1)}, bf16[32,2048]{1,0:T(8,128)(2,1)}, bf16[32,2048]{1,0:T(8,128)(2,1)}, bf16[32,2048]{1,0:T(8,128)(2,1)}, bf16[3,384,256]{2,1,0:T(8,128)(2,1)}) custom-call(s32[32]{0:T(128)} %sizes.3, bf16[1,32,8192]{2,1,0:T(8,128)(2,1)} %q_hbm.3, bf16[1,32,8192]{2,1,0:T(8,128)(2,1)} %k_hbm.1, bf16[1,32,8192]{2,1,0:T(8,128)(2,1)} %v_hbm.1, ...), custom_call_target="tpu_custom_call" | custom-call | flops 100000000 | bytes 4000000 | tf_op jit(solution)/shard_map/pallas_call | solution.py:262
  48.0 1.4 %collective-permute-start.8 = (bf16[3,384,256]{2,1,0:T(8,128)(2,1)}, bf16[3,384,256]{2,1,0:T(8,128)(2,1)S(1)}, u32[]{:S(2)}, u32[]{:S(2)}) collective-permute-start(bf16[3,384,256]{2,1,0:T(8,128)(2,1)} %get-tuple-element.71.m0), channel_id=1, source_target_pairs={{0,64},{32,96},{64,0},{96,32},{128,192},{160,224},{192,128},{224,1... | collective-permute-start | bytes 1769480 | tf_op jit(solution)/shard_map/ppermute | solution.py:48
  49.4 5.0 %collective-permute-start.4 = (bf16[32,2048]{1,0:T(8,128)(2,1)}, bf16[32,2048]{1,0:T(8,128)(2,1)S(1)}, u32[]{:S(2)}, u32[]{:S(2)}) collective-permute-start(bf16[32,2048]{1,0:T(8,128)(2,1)} %get-tuple-element.61), channel_id=1, source_target_pairs={{0,16},{1,17},{2,18},{3,19},{4,20},{5,21},{6,22},{7,23},{8,24},{9,... | collective-permute-start | bytes 393224 | tf_op jit(solution)/shard_map/ppermute | solution.py:44
  54.4 1.7 %collective-permute-done.3.refs_1_ = bf16[32,2048]{1,0:T(8,128)(2,1)S(1)} collective-permute-done((bf16[32,2048]{1,0:T(8,128)(2,1)}, bf16[32,2048]{1,0:T(8,128)(2,1)S(1)}, u32[]{:S(2)}, u32[]{:S(2)}) %collective-permute-start.3) | collective-permute-done | bytes 131104 | tf_op jit(solution)/shard_map/ppermute | solution.py:44
  56.1 2.4 %shard_map.104 = (bf16[192,2048]{1,0:T(8,128)(2,1)}, bf16[4,256,256]{2,1,0:T(8,128)(2,1)}) custom-call(bf16[192,8192]{1,0:T(8,128)(2,1)} %bitcast.13, bf16[256,256]{1,0:T(8,128)(2,1)} %get-tuple-element.64.m0, bf16[640,256]{1,0:T(8,128)(2,1)} %copy-done.10, bf16[640,256]{1,0:T(8,128)(2,1)} %collective-permute-done.2.m2, bf16[640,256]{1,0:T(8,128)(2,1)} %copy-done.11), custom_call_target="tpu_custom_call" | custom-call | bytes 3000000 | tf_op jit(solution)/shard_map/pallas_call | solution.py:296
  59.6 1.0 copy-done.4
  60.7 2.8 %shard_map.105.refs_0_ = bf16[2,1040,128]{2,1,0:T(8,128)(2,1)S(1)} custom-call(s32[32]{0:T(128)S(1)} %copy-done.9, bf16[8,128,256]{2,1,0:T(8,128)(2,1)S(1)} %all-to-all-done.1.inter_hbm, f32[64,128]{1,0:T(8,128)S(1)} %bitcast.11, bf16[32,8,128]{2,1,0:T(8,128)(2,1)S(1)} %copy-done.6, s32[32,32,32]{2,1,0:T(8,128)S(1)} %copy-done.2, ...), custom_call_target="tpu_custom_call" | custom-call | flops 10000000 | bytes 4000000 | tf_op jit(solution)/shard_map/pallas_call | solution.py:362
  63.8 2.1 %collective-permute-start.6 = (bf16[2,1040,128]{2,1,0:T(8,128)(2,1)S(1)}, bf16[2,1040,128]{2,1,0:T(8,128)(2,1)S(1)}, u32[]{:S(2)}, u32[]{:S(2)}) collective-permute-start(bf16[2,1040,128]{2,1,0:T(8,128)(2,1)S(1)} %shard_map.105.refs_0_), channel_id=1, source_target_pairs={{0,1},{1,2},{2,3},{3,4},{4,5},{5,6},{6,7},{7,0},{8,9},{9,10},{10,1... | collective-permute-start | bytes 1597448 | tf_op jit(solution)/shard_map/ppermute | solution.py:39
  65.8 1.3 %collective-permute-start.7 = (bf16[2,1040,128]{2,1,0:T(8,128)(2,1)S(1)}, bf16[2,1040,128]{2,1,0:T(8,128)(2,1)S(1)}, u32[]{:S(2)}, u32[]{:S(2)}) collective-permute-start(bf16[2,1040,128]{2,1,0:T(8,128)(2,1)S(1)} %shard_map.105.refs_0_), channel_id=1, source_target_pairs={{0,7},{1,0},{2,1},{3,2},{4,3},{5,4},{6,5},{7,6},{8,15},{9,8},{10,9... | collective-permute-start | bytes 1597448 | tf_op jit(solution)/shard_map/ppermute | solution.py:39
  67.5 1.0 shard_map.107
  68.5 1.7 %collective-permute-start.10 = (bf16[208,128]{1,0:T(8,128)(2,1)S(1)}, bf16[208,128]{1,0:T(8,128)(2,1)S(1)}, u32[]{:S(2)}, u32[]{:S(2)}) collective-permute-start(bf16[208,128]{1,0:T(8,128)(2,1)S(1)} %get-tuple-element.74), channel_id=1, source_target_pairs={{0,24},{1,25},{2,26},{3,27},{4,28},{5,29},{6,30},{7,31},{8,0},{9,1... | collective-permute-start | bytes 159752 | tf_op jit(solution)/shard_map/ppermute | solution.py:44
  70.6 1.1 collective-permute-start.12
  71.7 8.0 %collective-permute-done.6.refs_0_ = bf16[2,1040,128]{2,1,0:T(8,128)(2,1)S(1)} collective-permute-done((bf16[2,1040,128]{2,1,0:T(8,128)(2,1)S(1)}, bf16[2,1040,128]{2,1,0:T(8,128)(2,1)S(1)}, u32[]{:S(2)}, u32[]{:S(2)}) %collective-permute-start.6) | collective-permute-done | bytes 532512 | tf_op jit(solution)/shard_map/ppermute | solution.py:39
  80.0 1.5 %collective-permute-start.13 = (bf16[2,1040,128]{2,1,0:T(8,128)(2,1)S(1)}, bf16[2,1040,128]{2,1,0:T(8,128)(2,1)S(1)}, u32[]{:S(2)}, u32[]{:S(2)}) collective-permute-start(bf16[2,1040,128]{2,1,0:T(8,128)(2,1)S(1)} %collective-permute-done.6.refs_0_), channel_id=1, source_target_pairs={{0,1},{1,2},{2,3},{3,4},{4,5},{5,6},{6,7},{7,0},{8,9},{9,10},{10,1... | collective-permute-start | bytes 1597448 | tf_op jit(solution)/shard_map/ppermute | solution.py:39
  81.6 1.8 %collective-permute-start.14 = (bf16[2,1040,128]{2,1,0:T(8,128)(2,1)S(1)}, bf16[2,1040,128]{2,1,0:T(8,128)(2,1)S(1)}, u32[]{:S(2)}, u32[]{:S(2)}) collective-permute-start(bf16[2,1040,128]{2,1,0:T(8,128)(2,1)S(1)} %collective-permute-done.7.refs_1_), channel_id=1, source_target_pairs={{0,7},{1,0},{2,1},{3,2},{4,3},{5,4},{6,5},{7,6},{8,15},{9,8},{10,9... | collective-permute-start | bytes 1597448 | tf_op jit(solution)/shard_map/ppermute | solution.py:39
  83.3 1.1 shard_map.108
  84.5 1.5 %collective-permute-start.15 = (bf16[208,256]{1,0:T(8,128)(2,1)S(1)}, bf16[208,256]{1,0:T(8,128)(2,1)S(1)}, u32[]{:S(2)}, u32[]{:S(2)}) collective-permute-start(bf16[208,256]{1,0:T(8,128)(2,1)S(1)} %get-tuple-element.80), channel_id=1, source_target_pairs={{0,24},{1,25},{2,26},{3,27},{4,28},{5,29},{6,30},{7,31},{8,0},{9,1... | collective-permute-start | bytes 319496 | tf_op jit(solution)/shard_map/ppermute | solution.py:44
  86.4 1.1 collective-permute-start.17
  87.5 2.1 %collective-permute-done.15.refs_5_ = bf16[208,256]{1,0:T(8,128)(2,1)S(1)} collective-permute-done((bf16[208,256]{1,0:T(8,128)(2,1)S(1)}, bf16[208,256]{1,0:T(8,128)(2,1)S(1)}, u32[]{:S(2)}, u32[]{:S(2)}) %collective-permute-start.15) | collective-permute-done | bytes 106528 | tf_op jit(solution)/shard_map/ppermute | solution.py:44
  89.6 2.8 %collective-permute-done.16.refs_6_ = bf16[208,256]{1,0:T(8,128)(2,1)S(1)} collective-permute-done((bf16[208,256]{1,0:T(8,128)(2,1)S(1)}, bf16[208,256]{1,0:T(8,128)(2,1)S(1)}, u32[]{:S(2)}, u32[]{:S(2)}) %collective-permute-start.16) | collective-permute-done | bytes 106528 | tf_op jit(solution)/shard_map/ppermute | solution.py:44
  93.4 1.5 %collective-permute-done.13.refs_0_ = bf16[2,1040,128]{2,1,0:T(8,128)(2,1)S(1)} collective-permute-done((bf16[2,1040,128]{2,1,0:T(8,128)(2,1)S(1)}, bf16[2,1040,128]{2,1,0:T(8,128)(2,1)S(1)}, u32[]{:S(2)}, u32[]{:S(2)}) %collective-permute-start.13) | collective-permute-done | bytes 532512 | tf_op jit(solution)/shard_map/ppermute | solution.py:39
  95.6 2.6 %collective-permute-start.18 = (bf16[2,1040,128]{2,1,0:T(8,128)(2,1)S(1)}, bf16[2,1040,128]{2,1,0:T(8,128)(2,1)S(1)}, u32[]{:S(2)}, u32[]{:S(2)}) collective-permute-start(bf16[2,1040,128]{2,1,0:T(8,128)(2,1)S(1)} %collective-permute-done.13.refs_0_), channel_id=1, source_target_pairs={{0,1},{1,2},{2,3},{3,4},{4,5},{5,6},{6,7},{7,0},{8,9},{9,10},{10,1... | collective-permute-start | bytes 1597448 | tf_op jit(solution)/shard_map/ppermute | solution.py:39
  98.8 1.1 shard_map.109
  100.0 1.5 %collective-permute-start.20 = (bf16[208,256]{1,0:T(8,128)(2,1)S(1)}, bf16[208,256]{1,0:T(8,128)(2,1)S(1)}, u32[]{:S(2)}, u32[]{:S(2)}) collective-permute-start(bf16[208,256]{1,0:T(8,128)(2,1)S(1)} %get-tuple-element.86), channel_id=1, source_target_pairs={{0,24},{1,25},{2,26},{3,27},{4,28},{5,29},{6,30},{7,31},{8,0},{9,1... | collective-permute-start | bytes 319496 | tf_op jit(solution)/shard_map/ppermute | solution.py:44
  101.8 1.1 collective-permute-start.22
  103.0 1.8 %collective-permute-done.20.refs_9_ = bf16[208,256]{1,0:T(8,128)(2,1)S(1)} collective-permute-done((bf16[208,256]{1,0:T(8,128)(2,1)S(1)}, bf16[208,256]{1,0:T(8,128)(2,1)S(1)}, u32[]{:S(2)}, u32[]{:S(2)}) %collective-permute-start.20) | collective-permute-done | bytes 106528 | tf_op jit(solution)/shard_map/ppermute | solution.py:44
  104.7 3.1 %collective-permute-done.21.refs_10_ = bf16[208,256]{1,0:T(8,128)(2,1)S(1)} collective-permute-done((bf16[208,256]{1,0:T(8,128)(2,1)S(1)}, bf16[208,256]{1,0:T(8,128)(2,1)S(1)}, u32[]{:S(2)}, u32[]{:S(2)}) %collective-permute-start.21) | collective-permute-done | bytes 106528 | tf_op jit(solution)/shard_map/ppermute | solution.py:44
  107.8 1.0 collective-permute-done.22.refs_11_
  110.4 1.9 %collective-permute-start.26 = (bf16[1040,128]{1,0:T(8,128)(2,1)S(1)}, bf16[1040,128]{1,0:T(8,128)(2,1)S(1)}, u32[]{:S(2)}, u32[]{:S(2)}) collective-permute-start(bf16[1040,128]{1,0:T(8,128)(2,1)S(1)} %slice_bitcast_fusion.1), channel_id=1, source_target_pairs={{0,1},{1,2},{2,3},{3,4},{4,5},{5,6},{6,7},{7,0},{8,9},{9,10},{10,1... | collective-permute-start | bytes 798728 | tf_op jit(solution)/shard_map/ppermute | solution.py:39
  112.3 1.7 %collective-permute-start.27 = (bf16[1040,128]{1,0:T(8,128)(2,1)S(1)}, bf16[1040,128]{1,0:T(8,128)(2,1)S(1)}, u32[]{:S(2)}, u32[]{:S(2)}) collective-permute-start(bf16[1040,128]{1,0:T(8,128)(2,1)S(1)} %slice_bitcast_fusion), channel_id=1, source_target_pairs={{0,7},{1,0},{2,1},{3,2},{4,3},{5,4},{6,5},{7,6},{8,15},{9,8},{10,9... | collective-permute-start | bytes 798728 | tf_op jit(solution)/shard_map/ppermute | solution.py:39
  114.0 1.1 shard_map.110
  115.1 1.5 %collective-permute-start.23 = (bf16[208,256]{1,0:T(8,128)(2,1)S(1)}, bf16[208,256]{1,0:T(8,128)(2,1)S(1)}, u32[]{:S(2)}, u32[]{:S(2)}) collective-permute-start(bf16[208,256]{1,0:T(8,128)(2,1)S(1)} %get-tuple-element.92), channel_id=1, source_target_pairs={{0,24},{1,25},{2,26},{3,27},{4,28},{5,29},{6,30},{7,31},{8,0},{9,1... | collective-permute-start | bytes 319496 | tf_op jit(solution)/shard_map/ppermute | solution.py:44
  117.0 1.1 collective-permute-start.25
  119.0 1.0 shard_map.111
  120.1 1.5 %collective-permute-start.28 = (bf16[208,128]{1,0:T(8,128)(2,1)S(1)}, bf16[208,128]{1,0:T(8,128)(2,1)S(1)}, u32[]{:S(2)}, u32[]{:S(2)}) collective-permute-start(bf16[208,128]{1,0:T(8,128)(2,1)S(1)} %get-tuple-element.98), channel_id=1, source_target_pairs={{0,24},{1,25},{2,26},{3,27},{4,28},{5,29},{6,30},{7,31},{8,0},{9,1... | collective-permute-start | bytes 159752 | tf_op jit(solution)/shard_map/ppermute | solution.py:44
  121.6 1.7 %collective-permute-start.29 = (bf16[208,128]{1,0:T(8,128)(2,1)S(1)}, bf16[208,128]{1,0:T(8,128)(2,1)S(1)}, u32[]{:S(2)}, u32[]{:S(2)}) collective-permute-start(bf16[208,128]{1,0:T(8,128)(2,1)S(1)} %get-tuple-element.99), channel_id=1, source_target_pairs={{0,16},{1,17},{2,18},{3,19},{4,20},{5,21},{6,22},{7,23},{8,24},{9,... | collective-permute-start | bytes 159752 | tf_op jit(solution)/shard_map/ppermute | solution.py:44
  123.9 1.0 shard_map.112.refs_8_
  125.0 2.2 %collective-permute-done.29.refs_6_ = bf16[208,128]{1,0:T(8,128)(2,1)S(1)} collective-permute-done((bf16[208,128]{1,0:T(8,128)(2,1)S(1)}, bf16[208,128]{1,0:T(8,128)(2,1)S(1)}, u32[]{:S(2)}, u32[]{:S(2)}) %collective-permute-start.29) | collective-permute-done | bytes 53280 | tf_op jit(solution)/shard_map/ppermute | solution.py:44
  127.2 1.5 %collective-permute-done.30.refs_7_ = bf16[208,128]{1,0:T(8,128)(2,1)S(1)} collective-permute-done((bf16[208,128]{1,0:T(8,128)(2,1)S(1)}, bf16[208,128]{1,0:T(8,128)(2,1)S(1)}, u32[]{:S(2)}, u32[]{:S(2)}) %collective-permute-start.30) | collective-permute-done | bytes 53280 | tf_op jit(solution)/shard_map/ppermute | solution.py:44
  (59 shorter events, 10.1 us)
Async XLA Ops:
  2.7 29.8 %all-to-all-start = ((bf16[32,72,128]{2,1,0:T(8,128)(2,1)}), bf16[32,72,128]{2,1,0:T(8,128)(2,1)S(1)}, u32[]{:S(2)}, u32[]{:S(2)}) async-start(bf16[32,72,128]{2,1,0:T(8,128)(2,1)} %shard_map.100.after), calls=%async_computation | async-start | bytes 1179648 | tf_op jit(solution)/shard_map/all_to_all | solution.py:467
  14.0 18.5 %copy-start.1 = (bf16[32,2,128,128]{3,2,1,0:T(8,128)(2,1)S(1)}, bf16[32,2,128,128]{3,2,1,0:T(8,128)(2,1)}, u32[]{:S(2)}) copy-start(bf16[32,2,128,128]{3,2,1,0:T(8,128)(2,1)} %states.1) | copy-start | bytes 6291460
  16.4 18.1 %collective-permute-start = (bf16[640,256]{1,0:T(8,128)(2,1)}, bf16[640,256]{1,0:T(8,128)(2,1)S(1)}, u32[]{:S(2)}, u32[]{:S(2)}) collective-permute-start(bf16[640,256]{1,0:T(8,128)(2,1)} %get-tuple-element.54), channel_id=1, source_target_pairs={{0,8},{1,9},{2,10},{3,11},{4,12},{5,13},{6,14},{7,15},{8,16},{9,17... | collective-permute-start | bytes 983048 | tf_op jit(solution)/shard_map/ppermute | solution.py:44
  18.3 16.2 %collective-permute-start.1 = (bf16[640,256]{1,0:T(8,128)(2,1)}, bf16[640,256]{1,0:T(8,128)(2,1)S(1)}, u32[]{:S(2)}, u32[]{:S(2)}) collective-permute-start(bf16[640,256]{1,0:T(8,128)(2,1)} %get-tuple-element.55), channel_id=1, source_target_pairs={{0,24},{1,25},{2,26},{3,27},{4,28},{5,29},{6,30},{7,31},{8,0},{9,1... | collective-permute-start | bytes 983048 | tf_op jit(solution)/shard_map/ppermute | solution.py:44
  19.8 22.6 %collective-permute-start.2 = (bf16[640,256]{1,0:T(8,128)(2,1)}, bf16[640,256]{1,0:T(8,128)(2,1)}, u32[]{:S(2)}, u32[]{:S(2)}) collective-permute-start(bf16[640,256]{1,0:T(8,128)(2,1)} %get-tuple-element.58), channel_id=1, source_target_pairs={{0,16},{1,17},{2,18},{3,19},{4,20},{5,21},{6,22},{7,23},{8,24},{9,... | collective-permute-start | bytes 983048 | tf_op jit(solution)/shard_map/ppermute | solution.py:44
  33.9 0.6 copy-start.5
  34.5 7.9 %copy-start.10 = (bf16[640,256]{1,0:T(8,128)(2,1)}, bf16[640,256]{1,0:T(8,128)(2,1)S(1)}, u32[]{:S(2)}) copy-start(bf16[640,256]{1,0:T(8,128)(2,1)S(1)} %collective-permute-done.m1) | copy-start | bytes 983044
  34.5 7.9 %copy-start.11 = (bf16[640,256]{1,0:T(8,128)(2,1)}, bf16[640,256]{1,0:T(8,128)(2,1)S(1)}, u32[]{:S(2)}) copy-start(bf16[640,256]{1,0:T(8,128)(2,1)S(1)} %collective-permute-done.1.m3) | copy-start | bytes 983044
  34.6 25.0 %all-to-all-start.1 = ((bf16[8,128,256]{2,1,0:T(8,128)(2,1)}), bf16[8,128,256]{2,1,0:T(8,128)(2,1)S(1)}, u32[]{:S(2)}, u32[]{:S(2)}) async-start(bf16[8,128,256]{2,1,0:T(8,128)(2,1)} %get-tuple-element.56), calls=%async_computation.1 | async-start | bytes 1048576 | tf_op jit(solution)/shard_map/all_to_all | solution.py:470
  48.0 15.5 %collective-permute-start.8 = (bf16[3,384,256]{2,1,0:T(8,128)(2,1)}, bf16[3,384,256]{2,1,0:T(8,128)(2,1)S(1)}, u32[]{:S(2)}, u32[]{:S(2)}) collective-permute-start(bf16[3,384,256]{2,1,0:T(8,128)(2,1)} %get-tuple-element.71.m0), channel_id=1, source_target_pairs={{0,64},{32,96},{64,0},{96,32},{128,192},{160,224},{192,128},{224,1... | collective-permute-start | bytes 1769480 | tf_op jit(solution)/shard_map/ppermute | solution.py:48
  49.4 6.7 %collective-permute-start.3 = (bf16[32,2048]{1,0:T(8,128)(2,1)}, bf16[32,2048]{1,0:T(8,128)(2,1)S(1)}, u32[]{:S(2)}, u32[]{:S(2)}) collective-permute-start(bf16[32,2048]{1,0:T(8,128)(2,1)} %get-tuple-element.60), channel_id=1, source_target_pairs={{0,8},{1,9},{2,10},{3,11},{4,12},{5,13},{6,14},{7,15},{8,16},{9,17... | collective-permute-start | bytes 393224 | tf_op jit(solution)/shard_map/ppermute | solution.py:44
  49.4 9.6 %collective-permute-start.4 = (bf16[32,2048]{1,0:T(8,128)(2,1)}, bf16[32,2048]{1,0:T(8,128)(2,1)S(1)}, u32[]{:S(2)}, u32[]{:S(2)}) collective-permute-start(bf16[32,2048]{1,0:T(8,128)(2,1)} %get-tuple-element.61), channel_id=1, source_target_pairs={{0,16},{1,17},{2,18},{3,19},{4,20},{5,21},{6,22},{7,23},{8,24},{9,... | collective-permute-start | bytes 393224 | tf_op jit(solution)/shard_map/ppermute | solution.py:44
  54.4 5.2 %collective-permute-start.5 = (bf16[32,2048]{1,0:T(8,128)(2,1)}, bf16[32,2048]{1,0:T(8,128)(2,1)S(1)}, u32[]{:S(2)}, u32[]{:S(2)}) collective-permute-start(bf16[32,2048]{1,0:T(8,128)(2,1)} %get-tuple-element.62), channel_id=1, source_target_pairs={{0,24},{1,25},{2,26},{3,27},{4,28},{5,29},{6,30},{7,31},{8,0},{9,1... | collective-permute-start | bytes 393224 | tf_op jit(solution)/shard_map/ppermute | solution.py:44
  56.1 3.5 %copy-start.2 = (s32[32,32,32]{2,1,0:T(8,128)S(1)}, s32[32,32,32]{2,1,0:T(8,128)}, u32[]{:S(2)}) copy-start(s32[32,32,32]{2,1,0:T(8,128)} %anc_hbm.3) | copy-start | bytes 393220
  56.1 3.5 %copy-start.6 = (bf16[32,8,128]{2,1,0:T(8,128)(2,1)S(1)}, bf16[32,8,128]{2,1,0:T(8,128)(2,1)}, u32[]{:S(2)}) copy-start(bf16[32,8,128]{2,1,0:T(8,128)(2,1)} %copy-done.5) | copy-start | bytes 196612
  56.1 3.5 %copy-start.7 = (bf16[32,2048]{1,0:T(8,128)(2,1)S(1)}, bf16[32,2048]{1,0:T(8,128)(2,1)}, u32[]{:S(2)}) copy-start(bf16[32,2048]{1,0:T(8,128)(2,1)} %get-tuple-element.59.refs_0_) | copy-start | bytes 393220
  56.1 3.5 %copy-start.8 = (f32[8192]{0:T(1024)S(1)}, f32[8192]{0:T(1024)}, u32[]{:S(2)}) copy-start(f32[8192]{0:T(1024)} %param.18) | copy-start | bytes 98308
  56.1 3.5 %copy-start.9 = (s32[32]{0:T(128)S(1)}, s32[32]{0:T(128)}, u32[]{:S(2)}) copy-start(s32[32]{0:T(128)} %sizes.3) | copy-start | bytes 388
  59.6 1.0 copy-start.4
  60.6 2.9 %copy-start = (bf16[3,384,256]{2,1,0:T(8,128)(2,1)S(1)}, bf16[3,384,256]{2,1,0:T(8,128)(2,1)}, u32[]{:S(2)}) copy-start(bf16[3,384,256]{2,1,0:T(8,128)(2,1)} %get-tuple-element.71.m0) | copy-start | bytes 1769476
  63.5 3.6 %copy-start.3 = (bf16[192,2048]{1,0:T(8,128)(2,1)S(1)}, bf16[192,2048]{1,0:T(8,128)(2,1)}, u32[]{:S(2)}) copy-start(bf16[192,2048]{1,0:T(8,128)(2,1)} %get-tuple-element.69.w0) | copy-start | bytes 2359300
  63.7 3.5 %collective-permute-start.9 = (bf16[2,3,384,256]{3,2,1,0:T(8,128)(2,1)S(1)}, bf16[2,3,384,256]{3,2,1,0:T(8,128)(2,1)S(1)}, u32[]{:S(2)}, u32[]{:S(2)}) collective-permute-start(bf16[2,3,384,256]{3,2,1,0:T(8,128)(2,1)S(1)} %pad_maximum_fusion), channel_id=1, source_target_pairs={{0,32},{32,0},{64,96},{96,64},{128,160},{160,128},{192,224},{224,1... | collective-permute-start | bytes 3538952 | tf_op jit(solution)/shard_map/ppermute | solution.py:52
  63.8 16.0 %collective-permute-start.6 = (bf16[2,1040,128]{2,1,0:T(8,128)(2,1)S(1)}, bf16[2,1040,128]{2,1,0:T(8,128)(2,1)S(1)}, u32[]{:S(2)}, u32[]{:S(2)}) collective-permute-start(bf16[2,1040,128]{2,1,0:T(8,128)(2,1)S(1)} %shard_map.105.refs_0_), channel_id=1, source_target_pairs={{0,1},{1,2},{2,3},{3,4},{4,5},{5,6},{6,7},{7,0},{8,9},{9,10},{10,1... | collective-permute-start | bytes 1597448 | tf_op jit(solution)/shard_map/ppermute | solution.py:39
  65.8 14.2 %collective-permute-start.7 = (bf16[2,1040,128]{2,1,0:T(8,128)(2,1)S(1)}, bf16[2,1040,128]{2,1,0:T(8,128)(2,1)S(1)}, u32[]{:S(2)}, u32[]{:S(2)}) collective-permute-start(bf16[2,1040,128]{2,1,0:T(8,128)(2,1)S(1)} %shard_map.105.refs_0_), channel_id=1, source_target_pairs={{0,7},{1,0},{2,1},{3,2},{4,3},{5,4},{6,5},{7,6},{8,15},{9,8},{10,9... | collective-permute-start | bytes 1597448 | tf_op jit(solution)/shard_map/ppermute | solution.py:39
  68.5 11.5 %collective-permute-start.10 = (bf16[208,128]{1,0:T(8,128)(2,1)S(1)}, bf16[208,128]{1,0:T(8,128)(2,1)S(1)}, u32[]{:S(2)}, u32[]{:S(2)}) collective-permute-start(bf16[208,128]{1,0:T(8,128)(2,1)S(1)} %get-tuple-element.74), channel_id=1, source_target_pairs={{0,24},{1,25},{2,26},{3,27},{4,28},{5,29},{6,30},{7,31},{8,0},{9,1... | collective-permute-start | bytes 159752 | tf_op jit(solution)/shard_map/ppermute | solution.py:44
  70.2 9.8 %collective-permute-start.11 = (bf16[208,128]{1,0:T(8,128)(2,1)S(1)}, bf16[208,128]{1,0:T(8,128)(2,1)S(1)}, u32[]{:S(2)}, u32[]{:S(2)}) collective-permute-start(bf16[208,128]{1,0:T(8,128)(2,1)S(1)} %get-tuple-element.75), channel_id=1, source_target_pairs={{0,16},{1,17},{2,18},{3,19},{4,20},{5,21},{6,22},{7,23},{8,24},{9,... | collective-permute-start | bytes 159752 | tf_op jit(solution)/shard_map/ppermute | solution.py:44
  70.6 9.4 %collective-permute-start.12 = (bf16[208,128]{1,0:T(8,128)(2,1)S(1)}, bf16[208,128]{1,0:T(8,128)(2,1)S(1)}, u32[]{:S(2)}, u32[]{:S(2)}) collective-permute-start(bf16[208,128]{1,0:T(8,128)(2,1)S(1)} %get-tuple-element.76), channel_id=1, source_target_pairs={{0,8},{1,9},{2,10},{3,11},{4,12},{5,13},{6,14},{7,15},{8,16},{9,17... | collective-permute-start | bytes 159752 | tf_op jit(solution)/shard_map/ppermute | solution.py:44
  80.0 14.9 %collective-permute-start.13 = (bf16[2,1040,128]{2,1,0:T(8,128)(2,1)S(1)}, bf16[2,1040,128]{2,1,0:T(8,128)(2,1)S(1)}, u32[]{:S(2)}, u32[]{:S(2)}) collective-permute-start(bf16[2,1040,128]{2,1,0:T(8,128)(2,1)S(1)} %collective-permute-done.6.refs_0_), channel_id=1, source_target_pairs={{0,1},{1,2},{2,3},{3,4},{4,5},{5,6},{6,7},{7,0},{8,9},{9,10},{10,1... | collective-permute-start | bytes 1597448 | tf_op jit(solution)/shard_map/ppermute | solution.py:39
  81.6 14.0 %collective-permute-start.14 = (bf16[2,1040,128]{2,1,0:T(8,128)(2,1)S(1)}, bf16[2,1040,128]{2,1,0:T(8,128)(2,1)S(1)}, u32[]{:S(2)}, u32[]{:S(2)}) collective-permute-start(bf16[2,1040,128]{2,1,0:T(8,128)(2,1)S(1)} %collective-permute-done.7.refs_1_), channel_id=1, source_target_pairs={{0,7},{1,0},{2,1},{3,2},{4,3},{5,4},{6,5},{7,6},{8,15},{9,8},{10,9... | collective-permute-start | bytes 1597448 | tf_op jit(solution)/shard_map/ppermute | solution.py:39
  84.5 5.1 %collective-permute-start.15 = (bf16[208,256]{1,0:T(8,128)(2,1)S(1)}, bf16[208,256]{1,0:T(8,128)(2,1)S(1)}, u32[]{:S(2)}, u32[]{:S(2)}) collective-permute-start(bf16[208,256]{1,0:T(8,128)(2,1)S(1)} %get-tuple-element.80), channel_id=1, source_target_pairs={{0,24},{1,25},{2,26},{3,27},{4,28},{5,29},{6,30},{7,31},{8,0},{9,1... | collective-permute-start | bytes 319496 | tf_op jit(solution)/shard_map/ppermute | solution.py:44
  86.0 6.4 %collective-permute-start.16 = (bf16[208,256]{1,0:T(8,128)(2,1)S(1)}, bf16[208,256]{1,0:T(8,128)(2,1)S(1)}, u32[]{:S(2)}, u32[]{:S(2)}) collective-permute-start(bf16[208,256]{1,0:T(8,128)(2,1)S(1)} %get-tuple-element.81), channel_id=1, source_target_pairs={{0,16},{1,17},{2,18},{3,19},{4,20},{5,21},{6,22},{7,23},{8,24},{9,... | collective-permute-start | bytes 319496 | tf_op jit(solution)/shard_map/ppermute | solution.py:44
  86.4 7.1 %collective-permute-start.17 = (bf16[208,256]{1,0:T(8,128)(2,1)S(1)}, bf16[208,256]{1,0:T(8,128)(2,1)S(1)}, u32[]{:S(2)}, u32[]{:S(2)}) collective-permute-start(bf16[208,256]{1,0:T(8,128)(2,1)S(1)} %get-tuple-element.82), channel_id=1, source_target_pairs={{0,8},{1,9},{2,10},{3,11},{4,12},{5,13},{6,14},{7,15},{8,16},{9,17... | collective-permute-start | bytes 319496 | tf_op jit(solution)/shard_map/ppermute | solution.py:44
  95.6 14.0 %collective-permute-start.18 = (bf16[2,1040,128]{2,1,0:T(8,128)(2,1)S(1)}, bf16[2,1040,128]{2,1,0:T(8,128)(2,1)S(1)}, u32[]{:S(2)}, u32[]{:S(2)}) collective-permute-start(bf16[2,1040,128]{2,1,0:T(8,128)(2,1)S(1)} %collective-permute-done.13.refs_0_), channel_id=1, source_target_pairs={{0,1},{1,2},{2,3},{3,4},{4,5},{5,6},{6,7},{7,0},{8,9},{9,10},{10,1... | collective-permute-start | bytes 1597448 | tf_op jit(solution)/shard_map/ppermute | solution.py:39
  98.2 12.1 %collective-permute-start.19 = (bf16[2,1040,128]{2,1,0:T(8,128)(2,1)S(1)}, bf16[2,1040,128]{2,1,0:T(8,128)(2,1)S(1)}, u32[]{:S(2)}, u32[]{:S(2)}) collective-permute-start(bf16[2,1040,128]{2,1,0:T(8,128)(2,1)S(1)} %collective-permute-done.14.refs_1_), channel_id=1, source_target_pairs={{0,7},{1,0},{2,1},{3,2},{4,3},{5,4},{6,5},{7,6},{8,15},{9,8},{10,9... | collective-permute-start | bytes 1597448 | tf_op jit(solution)/shard_map/ppermute | solution.py:39
  100.0 4.8 %collective-permute-start.20 = (bf16[208,256]{1,0:T(8,128)(2,1)S(1)}, bf16[208,256]{1,0:T(8,128)(2,1)S(1)}, u32[]{:S(2)}, u32[]{:S(2)}) collective-permute-start(bf16[208,256]{1,0:T(8,128)(2,1)S(1)} %get-tuple-element.86), channel_id=1, source_target_pairs={{0,24},{1,25},{2,26},{3,27},{4,28},{5,29},{6,30},{7,31},{8,0},{9,1... | collective-permute-start | bytes 319496 | tf_op jit(solution)/shard_map/ppermute | solution.py:44
  101.5 6.3 %collective-permute-start.21 = (bf16[208,256]{1,0:T(8,128)(2,1)S(1)}, bf16[208,256]{1,0:T(8,128)(2,1)S(1)}, u32[]{:S(2)}, u32[]{:S(2)}) collective-permute-start(bf16[208,256]{1,0:T(8,128)(2,1)S(1)} %get-tuple-element.87), channel_id=1, source_target_pairs={{0,16},{1,17},{2,18},{3,19},{4,20},{5,21},{6,22},{7,23},{8,24},{9,... | collective-permute-start | bytes 319496 | tf_op jit(solution)/shard_map/ppermute | solution.py:44
  101.8 7.0 %collective-permute-start.22 = (bf16[208,256]{1,0:T(8,128)(2,1)S(1)}, bf16[208,256]{1,0:T(8,128)(2,1)S(1)}, u32[]{:S(2)}, u32[]{:S(2)}) collective-permute-start(bf16[208,256]{1,0:T(8,128)(2,1)S(1)} %get-tuple-element.88), channel_id=1, source_target_pairs={{0,8},{1,9},{2,10},{3,11},{4,12},{5,13},{6,14},{7,15},{8,16},{9,17... | collective-permute-start | bytes 319496 | tf_op jit(solution)/shard_map/ppermute | solution.py:44
  110.4 7.8 %collective-permute-start.26 = (bf16[1040,128]{1,0:T(8,128)(2,1)S(1)}, bf16[1040,128]{1,0:T(8,128)(2,1)S(1)}, u32[]{:S(2)}, u32[]{:S(2)}) collective-permute-start(bf16[1040,128]{1,0:T(8,128)(2,1)S(1)} %slice_bitcast_fusion.1), channel_id=1, source_target_pairs={{0,1},{1,2},{2,3},{3,4},{4,5},{5,6},{6,7},{7,0},{8,9},{9,10},{10,1... | collective-permute-start | bytes 798728 | tf_op jit(solution)/shard_map/ppermute | solution.py:39
  112.3 6.7 %collective-permute-start.27 = (bf16[1040,128]{1,0:T(8,128)(2,1)S(1)}, bf16[1040,128]{1,0:T(8,128)(2,1)S(1)}, u32[]{:S(2)}, u32[]{:S(2)}) collective-permute-start(bf16[1040,128]{1,0:T(8,128)(2,1)S(1)} %slice_bitcast_fusion), channel_id=1, source_target_pairs={{0,7},{1,0},{2,1},{3,2},{4,3},{5,4},{6,5},{7,6},{8,15},{9,8},{10,9... | collective-permute-start | bytes 798728 | tf_op jit(solution)/shard_map/ppermute | solution.py:39
  115.1 8.2 %collective-permute-start.23 = (bf16[208,256]{1,0:T(8,128)(2,1)S(1)}, bf16[208,256]{1,0:T(8,128)(2,1)S(1)}, u32[]{:S(2)}, u32[]{:S(2)}) collective-permute-start(bf16[208,256]{1,0:T(8,128)(2,1)S(1)} %get-tuple-element.92), channel_id=1, source_target_pairs={{0,24},{1,25},{2,26},{3,27},{4,28},{5,29},{6,30},{7,31},{8,0},{9,1... | collective-permute-start | bytes 319496 | tf_op jit(solution)/shard_map/ppermute | solution.py:44
  116.7 8.3 %collective-permute-start.24 = (bf16[208,256]{1,0:T(8,128)(2,1)S(1)}, bf16[208,256]{1,0:T(8,128)(2,1)S(1)}, u32[]{:S(2)}, u32[]{:S(2)}) collective-permute-start(bf16[208,256]{1,0:T(8,128)(2,1)S(1)} %get-tuple-element.93), channel_id=1, source_target_pairs={{0,16},{1,17},{2,18},{3,19},{4,20},{5,21},{6,22},{7,23},{8,24},{9,... | collective-permute-start | bytes 319496 | tf_op jit(solution)/shard_map/ppermute | solution.py:44
  117.0 8.0 %collective-permute-start.25 = (bf16[208,256]{1,0:T(8,128)(2,1)S(1)}, bf16[208,256]{1,0:T(8,128)(2,1)S(1)}, u32[]{:S(2)}, u32[]{:S(2)}) collective-permute-start(bf16[208,256]{1,0:T(8,128)(2,1)S(1)} %get-tuple-element.94), channel_id=1, source_target_pairs={{0,8},{1,9},{2,10},{3,11},{4,12},{5,13},{6,14},{7,15},{8,16},{9,17... | collective-permute-start | bytes 319496 | tf_op jit(solution)/shard_map/ppermute | solution.py:44
  120.1 4.9 %collective-permute-start.28 = (bf16[208,128]{1,0:T(8,128)(2,1)S(1)}, bf16[208,128]{1,0:T(8,128)(2,1)S(1)}, u32[]{:S(2)}, u32[]{:S(2)}) collective-permute-start(bf16[208,128]{1,0:T(8,128)(2,1)S(1)} %get-tuple-element.98), channel_id=1, source_target_pairs={{0,24},{1,25},{2,26},{3,27},{4,28},{5,29},{6,30},{7,31},{8,0},{9,1... | collective-permute-start | bytes 159752 | tf_op jit(solution)/shard_map/ppermute | solution.py:44
  121.6 5.6 %collective-permute-start.29 = (bf16[208,128]{1,0:T(8,128)(2,1)S(1)}, bf16[208,128]{1,0:T(8,128)(2,1)S(1)}, u32[]{:S(2)}, u32[]{:S(2)}) collective-permute-start(bf16[208,128]{1,0:T(8,128)(2,1)S(1)} %get-tuple-element.99), channel_id=1, source_target_pairs={{0,16},{1,17},{2,18},{3,19},{4,20},{5,21},{6,22},{7,23},{8,24},{9,... | collective-permute-start | bytes 159752 | tf_op jit(solution)/shard_map/ppermute | solution.py:44
  123.4 5.3 %collective-permute-start.30 = (bf16[208,128]{1,0:T(8,128)(2,1)S(1)}, bf16[208,128]{1,0:T(8,128)(2,1)S(1)}, u32[]{:S(2)}, u32[]{:S(2)}) collective-permute-start(bf16[208,128]{1,0:T(8,128)(2,1)S(1)} %get-tuple-element.100), channel_id=1, source_target_pairs={{0,8},{1,9},{2,10},{3,11},{4,12},{5,13},{6,14},{7,15},{8,16},{9,17... | collective-permute-start | bytes 159752 | tf_op jit(solution)/shard_map/ppermute | solution.py:44

commit v6 on v5

--- a/solution.py
+++ b/solution.py
@@ -74,7 +74,7 @@
     return hi, mid, value - hi - mid
 
 
-def pack_queries_kernel(decay, q_hbm, out, q, sems):
+def pack_queries_kernel(decay, q_hbm, out_hbm, out, q, sems):
     cuts = [slice(n * QUART, (n + 1) * QUART) for n in range(NX)]
     copies = run_copies([(q_hbm.at[0, :, cut], q.at[:, cut]) for cut in cuts], sems)
     row = lax.broadcasted_iota(jnp.int32, (EXTRA, HD), 0)
@@ -85,20 +85,30 @@
     tail = rows.astype(BF)
     for n in range(NX * NZ):
         out[n, 2 * NODES :, :] = tail
-    for n in range(NX * NZ):
-        if n % NZ == 0:
-            copies[n // NZ].wait()
-        for j in range(2):
-            out[n, j * NODES : (j + 1) * NODES, :] = q[:, (2 * n + j) * HD : (2 * n + j + 1) * HD]
+    sends = []
+    for x in range(NX):
+        copies[x].wait()
+        for n in range(x * NZ, (x + 1) * NZ):
+            for j in range(2):
+                out[n, j * NODES : (j + 1) * NODES, :] = q[:, (2 * n + j) * HD : (2 * n + j + 1) * HD]
+        cut = pl.ds(x * NZ, NZ)
+        sends.append(pltpu.make_async_copy(out.at[cut], out_hbm.at[cut], sems.at[NX + x]))
+        sends[-1].start()
+    for send in sends:
+        send.wait()
 
 
 def pack_queries(decay, q):
     return pl.pallas_call(
         pack_queries_kernel,
         in_specs=[SMEM, HBM],
-        out_specs=VMEM,
+        out_specs=HBM,
         out_shape=jax.ShapeDtypeStruct((NX * NZ, QROWS, HD), BF),
-        scratch_shapes=[pltpu.VMEM((NODES, HEADS * HD), BF), pltpu.SemaphoreType.DMA((NX,))],
+        scratch_shapes=[
+            pltpu.VMEM((NX * NZ, QROWS, HD), BF),
+            pltpu.VMEM((NODES, HEADS * HD), BF),
+            pltpu.SemaphoreType.DMA((2 * NX,)),
+        ],
         cost_estimate=cost(0, 1_000_000),
         compiler_params=WIDEST,
     )(decay, q)
@@ -175,29 +185,41 @@
     )(w0, m0, m1, theirs)
 
 
-def inter_kernel(queries, states, *refs):
-    out, extras = refs[-2:]
-    for r in range(NX * NZ):
-        x, z = divmod(r, NZ)
-        for j in range(2):
-            rows = slice(j * NODES, (j + 1) * NODES)
-            inter = jnp.dot(queries[r, rows, :], states[r, j], preferred_element_type=F32)
-            out[z, x * NODES : (x + 1) * NODES, j * HD : (j + 1) * HD] = inter.astype(BF)
-        extras[r] = queries[r, 2 * NODES :, :]
-
-
-def inter_part(queries, states, marks):
+def inter_kernel(queries, states, out_hbm, extras_hbm, out, extras, sems):
+    sends = []
+    for z in range(NZ):
+        for x in range(NX):
+            r = x * NZ + z
+            for j in range(2):
+                rows = slice(j * NODES, (j + 1) * NODES)
+                inter = jnp.dot(queries[r, rows, :], states[r, j], preferred_element_type=F32)
+                out[z, x * NODES : (x + 1) * NODES, j * HD : (j + 1) * HD] = inter.astype(BF)
+            extras[r] = queries[r, 2 * NODES :, :]
+        sends.append(pltpu.make_async_copy(out.at[z], out_hbm.at[z], sems.at[z]))
+        sends[-1].start()
+    sends.append(pltpu.make_async_copy(extras, extras_hbm, sems.at[NZ]))
+    sends[-1].start()
+    for send in sends:
+        send.wait()
+
+
+def inter_part(queries, states):
     return pl.pallas_call(
         inter_kernel,
-        in_specs=[VMEM] * 2 + [ANY] * len(marks),
-        out_specs=[VMEM] * 2,
+        in_specs=[VMEM] * 2,
+        out_specs=[HBM] * 2,
         out_shape=[
             jax.ShapeDtypeStruct((NZ, ROWS, PAIR), BF),
             jax.ShapeDtypeStruct((NX * NZ, EXTRA, HD), BF),
         ],
+        scratch_shapes=[
+            pltpu.VMEM((NZ, ROWS, PAIR), BF),
+            pltpu.VMEM((NX * NZ, EXTRA, HD), BF),
+            pltpu.SemaphoreType.DMA((NZ + 1,)),
+        ],
         cost_estimate=cost(70_000_000, 4_000_000, 100_000),
         compiler_params=PARAMS,
-    )(queries, states, *marks)
+    )(queries, states)
 
 
 def decay_rows(extra):
@@ -308,31 +330,28 @@
     )(w, *messages)
 
 
-def merge_kernel(sizes, inter_hbm, gain_hbm, extras_hbm, anc_hbm, *refs):
-    intras, gates, refs = refs[:NX], refs[NX], refs[NX + 1 :]
-    out, inter_ref, gate_ref, gain, extras, tree, square_ref, sems = refs
+def merge_kernel(sizes, inter_ref, gain_hbm, extras_hbm, anc_hbm, *refs):
+    intras, gate_ref, refs = refs[:NX], refs[NX], refs[NX + 1 :]
+    out, gain, extras, tree, square_ref, sems = refs
     x, z = place()
     spots = [lax.rem(x - slot + NX, NX) for slot in range(NX)]
-    pairs = [(inter_hbm, inter_ref), (extras_hbm.at[pl.ds(x * NZ, NZ)], extras)]
+    pairs = [(extras_hbm.at[pl.ds(x * NZ, NZ)], extras)]
     pairs.append((gain_hbm.at[pl.ds(pl.multiple_of(x * 2 * NZ, 2 * NZ), 2 * NZ)], gain))
     for slot, xa in enumerate(spots):
         pairs.append((anc_hbm.at[xa * NZ + z], tree.at[slot]))
-        pairs.append((gates.at[slot], gate_ref.at[slot]))
     copies = run_copies(pairs, sems)
     node = lax.broadcasted_iota(jnp.int32, (NODES, HD), 0)
     lane = lax.broadcasted_iota(jnp.int32, (1, HD), 1)
-    copies[1].wait()
+    copies[0].wait()
     rates = jnp.zeros((1, HD), F32)
     for h in range(2 * NZ):
         rates = jnp.where(lane == h, decay_rows(extras[h // 2])[h % 2], rates)
-    copies[0].wait()
-    copies[2].wait()
+    copies[1].wait()
     for slot, xa in enumerate(spots):
         rows = pl.ds(pl.multiple_of(xa * NODES, NODES), NODES)
         half = lax.div(xa, 2)
         near = lax.rem(xa, 2) * NODES
-        for copy in copies[3 + 2 * slot : 5 + 2 * slot]:
-            copy.wait()
+        copies[2 + slot].wait()
         depth = jnp.sum(tree[slot].astype(F32), axis=1, keepdims=True)
         live = (node < sizes[xa * NZ + z]).astype(F32)
         fade = live * jnp.exp(-rates * depth)
@@ -361,17 +380,15 @@
 def merge(sizes, inter, gain, extras, anc, intras, gates):
     return pl.pallas_call(
         merge_kernel,
-        in_specs=[SMEM] + [HBM] * 4 + [VMEM] * NX + [HBM],
+        in_specs=[SMEM, VMEM] + [HBM] * 3 + [VMEM] * (NX + 1),
         out_specs=VMEM,
         out_shape=jax.ShapeDtypeStruct((2, PIECE, HD), BF),
         scratch_shapes=[
-            pltpu.VMEM((NZ, ROWS, PAIR), BF),
-            pltpu.VMEM((NX, NZ * NODES, PAIR), BF),
             pltpu.VMEM((2 * NZ, HD), F32),
             pltpu.VMEM((NZ, EXTRA, HD), BF),
             pltpu.VMEM((NX, NODES, NODES), jnp.int32),
             pltpu.VMEM((ROWS, HD), F32),
-            pltpu.SemaphoreType.DMA((3 + 2 * NX,)),
+            pltpu.SemaphoreType.DMA((2 + NX,)),
         ],
         cost_estimate=cost(10_000_000, 4_000_000),
         compiler_params=PARAMS,
@@ -465,7 +482,7 @@
     m0, m1, m2, m3 = pack_messages(gate, out_weight.T, packed)
     m2, m1, m3 = xsend(m2, 2), xsend(m1, 1), xsend(m3, 3)
     spread = lax.all_to_all(packed, "head", 0, 0, tiled=True)
-    inter, extras = inter_part(spread, states, [])
+    inter, extras = inter_part(spread, states)
     (inter,) = tie((inter,), m1, m3)
     inter = lax.all_to_all(inter, "head", 0, 0, axis_index_groups=ZLINES, tiled=True)
     t0, t1, t2, t3, mine = intra_part(tree_sizes, queries, keys, values, extras, ancestors, (m1, m2, m3))

time: 130 us -> 129 us (level)
  transfers between devices with their start and end apart: 33 -> 33, of which waited for: 19 -> 19; matrix products, arithmetic and copies ran while one was open for 0% -> 0% of each run, Pallas kernels for 17% -> 16%
where the time goes in v6:
time: 129 us
  starting transfers between devices  60.7 us (47%)
  waiting for transfers between devices  41.7 us (32%)
  Pallas kernels  24.2 us (19%)
  local copies, waits for them, and re-layouts  1.72 us (1%)
    ppermute x21, starting transfers between devices, xsend(): return lax.ppermute(array, 'head', pairs)  26.5 us
    ppermute x21, waiting for transfers between devices, xsend(): return lax.ppermute(array, 'head', pairs)  18.2 us
    ppermute x8, starting transfers between devices, zsend(): return lax.ppermute(array, 'head', pairs)  13.6 us
    ppermute x8, waiting for transfers between devices, zsend(): return lax.ppermute(array, 'head', pairs)  12.8 us
    all_to_all x1, starting transfers between devices, per_device(): spread = lax.all_to_all(packed, 'head', 0, 0, tiled=True)  11.3 us
    all_to_all x1, waiting for transfers between devices, per_device(): spread = lax.all_to_all(packed, 'head', 0, 0, tiled=True)  10.6 us
    all_to_all x1, starting transfers between devices, per_device(): lax.all_to_all(inter, 'head', 0, 0, axis_index_groups=ZLINES, tiled=True)  7.9 us
    pallas_call x1, Pallas kernels, intra_part(): pl.pallas_call(intra_kernel, in_specs=[SMEM] + [HBM] * 8, out_specs=[HBM]...  5.59 us
  transfers between devices with their start and end apart: 33, of which 19 were waited for; matrix products, arithmetic and copies ran while one was open for 0% of the time, Pallas kernels for 16%

profile of v6, /device:TPU:16, one launch (start us, length us, event | category | flops | bytes accessed | tf_op | source)
XLA Modules:
  0.0 128.9 jit_solution(11351355646744057902)
XLA Ops:
  0.0 2.5 %shard_map.100.after = bf16[32,72,128]{2,1,0:T(8,128)(2,1)} custom-call(f32[2]{0:T(128)} %decay.1, bf16[1,32,8192]{2,1,0:T(8,128)(2,1)} %q_hbm.3), custom_call_target="tpu_custom_call" | custom-call | bytes 1000000 | tf_op jit(solution)/shard_map/pallas_call | solution.py:102
  2.5 11.3 %all-to-all-start = ((bf16[32,72,128]{2,1,0:T(8,128)(2,1)}), bf16[32,72,128]{2,1,0:T(8,128)(2,1)S(1)}, u32[]{:S(2)}, u32[]{:S(2)}) async-start(bf16[32,72,128]{2,1,0:T(8,128)(2,1)} %shard_map.100.after), calls=%async_computation | async-start | bytes 1179648 | tf_op jit(solution)/shard_map/all_to_all | solution.py:484
  13.9 2.4 %shard_map.102 = (bf16[256,256]{1,0:T(8,128)(2,1)}, bf16[640,256]{1,0:T(8,128)(2,1)}, bf16[640,256]{1,0:T(8,128)(2,1)}, bf16[640,256]{1,0:T(8,128)(2,1)}) custom-call(bf16[1,32,8192]{2,1,0:T(8,128)(2,1)} %gate_hbm.1, bf16[192,8192]{1,0:T(8,128)(2,1)} %bitcast.12, bf16[32,72,128]{2,1,0:T(8,128)(2,1)} %shard_map.100.after), custom_call_target="tpu_custom_call" | custom-call | bytes 4000000 | tf_op jit(solution)/shard_map/pallas_call | solution.py:147
  16.3 1.9 %collective-permute-start = (bf16[640,256]{1,0:T(8,128)(2,1)}, bf16[640,256]{1,0:T(8,128)(2,1)S(1)}, u32[]{:S(2)}, u32[]{:S(2)}) collective-permute-start(bf16[640,256]{1,0:T(8,128)(2,1)} %get-tuple-element.54), channel_id=1, source_target_pairs={{0,8},{1,9},{2,10},{3,11},{4,12},{5,13},{6,14},{7,15},{8,16},{9,17... | collective-permute-start | bytes 983048 | tf_op jit(solution)/shard_map/ppermute | solution.py:44
  18.2 1.4 %collective-permute-start.1 = (bf16[640,256]{1,0:T(8,128)(2,1)}, bf16[640,256]{1,0:T(8,128)(2,1)S(1)}, u32[]{:S(2)}, u32[]{:S(2)}) collective-permute-start(bf16[640,256]{1,0:T(8,128)(2,1)} %get-tuple-element.55), channel_id=1, source_target_pairs={{0,24},{1,25},{2,26},{3,27},{4,28},{5,29},{6,30},{7,31},{8,0},{9,1... | collective-permute-start | bytes 983048 | tf_op jit(solution)/shard_map/ppermute | solution.py:44
  19.6 2.1 %collective-permute-start.2 = (bf16[640,256]{1,0:T(8,128)(2,1)}, bf16[640,256]{1,0:T(8,128)(2,1)}, u32[]{:S(2)}, u32[]{:S(2)}) collective-permute-start(bf16[640,256]{1,0:T(8,128)(2,1)} %get-tuple-element.58), channel_id=1, source_target_pairs={{0,16},{1,17},{2,18},{3,19},{4,20},{5,21},{6,22},{7,23},{8,24},{9,... | collective-permute-start | bytes 983048 | tf_op jit(solution)/shard_map/ppermute | solution.py:44
  21.7 10.6 %all-to-all-done.queries = bf16[32,72,128]{2,1,0:T(8,128)(2,1)S(1)} async-done(((bf16[32,72,128]{2,1,0:T(8,128)(2,1)}), bf16[32,72,128]{2,1,0:T(8,128)(2,1)S(1)}, u32[]{:S(2)}, u32[]{:S(2)}) %all-to-all-start) | async-done | bytes 589856 | tf_op jit(solution)/shard_map/all_to_all | solution.py:484
  32.3 1.4 %shard_map.101 = (bf16[8,128,256]{2,1,0:T(8,128)(2,1)}, bf16[32,8,128]{2,1,0:T(8,128)(2,1)S(1)}) custom-call(bf16[32,72,128]{2,1,0:T(8,128)(2,1)S(1)} %all-to-all-done.queries, bf16[32,2,128,128]{3,2,1,0:T(8,128)(2,1)S(1)} %copy-done.1), custom_call_target="tpu_custom_call" | custom-call | flops 70000000 | bytes 4000000 | tf_op jit(solution)/shard_map/pallas_call | solution.py:207
  34.4 7.9 %all-to-all-start.1 = ((bf16[8,128,256]{2,1,0:T(8,128)(2,1)}), bf16[8,128,256]{2,1,0:T(8,128)(2,1)S(1)}, u32[]{:S(2)}, u32[]{:S(2)}) async-start(bf16[8,128,256]{2,1,0:T(8,128)(2,1)} %get-tuple-element.56), calls=%async_computation.1 | async-start | bytes 1048576 | tf_op jit(solution)/shard_map/all_to_all | solution.py:487
  42.3 5.6 %shard_map.103 = (bf16[32,2048]{1,0:T(8,128)(2,1)}, bf16[32,2048]{1,0:T(8,128)(2,1)}, bf16[32,2048]{1,0:T(8,128)(2,1)}, bf16[32,2048]{1,0:T(8,128)(2,1)}, bf16[3,384,256]{2,1,0:T(8,128)(2,1)}) custom-call(s32[32]{0:T(128)} %sizes.3, bf16[1,32,8192]{2,1,0:T(8,128)(2,1)} %q_hbm.3, bf16[1,32,8192]{2,1,0:T(8,128)(2,1)} %k_hbm.1, bf16[1,32,8192]{2,1,0:T(8,128)(2,1)} %v_hbm.1, ...), custom_call_target="tpu_custom_call" | custom-call | flops 100000000 | bytes 4000000 | tf_op jit(solution)/shard_map/pallas_call | solution.py:284
  47.9 1.4 %collective-permute-start.8 = (bf16[3,384,256]{2,1,0:T(8,128)(2,1)}, bf16[3,384,256]{2,1,0:T(8,128)(2,1)S(1)}, u32[]{:S(2)}, u32[]{:S(2)}) collective-permute-start(bf16[3,384,256]{2,1,0:T(8,128)(2,1)} %get-tuple-element.71.m0), channel_id=1, source_target_pairs={{0,64},{32,96},{64,0},{96,32},{128,192},{160,224},{192,128},{224,1... | collective-permute-start | bytes 1769480 | tf_op jit(solution)/shard_map/ppermute | solution.py:48
  49.2 5.0 %collective-permute-start.4 = (bf16[32,2048]{1,0:T(8,128)(2,1)}, bf16[32,2048]{1,0:T(8,128)(2,1)S(1)}, u32[]{:S(2)}, u32[]{:S(2)}) collective-permute-start(bf16[32,2048]{1,0:T(8,128)(2,1)} %get-tuple-element.61), channel_id=1, source_target_pairs={{0,16},{1,17},{2,18},{3,19},{4,20},{5,21},{6,22},{7,23},{8,24},{9,... | collective-permute-start | bytes 393224 | tf_op jit(solution)/shard_map/ppermute | solution.py:44
  54.3 1.7 %collective-permute-done.3.refs_1_ = bf16[32,2048]{1,0:T(8,128)(2,1)S(1)} collective-permute-done((bf16[32,2048]{1,0:T(8,128)(2,1)}, bf16[32,2048]{1,0:T(8,128)(2,1)S(1)}, u32[]{:S(2)}, u32[]{:S(2)}) %collective-permute-start.3) | collective-permute-done | bytes 131104 | tf_op jit(solution)/shard_map/ppermute | solution.py:44
  56.0 2.4 %shard_map.104 = (bf16[192,2048]{1,0:T(8,128)(2,1)}, bf16[4,256,256]{2,1,0:T(8,128)(2,1)}) custom-call(bf16[192,8192]{1,0:T(8,128)(2,1)} %bitcast.13, bf16[256,256]{1,0:T(8,128)(2,1)} %get-tuple-element.64.m0, bf16[640,256]{1,0:T(8,128)(2,1)} %copy-done.10, bf16[640,256]{1,0:T(8,128)(2,1)} %collective-permute-done.2.m2, bf16[640,256]{1,0:T(8,128)(2,1)} %copy-done.11), custom_call_target="tpu_custom_call" | custom-call | bytes 3000000 | tf_op jit(solution)/shard_map/pallas_call | solution.py:318
  59.5 1.0 copy-done.4
  60.5 2.1 %shard_map.105.refs_0_ = bf16[2,1040,128]{2,1,0:T(8,128)(2,1)S(1)} custom-call(s32[32]{0:T(128)S(1)} %copy-done.9, bf16[8,128,256]{2,1,0:T(8,128)(2,1)S(1)} %all-to-all-done.1.inter_ref, f32[64,128]{1,0:T(8,128)S(1)} %bitcast.11, bf16[32,8,128]{2,1,0:T(8,128)(2,1)S(1)} %copy-done.6, s32[32,32,32]{2,1,0:T(8,128)S(1)} %copy-done.2, ...), custom_call_target="tpu_custom_call" | custom-call | flops 10000000 | bytes 4000000 | tf_op jit(solution)/shard_map/pallas_call | solution.py:381
  62.9 2.1 %collective-permute-start.6 = (bf16[2,1040,128]{2,1,0:T(8,128)(2,1)S(1)}, bf16[2,1040,128]{2,1,0:T(8,128)(2,1)S(1)}, u32[]{:S(2)}, u32[]{:S(2)}) collective-permute-start(bf16[2,1040,128]{2,1,0:T(8,128)(2,1)S(1)} %shard_map.105.refs_0_), channel_id=1, source_target_pairs={{0,1},{1,2},{2,3},{3,4},{4,5},{5,6},{6,7},{7,0},{8,9},{9,10},{10,1... | collective-permute-start | bytes 1597448 | tf_op jit(solution)/shard_map/ppermute | solution.py:39
  65.0 1.3 %collective-permute-start.7 = (bf16[2,1040,128]{2,1,0:T(8,128)(2,1)S(1)}, bf16[2,1040,128]{2,1,0:T(8,128)(2,1)S(1)}, u32[]{:S(2)}, u32[]{:S(2)}) collective-permute-start(bf16[2,1040,128]{2,1,0:T(8,128)(2,1)S(1)} %shard_map.105.refs_0_), channel_id=1, source_target_pairs={{0,7},{1,0},{2,1},{3,2},{4,3},{5,4},{6,5},{7,6},{8,15},{9,8},{10,9... | collective-permute-start | bytes 1597448 | tf_op jit(solution)/shard_map/ppermute | solution.py:39
  66.6 1.0 shard_map.107
  67.7 1.7 %collective-permute-start.10 = (bf16[208,128]{1,0:T(8,128)(2,1)S(1)}, bf16[208,128]{1,0:T(8,128)(2,1)S(1)}, u32[]{:S(2)}, u32[]{:S(2)}) collective-permute-start(bf16[208,128]{1,0:T(8,128)(2,1)S(1)} %get-tuple-element.74), channel_id=1, source_target_pairs={{0,24},{1,25},{2,26},{3,27},{4,28},{5,29},{6,30},{7,31},{8,0},{9,1... | collective-permute-start | bytes 159752 | tf_op jit(solution)/shard_map/ppermute | solution.py:44
  69.7 1.1 collective-permute-start.12
  70.8 8.0 %collective-permute-done.6.refs_0_ = bf16[2,1040,128]{2,1,0:T(8,128)(2,1)S(1)} collective-permute-done((bf16[2,1040,128]{2,1,0:T(8,128)(2,1)S(1)}, bf16[2,1040,128]{2,1,0:T(8,128)(2,1)S(1)}, u32[]{:S(2)}, u32[]{:S(2)}) %collective-permute-start.6) | collective-permute-done | bytes 532512 | tf_op jit(solution)/shard_map/ppermute | solution.py:39
  79.1 1.5 %collective-permute-start.13 = (bf16[2,1040,128]{2,1,0:T(8,128)(2,1)S(1)}, bf16[2,1040,128]{2,1,0:T(8,128)(2,1)S(1)}, u32[]{:S(2)}, u32[]{:S(2)}) collective-permute-start(bf16[2,1040,128]{2,1,0:T(8,128)(2,1)S(1)} %collective-permute-done.6.refs_0_), channel_id=1, source_target_pairs={{0,1},{1,2},{2,3},{3,4},{4,5},{5,6},{6,7},{7,0},{8,9},{9,10},{10,1... | collective-permute-start | bytes 1597448 | tf_op jit(solution)/shard_map/ppermute | solution.py:39
  80.7 1.8 %collective-permute-start.14 = (bf16[2,1040,128]{2,1,0:T(8,128)(2,1)S(1)}, bf16[2,1040,128]{2,1,0:T(8,128)(2,1)S(1)}, u32[]{:S(2)}, u32[]{:S(2)}) collective-permute-start(bf16[2,1040,128]{2,1,0:T(8,128)(2,1)S(1)} %collective-permute-done.7.refs_1_), channel_id=1, source_target_pairs={{0,7},{1,0},{2,1},{3,2},{4,3},{5,4},{6,5},{7,6},{8,15},{9,8},{10,9... | collective-permute-start | bytes 1597448 | tf_op jit(solution)/shard_map/ppermute | solution.py:39
  82.5 1.1 shard_map.108
  83.6 1.5 %collective-permute-start.15 = (bf16[208,256]{1,0:T(8,128)(2,1)S(1)}, bf16[208,256]{1,0:T(8,128)(2,1)S(1)}, u32[]{:S(2)}, u32[]{:S(2)}) collective-permute-start(bf16[208,256]{1,0:T(8,128)(2,1)S(1)} %get-tuple-element.80), channel_id=1, source_target_pairs={{0,24},{1,25},{2,26},{3,27},{4,28},{5,29},{6,30},{7,31},{8,0},{9,1... | collective-permute-start | bytes 319496 | tf_op jit(solution)/shard_map/ppermute | solution.py:44
  85.5 1.1 collective-permute-start.17
  86.6 2.1 %collective-permute-done.15.refs_5_ = bf16[208,256]{1,0:T(8,128)(2,1)S(1)} collective-permute-done((bf16[208,256]{1,0:T(8,128)(2,1)S(1)}, bf16[208,256]{1,0:T(8,128)(2,1)S(1)}, u32[]{:S(2)}, u32[]{:S(2)}) %collective-permute-start.15) | collective-permute-done | bytes 106528 | tf_op jit(solution)/shard_map/ppermute | solution.py:44
  88.7 2.8 %collective-permute-done.16.refs_6_ = bf16[208,256]{1,0:T(8,128)(2,1)S(1)} collective-permute-done((bf16[208,256]{1,0:T(8,128)(2,1)S(1)}, bf16[208,256]{1,0:T(8,128)(2,1)S(1)}, u32[]{:S(2)}, u32[]{:S(2)}) %collective-permute-start.16) | collective-permute-done | bytes 106528 | tf_op jit(solution)/shard_map/ppermute | solution.py:44
  92.5 1.5 %collective-permute-done.13.refs_0_ = bf16[2,1040,128]{2,1,0:T(8,128)(2,1)S(1)} collective-permute-done((bf16[2,1040,128]{2,1,0:T(8,128)(2,1)S(1)}, bf16[2,1040,128]{2,1,0:T(8,128)(2,1)S(1)}, u32[]{:S(2)}, u32[]{:S(2)}) %collective-permute-start.13) | collective-permute-done | bytes 532512 | tf_op jit(solution)/shard_map/ppermute | solution.py:39
  94.7 2.6 %collective-permute-start.18 = (bf16[2,1040,128]{2,1,0:T(8,128)(2,1)S(1)}, bf16[2,1040,128]{2,1,0:T(8,128)(2,1)S(1)}, u32[]{:S(2)}, u32[]{:S(2)}) collective-permute-start(bf16[2,1040,128]{2,1,0:T(8,128)(2,1)S(1)} %collective-permute-done.13.refs_0_), channel_id=1, source_target_pairs={{0,1},{1,2},{2,3},{3,4},{4,5},{5,6},{6,7},{7,0},{8,9},{9,10},{10,1... | collective-permute-start | bytes 1597448 | tf_op jit(solution)/shard_map/ppermute | solution.py:39
  97.9 1.1 shard_map.109
  99.1 1.5 %collective-permute-start.20 = (bf16[208,256]{1,0:T(8,128)(2,1)S(1)}, bf16[208,256]{1,0:T(8,128)(2,1)S(1)}, u32[]{:S(2)}, u32[]{:S(2)}) collective-permute-start(bf16[208,256]{1,0:T(8,128)(2,1)S(1)} %get-tuple-element.86), channel_id=1, source_target_pairs={{0,24},{1,25},{2,26},{3,27},{4,28},{5,29},{6,30},{7,31},{8,0},{9,1... | collective-permute-start | bytes 319496 | tf_op jit(solution)/shard_map/ppermute | solution.py:44
  101.0 1.1 collective-permute-start.22
  102.1 1.8 %collective-permute-done.20.refs_9_ = bf16[208,256]{1,0:T(8,128)(2,1)S(1)} collective-permute-done((bf16[208,256]{1,0:T(8,128)(2,1)S(1)}, bf16[208,256]{1,0:T(8,128)(2,1)S(1)}, u32[]{:S(2)}, u32[]{:S(2)}) %collective-permute-start.20) | collective-permute-done | bytes 106528 | tf_op jit(solution)/shard_map/ppermute | solution.py:44
  103.9 3.1 %collective-permute-done.21.refs_10_ = bf16[208,256]{1,0:T(8,128)(2,1)S(1)} collective-permute-done((bf16[208,256]{1,0:T(8,128)(2,1)S(1)}, bf16[208,256]{1,0:T(8,128)(2,1)S(1)}, u32[]{:S(2)}, u32[]{:S(2)}) %collective-permute-start.21) | collective-permute-done | bytes 106528 | tf_op jit(solution)/shard_map/ppermute | solution.py:44
  106.9 1.0 collective-permute-done.22.refs_11_
  109.5 1.9 %collective-permute-start.26 = (bf16[1040,128]{1,0:T(8,128)(2,1)S(1)}, bf16[1040,128]{1,0:T(8,128)(2,1)S(1)}, u32[]{:S(2)}, u32[]{:S(2)}) collective-permute-start(bf16[1040,128]{1,0:T(8,128)(2,1)S(1)} %slice_bitcast_fusion.1), channel_id=1, source_target_pairs={{0,1},{1,2},{2,3},{3,4},{4,5},{5,6},{6,7},{7,0},{8,9},{9,10},{10,1... | collective-permute-start | bytes 798728 | tf_op jit(solution)/shard_map/ppermute | solution.py:39
  111.4 1.7 %collective-permute-start.27 = (bf16[1040,128]{1,0:T(8,128)(2,1)S(1)}, bf16[1040,128]{1,0:T(8,128)(2,1)S(1)}, u32[]{:S(2)}, u32[]{:S(2)}) collective-permute-start(bf16[1040,128]{1,0:T(8,128)(2,1)S(1)} %slice_bitcast_fusion), channel_id=1, source_target_pairs={{0,7},{1,0},{2,1},{3,2},{4,3},{5,4},{6,5},{7,6},{8,15},{9,8},{10,9... | collective-permute-start | bytes 798728 | tf_op jit(solution)/shard_map/ppermute | solution.py:39
  113.1 1.1 shard_map.110
  114.3 1.5 %collective-permute-start.23 = (bf16[208,256]{1,0:T(8,128)(2,1)S(1)}, bf16[208,256]{1,0:T(8,128)(2,1)S(1)}, u32[]{:S(2)}, u32[]{:S(2)}) collective-permute-start(bf16[208,256]{1,0:T(8,128)(2,1)S(1)} %get-tuple-element.92), channel_id=1, source_target_pairs={{0,24},{1,25},{2,26},{3,27},{4,28},{5,29},{6,30},{7,31},{8,0},{9,1... | collective-permute-start | bytes 319496 | tf_op jit(solution)/shard_map/ppermute | solution.py:44
  116.1 1.1 collective-permute-start.25
  118.2 1.0 shard_map.111
  119.2 1.5 %collective-permute-start.28 = (bf16[208,128]{1,0:T(8,128)(2,1)S(1)}, bf16[208,128]{1,0:T(8,128)(2,1)S(1)}, u32[]{:S(2)}, u32[]{:S(2)}) collective-permute-start(bf16[208,128]{1,0:T(8,128)(2,1)S(1)} %get-tuple-element.98), channel_id=1, source_target_pairs={{0,24},{1,25},{2,26},{3,27},{4,28},{5,29},{6,30},{7,31},{8,0},{9,1... | collective-permute-start | bytes 159752 | tf_op jit(solution)/shard_map/ppermute | solution.py:44
  120.7 1.7 %collective-permute-start.29 = (bf16[208,128]{1,0:T(8,128)(2,1)S(1)}, bf16[208,128]{1,0:T(8,128)(2,1)S(1)}, u32[]{:S(2)}, u32[]{:S(2)}) collective-permute-start(bf16[208,128]{1,0:T(8,128)(2,1)S(1)} %get-tuple-element.99), channel_id=1, source_target_pairs={{0,16},{1,17},{2,18},{3,19},{4,20},{5,21},{6,22},{7,23},{8,24},{9,... | collective-permute-start | bytes 159752 | tf_op jit(solution)/shard_map/ppermute | solution.py:44
  123.1 1.0 shard_map.112.refs_8_
  124.1 2.2 %collective-permute-done.29.refs_6_ = bf16[208,128]{1,0:T(8,128)(2,1)S(1)} collective-permute-done((bf16[208,128]{1,0:T(8,128)(2,1)S(1)}, bf16[208,128]{1,0:T(8,128)(2,1)S(1)}, u32[]{:S(2)}, u32[]{:S(2)}) %collective-permute-start.29) | collective-permute-done | bytes 53280 | tf_op jit(solution)/shard_map/ppermute | solution.py:44
  126.4 1.5 %collective-permute-done.30.refs_7_ = bf16[208,128]{1,0:T(8,128)(2,1)S(1)} collective-permute-done((bf16[208,128]{1,0:T(8,128)(2,1)S(1)}, bf16[208,128]{1,0:T(8,128)(2,1)S(1)}, u32[]{:S(2)}, u32[]{:S(2)}) %collective-permute-start.30) | collective-permute-done | bytes 53280 | tf_op jit(solution)/shard_map/ppermute | solution.py:44
  (59 shorter events, 10.1 us)
Async XLA Ops:
  2.5 29.8 %all-to-all-start = ((bf16[32,72,128]{2,1,0:T(8,128)(2,1)}), bf16[32,72,128]{2,1,0:T(8,128)(2,1)S(1)}, u32[]{:S(2)}, u32[]{:S(2)}) async-start(bf16[32,72,128]{2,1,0:T(8,128)(2,1)} %shard_map.100.after), calls=%async_computation | async-start | bytes 1179648 | tf_op jit(solution)/shard_map/all_to_all | solution.py:484
  13.9 18.5 %copy-start.1 = (bf16[32,2,128,128]{3,2,1,0:T(8,128)(2,1)S(1)}, bf16[32,2,128,128]{3,2,1,0:T(8,128)(2,1)}, u32[]{:S(2)}) copy-start(bf16[32,2,128,128]{3,2,1,0:T(8,128)(2,1)} %states.1) | copy-start | bytes 6291460
  16.3 18.0 %collective-permute-start = (bf16[640,256]{1,0:T(8,128)(2,1)}, bf16[640,256]{1,0:T(8,128)(2,1)S(1)}, u32[]{:S(2)}, u32[]{:S(2)}) collective-permute-start(bf16[640,256]{1,0:T(8,128)(2,1)} %get-tuple-element.54), channel_id=1, source_target_pairs={{0,8},{1,9},{2,10},{3,11},{4,12},{5,13},{6,14},{7,15},{8,16},{9,17... | collective-permute-start | bytes 983048 | tf_op jit(solution)/shard_map/ppermute | solution.py:44
  18.2 16.2 %collective-permute-start.1 = (bf16[640,256]{1,0:T(8,128)(2,1)}, bf16[640,256]{1,0:T(8,128)(2,1)S(1)}, u32[]{:S(2)}, u32[]{:S(2)}) collective-permute-start(bf16[640,256]{1,0:T(8,128)(2,1)} %get-tuple-element.55), channel_id=1, source_target_pairs={{0,24},{1,25},{2,26},{3,27},{4,28},{5,29},{6,30},{7,31},{8,0},{9,1... | collective-permute-start | bytes 983048 | tf_op jit(solution)/shard_map/ppermute | solution.py:44
  19.6 22.6 %collective-permute-start.2 = (bf16[640,256]{1,0:T(8,128)(2,1)}, bf16[640,256]{1,0:T(8,128)(2,1)}, u32[]{:S(2)}, u32[]{:S(2)}) collective-permute-start(bf16[640,256]{1,0:T(8,128)(2,1)} %get-tuple-element.58), channel_id=1, source_target_pairs={{0,16},{1,17},{2,18},{3,19},{4,20},{5,21},{6,22},{7,23},{8,24},{9,... | collective-permute-start | bytes 983048 | tf_op jit(solution)/shard_map/ppermute | solution.py:44
  33.7 0.6 copy-start.5
  34.3 7.9 %copy-start.10 = (bf16[640,256]{1,0:T(8,128)(2,1)}, bf16[640,256]{1,0:T(8,128)(2,1)S(1)}, u32[]{:S(2)}) copy-start(bf16[640,256]{1,0:T(8,128)(2,1)S(1)} %collective-permute-done.m1) | copy-start | bytes 983044
  34.3 7.9 %copy-start.11 = (bf16[640,256]{1,0:T(8,128)(2,1)}, bf16[640,256]{1,0:T(8,128)(2,1)S(1)}, u32[]{:S(2)}) copy-start(bf16[640,256]{1,0:T(8,128)(2,1)S(1)} %collective-permute-done.1.m3) | copy-start | bytes 983044
  34.4 25.1 %all-to-all-start.1 = ((bf16[8,128,256]{2,1,0:T(8,128)(2,1)}), bf16[8,128,256]{2,1,0:T(8,128)(2,1)S(1)}, u32[]{:S(2)}, u32[]{:S(2)}) async-start(bf16[8,128,256]{2,1,0:T(8,128)(2,1)} %get-tuple-element.56), calls=%async_computation.1 | async-start | bytes 1048576 | tf_op jit(solution)/shard_map/all_to_all | solution.py:487
  47.9 14.8 %collective-permute-start.8 = (bf16[3,384,256]{2,1,0:T(8,128)(2,1)}, bf16[3,384,256]{2,1,0:T(8,128)(2,1)S(1)}, u32[]{:S(2)}, u32[]{:S(2)}) collective-permute-start(bf16[3,384,256]{2,1,0:T(8,128)(2,1)} %get-tuple-element.71.m0), channel_id=1, source_target_pairs={{0,64},{32,96},{64,0},{96,32},{128,192},{160,224},{192,128},{224,1... | collective-permute-start | bytes 1769480 | tf_op jit(solution)/shard_map/ppermute | solution.py:48
  49.2 6.7 %collective-permute-start.3 = (bf16[32,2048]{1,0:T(8,128)(2,1)}, bf16[32,2048]{1,0:T(8,128)(2,1)S(1)}, u32[]{:S(2)}, u32[]{:S(2)}) collective-permute-start(bf16[32,2048]{1,0:T(8,128)(2,1)} %get-tuple-element.60), channel_id=1, source_target_pairs={{0,8},{1,9},{2,10},{3,11},{4,12},{5,13},{6,14},{7,15},{8,16},{9,17... | collective-permute-start | bytes 393224 | tf_op jit(solution)/shard_map/ppermute | solution.py:44
  49.2 9.6 %collective-permute-start.4 = (bf16[32,2048]{1,0:T(8,128)(2,1)}, bf16[32,2048]{1,0:T(8,128)(2,1)S(1)}, u32[]{:S(2)}, u32[]{:S(2)}) collective-permute-start(bf16[32,2048]{1,0:T(8,128)(2,1)} %get-tuple-element.61), channel_id=1, source_target_pairs={{0,16},{1,17},{2,18},{3,19},{4,20},{5,21},{6,22},{7,23},{8,24},{9,... | collective-permute-start | bytes 393224 | tf_op jit(solution)/shard_map/ppermute | solution.py:44
  54.3 5.2 %collective-permute-start.5 = (bf16[32,2048]{1,0:T(8,128)(2,1)}, bf16[32,2048]{1,0:T(8,128)(2,1)S(1)}, u32[]{:S(2)}, u32[]{:S(2)}) collective-permute-start(bf16[32,2048]{1,0:T(8,128)(2,1)} %get-tuple-element.62), channel_id=1, source_target_pairs={{0,24},{1,25},{2,26},{3,27},{4,28},{5,29},{6,30},{7,31},{8,0},{9,1... | collective-permute-start | bytes 393224 | tf_op jit(solution)/shard_map/ppermute | solution.py:44
  56.0 3.5 %copy-start.2 = (s32[32,32,32]{2,1,0:T(8,128)S(1)}, s32[32,32,32]{2,1,0:T(8,128)}, u32[]{:S(2)}) copy-start(s32[32,32,32]{2,1,0:T(8,128)} %anc_hbm.3) | copy-start | bytes 393220
  56.0 3.5 %copy-start.6 = (bf16[32,8,128]{2,1,0:T(8,128)(2,1)S(1)}, bf16[32,8,128]{2,1,0:T(8,128)(2,1)}, u32[]{:S(2)}) copy-start(bf16[32,8,128]{2,1,0:T(8,128)(2,1)} %copy-done.5) | copy-start | bytes 196612
  56.0 3.5 %copy-start.7 = (bf16[32,2048]{1,0:T(8,128)(2,1)S(1)}, bf16[32,2048]{1,0:T(8,128)(2,1)}, u32[]{:S(2)}) copy-start(bf16[32,2048]{1,0:T(8,128)(2,1)} %get-tuple-element.59.refs_0_) | copy-start | bytes 393220
  56.0 3.5 %copy-start.8 = (f32[8192]{0:T(1024)S(1)}, f32[8192]{0:T(1024)}, u32[]{:S(2)}) copy-start(f32[8192]{0:T(1024)} %param.18) | copy-start | bytes 98308
  56.0 3.5 %copy-start.9 = (s32[32]{0:T(128)S(1)}, s32[32]{0:T(128)}, u32[]{:S(2)}) copy-start(s32[32]{0:T(128)} %sizes.3) | copy-start | bytes 388
  59.5 1.0 copy-start.4
  60.5 2.1 %copy-start = (bf16[3,384,256]{2,1,0:T(8,128)(2,1)S(1)}, bf16[3,384,256]{2,1,0:T(8,128)(2,1)}, u32[]{:S(2)}) copy-start(bf16[3,384,256]{2,1,0:T(8,128)(2,1)} %get-tuple-element.71.m0) | copy-start | bytes 1769476
  62.7 3.6 %copy-start.3 = (bf16[192,2048]{1,0:T(8,128)(2,1)S(1)}, bf16[192,2048]{1,0:T(8,128)(2,1)}, u32[]{:S(2)}) copy-start(bf16[192,2048]{1,0:T(8,128)(2,1)} %get-tuple-element.69.w0) | copy-start | bytes 2359300
  62.8 3.5 %collective-permute-start.9 = (bf16[2,3,384,256]{3,2,1,0:T(8,128)(2,1)S(1)}, bf16[2,3,384,256]{3,2,1,0:T(8,128)(2,1)S(1)}, u32[]{:S(2)}, u32[]{:S(2)}) collective-permute-start(bf16[2,3,384,256]{3,2,1,0:T(8,128)(2,1)S(1)} %pad_maximum_fusion), channel_id=1, source_target_pairs={{0,32},{32,0},{64,96},{96,64},{128,160},{160,128},{192,224},{224,1... | collective-permute-start | bytes 3538952 | tf_op jit(solution)/shard_map/ppermute | solution.py:52
  62.9 16.0 %collective-permute-start.6 = (bf16[2,1040,128]{2,1,0:T(8,128)(2,1)S(1)}, bf16[2,1040,128]{2,1,0:T(8,128)(2,1)S(1)}, u32[]{:S(2)}, u32[]{:S(2)}) collective-permute-start(bf16[2,1040,128]{2,1,0:T(8,128)(2,1)S(1)} %shard_map.105.refs_0_), channel_id=1, source_target_pairs={{0,1},{1,2},{2,3},{3,4},{4,5},{5,6},{6,7},{7,0},{8,9},{9,10},{10,1... | collective-permute-start | bytes 1597448 | tf_op jit(solution)/shard_map/ppermute | solution.py:39
  65.0 14.2 %collective-permute-start.7 = (bf16[2,1040,128]{2,1,0:T(8,128)(2,1)S(1)}, bf16[2,1040,128]{2,1,0:T(8,128)(2,1)S(1)}, u32[]{:S(2)}, u32[]{:S(2)}) collective-permute-start(bf16[2,1040,128]{2,1,0:T(8,128)(2,1)S(1)} %shard_map.105.refs_0_), channel_id=1, source_target_pairs={{0,7},{1,0},{2,1},{3,2},{4,3},{5,4},{6,5},{7,6},{8,15},{9,8},{10,9... | collective-permute-start | bytes 1597448 | tf_op jit(solution)/shard_map/ppermute | solution.py:39
  67.7 11.5 %collective-permute-start.10 = (bf16[208,128]{1,0:T(8,128)(2,1)S(1)}, bf16[208,128]{1,0:T(8,128)(2,1)S(1)}, u32[]{:S(2)}, u32[]{:S(2)}) collective-permute-start(bf16[208,128]{1,0:T(8,128)(2,1)S(1)} %get-tuple-element.74), channel_id=1, source_target_pairs={{0,24},{1,25},{2,26},{3,27},{4,28},{5,29},{6,30},{7,31},{8,0},{9,1... | collective-permute-start | bytes 159752 | tf_op jit(solution)/shard_map/ppermute | solution.py:44
  69.4 9.8 %collective-permute-start.11 = (bf16[208,128]{1,0:T(8,128)(2,1)S(1)}, bf16[208,128]{1,0:T(8,128)(2,1)S(1)}, u32[]{:S(2)}, u32[]{:S(2)}) collective-permute-start(bf16[208,128]{1,0:T(8,128)(2,1)S(1)} %get-tuple-element.75), channel_id=1, source_target_pairs={{0,16},{1,17},{2,18},{3,19},{4,20},{5,21},{6,22},{7,23},{8,24},{9,... | collective-permute-start | bytes 159752 | tf_op jit(solution)/shard_map/ppermute | solution.py:44
  69.7 9.4 %collective-permute-start.12 = (bf16[208,128]{1,0:T(8,128)(2,1)S(1)}, bf16[208,128]{1,0:T(8,128)(2,1)S(1)}, u32[]{:S(2)}, u32[]{:S(2)}) collective-permute-start(bf16[208,128]{1,0:T(8,128)(2,1)S(1)} %get-tuple-element.76), channel_id=1, source_target_pairs={{0,8},{1,9},{2,10},{3,11},{4,12},{5,13},{6,14},{7,15},{8,16},{9,17... | collective-permute-start | bytes 159752 | tf_op jit(solution)/shard_map/ppermute | solution.py:44
  79.1 14.9 %collective-permute-start.13 = (bf16[2,1040,128]{2,1,0:T(8,128)(2,1)S(1)}, bf16[2,1040,128]{2,1,0:T(8,128)(2,1)S(1)}, u32[]{:S(2)}, u32[]{:S(2)}) collective-permute-start(bf16[2,1040,128]{2,1,0:T(8,128)(2,1)S(1)} %collective-permute-done.6.refs_0_), channel_id=1, source_target_pairs={{0,1},{1,2},{2,3},{3,4},{4,5},{5,6},{6,7},{7,0},{8,9},{9,10},{10,1... | collective-permute-start | bytes 1597448 | tf_op jit(solution)/shard_map/ppermute | solution.py:39
  80.7 14.0 %collective-permute-start.14 = (bf16[2,1040,128]{2,1,0:T(8,128)(2,1)S(1)}, bf16[2,1040,128]{2,1,0:T(8,128)(2,1)S(1)}, u32[]{:S(2)}, u32[]{:S(2)}) collective-permute-start(bf16[2,1040,128]{2,1,0:T(8,128)(2,1)S(1)} %collective-permute-done.7.refs_1_), channel_id=1, source_target_pairs={{0,7},{1,0},{2,1},{3,2},{4,3},{5,4},{6,5},{7,6},{8,15},{9,8},{10,9... | collective-permute-start | bytes 1597448 | tf_op jit(solution)/shard_map/ppermute | solution.py:39
  83.6 5.1 %collective-permute-start.15 = (bf16[208,256]{1,0:T(8,128)(2,1)S(1)}, bf16[208,256]{1,0:T(8,128)(2,1)S(1)}, u32[]{:S(2)}, u32[]{:S(2)}) collective-permute-start(bf16[208,256]{1,0:T(8,128)(2,1)S(1)} %get-tuple-element.80), channel_id=1, source_target_pairs={{0,24},{1,25},{2,26},{3,27},{4,28},{5,29},{6,30},{7,31},{8,0},{9,1... | collective-permute-start | bytes 319496 | tf_op jit(solution)/shard_map/ppermute | solution.py:44
  85.1 6.4 %collective-permute-start.16 = (bf16[208,256]{1,0:T(8,128)(2,1)S(1)}, bf16[208,256]{1,0:T(8,128)(2,1)S(1)}, u32[]{:S(2)}, u32[]{:S(2)}) collective-permute-start(bf16[208,256]{1,0:T(8,128)(2,1)S(1)} %get-tuple-element.81), channel_id=1, source_target_pairs={{0,16},{1,17},{2,18},{3,19},{4,20},{5,21},{6,22},{7,23},{8,24},{9,... | collective-permute-start | bytes 319496 | tf_op jit(solution)/shard_map/ppermute | solution.py:44
  85.5 7.1 %collective-permute-start.17 = (bf16[208,256]{1,0:T(8,128)(2,1)S(1)}, bf16[208,256]{1,0:T(8,128)(2,1)S(1)}, u32[]{:S(2)}, u32[]{:S(2)}) collective-permute-start(bf16[208,256]{1,0:T(8,128)(2,1)S(1)} %get-tuple-element.82), channel_id=1, source_target_pairs={{0,8},{1,9},{2,10},{3,11},{4,12},{5,13},{6,14},{7,15},{8,16},{9,17... | collective-permute-start | bytes 319496 | tf_op jit(solution)/shard_map/ppermute | solution.py:44
  94.7 14.0 %collective-permute-start.18 = (bf16[2,1040,128]{2,1,0:T(8,128)(2,1)S(1)}, bf16[2,1040,128]{2,1,0:T(8,128)(2,1)S(1)}, u32[]{:S(2)}, u32[]{:S(2)}) collective-permute-start(bf16[2,1040,128]{2,1,0:T(8,128)(2,1)S(1)} %collective-permute-done.13.refs_0_), channel_id=1, source_target_pairs={{0,1},{1,2},{2,3},{3,4},{4,5},{5,6},{6,7},{7,0},{8,9},{9,10},{10,1... | collective-permute-start | bytes 1597448 | tf_op jit(solution)/shard_map/ppermute | solution.py:39
  97.3 12.1 %collective-permute-start.19 = (bf16[2,1040,128]{2,1,0:T(8,128)(2,1)S(1)}, bf16[2,1040,128]{2,1,0:T(8,128)(2,1)S(1)}, u32[]{:S(2)}, u32[]{:S(2)}) collective-permute-start(bf16[2,1040,128]{2,1,0:T(8,128)(2,1)S(1)} %collective-permute-done.14.refs_1_), channel_id=1, source_target_pairs={{0,7},{1,0},{2,1},{3,2},{4,3},{5,4},{6,5},{7,6},{8,15},{9,8},{10,9... | collective-permute-start | bytes 1597448 | tf_op jit(solution)/shard_map/ppermute | solution.py:39
  99.1 4.8 %collective-permute-start.20 = (bf16[208,256]{1,0:T(8,128)(2,1)S(1)}, bf16[208,256]{1,0:T(8,128)(2,1)S(1)}, u32[]{:S(2)}, u32[]{:S(2)}) collective-permute-start(bf16[208,256]{1,0:T(8,128)(2,1)S(1)} %get-tuple-element.86), channel_id=1, source_target_pairs={{0,24},{1,25},{2,26},{3,27},{4,28},{5,29},{6,30},{7,31},{8,0},{9,1... | collective-permute-start | bytes 319496 | tf_op jit(solution)/shard_map/ppermute | solution.py:44
  100.6 6.3 %collective-permute-start.21 = (bf16[208,256]{1,0:T(8,128)(2,1)S(1)}, bf16[208,256]{1,0:T(8,128)(2,1)S(1)}, u32[]{:S(2)}, u32[]{:S(2)}) collective-permute-start(bf16[208,256]{1,0:T(8,128)(2,1)S(1)} %get-tuple-element.87), channel_id=1, source_target_pairs={{0,16},{1,17},{2,18},{3,19},{4,20},{5,21},{6,22},{7,23},{8,24},{9,... | collective-permute-start | bytes 319496 | tf_op jit(solution)/shard_map/ppermute | solution.py:44
  101.0 7.0 %collective-permute-start.22 = (bf16[208,256]{1,0:T(8,128)(2,1)S(1)}, bf16[208,256]{1,0:T(8,128)(2,1)S(1)}, u32[]{:S(2)}, u32[]{:S(2)}) collective-permute-start(bf16[208,256]{1,0:T(8,128)(2,1)S(1)} %get-tuple-element.88), channel_id=1, source_target_pairs={{0,8},{1,9},{2,10},{3,11},{4,12},{5,13},{6,14},{7,15},{8,16},{9,17... | collective-permute-start | bytes 319496 | tf_op jit(solution)/shard_map/ppermute | solution.py:44
  109.5 7.8 %collective-permute-start.26 = (bf16[1040,128]{1,0:T(8,128)(2,1)S(1)}, bf16[1040,128]{1,0:T(8,128)(2,1)S(1)}, u32[]{:S(2)}, u32[]{:S(2)}) collective-permute-start(bf16[1040,128]{1,0:T(8,128)(2,1)S(1)} %slice_bitcast_fusion.1), channel_id=1, source_target_pairs={{0,1},{1,2},{2,3},{3,4},{4,5},{5,6},{6,7},{7,0},{8,9},{9,10},{10,1... | collective-permute-start | bytes 798728 | tf_op jit(solution)/shard_map/ppermute | solution.py:39
  111.4 6.7 %collective-permute-start.27 = (bf16[1040,128]{1,0:T(8,128)(2,1)S(1)}, bf16[1040,128]{1,0:T(8,128)(2,1)S(1)}, u32[]{:S(2)}, u32[]{:S(2)}) collective-permute-start(bf16[1040,128]{1,0:T(8,128)(2,1)S(1)} %slice_bitcast_fusion), channel_id=1, source_target_pairs={{0,7},{1,0},{2,1},{3,2},{4,3},{5,4},{6,5},{7,6},{8,15},{9,8},{10,9... | collective-permute-start | bytes 798728 | tf_op jit(solution)/shard_map/ppermute | solution.py:39
  114.3 8.2 %collective-permute-start.23 = (bf16[208,256]{1,0:T(8,128)(2,1)S(1)}, bf16[208,256]{1,0:T(8,128)(2,1)S(1)}, u32[]{:S(2)}, u32[]{:S(2)}) collective-permute-start(bf16[208,256]{1,0:T(8,128)(2,1)S(1)} %get-tuple-element.92), channel_id=1, source_target_pairs={{0,24},{1,25},{2,26},{3,27},{4,28},{5,29},{6,30},{7,31},{8,0},{9,1... | collective-permute-start | bytes 319496 | tf_op jit(solution)/shard_map/ppermute | solution.py:44
  115.8 8.3 %collective-permute-start.24 = (bf16[208,256]{1,0:T(8,128)(2,1)S(1)}, bf16[208,256]{1,0:T(8,128)(2,1)S(1)}, u32[]{:S(2)}, u32[]{:S(2)}) collective-permute-start(bf16[208,256]{1,0:T(8,128)(2,1)S(1)} %get-tuple-element.93), channel_id=1, source_target_pairs={{0,16},{1,17},{2,18},{3,19},{4,20},{5,21},{6,22},{7,23},{8,24},{9,... | collective-permute-start | bytes 319496 | tf_op jit(solution)/shard_map/ppermute | solution.py:44
  116.1 8.0 %collective-permute-start.25 = (bf16[208,256]{1,0:T(8,128)(2,1)S(1)}, bf16[208,256]{1,0:T(8,128)(2,1)S(1)}, u32[]{:S(2)}, u32[]{:S(2)}) collective-permute-start(bf16[208,256]{1,0:T(8,128)(2,1)S(1)} %get-tuple-element.94), channel_id=1, source_target_pairs={{0,8},{1,9},{2,10},{3,11},{4,12},{5,13},{6,14},{7,15},{8,16},{9,17... | collective-permute-start | bytes 319496 | tf_op jit(solution)/shard_map/ppermute | solution.py:44
  119.2 4.9 %collective-permute-start.28 = (bf16[208,128]{1,0:T(8,128)(2,1)S(1)}, bf16[208,128]{1,0:T(8,128)(2,1)S(1)}, u32[]{:S(2)}, u32[]{:S(2)}) collective-permute-start(bf16[208,128]{1,0:T(8,128)(2,1)S(1)} %get-tuple-element.98), channel_id=1, source_target_pairs={{0,24},{1,25},{2,26},{3,27},{4,28},{5,29},{6,30},{7,31},{8,0},{9,1... | collective-permute-start | bytes 159752 | tf_op jit(solution)/shard_map/ppermute | solution.py:44
  120.7 5.6 %collective-permute-start.29 = (bf16[208,128]{1,0:T(8,128)(2,1)S(1)}, bf16[208,128]{1,0:T(8,128)(2,1)S(1)}, u32[]{:S(2)}, u32[]{:S(2)}) collective-permute-start(bf16[208,128]{1,0:T(8,128)(2,1)S(1)} %get-tuple-element.99), channel_id=1, source_target_pairs={{0,16},{1,17},{2,18},{3,19},{4,20},{5,21},{6,22},{7,23},{8,24},{9,... | collective-permute-start | bytes 159752 | tf_op jit(solution)/shard_map/ppermute | solution.py:44
  122.5 5.3 %collective-permute-start.30 = (bf16[208,128]{1,0:T(8,128)(2,1)S(1)}, bf16[208,128]{1,0:T(8,128)(2,1)S(1)}, u32[]{:S(2)}, u32[]{:S(2)}) collective-permute-start(bf16[208,128]{1,0:T(8,128)(2,1)S(1)} %get-tuple-element.100), channel_id=1, source_target_pairs={{0,8},{1,9},{2,10},{3,11},{4,12},{5,13},{6,14},{7,15},{8,16},{9,17... | collective-permute-start | bytes 159752 | tf_op jit(solution)/shard_map/ppermute | solution.py:44
